TPU v7x, 128 devices: a whole 4x4x4 slice. The times are simulated.
128 devices in a mesh: batch: 16 (over z, y), tp: 8 (over x, core).
Axes of the slice: x: 4, y: 4, z: 4, core: 2. Of those that a mesh axis runs over, the one named last changes fastest.
Arguments:
- tokens: bfloat16 [1024, 6144], P('batch', 'tp'), may hold values from -6 to 6
- queries: bfloat16 [1024, 48, 128], P('batch', 'tp'), may hold values from -6 to 6
- new_keys: bfloat16 [1024, 8, 128], P('batch', 'tp'), may hold values from -6 to 6
- new_values: bfloat16 [1024, 8, 128], P('batch', 'tp'), may hold values from -16 to 16
- key_cache: bfloat16 [1024, 8, 128, 128], P('batch', 'tp'), may hold values from -6 to 6
- value_cache: bfloat16 [1024, 8, 128, 128], P('batch', 'tp'), may hold values from -16 to 16
- lengths: int32 [1024], P('batch'), may hold values from 1 to 128, 65536 in all
- routes: int32 [1024, 2], P('batch'), may hold values from 0 to 3, all different within a row; in each aligned block of 64 rows (0 to 63, 64 to 127, ...) at most 40 rows name the same one
- out_weight: bfloat16 [6144, 6144], P('tp'), may hold values from -0.078125 to 0.078125
- norm_gain: bfloat16 [6144], replicated, may hold values from 0.099609375 to 1.8984375
- router: float32 [6144, 4], replicated, may hold values from -0.078125 to 0.078125
- gate_weight: bfloat16 [6144, 32768], P(None, ('batch', 'tp')), may hold values from -0.078125 to 0.078125
- up_weight: bfloat16 [6144, 32768], P(None, ('batch', 'tp')), may hold values from -0.078125 to 0.078125
- down_weight: bfloat16 [32768, 6144], P(('batch', 'tp')), may hold values from -0.0625 to 0.0625
Outputs:
- mixed: bfloat16 [1024, 6144], P('batch', 'tp')
Inputs may be any that keep to these rules, and one draw needn't show every extreme that they name: `routes`: the two experts of a token differ. In each aligned block of 64 rows (the rows of one batch index) no expert is named by more than 40 rows, a bound that some block reaches.
All inputs are finite; a program needn't handle non-finite values. No bound on the sum of `lengths` on one device may be relied on, other than what follows from the above.
Results may differ from a plain program's by a relative error of at most 0.024.
Values may be sent and summed in bfloat16 or wider, within the bound.
No kernel may reach another device: no remote copies, remote signals or barrier semaphores. Data moves between devices by JAX's collectives and lax.ppermute only.
A program may use at most 128 MiB of HBM per device.

v0:
```python
import math

import jax
import jax.numpy as jnp
from jax import lax
from jax.sharding import PartitionSpec as P

CAP = 40


EPS = 1e-05


def attend_local(queries, new_keys, new_values, key_cache, value_cache, lengths):
    row_count, head_count, head_size = queries.shape
    kv_local = new_keys.shape[1]
    cache_len = key_cache.shape[2]
    grouped = queries.reshape(row_count, kv_local, head_count // kv_local, head_size)
    scale = 1.0 / math.sqrt(head_size)
    scores = (
        jnp.einsum("tgqd,tgld->tgql", grouped, key_cache, preferred_element_type=jnp.float32)
        * scale
    )
    own = jnp.einsum("tgqd,tgd->tgq", grouped, new_keys, preferred_element_type=jnp.float32) * scale
    position = jnp.arange(cache_len, dtype=jnp.int32)
    valid = position[None, None, None, :] < lengths[:, None, None, None]
    masked = jnp.where(valid, scores, -jnp.inf)
    top = jnp.maximum(jnp.max(masked, axis=-1), own)
    weights = jnp.where(valid, jnp.exp(scores - top[..., None]), 0.0)
    own_weight = jnp.exp(own - top)
    total = jnp.sum(weights, axis=-1) + own_weight
    probs = (weights / total[..., None]).astype(jnp.bfloat16)
    own_prob = (own_weight / total).astype(jnp.bfloat16)
    context = jnp.einsum("tgql,tgld->tgqd", probs, value_cache, preferred_element_type=jnp.float32)
    context = (
        context
        + own_prob.astype(jnp.float32)[..., None] * new_values.astype(jnp.float32)[:, :, None, :]
    )
    return context.astype(jnp.bfloat16).reshape(row_count, head_count * head_size)


def routing(routes, logits, expert_count, capacity):
    row_count = routes.shape[0]
    expert_ids = jnp.arange(expert_count, dtype=jnp.int32)
    picked = routes[:, :, None] == expert_ids[None, None, :]
    flat = picked.reshape(row_count * 2, expert_count).astype(jnp.int32)
    ranks = (jnp.cumsum(flat, axis=0) - flat).reshape(row_count, 2, expert_count)
    slot_index = jnp.sum(jnp.where(picked, ranks, 0), axis=-1)
    chosen = jnp.sum(jnp.where(picked, logits[:, None, :], 0.0), axis=-1)
    first_weight = jax.nn.sigmoid(chosen[:, 0] - chosen[:, 1])
    route_weights = jnp.stack([first_weight, 1.0 - first_weight], axis=1)
    slot_hit = slot_index[:, :, None] == jnp.arange(capacity, dtype=jnp.int32)[None, None, :]
    matched = picked[:, :, :, None] & slot_hit[:, :, None, :]
    selection = jnp.any(matched, axis=1).astype(jnp.bfloat16)
    weighted = jnp.sum(jnp.where(matched, route_weights[:, :, None, None], 0.0), axis=1)
    return (selection, weighted)


def dispatch(selection, normed, holder_count):
    gathered = jnp.einsum(
        "rec,rd->ecd", selection, normed, preferred_element_type=jnp.float32
    ).astype(jnp.bfloat16)
    return jnp.repeat(gathered, holder_count, axis=0)


def finish(gate, upper, down_weight, source_count, slot_count):
    activation = (jax.nn.silu(gate) * upper).astype(jnp.bfloat16)
    term = jnp.dot(activation, down_weight, preferred_element_type=jnp.float32)
    term = term.reshape(source_count, slot_count, down_weight.shape[1])
    summed = lax.psum_scatter(
        term.astype(jnp.bfloat16), "tp", scatter_dimension=2, tiled=True
    ).astype(jnp.float32)
    return lax.all_to_all(
        summed.astype(jnp.bfloat16), "batch", split_axis=0, concat_axis=0, tiled=True
    ).astype(summed.dtype)


def full_experts(gate_weight, up_weight, down_weight, arrivals):
    source_count, slot_count, width = arrivals.shape
    flat_rows = arrivals.reshape(source_count * slot_count, width)
    gate = jnp.dot(flat_rows, gate_weight, preferred_element_type=jnp.float32)
    upper = jnp.dot(flat_rows, up_weight, preferred_element_type=jnp.float32)
    return finish(gate, upper, down_weight, source_count, slot_count)


def shards(
    tokens,
    queries,
    new_keys,
    new_values,
    key_cache,
    value_cache,
    lengths,
    routes,
    out_weight,
    norm_gain,
    router,
    gate_weight,
    up_weight,
    down_weight,
):
    col_count = tokens.shape[1]
    tp_index = lax.axis_index("tp")
    expert_count = router.shape[1]
    holder_count = lax.axis_size("batch") // expert_count
    capacity = CAP
    context = attend_local(queries, new_keys, new_values, key_cache, value_cache, lengths)
    head_terms = jnp.dot(context, out_weight, preferred_element_type=jnp.float32)
    own_cols = lax.dynamic_slice_in_dim(
        head_terms, tp_index * col_count, col_count, 1
    ) + tokens.astype(jnp.float32)
    placed = lax.dynamic_update_slice_in_dim(head_terms, own_cols, tp_index * col_count, 1)
    hidden_full = lax.psum(placed.astype(jnp.bfloat16), "tp").astype(jnp.float32)
    inverse_rms = lax.rsqrt(jnp.mean(hidden_full * hidden_full, axis=-1, keepdims=True) + EPS)
    scaled = hidden_full * inverse_rms * norm_gain.astype(jnp.float32)
    logits = jnp.dot(scaled, router, precision=lax.Precision.HIGHEST)
    normed = scaled.astype(jnp.bfloat16)
    hidden_state = lax.dynamic_slice_in_dim(hidden_full, tp_index * col_count, col_count, 1)
    selection, weighted = routing(routes, logits, expert_count, capacity)
    outgoing = dispatch(selection, normed, holder_count)
    returned = full_experts(
        gate_weight,
        up_weight,
        down_weight,
        lax.all_to_all(outgoing, "batch", split_axis=0, concat_axis=0, tiled=True),
    )
    arrived = jnp.sum(returned.reshape(expert_count, holder_count, capacity, col_count), axis=1)
    mixture = jnp.einsum("rec,ecd->rd", weighted, arrived, precision=lax.Precision.HIGHEST)
    return (hidden_state + mixture).astype(jnp.bfloat16)


def solution(mesh):
    return jax.shard_map(
        shards,
        mesh=mesh,
        in_specs=(
            P("batch", "tp"),
            P("batch", "tp", None),
            P("batch", "tp", None),
            P("batch", "tp", None),
            P("batch", "tp", None, None),
            P("batch", "tp", None, None),
            P("batch"),
            P("batch", None),
            P("tp", None),
            P(),
            P(),
            P(None, ("batch", "tp")),
            P(None, ("batch", "tp")),
            P(("batch", "tp"), None),
        ),
        out_specs=P("batch", "tp"),
        check_vma=False,
    )
```

profile of v0, /device:TPU:1, one launch (start us, length us, event | category | flops | bytes accessed | tf_op | source)
XLA Modules:
  0.0 292.1 jit_solution(3115919316546346477)
XLA Ops:
  6.5 0.0 copy-start
  6.5 0.0 all-reduce.2.cloned.1.call-start
  6.5 0.0 copy-start.4
  6.5 0.9 iota_compare_fusion.2
  7.4 1.2 fusion.33
  8.6 2.9 %select_reduce_fusion = (f32[64,6]{1,0:T(8,128)S(1)}, f32[64,6,128]{2,1,0:T(8,128)S(1)}) fusion(pred[64,128]{1,0:T(8,128)(4,1)S(1)} %iota_compare_fusion.2, bf16[64,1,128,128]{3,2,1,0:T(8,128)(2,1)} %param.18, bf16[64,6,128]{2,0,1:T(8,128)(2,1)} %param.15), kind=kOutput, calls=%fused_computation.33 | convolution fusion | flops 12729984 | bytes 2401792 | tf_op jit(solution)/shard_map/tgqd,tgld->tgql/dot_general | solution.py:21
  11.6 0.2 fusion.31
  11.8 0.0 copy-done.4
  11.8 2.3 fusion.14
  14.2 0.0 copy-start.3
  14.2 6.6 %fusion.40 = f32[64,6144]{1,0:T(8,128)} fusion(bf16[768,6144]{1,0:T(8,128)(2,1)} %param.22, bf16[8,8,6,128]{3,2,1,0:T(8,128)(2,1)S(1)} %bitcast.54), kind=kOutput, calls=%fused_computation.46 | convolution fusion | flops 603979776 | bytes 11108352 | tf_op jit(solution)/shard_map/dot_general | solution.py:108
  20.8 0.0 copy-start.6
  20.8 0.0 copy-start.5
  20.8 0.0 copy-done.3
  20.8 1.7 add_dynamic-update-slice_fusion
  22.5 2.4 convert_element_type.61
  24.9 0.0 all-reduce.2.cloned.1.call-update
  24.9 0.0 reduce-scatter.2.cloned.1.call-start
  25.0 0.0 copy-done.6
  25.0 0.1 copy.29
  25.1 0.1 eq.51
  25.2 0.1 fusion.43
  25.3 0.2 reduce_window_sum.11
  25.5 0.2 select_reduce_fusion.1
  25.6 0.1 eq.55
  25.8 0.1 copy.30
  25.9 0.0 copy-done.5
  25.9 61.8 %all-reduce.2.cloned.1.call-done = bf16[64,6144]{1,0:T(8,128)(2,1)} async-done(((bf16[64,6144]{1,0:T(8,128)(2,1)}), bf16[64,6144]{1,0:T(8,128)(2,1)}) %all-reduce.2.cloned.1.call-update) | async-done | bytes 786448 | tf_op jit(solution)/shard_map/psum | solution.py:113
  87.7 1.4 multiply_reduce_fusion
  89.1 1.9 convolution_convert_fusion.1
  91.0 1.0 broadcast_in_dim.73
  92.0 0.0 copy-start.7
  92.0 94.6 %all_to_all.10 = bf16[16,40,6144]{2,1,0:T(8,128)(2,1)S(1)} all-to-all(bf16[16,40,6144]{2,1,0:T(8,128)(2,1)S(1)} %bitcast.50), channel_id=1, replica_groups=mesh['batch'=16,'tp'=8] {'batch'}, dimensions={0} | all-to-all | bytes 15728640 | tf_op jit(solution)/shard_map/all_to_all | solution.py:125
  186.6 0.0 copy-start.1
  186.6 3.2 %copy-done.1 = bf16[16,40,6144]{2,1,0:T(8,128)(2,1)} copy-done((bf16[16,40,6144]{2,1,0:T(8,128)(2,1)}, bf16[16,40,6144]{2,1,0:T(8,128)(2,1)S(1)}, u32[]{:S(2)}) %copy-start.1) | copy-done | bytes 7864344
  189.8 0.0 copy-done.7
  189.8 3.0 %fusion.49 = f32[640,256]{1,0:T(8,128)} fusion(bf16[640,6144]{1,0:T(8,128)(2,1)S(1)} %bitcast.52, bf16[6144,256]{1,0:T(8,128)(2,1)S(1)} %copy-done.7), kind=kOutput, calls=%fused_computation.69 | convolution fusion | flops 2013265920 | bytes 11665408 | tf_op jit(solution)/shard_map/dot_general | solution.py:81
  192.8 0.0 copy-done
  192.8 16.6 %convolution_convert_fusion = bf16[640,6144]{1,0:T(8,128)(2,1)} fusion(bf16[256,6144]{1,0:T(8,128)(2,1)S(1)} %copy-done, bf16[640,6144]{1,0:T(8,128)(2,1)} %bitcast.53, bf16[6144,256]{1,0:T(8,128)(2,1)} %param.26, f32[640,256]{1,0:T(8,128)} %fusion.49), kind=kOutput, calls=%fused_computation | convolution fusion | flops 4031447040 | bytes 22675456 | tf_op jit(solution)/shard_map/dot_general | solution.py:68
  209.4 0.0 reduce-scatter.2.cloned.1.call-update
  209.5 0.0 copy-start.8
  209.5 50.9 %reduce-scatter.2.cloned.1.call-done = bf16[16,40,768]{2,1,0:T(8,128)(2,1)} async-done(((bf16[16,40,6144]{2,1,0:T(8,128)(2,1)}), bf16[16,40,768]{2,1,0:T(8,128)(2,1)}) %reduce-scatter.2.cloned.1.call-update) | async-done | bytes 983056 | tf_op jit(solution)/shard_map/reduce_scatter | solution.py:70
  260.4 6.7 %all-to-all-start.1 = ((bf16[16,40,768]{2,1,0:T(8,128)(2,1)}), bf16[16,40,768]{2,1,0:T(8,128)(2,1)}, u32[]{:S(2)}, u32[]{:S(2)}) async-start(bf16[16,40,768]{2,1,0:T(8,128)(2,1)} %reduce-scatter.2.cloned.1.call-done), calls=%async_computation.2 | async-start | bytes 1966080 | tf_op jit(solution)/shard_map/all_to_all | solution.py:73
  267.1 0.0 copy-start.2
  267.1 2.5 convert_element_type.62
  269.6 0.0 copy-done.8
  269.6 0.0 copy-done.2
  269.6 1.5 fusion.5
  271.2 10.7 %all-to-all-done.1 = bf16[16,40,768]{2,1,0:T(8,128)(2,1)} async-done(((bf16[16,40,768]{2,1,0:T(8,128)(2,1)}), bf16[16,40,768]{2,1,0:T(8,128)(2,1)}, u32[]{:S(2)}, u32[]{:S(2)}) %all-to-all-start.1) | async-done | bytes 983072 | tf_op jit(solution)/shard_map/all_to_all | solution.py:73
  281.9 1.4 convert_reduce_fusion
  283.3 2.0 fusion.18
  (12 shorter events, 0.2 us)
Async XLA Ops:
  6.5 186.3 %copy-start = (bf16[256,6144]{1,0:T(8,128)(2,1)S(1)}, bf16[256,6144]{1,0:T(8,128)(2,1)}, u32[]{:S(2)}) copy-start(bf16[256,6144]{1,0:T(8,128)(2,1)} %param.27) | copy-start | bytes 9437188
  6.5 81.2 %all-reduce.2.cloned.1.call-start = ((), (), s32[]{:S(2)}) async-start(), calls=%async_computation.3 | async-start | bytes 1572864 | tf_op jit(solution)/shard_map/psum | solution.py:113
  6.5 5.3 %copy-start.4 = (bf16[64,1,128]{2,0,1:T(8,128)(2,1)S(1)}, bf16[64,1,128]{2,0,1:T(8,128)(2,1)}, u32[]{:S(2)}) copy-start(bf16[64,1,128]{2,0,1:T(8,128)(2,1)} %param.17) | copy-start | bytes 49156
  14.2 6.6 %copy-start.3 = (bf16[64,768]{1,0:T(8,128)(2,1)S(1)}, bf16[64,768]{1,0:T(8,128)(2,1)}, u32[]{:S(2)}) copy-start(bf16[64,768]{1,0:T(8,128)(2,1)} %param.14) | copy-start | bytes 294916
  20.8 4.2 %copy-start.6 = (s32[64,2]{0,1:T(2,128)S(1)}, s32[64,2]{0,1:T(2,128)}, u32[]{:S(2)}) copy-start(s32[64,2]{0,1:T(2,128)} %param.21) | copy-start | bytes 1540
  20.8 5.1 %copy-start.5 = (bf16[6144]{0:T(1024)(128)(2,1)S(1)}, bf16[6144]{0:T(1024)(128)(2,1)}, u32[]{:S(2)}) copy-start(bf16[6144]{0:T(1024)(128)(2,1)} %param.23) | copy-start | bytes 36868
  24.9 235.5 %reduce-scatter.2.cloned.1.call-start = ((), (), s32[]{:S(2)}) async-start(), calls=%async_computation.4 | async-start | bytes 8847360 | tf_op jit(solution)/shard_map/reduce_scatter | solution.py:70
  92.0 97.8 %copy-start.7 = (bf16[6144,256]{1,0:T(8,128)(2,1)S(1)}, bf16[6144,256]{1,0:T(8,128)(2,1)}, u32[]{:S(2)}) copy-start(bf16[6144,256]{1,0:T(8,128)(2,1)} %param.25) | copy-start | bytes 9437188
  186.6 3.2 %copy-start.1 = (bf16[16,40,6144]{2,1,0:T(8,128)(2,1)}, bf16[16,40,6144]{2,1,0:T(8,128)(2,1)S(1)}, u32[]{:S(2)}) copy-start(bf16[16,40,6144]{2,1,0:T(8,128)(2,1)S(1)} %all_to_all.10) | copy-start | bytes 23592964
  209.5 60.1 %copy-start.8 = (f32[6144,4]{0,1:T(4,128)S(1)}, f32[6144,4]{0,1:T(4,128)}, u32[]{:S(2)}) copy-start(f32[6144,4]{0,1:T(4,128)} %param.24) | copy-start | bytes 294916
  260.4 21.5 %all-to-all-start.1 = ((bf16[16,40,768]{2,1,0:T(8,128)(2,1)}), bf16[16,40,768]{2,1,0:T(8,128)(2,1)}, u32[]{:S(2)}, u32[]{:S(2)}) async-start(bf16[16,40,768]{2,1,0:T(8,128)(2,1)} %reduce-scatter.2.cloned.1.call-done), calls=%async_computation.2 | async-start | bytes 1966080 | tf_op jit(solution)/shard_map/all_to_all | solution.py:73
  267.1 2.5 copy-start.2
Sparse Core Ops, SparseCore 0:
  25.0 62.6 all-reduce.1
  209.6 50.7 reduce-scatter.1
where the time goes:
time: 296 us; the launch traced here: 292 us
  waiting for transfers between devices  123 us (42%)
  blocking collectives  94.6 us (32%)
  matrix products  38 us (13%)
  between operations  13.6 us (5%)
  other arithmetic  11 us (4%)
  starting transfers between devices  6.78 us (2%)
  local copies, waits for them, and re-layouts  4.59 us (2%)
    all_to_all x1, blocking collectives, shards(): lax.all_to_all(outgoing, 'batch', split_axis=0, concat_axis=0, tiled=True)  94.6 us
    psum x1, waiting for transfers between devices, shards(): lax.psum(placed.astype(jnp.bfloat16), 'tp').astype(jnp.float32)  61.8 us
    reduce_scatter x1, waiting for transfers between devices, finish(): lax.psum_scatter(term.astype(jnp.bfloat16), 'tp', scatter_dimension=2, ti...  50.9 us
    dot_general x1, matrix products, finish(): term = jnp.dot(activation, down_weight, preferred_element_type=jnp.float32)  16.6 us
    all_to_all x1, waiting for transfers between devices, finish(): lax.all_to_all(summed.astype(jnp.bfloat16), 'batch', split_axis=0, concat...  10.7 us
    all_to_all x1, starting transfers between devices, finish(): lax.all_to_all(summed.astype(jnp.bfloat16), 'batch', split_axis=0, concat...  6.74 us
    dot_general x1, matrix products, shards(): jnp.dot(context, out_weight, preferred_element_type=jnp.float32)  6.62 us
  transfers between devices with their start and end apart: 3, of which 3 were waited for; matrix products, arithmetic and copies ran while one was open for 2% of the time, Pallas kernels for 0%

commit v1 on v0

v1 whole, which is shorter than its diff:
```python
import functools
import math

import jax
import jax.numpy as jnp
from jax import lax
from jax.experimental import pallas as pl
from jax.experimental.pallas import tpu as pltpu
from jax.sharding import Mesh
from jax.sharding import PartitionSpec as P

CAP = 40
EPS = 1e-05
D = 6144
BLK = 768
ROWS = 160
HID = 256
OFFS = (0, 1, -1, 2)
AXES = ("z", "y", "x", "c")
VMEM = pl.BlockSpec(memory_space=pltpu.VMEM)
SMEM = pl.BlockSpec(memory_space=pltpu.SMEM)
LIMIT = 56 * 1024 * 1024


def device_index(z, y, x, c):
    return ((z * 4 + y) * 4 + x) * 2 + c


def second_pairs(shift):
    pairs = []
    for z in range(4):
        for y in range(4):
            for x in range(4):
                pairs.append((device_index(z, y, x, 0), device_index(z, (y + shift) % 4, x, 0)))
                pairs.append((device_index(z, y, x, 1), device_index(z, y, (x + shift) % 4, 1)))
    return pairs


def first_groups():
    four = range(4)
    groups = [[device_index(z, y, x, 0) for x in four for z in four] for y in four]
    groups += [[device_index(z, y, x, 1) for y in four for z in four] for x in four]
    return groups


def along_second(a, shift):
    return lax.ppermute(a, AXES, second_pairs(shift))


def along_first(a):
    return lax.all_to_all(a, AXES, 0, 0, tiled=True, axis_index_groups=first_groups())


def along_x(a, shift):
    return lax.ppermute(a, "x", [(i, (i + shift) % 4) for i in range(4)])


def swap_cores(a):
    return lax.ppermute(a, "c", [(0, 1), (1, 0)])


def attend_local(queries, new_keys, new_values, key_cache, value_cache, lengths):
    row_count, head_count, head_size = queries.shape
    kv_local = new_keys.shape[1]
    cache_len = key_cache.shape[2]
    grouped = queries.reshape(row_count, kv_local, head_count // kv_local, head_size)
    scale = 1.0 / math.sqrt(head_size)
    scores = (
        jnp.einsum("tgqd,tgld->tgql", grouped, key_cache, preferred_element_type=jnp.float32)
        * scale
    )
    own = jnp.einsum("tgqd,tgd->tgq", grouped, new_keys, preferred_element_type=jnp.float32) * scale
    position = jnp.arange(cache_len, dtype=jnp.int32)
    valid = position[None, None, None, :] < lengths[:, None, None, None]
    masked = jnp.where(valid, scores, -jnp.inf)
    top = jnp.maximum(jnp.max(masked, axis=-1), own)
    weights = jnp.where(valid, jnp.exp(scores - top[..., None]), 0.0)
    own_weight = jnp.exp(own - top)
    total = jnp.sum(weights, axis=-1) + own_weight
    probs = (weights / total[..., None]).astype(jnp.bfloat16)
    own_prob = (own_weight / total).astype(jnp.bfloat16)
    context = jnp.einsum("tgql,tgld->tgqd", probs, value_cache, preferred_element_type=jnp.float32)
    context = (
        context
        + own_prob.astype(jnp.float32)[..., None] * new_values.astype(jnp.float32)[:, :, None, :]
    )
    return context.astype(jnp.bfloat16).reshape(row_count, head_count * head_size)


def project_kernel(half_ref, context_ref, weight_ref, out_ref):
    out_ref[0] = jnp.dot(
        context_ref[...], weight_ref[...], preferred_element_type=jnp.float32
    ).astype(out_ref.dtype)


def project(half, context, out_weight, dtype):
    rows = context.shape[0]
    return pl.pallas_call(
        project_kernel,
        out_shape=jax.ShapeDtypeStruct((4, rows, BLK), dtype),
        grid_spec=pltpu.PrefetchScalarGridSpec(
            num_scalar_prefetch=1,
            grid=(4,),
            in_specs=[
                pl.BlockSpec((rows, BLK), lambda i, half: (0, 0)),
                pl.BlockSpec((BLK, BLK), lambda i, half: (0, 2 * i + half[0])),
            ],
            out_specs=pl.BlockSpec((1, rows, BLK), lambda i, half: (i, 0, 0)),
        ),
        compiler_params=pltpu.CompilerParams(vmem_limit_bytes=LIMIT),
        cost_estimate=pl.CostEstimate(
            flops=2 * rows * BLK * BLK * 4, bytes_accessed=BLK * BLK * 8, transcendentals=0
        ),
    )(half, context, out_weight)


def block_rows(index):
    return pl.ds(pl.multiple_of(index * BLK, BLK), BLK)


def line_rows(index):
    return pl.ds(pl.multiple_of(index * ROWS, ROWS), ROWS)


def enter_kernel(place, g0, g1, g2, g3, gate, up, gate_far, up_far, inverse, mine, far):
    x, y, c = place[0], place[1], place[2]
    pieces = (g0, g1, g2, g3)

    def squares(piece, block):
        value = piece.astype(jnp.float32) * inverse[pl.ds(block, 1), :]
        value = value * value
        total = value[:, :128]
        for i in range(1, BLK // 128):
            total += value[:, i * 128 : (i + 1) * 128]
        return total

    def dot(a, b):
        return jnp.dot(a, b, preferred_element_type=jnp.float32)

    @pl.when(c == 0)
    def _():
        for j, shift in enumerate(OFFS):
            rows = line_rows((y - shift + 4) % 4)
            parts = None
            for k in range(4):
                block = 2 * k
                piece = pieces[j][k * ROWS : (k + 1) * ROWS, :]
                terms = [
                    dot(piece, gate[block * BLK : (block + 1) * BLK, :]),
                    dot(piece, up[block * BLK : (block + 1) * BLK, :]),
                    dot(piece, gate_far[k * BLK : (k + 1) * BLK, :]),
                    dot(piece, up_far[k * BLK : (k + 1) * BLK, :]),
                    squares(piece, block),
                ]
                parts = terms if parts is None else [a + b for a, b in zip(parts, terms)]
            mine[rows, :HID] = parts[0]
            mine[rows, HID : 2 * HID] = parts[1]
            mine[rows, 2 * HID :] = parts[4]
            far[rows, :HID] = parts[2]
            far[rows, HID : 2 * HID] = parts[3]
            far[rows, 2 * HID :] = parts[4]

    @pl.when(c == 1)
    def _():
        for j, shift in enumerate(OFFS):
            k = (x - shift + 4) % 4
            block = 2 * k + 1

            def step(r, carry, j=j, k=k, block=block):
                rows = line_rows(r)
                piece = pieces[j][rows, :]
                square = squares(piece, block)
                terms = [
                    dot(piece, gate[block_rows(block), :]),
                    dot(piece, up[block_rows(block), :]),
                    square,
                    dot(piece, gate_far[block_rows(k), :]),
                    dot(piece, up_far[block_rows(k), :]),
                    square,
                ]
                spots = (slice(0, HID), slice(HID, 2 * HID), slice(2 * HID, None))
                for n, term in enumerate(terms):
                    ref = mine if n < 3 else far
                    if j == 0:
                        ref[rows, spots[n % 3]] = term
                    else:
                        ref[rows, spots[n % 3]] += term
                return carry

            lax.fori_loop(0, 4, step, 0)


def enter(place, pieces, gate, up, gate_far, up_far, inverse):
    shape = jax.ShapeDtypeStruct((4 * ROWS, 2 * HID + 128), jnp.float32)
    return pl.pallas_call(
        enter_kernel,
        out_shape=(shape, shape),
        in_specs=[SMEM] + [VMEM] * 9,
        out_specs=(VMEM, VMEM),
        compiler_params=pltpu.CompilerParams(vmem_limit_bytes=LIMIT),
        cost_estimate=pl.CostEstimate(
            flops=2 * 4 * ROWS * 4 * BLK * 4 * HID, bytes_accessed=4000000, transcendentals=0
        ),
    )(place, *pieces, gate, up, gate_far, up_far, inverse)


def activate_kernel(mine, far, out):
    for r in range(4):
        rows = slice(r * ROWS, (r + 1) * ROWS)
        total = mine[rows, :] + far[rows, :]
        mean = jnp.sum(total[:, 2 * HID :], axis=1, keepdims=True) * (1.0 / D)
        scale = lax.rsqrt(mean + EPS)
        gate = total[:, :HID] * scale
        upper = total[:, HID : 2 * HID] * scale
        out[rows, :] = (gate * (1.0 / (1.0 + jnp.exp(-gate))) * upper).astype(jnp.bfloat16)


def activate(mine, far):
    return pl.pallas_call(
        activate_kernel,
        out_shape=jax.ShapeDtypeStruct((4 * ROWS, HID), jnp.bfloat16),
        in_specs=[VMEM] * 2,
        out_specs=VMEM,
        compiler_params=pltpu.CompilerParams(vmem_limit_bytes=LIMIT),
    )(mine, far)


def leave_kernel(place, act, act_far, down, down_far, o0, o1, o2, o3):
    x, y, c = place[0], place[1], place[2]
    outs = (o0, o1, o2, o3)

    def dot(a, b):
        return jnp.dot(a, b, preferred_element_type=jnp.float32)

    @pl.when(c == 0)
    def _():
        for j, shift in enumerate(OFFS):
            rows = line_rows((y + shift + 4) % 4)
            for k in range(4):
                term = dot(act[rows, :], down[:, 2 * k * BLK : (2 * k + 1) * BLK])
                term += dot(act_far[rows, :], down_far[:, k * BLK : (k + 1) * BLK])
                outs[j][k * ROWS : (k + 1) * ROWS, :] = term.astype(jnp.bfloat16)

    @pl.when(c == 1)
    def _():
        for j, shift in enumerate(OFFS):
            k = (x + shift + 4) % 4

            def step(r, carry, j=j, k=k):
                rows = line_rows(r)
                term = dot(act[rows, :], down[:, block_rows(2 * k + 1)])
                term += dot(act_far[rows, :], down_far[:, block_rows(k)])
                outs[j][rows, :] = term.astype(jnp.bfloat16)
                return carry

            lax.fori_loop(0, 4, step, 0)


def leave(place, act, act_far, down, down_far):
    shape = jax.ShapeDtypeStruct((4 * ROWS, BLK), jnp.bfloat16)
    return pl.pallas_call(
        leave_kernel,
        out_shape=(shape,) * 4,
        in_specs=[SMEM] + [VMEM] * 4,
        out_specs=(VMEM,) * 4,
        compiler_params=pltpu.CompilerParams(vmem_limit_bytes=LIMIT),
        cost_estimate=pl.CostEstimate(
            flops=2 * 4 * ROWS * 4 * BLK * 2 * HID, bytes_accessed=4000000, transcendentals=0
        ),
    )(place, act, act_far, down, down_far)


def slots(routes, expert_count):
    row_count = routes.shape[0]
    expert_ids = jnp.arange(expert_count, dtype=jnp.int32)
    picked = routes[:, :, None] == expert_ids[None, None, :]
    flat = picked.reshape(row_count * 2, expert_count).astype(jnp.int32)
    ranks = (jnp.cumsum(flat, axis=0) - flat).reshape(row_count, 2, expert_count)
    slot_index = jnp.sum(jnp.where(picked, ranks, 0), axis=-1)
    slot_hit = slot_index[:, :, None] == jnp.arange(CAP, dtype=jnp.int32)[None, None, :]
    return picked, picked[:, :, :, None] & slot_hit[:, :, None, :]


def shards(
    tokens,
    queries,
    new_keys,
    new_values,
    key_cache,
    value_cache,
    lengths,
    routes,
    out_weight,
    norm_gain,
    router,
    gate_weight,
    up_weight,
    down_weight,
):
    row_count = tokens.shape[0]
    expert_count = router.shape[1]
    x, y, c = lax.axis_index("x"), lax.axis_index("y"), lax.axis_index("c")
    place = jnp.stack([x, y, c]).astype(jnp.int32)
    here = 2 * x + c

    def other_half(weight):
        return lax.dynamic_index_in_dim(weight.reshape(4, 2, BLK, HID), 1 - c, 1, keepdims=False)

    gate_far = swap_cores(other_half(gate_weight).reshape(4 * BLK, HID))
    up_far = swap_cores(other_half(up_weight).reshape(4 * BLK, HID))
    down_far = swap_cores(
        lax.dynamic_index_in_dim(
            down_weight.reshape(HID, 4, 2, BLK), 1 - c, 2, keepdims=False
        ).reshape(HID, 4 * BLK)
    )
    gain = norm_gain.astype(jnp.float32).reshape(8, BLK)
    inverse = 1.0 / gain

    context = attend_local(queries, new_keys, new_values, key_cache, value_cache, lengths)
    core = c.astype(jnp.int32)[None]
    for_other = project(1 - core, context, out_weight, jnp.bfloat16)
    from_other = swap_cores(for_other)
    terms = project(core, context, out_weight, jnp.float32) + from_other.astype(jnp.float32)

    def column(shift):
        return lax.dynamic_index_in_dim(terms, (x + shift + 4) % 4, 0, keepdims=False)

    hidden = column(0) + tokens.astype(jnp.float32)
    for shift in (2, 1, -1):
        hidden = hidden + along_x(column(shift).astype(jnp.bfloat16), shift).astype(jnp.float32)

    picked, matched = slots(routes, expert_count)
    scaled = hidden * lax.dynamic_index_in_dim(gain, here, 0)
    selection = jnp.any(matched, axis=1).astype(jnp.bfloat16)
    outgoing = jnp.einsum(
        "rec,rd->ecd", selection, scaled.astype(jnp.bfloat16), preferred_element_type=jnp.float32
    ).astype(jnp.bfloat16)
    outgoing = jnp.broadcast_to(outgoing[None], (4, 4, CAP, BLK)).reshape(16, CAP, BLK)
    line = along_first(outgoing).reshape(4 * ROWS, BLK)
    pieces = [line] + [along_second(line, shift) for shift in OFFS[1:]]

    own_router = lax.dynamic_slice_in_dim(router, here * BLK, BLK, 0)
    partial = jnp.concatenate(
        [
            jnp.dot(scaled, own_router, precision=lax.Precision.HIGHEST),
            jnp.sum(hidden * hidden, axis=1, keepdims=True),
        ],
        axis=1,
    )
    partial = jnp.pad(partial, ((0, 0), (0, 128 - partial.shape[1])))
    partial = partial + swap_cores(partial)
    stats = partial + along_x(partial, 1) + along_x(partial, -1) + along_x(partial, 2)
    inverse_rms = lax.rsqrt(stats[:, expert_count : expert_count + 1] * (1.0 / D) + EPS)
    logits = stats[:, :expert_count] * inverse_rms
    chosen = jnp.sum(jnp.where(picked, logits[:, None, :], 0.0), axis=-1)
    first_weight = jax.nn.sigmoid(chosen[:, 0] - chosen[:, 1])
    route_weights = jnp.stack([first_weight, 1.0 - first_weight], axis=1)
    weighted = jnp.sum(jnp.where(matched, route_weights[:, :, None, None], 0.0), axis=1)

    mine, far = enter(place, pieces, gate_weight, up_weight, gate_far, up_far, inverse)
    act = activate(mine, swap_cores(far))
    outs = leave(place, act, swap_cores(act), down_weight, down_far)
    total = outs[0].astype(jnp.float32)
    for out, shift in zip(outs[1:], OFFS[1:]):
        total = total + along_second(out, shift).astype(jnp.float32)
    returned = along_first(total.astype(jnp.bfloat16).reshape(16, CAP, BLK))
    arrived = jnp.sum(returned.reshape(4, 4, CAP, BLK).astype(jnp.float32), axis=0)
    mixture = jnp.einsum("rec,ecd->rd", weighted, arrived, precision=lax.Precision.HIGHEST)
    return (hidden + mixture).astype(jnp.bfloat16)


def solution(mesh):
    grid = Mesh(mesh.devices.reshape(4, 4, 4, 2), AXES)
    batch, tp = ("z", "y"), ("x", "c")
    return jax.shard_map(
        shards,
        mesh=grid,
        in_specs=(
            P(batch, tp),
            P(batch, tp, None),
            P(batch, tp, None),
            P(batch, tp, None),
            P(batch, tp, None, None),
            P(batch, tp, None, None),
            P(batch),
            P(batch, None),
            P(tp, None),
            P(),
            P(),
            P(None, (*batch, *tp)),
            P(None, (*batch, *tp)),
            P((*batch, *tp), None),
        ),
        out_specs=P(batch, tp),
        check_vma=False,
    )
```

time: 296 us -> 181 us (0.61); the launches traced: 292 us -> 180 us
  blocking collectives: 94.6 us -> 0 us
  waiting for transfers between devices: 123 us -> 64.8 us
  Pallas kernels: 0 us -> 35.5 us
  matrix products: 38 us -> 6.57 us
  starting transfers between devices: 6.78 us -> 35.2 us
  local copies, waits for them, and re-layouts: 4.59 us -> 30 us
  between operations: 13.6 us -> 0.3 us
  other arithmetic: 11 us -> 7.82 us
    all_to_all x1 -> x0, blocking collectives: 94.6 us -> none  [shards(): lax.all_to_all(outgoing, 'batch', split_axis=0, concat_axis=0, tiled=True)]
    psum x1 -> x0, waiting for transfers between devices: 61.8 us -> none  [shards(): lax.psum(placed.astype(jnp.bfloat16), 'tp').astype(jnp.float32)]
    reduce_scatter x1 -> x0, waiting for transfers between devices: 50.9 us -> none  [finish(): lax.psum_scatter(term.astype(jnp.bfloat16), 'tp', scatter_dimension=2, ti...]
    ppermute x0 -> x19, waiting for transfers between devices: none -> 44.7 us  [the longest x6 22.2 us: along_x(): return lax.ppermute(a, 'x', [(i, (i + shift) % 4) for i in range(4)])]
    pallas_call x0 -> x5, Pallas kernels: none -> 35.5 us  [the longest x1 13.5 us: enter(): pl.pallas_call(enter_kernel, out_shape=(shape, shape), in_specs=[SMEM] +...]
    dot_general x5 -> x2, matrix products: 29.6 us -> 1.12 us  [the longest x1 0.92 us: shards(): jnp.dot(scaled, own_router, precision=lax.Precision.HIGHEST)]
    ppermute x0 -> x19, starting transfers between devices: none -> 22 us  [the longest x6 10 us: along_x(): return lax.ppermute(a, 'x', [(i, (i + shift) % 4) for i in range(4)])]
    dynamic_slice x0 -> x4, local copies, waits for them, and re-layouts: none -> 17.3 us  [the longest x1 13.2 us: shards(): lax.dynamic_index_in_dim(down_weight.reshape(HID, 4, 2, BLK), 1 - c, 2, k...]
  transfers between devices with their start and end apart: 3 -> 21, of which waited for: 3 -> 11; matrix products, arithmetic and copies ran while one was open for 2% -> 17% of each run, Pallas kernels for 0% -> 4%
where the time goes in v1:
time: 181 us; the launch traced here: 180 us
  waiting for transfers between devices  64.8 us (36%)
  Pallas kernels  35.5 us (20%)
  starting transfers between devices  35.2 us (19%)
  local copies, waits for them, and re-layouts  30 us (17%)
  other arithmetic  7.82 us (4%)
  matrix products  6.57 us (4%)
    ppermute x6, waiting for transfers between devices, along_x(): return lax.ppermute(a, 'x', [(i, (i + shift) % 4) for i in range(4)])  22.2 us
    all_to_all x2, waiting for transfers between devices, along_first(): lax.all_to_all(a, AXES, 0, 0, tiled=True, axis_index_groups=first_groups())  20 us
    ppermute x6, waiting for transfers between devices, along_second(): return lax.ppermute(a, AXES, second_pairs(shift))  19.4 us
    pallas_call x1, Pallas kernels, enter(): pl.pallas_call(enter_kernel, out_shape=(shape, shape), in_specs=[SMEM] +...  13.5 us
    all_to_all x2, starting transfers between devices, along_first(): lax.all_to_all(a, AXES, 0, 0, tiled=True, axis_index_groups=first_groups())  13.3 us
    dynamic_slice x1, local copies, waits for them, and re-layouts, shards(): lax.dynamic_index_in_dim(down_weight.reshape(HID, 4, 2, BLK), 1 - c, 2, k...  13.2 us
    ppermute x6, starting transfers between devices, along_x(): return lax.ppermute(a, 'x', [(i, (i + shift) % 4) for i in range(4)])  10 us
    pallas_call x1, Pallas kernels, leave(): pl.pallas_call(leave_kernel, out_shape=(shape,) * 4, in_specs=[SMEM] + [V...  9.7 us
  transfers between devices with their start and end apart: 21, of which 11 were waited for; matrix products, arithmetic and copies ran while one was open for 17% of the time, Pallas kernels for 4%

profile of v1, /device:TPU:1, one launch (start us, length us, event | category | flops | bytes accessed | tf_op | source)
XLA Modules:
  0.0 180.2 jit_solution(2662685818553728265)
XLA Ops:
  0.0 0.9 iota_compare_fusion.3
  0.9 1.5 fusion.22
  2.4 2.2 %select_reduce_fusion = (f32[64,6]{1,0:T(8,128)S(1)}, f32[64,6,128]{2,1,0:T(8,128)S(1)}) fusion(pred[64,128]{1,0:T(8,128)(4,1)S(1)} %iota_compare_fusion.3, bf16[64,1,128,128]{3,2,1,0:T(8,128)(2,1)S(1)} %copy-done, bf16[64,6,128]{2,0,1:T(8,128)(2,1)} %param.15), kind=kOutput, calls=%fused_computation.17 | convolution fusion | flops 12729984 | bytes 2401792 | tf_op jit(solution)/shard_map/tgqd,tgld->tgql/dot_general | solution.py:69
  4.6 0.2 fusion.15
  4.9 0.7 fusion.10
  5.6 0.7 copy.59
  6.3 4.6 %shard_map.137 = bf16[4,64,768]{2,1,0:T(8,128)(2,1)} custom-call(s32[1]{0:T(128)S(6)} %sub.38.half_ref, bf16[64,768]{1,0:T(8,128)(2,1)} %bitcast.80, bf16[768,6144]{1,0:T(8,128)(2,1)} %weight_ref.3), custom_call_target="tpu_custom_call" | custom-call | flops 301989888 | bytes 4718592 | tf_op jit(solution)/shard_map/pallas_call | solution.py:98
  10.9 1.4 collective-permute-start
  12.3 4.7 %shard_map.136 = f32[4,64,768]{2,1,0:T(8,128)} custom-call(s32[1]{0:T(128)} %bitcast.half_ref, bf16[64,768]{1,0:T(8,128)(2,1)} %bitcast.81, bf16[768,6144]{1,0:T(8,128)(2,1)} %weight_ref.3), custom_call_target="tpu_custom_call" | custom-call | flops 301989888 | bytes 4718592 | tf_op jit(solution)/shard_map/pallas_call | solution.py:98
  17.0 0.1 copy.38
  17.1 0.1 eq.56
  17.2 0.1 fusion.36
  17.3 0.2 reduce_window_sum.11
  17.5 0.2 select_reduce_fusion.1
  17.7 0.1 eq.60
  17.8 0.1 copy.39
  18.0 1.2 convert_add_fusion
  19.2 2.9 %collective-permute-start.1 = (bf16[64,768]{1,0:T(8,128)(2,1)S(1)}, bf16[64,768]{1,0:T(8,128)(2,1)S(1)}, u32[]{:S(2)}, u32[]{:S(2)}) collective-permute-start(bf16[64,768]{1,0:T(8,128)(2,1)S(1)} %get-tuple-element.21), channel_id=1, source_target_pairs={{0,4},{2,6},{4,0},{6,2},{1,5},{3,7},{5,1},{7,3},{8,12},{10,14},{12... | collective-permute-start | bytes 294920 | tf_op jit(solution)/shard_map/ppermute | solution.py:55
  22.2 0.3 collective-permute-start.2
  22.5 2.4 %collective-permute-start.3 = (bf16[64,768]{1,0:T(8,128)(2,1)S(1)}, bf16[64,768]{1,0:T(8,128)(2,1)S(1)}, u32[]{:S(2)}, u32[]{:S(2)}) collective-permute-start(bf16[64,768]{1,0:T(8,128)(2,1)S(1)} %get-tuple-element.22), channel_id=1, source_target_pairs={{0,6},{2,0},{4,2},{6,4},{1,7},{3,1},{5,3},{7,5},{8,14},{10,8},{12,... | collective-permute-start | bytes 294920 | tf_op jit(solution)/shard_map/ppermute | solution.py:55
  24.9 0.4 collective-permute-done.1
  25.3 2.2 %collective-permute-done.2 = bf16[64,768]{1,0:T(8,128)(2,1)S(1)} collective-permute-done((bf16[64,768]{1,0:T(8,128)(2,1)S(1)}, bf16[64,768]{1,0:T(8,128)(2,1)S(1)}, u32[]{:S(2)}, u32[]{:S(2)}) %collective-permute-start.2) | collective-permute-done | bytes 98336 | tf_op jit(solution)/shard_map/ppermute | solution.py:55
  27.5 0.2 multiply_reduce_fusion
  27.6 0.2 convolution_convert_fusion
  27.9 1.0 broadcast_in_dim.82
  28.9 7.8 %all-to-all-start = ((bf16[16,40,768]{2,1,0:T(8,128)(2,1)}), bf16[16,40,768]{2,1,0:T(8,128)(2,1)S(1)}, u32[]{:S(2)}, u32[]{:S(2)}) async-start(bf16[16,40,768]{2,1,0:T(8,128)(2,1)} %bitcast.17), calls=%async_computation | async-start | bytes 1966080 | tf_op jit(solution)/shard_map/all_to_all | solution.py:51
  36.7 2.8 %constant_dynamic-slice_fusion.1 = bf16[4,1,768,256]{3,2,1,0:T(8,128)(2,1)} fusion(bf16[4,2,768,256]{3,2,1,0:T(8,128)(2,1)} %bitcast.82, s32[]{:T(128)S(6)} %select_n.83), kind=kLoop, calls=%fused_computation.69 | loop fusion | bytes 3145732 | tf_op jit(solution)/shard_map/jit(dynamic_index_in_dim)/dynamic_slice | solution.py:307
  39.5 1.1 collective-permute-start.11
  40.6 1.3 constant_dynamic-slice_fusion
  41.9 8.8 %all-to-all-done = bf16[16,40,768]{2,1,0:T(8,128)(2,1)S(1)} async-done(((bf16[16,40,768]{2,1,0:T(8,128)(2,1)}), bf16[16,40,768]{2,1,0:T(8,128)(2,1)S(1)}, u32[]{:S(2)}, u32[]{:S(2)}) %all-to-all-start) | async-done | bytes 983072 | tf_op jit(solution)/shard_map/all_to_all | solution.py:51
  50.7 2.0 %collective-permute-start.10 = (bf16[640,768]{1,0:T(8,128)(2,1)S(1)}, bf16[640,768]{1,0:T(8,128)(2,1)}, u32[]{:S(2)}, u32[]{:S(2)}) collective-permute-start(bf16[640,768]{1,0:T(8,128)(2,1)S(1)} %bitcast.76), channel_id=1, source_target_pairs={{0,16},{1,5},{2,18},{3,7},{4,20},{5,1},{6,22},{7,3},{8,24},{9,13},... | collective-permute-start | bytes 2949128 | tf_op jit(solution)/shard_map/ppermute | solution.py:47
  52.7 0.9 collective-permute-start.8
  53.7 1.7 collective-permute-start.9
  55.4 0.6 pad_add_fusion.place
  56.1 0.6 broadcast_divide_fusion.inverse
  56.7 8.9 %collective-permute-done.10.g3 = bf16[640,768]{1,0:T(8,128)(2,1)} collective-permute-done((bf16[640,768]{1,0:T(8,128)(2,1)S(1)}, bf16[640,768]{1,0:T(8,128)(2,1)}, u32[]{:S(2)}, u32[]{:S(2)}) %collective-permute-start.10) | collective-permute-done | bytes 983072 | tf_op jit(solution)/shard_map/ppermute | solution.py:47
  65.6 10.5 %collective-permute-done.8.g1 = bf16[640,768]{1,0:T(8,128)(2,1)} collective-permute-done((bf16[640,768]{1,0:T(8,128)(2,1)S(1)}, bf16[640,768]{1,0:T(8,128)(2,1)}, u32[]{:S(2)}, u32[]{:S(2)}) %collective-permute-start.8) | collective-permute-done | bytes 983072 | tf_op jit(solution)/shard_map/ppermute | solution.py:47
  76.1 13.5 %shard_map.138 = (f32[640,640]{1,0:T(8,128)}, f32[640,640]{1,0:T(8,128)}) custom-call(s32[3]{0:T(128)} %pad_add_fusion.place, bf16[640,768]{1,0:T(8,128)(2,1)} %bitcast.79, bf16[640,768]{1,0:T(8,128)(2,1)} %collective-permute-done.8.g1, bf16[640,768]{1,0:T(8,128)(2,1)} %collective-permute-done.9.g2, bf16[640,768]{1,0:T(8,128)(2,1)} %collective-permute-done.10.g3, ...), custom_call_target="tpu_custom_call" | custom-call | flops 4026531840 | bytes 4000000 | tf_op jit(solution)/shard_map/pallas_call | solution.py:195
  89.6 8.1 %reshape.168 = bf16[256,4,2,768]{3,2,1,0:T(2,128)(2,1)} reshape(bf16[256,6144]{1,0:T(8,128)(2,1)} %down.1) | data formatting | bytes 6291456 | tf_op jit(solution)/shard_map/reshape | solution.py:313
  97.7 13.2 %dynamic-slice_reduce_fusion = bf16[256,4,768]{2,1,0:T(4,128)(2,1)} fusion(bf16[256,4,2,768]{3,2,1,0:T(2,128)(2,1)} %reshape.168, s32[]{:T(128)S(6)} %select_n.83), kind=kLoop, calls=%fused_computation | loop fusion | bytes 3145732 | tf_op jit(solution)/shard_map/jit(dynamic_index_in_dim)/dynamic_slice | solution.py:312
  110.9 1.7 copy.49
  112.6 0.6 collective-permute-start.15
  113.2 3.0 %shard_map.139.act = bf16[640,256]{1,0:T(8,128)(2,1)} custom-call(f32[640,640]{1,0:T(8,128)} %get-tuple-element.11.mine, f32[640,640]{1,0:T(8,128)} %collective-permute-done.13.far), custom_call_target="tpu_custom_call" | custom-call | tf_op jit(solution)/shard_map/pallas_call | solution.py:219
  116.2 1.8 %collective-permute-done.14.act_far = bf16[640,256]{1,0:T(8,128)(2,1)S(1)} collective-permute-done((bf16[640,256]{1,0:T(8,128)(2,1)}, bf16[640,256]{1,0:T(8,128)(2,1)S(1)}, u32[]{:S(2)}, u32[]{:S(2)}) %collective-permute-start.14) | collective-permute-done | bytes 327712 | tf_op jit(solution)/shard_map/ppermute | solution.py:59
  118.0 0.7 copy-done.9
  118.7 9.7 %shard_map.140 = (bf16[640,768]{1,0:T(8,128)(2,1)}, bf16[640,768]{1,0:T(8,128)(2,1)}, bf16[640,768]{1,0:T(8,128)(2,1)}, bf16[640,768]{1,0:T(8,128)(2,1)}) custom-call(s32[3]{0:T(128)} %pad_add_fusion.place, bf16[640,256]{1,0:T(8,128)(2,1)} %shard_map.139.act, bf16[640,256]{1,0:T(8,128)(2,1)} %copy-done.9, bf16[256,6144]{1,0:T(8,128)(2,1)} %down.1, ...), custom_call_target="tpu_custom_call" | custom-call | flops 2013265920 | bytes 4000000 | tf_op jit(solution)/shard_map/pallas_call | solution.py:261
  128.4 1.8 %collective-permute-start.16 = (bf16[640,768]{1,0:T(8,128)(2,1)}, bf16[640,768]{1,0:T(8,128)(2,1)S(1)}, u32[]{:S(2)}, u32[]{:S(2)}) collective-permute-start(bf16[640,768]{1,0:T(8,128)(2,1)} %get-tuple-element.14), channel_id=1, source_target_pairs={{0,8},{1,3},{2,10},{3,5},{4,12},{5,7},{6,14},{7,1},{8,16},{9,11},{... | collective-permute-start | bytes 2949128 | tf_op jit(solution)/shard_map/ppermute | solution.py:47
  130.3 0.8 collective-permute-start.17
  131.1 1.3 collective-permute-start.18
  132.4 0.9 fusion.19
  133.3 0.1 select_maximum_fusion
  133.4 0.1 collective-permute-start.4
  133.5 1.2 collective-permute-done.4
  134.7 0.5 collective-permute-start.5
  135.3 2.2 %collective-permute-start.6 = (f32[64,128]{0,1:T(8,128)S(1)}, f32[64,128]{0,1:T(8,128)S(1)}, u32[]{:S(2)}, u32[]{:S(2)}) collective-permute-start(f32[64,128]{0,1:T(8,128)S(1)} %fusion.41), channel_id=1, source_target_pairs={{0,6},{2,0},{4,2},{6,4},{1,7},{3,1},{5,3},{7,5},{8,14},{10,8},{12,... | collective-permute-start | bytes 98312 | tf_op jit(solution)/shard_map/ppermute | solution.py:55
  137.5 16.7 %collective-permute-done.5 = f32[64,128]{0,1:T(8,128)S(1)} collective-permute-done((f32[64,128]{0,1:T(8,128)S(1)}, f32[64,128]{0,1:T(8,128)S(1)}, u32[]{:S(2)}, u32[]{:S(2)}) %collective-permute-start.5) | collective-permute-done | bytes 32800 | tf_op jit(solution)/shard_map/ppermute | solution.py:55
  154.2 1.7 collective-permute-start.7
  155.9 0.2 collective-permute-done.6
  156.1 2.7 %collective-permute-done.7 = f32[64,128]{0,1:T(8,128)S(1)} collective-permute-done((f32[64,128]{0,1:T(8,128)S(1)}, f32[64,128]{0,1:T(8,128)S(1)}, u32[]{:S(2)}, u32[]{:S(2)}) %collective-permute-start.7) | collective-permute-done | bytes 32800 | tf_op jit(solution)/shard_map/ppermute | solution.py:55
  158.8 3.2 %add_convert_fusion = bf16[640,768]{1,0:T(8,128)(2,1)} fusion(bf16[640,768]{1,0:T(8,128)(2,1)} %collective-permute-done.18, bf16[640,768]{1,0:T(8,128)(2,1)} %collective-permute-done.17, bf16[640,768]{1,0:T(8,128)(2,1)S(1)} %collective-permute-done.16, bf16[640,768]{1,0:T(8,128)(2,1)} %get-tuple-element.13), kind=kLoop, calls=%fused_computation.6 | loop fusion | flops 3932160 | bytes 4915200 | tf_op jit(solution)/shard_map/convert_element_type | solution.py:366
  162.1 5.5 %all-to-all-start.1 = ((bf16[16,40,768]{2,1,0:T(8,128)(2,1)}), bf16[16,40,768]{2,1,0:T(8,128)(2,1)S(1)}, u32[]{:S(2)}, u32[]{:S(2)}) async-start(bf16[16,40,768]{2,1,0:T(8,128)(2,1)} %bitcast.23), calls=%async_computation.1 | async-start | bytes 1966080 | tf_op jit(solution)/shard_map/all_to_all | solution.py:51
  167.7 11.3 %all-to-all-done.1 = bf16[16,40,768]{2,1,0:T(8,128)(2,1)S(1)} async-done(((bf16[16,40,768]{2,1,0:T(8,128)(2,1)}), bf16[16,40,768]{2,1,0:T(8,128)(2,1)S(1)}, u32[]{:S(2)}, u32[]{:S(2)}) %all-to-all-start.1) | async-done | bytes 983072 | tf_op jit(solution)/shard_map/all_to_all | solution.py:51
  179.0 0.1 convert_reduce_fusion
  179.1 1.1 fusion.14
  (49 shorter events, 0.4 us)
Async XLA Ops:
  0.0 2.4 %copy-start = (bf16[64,1,128,128]{3,2,1,0:T(8,128)(2,1)S(1)}, bf16[64,1,128,128]{3,2,1,0:T(8,128)(2,1)}, u32[]{:S(2)}) copy-start(bf16[64,1,128,128]{3,2,1,0:T(8,128)(2,1)} %param.18) | copy-start | bytes 6291460
  0.0 4.8 %copy-start.4 = (bf16[64,1,128]{2,0,1:T(8,128)(2,1)S(1)}, bf16[64,1,128]{2,0,1:T(8,128)(2,1)}, u32[]{:S(2)}) copy-start(bf16[64,1,128]{2,0,1:T(8,128)(2,1)} %param.17) | copy-start | bytes 49156
  0.0 4.9 %copy-start.7 = (bf16[64,1,128,128]{3,2,1,0:T(8,128)(2,1)S(1)}, bf16[64,1,128,128]{3,2,1,0:T(8,128)(2,1)}, u32[]{:S(2)}) copy-start(bf16[64,1,128,128]{3,2,1,0:T(8,128)(2,1)} %param.19) | copy-start | bytes 6291460
  10.9 7.1 %collective-permute-start = (bf16[4,64,768]{2,1,0:T(8,128)(2,1)}, bf16[4,64,768]{2,1,0:T(8,128)(2,1)S(1)}, u32[]{:S(2)}, u32[]{:S(2)}) collective-permute-start(bf16[4,64,768]{2,1,0:T(8,128)(2,1)} %shard_map.137), channel_id=1, source_target_pairs={{0,1},{1,0},{2,3},{3,2},{4,5},{5,4},{6,7},{7,6},{8,9},{9,8},{10,11... | collective-permute-start | bytes 1179656 | tf_op jit(solution)/shard_map/ppermute | solution.py:59
  12.3 4.7 %copy-start.5 = (bf16[6144]{0:T(1024)(128)(2,1)S(1)}, bf16[6144]{0:T(1024)(128)(2,1)}, u32[]{:S(2)}) copy-start(bf16[6144]{0:T(1024)(128)(2,1)} %param.23) | copy-start | bytes 36868
  12.3 4.7 %copy-start.6 = (s32[64,2]{0,1:T(2,128)S(1)}, s32[64,2]{0,1:T(2,128)}, u32[]{:S(2)}) copy-start(s32[64,2]{0,1:T(2,128)} %param.21) | copy-start | bytes 1540
  17.0 10.5 %copy-start.3 = (bf16[64,768]{1,0:T(8,128)(2,1)S(1)}, bf16[64,768]{1,0:T(8,128)(2,1)}, u32[]{:S(2)}) copy-start(bf16[64,768]{1,0:T(8,128)(2,1)} %param.14) | copy-start | bytes 294916
  19.2 6.0 %collective-permute-start.1 = (bf16[64,768]{1,0:T(8,128)(2,1)S(1)}, bf16[64,768]{1,0:T(8,128)(2,1)S(1)}, u32[]{:S(2)}, u32[]{:S(2)}) collective-permute-start(bf16[64,768]{1,0:T(8,128)(2,1)S(1)} %get-tuple-element.21), channel_id=1, source_target_pairs={{0,4},{2,6},{4,0},{6,2},{1,5},{3,7},{5,1},{7,3},{8,12},{10,14},{12... | collective-permute-start | bytes 294920 | tf_op jit(solution)/shard_map/ppermute | solution.py:55
  22.2 5.3 %collective-permute-start.2 = (bf16[64,768]{1,0:T(8,128)(2,1)S(1)}, bf16[64,768]{1,0:T(8,128)(2,1)S(1)}, u32[]{:S(2)}, u32[]{:S(2)}) collective-permute-start(bf16[64,768]{1,0:T(8,128)(2,1)S(1)} %get-tuple-element.23), channel_id=1, source_target_pairs={{0,2},{2,4},{4,6},{6,0},{1,3},{3,5},{5,7},{7,1},{8,10},{10,12},{12... | collective-permute-start | bytes 294920 | tf_op jit(solution)/shard_map/ppermute | solution.py:55
  22.5 5.0 %collective-permute-start.3 = (bf16[64,768]{1,0:T(8,128)(2,1)S(1)}, bf16[64,768]{1,0:T(8,128)(2,1)S(1)}, u32[]{:S(2)}, u32[]{:S(2)}) collective-permute-start(bf16[64,768]{1,0:T(8,128)(2,1)S(1)} %get-tuple-element.22), channel_id=1, source_target_pairs={{0,6},{2,0},{4,2},{6,4},{1,7},{3,1},{5,3},{7,5},{8,14},{10,8},{12,... | collective-permute-start | bytes 294920 | tf_op jit(solution)/shard_map/ppermute | solution.py:55
  28.9 21.8 %all-to-all-start = ((bf16[16,40,768]{2,1,0:T(8,128)(2,1)}), bf16[16,40,768]{2,1,0:T(8,128)(2,1)S(1)}, u32[]{:S(2)}, u32[]{:S(2)}) async-start(bf16[16,40,768]{2,1,0:T(8,128)(2,1)} %bitcast.17), calls=%async_computation | async-start | bytes 1966080 | tf_op jit(solution)/shard_map/all_to_all | solution.py:51
  36.7 4.0 %copy-start.2 = (bf16[6144,256]{1,0:T(8,128)(2,1)S(1)}, bf16[6144,256]{1,0:T(8,128)(2,1)}, u32[]{:S(2)}) copy-start(bf16[6144,256]{1,0:T(8,128)(2,1)} %up.1) | copy-start | bytes 9437188
  39.5 17.2 %collective-permute-start.11 = (bf16[3072,256]{1,0:T(8,128)(2,1)}, bf16[3072,256]{1,0:T(8,128)(2,1)}, u32[]{:S(2)}, u32[]{:S(2)}) collective-permute-start(bf16[3072,256]{1,0:T(8,128)(2,1)} %bitcast.20), channel_id=1, source_target_pairs={{0,1},{1,0},{2,3},{3,2},{4,5},{5,4},{6,7},{7,6},{8,9},{9,8},{10,11... | collective-permute-start | bytes 4718600 | tf_op jit(solution)/shard_map/ppermute | solution.py:59
  41.9 14.8 %collective-permute-start.12 = (bf16[3072,256]{1,0:T(8,128)(2,1)}, bf16[3072,256]{1,0:T(8,128)(2,1)}, u32[]{:S(2)}, u32[]{:S(2)}) collective-permute-start(bf16[3072,256]{1,0:T(8,128)(2,1)} %bitcast.22), channel_id=1, source_target_pairs={{0,1},{1,0},{2,3},{3,2},{4,5},{5,4},{6,7},{7,6},{8,9},{9,8},{10,11... | collective-permute-start | bytes 4718600 | tf_op jit(solution)/shard_map/ppermute | solution.py:59
  50.7 25.4 %copy-start.1 = (bf16[16,40,768]{2,1,0:T(8,128)(2,1)}, bf16[16,40,768]{2,1,0:T(8,128)(2,1)S(1)}, u32[]{:S(2)}) copy-start(bf16[16,40,768]{2,1,0:T(8,128)(2,1)S(1)} %all-to-all-done) | copy-start | bytes 2949124
  50.7 14.9 %collective-permute-start.10 = (bf16[640,768]{1,0:T(8,128)(2,1)S(1)}, bf16[640,768]{1,0:T(8,128)(2,1)}, u32[]{:S(2)}, u32[]{:S(2)}) collective-permute-start(bf16[640,768]{1,0:T(8,128)(2,1)S(1)} %bitcast.76), channel_id=1, source_target_pairs={{0,16},{1,5},{2,18},{3,7},{4,20},{5,1},{6,22},{7,3},{8,24},{9,13},... | collective-permute-start | bytes 2949128 | tf_op jit(solution)/shard_map/ppermute | solution.py:47
  52.7 23.3 %collective-permute-start.8 = (bf16[640,768]{1,0:T(8,128)(2,1)S(1)}, bf16[640,768]{1,0:T(8,128)(2,1)}, u32[]{:S(2)}, u32[]{:S(2)}) collective-permute-start(bf16[640,768]{1,0:T(8,128)(2,1)S(1)} %bitcast.77), channel_id=1, source_target_pairs={{0,8},{1,3},{2,10},{3,5},{4,12},{5,7},{6,14},{7,1},{8,16},{9,11},{... | collective-permute-start | bytes 2949128 | tf_op jit(solution)/shard_map/ppermute | solution.py:47
  53.7 22.5 %collective-permute-start.9 = (bf16[640,768]{1,0:T(8,128)(2,1)S(1)}, bf16[640,768]{1,0:T(8,128)(2,1)}, u32[]{:S(2)}, u32[]{:S(2)}) collective-permute-start(bf16[640,768]{1,0:T(8,128)(2,1)S(1)} %bitcast.78), channel_id=1, source_target_pairs={{0,24},{1,7},{2,26},{3,1},{4,28},{5,3},{6,30},{7,5},{8,0},{9,15},{... | collective-permute-start | bytes 2949128 | tf_op jit(solution)/shard_map/ppermute | solution.py:47
  89.6 23.5 %collective-permute-start.13 = (f32[640,640]{1,0:T(8,128)}, f32[640,640]{1,0:T(8,128)}, u32[]{:S(2)}, u32[]{:S(2)}) collective-permute-start(f32[640,640]{1,0:T(8,128)} %get-tuple-element.12), channel_id=1, source_target_pairs={{0,1},{1,0},{2,3},{3,2},{4,5},{5,4},{6,7},{7,6},{8,9},{9,8},{10,11... | collective-permute-start | bytes 4915208 | tf_op jit(solution)/shard_map/ppermute | solution.py:59
  112.6 3.6 %collective-permute-start.15 = (bf16[256,3072]{1,0:T(8,128)(2,1)S(1)}, bf16[256,3072]{1,0:T(8,128)(2,1)S(1)}, u32[]{:S(2)}, u32[]{:S(2)}) collective-permute-start(bf16[256,3072]{1,0:T(8,128)(2,1)S(1)} %bitcast.75), channel_id=1, source_target_pairs={{0,1},{1,0},{2,3},{3,2},{4,5},{5,4},{6,7},{7,6},{8,9},{9,8},{10,11... | collective-permute-start | bytes 4718600 | tf_op jit(solution)/shard_map/ppermute | solution.py:59
  116.2 1.8 %collective-permute-start.14 = (bf16[640,256]{1,0:T(8,128)(2,1)}, bf16[640,256]{1,0:T(8,128)(2,1)S(1)}, u32[]{:S(2)}, u32[]{:S(2)}) collective-permute-start(bf16[640,256]{1,0:T(8,128)(2,1)} %shard_map.139.act), channel_id=1, source_target_pairs={{0,1},{1,0},{2,3},{3,2},{4,5},{5,4},{6,7},{7,6},{8,9},{9,8},{10,11... | collective-permute-start | bytes 983048 | tf_op jit(solution)/shard_map/ppermute | solution.py:59
  116.2 1.8 %copy-start.8 = (bf16[256,3072]{1,0:T(8,128)(2,1)}, bf16[256,3072]{1,0:T(8,128)(2,1)S(1)}, u32[]{:S(2)}) copy-start(bf16[256,3072]{1,0:T(8,128)(2,1)S(1)} %collective-permute-done.15.down_far) | copy-start | bytes 4718596
  118.0 0.7 copy-start.9
  128.4 30.4 %collective-permute-start.16 = (bf16[640,768]{1,0:T(8,128)(2,1)}, bf16[640,768]{1,0:T(8,128)(2,1)S(1)}, u32[]{:S(2)}, u32[]{:S(2)}) collective-permute-start(bf16[640,768]{1,0:T(8,128)(2,1)} %get-tuple-element.14), channel_id=1, source_target_pairs={{0,8},{1,3},{2,10},{3,5},{4,12},{5,7},{6,14},{7,1},{8,16},{9,11},{... | collective-permute-start | bytes 2949128 | tf_op jit(solution)/shard_map/ppermute | solution.py:47
  130.3 28.5 %collective-permute-start.17 = (bf16[640,768]{1,0:T(8,128)(2,1)}, bf16[640,768]{1,0:T(8,128)(2,1)}, u32[]{:S(2)}, u32[]{:S(2)}) collective-permute-start(bf16[640,768]{1,0:T(8,128)(2,1)} %get-tuple-element.15), channel_id=1, source_target_pairs={{0,24},{1,7},{2,26},{3,1},{4,28},{5,3},{6,30},{7,5},{8,0},{9,15},{... | collective-permute-start | bytes 2949128 | tf_op jit(solution)/shard_map/ppermute | solution.py:47
  131.1 27.7 %collective-permute-start.18 = (bf16[640,768]{1,0:T(8,128)(2,1)}, bf16[640,768]{1,0:T(8,128)(2,1)}, u32[]{:S(2)}, u32[]{:S(2)}) collective-permute-start(bf16[640,768]{1,0:T(8,128)(2,1)} %get-tuple-element.16), channel_id=1, source_target_pairs={{0,16},{1,5},{2,18},{3,7},{4,20},{5,1},{6,22},{7,3},{8,24},{9,13},... | collective-permute-start | bytes 2949128 | tf_op jit(solution)/shard_map/ppermute | solution.py:47
  133.4 1.3 collective-permute-start.4
  134.7 19.4 %collective-permute-start.5 = (f32[64,128]{0,1:T(8,128)S(1)}, f32[64,128]{0,1:T(8,128)S(1)}, u32[]{:S(2)}, u32[]{:S(2)}) collective-permute-start(f32[64,128]{0,1:T(8,128)S(1)} %fusion.41), channel_id=1, source_target_pairs={{0,2},{2,4},{4,6},{6,0},{1,3},{3,5},{5,7},{7,1},{8,10},{10,12},{12... | collective-permute-start | bytes 98312 | tf_op jit(solution)/shard_map/ppermute | solution.py:55
  135.3 20.9 %collective-permute-start.6 = (f32[64,128]{0,1:T(8,128)S(1)}, f32[64,128]{0,1:T(8,128)S(1)}, u32[]{:S(2)}, u32[]{:S(2)}) collective-permute-start(f32[64,128]{0,1:T(8,128)S(1)} %fusion.41), channel_id=1, source_target_pairs={{0,6},{2,0},{4,2},{6,4},{1,7},{3,1},{5,3},{7,5},{8,14},{10,8},{12,... | collective-permute-start | bytes 98312 | tf_op jit(solution)/shard_map/ppermute | solution.py:55
  154.2 4.6 %collective-permute-start.7 = (f32[64,128]{0,1:T(8,128)S(1)}, f32[64,128]{0,1:T(8,128)S(1)}, u32[]{:S(2)}, u32[]{:S(2)}) collective-permute-start(f32[64,128]{0,1:T(8,128)S(1)} %fusion.41), channel_id=1, source_target_pairs={{0,4},{2,6},{4,0},{6,2},{1,5},{3,7},{5,1},{7,3},{8,12},{10,14},{12... | collective-permute-start | bytes 98312 | tf_op jit(solution)/shard_map/ppermute | solution.py:55
  162.1 16.9 %all-to-all-start.1 = ((bf16[16,40,768]{2,1,0:T(8,128)(2,1)}), bf16[16,40,768]{2,1,0:T(8,128)(2,1)S(1)}, u32[]{:S(2)}, u32[]{:S(2)}) async-start(bf16[16,40,768]{2,1,0:T(8,128)(2,1)} %bitcast.23), calls=%async_computation.1 | async-start | bytes 1966080 | tf_op jit(solution)/shard_map/all_to_all | solution.py:51

commit v2 on v1

v2 whole, which is shorter than its diff:
```python
import functools
import math

import jax
import jax.numpy as jnp
from jax import lax
from jax.experimental import pallas as pl
from jax.experimental.pallas import tpu as pltpu
from jax.sharding import Mesh
from jax.sharding import PartitionSpec as P

CAP = 40
EPS = 1e-05
D = 6144
BLK = 768
ROWS = 160
HID = 256
OFFS = (0, 1, -1, 2)
AXES = ("z", "y", "x", "c")
VMEM = pl.BlockSpec(memory_space=pltpu.VMEM)
SMEM = pl.BlockSpec(memory_space=pltpu.SMEM)
LIMIT = 16 * 1024 * 1024


def device_index(z, y, x, c):
    return ((z * 4 + y) * 4 + x) * 2 + c


def second_pairs(shift):
    pairs = []
    for z in range(4):
        for y in range(4):
            for x in range(4):
                pairs.append((device_index(z, y, x, 0), device_index(z, (y + shift) % 4, x, 0)))
                pairs.append((device_index(z, y, x, 1), device_index(z, y, (x + shift) % 4, 1)))
    return pairs


def first_groups():
    four = range(4)
    groups = [[device_index(z, y, x, 0) for x in four for z in four] for y in four]
    groups += [[device_index(z, y, x, 1) for y in four for z in four] for x in four]
    return groups


def along_second(a, shift):
    return lax.ppermute(a, AXES, second_pairs(shift))


def along_first(a):
    return lax.all_to_all(a, AXES, 0, 0, tiled=True, axis_index_groups=first_groups())


def along_x(a, shift):
    return lax.ppermute(a, "x", [(i, (i + shift) % 4) for i in range(4)])


def swap_cores(a):
    return lax.ppermute(a, "c", [(0, 1), (1, 0)])


def attend_local(queries, new_keys, new_values, key_cache, value_cache, lengths):
    row_count, head_count, head_size = queries.shape
    kv_local = new_keys.shape[1]
    cache_len = key_cache.shape[2]
    grouped = queries.reshape(row_count, kv_local, head_count // kv_local, head_size)
    scale = 1.0 / math.sqrt(head_size)
    scores = (
        jnp.einsum("tgqd,tgld->tgql", grouped, key_cache, preferred_element_type=jnp.float32)
        * scale
    )
    own = jnp.einsum("tgqd,tgd->tgq", grouped, new_keys, preferred_element_type=jnp.float32) * scale
    position = jnp.arange(cache_len, dtype=jnp.int32)
    valid = position[None, None, None, :] < lengths[:, None, None, None]
    masked = jnp.where(valid, scores, -jnp.inf)
    top = jnp.maximum(jnp.max(masked, axis=-1), own)
    weights = jnp.where(valid, jnp.exp(scores - top[..., None]), 0.0)
    own_weight = jnp.exp(own - top)
    total = jnp.sum(weights, axis=-1) + own_weight
    probs = (weights / total[..., None]).astype(jnp.bfloat16)
    own_prob = (own_weight / total).astype(jnp.bfloat16)
    context = jnp.einsum("tgql,tgld->tgqd", probs, value_cache, preferred_element_type=jnp.float32)
    context = (
        context
        + own_prob.astype(jnp.float32)[..., None] * new_values.astype(jnp.float32)[:, :, None, :]
    )
    return context.astype(jnp.bfloat16).reshape(row_count, head_count * head_size)


def near(a):
    return pltpu.with_memory_space_constraint(a, pltpu.VMEM)


def params():
    return pltpu.CompilerParams(vmem_limit_bytes=LIMIT)


def dot(a, b):
    return jnp.dot(a, b, preferred_element_type=jnp.float32)


def project_kernel(half, context, weight, out):
    for parity in range(2):

        @pl.when(half[0] == parity)
        def _():
            for i in range(4):
                start = (2 * i + parity) * BLK
                out[i] = dot(context[...], weight[:, start : start + BLK]).astype(out.dtype)


def project(half, context, out_weight, dtype):
    rows = context.shape[0]
    return pl.pallas_call(
        project_kernel,
        out_shape=pltpu.VMEM((4, rows, BLK), dtype),
        in_specs=[SMEM, VMEM, VMEM],
        out_specs=VMEM,
        compiler_params=params(),
        cost_estimate=pl.CostEstimate(
            flops=2 * rows * BLK * BLK * 4, bytes_accessed=BLK * BLK * 8, transcendentals=0
        ),
    )(half, near(context), near(out_weight))


def block_rows(index):
    return pl.ds(pl.multiple_of(index * BLK, BLK), BLK)


def line_rows(index):
    return pl.ds(pl.multiple_of(index * ROWS, ROWS), ROWS)


def squares(piece, inverse):
    value = piece.astype(jnp.float32) * inverse
    value = value * value
    total = value[:, :128]
    for i in range(1, BLK // 128):
        total += value[:, i * 128 : (i + 1) * 128]
    return total


def walk(place, pieces, emit):
    x, y, c = place[0], place[1], place[2]

    @pl.when(c == 0)
    def _():
        for j, shift in enumerate(OFFS):
            rows = line_rows((y - shift + 4) % 4)
            emit(rows, [(pieces[j][k * ROWS : (k + 1) * ROWS, :], k, 2 * k) for k in range(4)])

    @pl.when(c == 1)
    def _():
        blocks = [(x - shift + 4) % 4 for shift in OFFS]

        def step(r, carry):
            rows = line_rows(r)
            emit(rows, [(pieces[j][rows, :], k, 2 * k + 1) for j, k in enumerate(blocks)])
            return carry

        lax.fori_loop(0, 4, step, 0)


def total_of(terms):
    return functools.reduce(lambda a, b: a + b, terms)


def enter_far_kernel(place, g0, g1, g2, g3, gate, up, inverse, far, own):
    def emit(rows, parts):
        far[rows, :HID] = total_of([dot(p, gate[block_rows(k), :]) for p, k, _ in parts]).astype(far.dtype)
        far[rows, HID : 2 * HID] = total_of([dot(p, up[block_rows(k), :]) for p, k, _ in parts]).astype(far.dtype)
        square = total_of([squares(p, inverse[pl.ds(b, 1), :]) for p, _, b in parts])
        far[rows, 2 * HID :] = square.astype(far.dtype)
        own[rows, :] = square

    walk(place, (g0, g1, g2, g3), emit)


def enter_far(place, pieces, gate, up, inverse):
    return pl.pallas_call(
        enter_far_kernel,
        out_shape=(
            pltpu.VMEM((4 * ROWS, 2 * HID + 128), jnp.bfloat16),
            pltpu.VMEM((4 * ROWS, 128), jnp.float32),
        ),
        in_specs=[SMEM] + [VMEM] * 7,
        out_specs=(VMEM, VMEM),
        compiler_params=params(),
        cost_estimate=pl.CostEstimate(
            flops=2 * 4 * ROWS * 4 * BLK * 2 * HID, bytes_accessed=4000000, transcendentals=0
        ),
    )(place, *map(near, pieces), near(gate), near(up), near(inverse))


def enter_own_kernel(place, g0, g1, g2, g3, gate, up, own):
    def emit(rows, parts):
        own[rows, :HID] = total_of([dot(p, gate[block_rows(b), :]) for p, _, b in parts])
        own[rows, HID:] = total_of([dot(p, up[block_rows(b), :]) for p, _, b in parts])

    walk(place, (g0, g1, g2, g3), emit)


def enter_own(place, pieces, gate, up):
    return pl.pallas_call(
        enter_own_kernel,
        out_shape=pltpu.VMEM((4 * ROWS, 2 * HID), jnp.float32),
        in_specs=[SMEM] + [VMEM] * 6,
        out_specs=VMEM,
        compiler_params=params(),
        cost_estimate=pl.CostEstimate(
            flops=2 * 4 * ROWS * 4 * BLK * 2 * HID, bytes_accessed=4000000, transcendentals=0
        ),
    )(place, *map(near, pieces), near(gate), near(up))


def activate_kernel(own, square, far, out):
    for r in range(4):
        rows = slice(r * ROWS, (r + 1) * ROWS)
        other = far[rows, :].astype(jnp.float32)
        mean = jnp.sum(square[rows, :] + other[:, 2 * HID :], axis=1, keepdims=True) * (1.0 / D)
        scale = lax.rsqrt(mean + EPS)
        gate = (own[rows, :HID] + other[:, :HID]) * scale
        upper = (own[rows, HID:] + other[:, HID : 2 * HID]) * scale
        out[rows, :] = (gate * (1.0 / (1.0 + jnp.exp(-gate))) * upper).astype(jnp.bfloat16)


def activate(own, square, far):
    return pl.pallas_call(
        activate_kernel,
        out_shape=pltpu.VMEM((4 * ROWS, HID), jnp.bfloat16),
        in_specs=[VMEM] * 3,
        out_specs=VMEM,
        compiler_params=params(),
    )(near(own), near(square), near(far))


def leave_kernel(offsets, place, act, act_far, down, down_far, *outs):
    x, y, c = place[0], place[1], place[2]

    def term(rows, k):
        return (dot(act[rows, :], down[k]) + dot(act_far[rows, :], down_far[k])).astype(jnp.bfloat16)

    @pl.when(c == 0)
    def _():
        for out, shift in zip(outs, offsets):
            rows = line_rows((y + shift + 4) % 4)
            for k in range(4):
                out[k * ROWS : (k + 1) * ROWS, :] = term(rows, k)

    @pl.when(c == 1)
    def _():
        for out, shift in zip(outs, offsets):
            for r in range(4):
                rows = slice(r * ROWS, (r + 1) * ROWS)
                out[rows, :] = term(rows, (x + shift + 4) % 4)


def leave(offsets, place, act, act_far, down, down_far):
    return pl.pallas_call(
        functools.partial(leave_kernel, offsets),
        out_shape=(pltpu.VMEM((4 * ROWS, BLK), jnp.bfloat16),) * len(offsets),
        in_specs=[SMEM] + [VMEM] * 4,
        out_specs=(VMEM,) * len(offsets),
        compiler_params=params(),
        cost_estimate=pl.CostEstimate(
            flops=2 * 4 * ROWS * len(offsets) * BLK * 2 * HID, bytes_accessed=2000000, transcendentals=0
        ),
    )(place, near(act), near(act_far), near(down), near(down_far))


def slots(routes, expert_count):
    row_count = routes.shape[0]
    expert_ids = jnp.arange(expert_count, dtype=jnp.int32)
    picked = routes[:, :, None] == expert_ids[None, None, :]
    flat = picked.reshape(row_count * 2, expert_count).astype(jnp.int32)
    ranks = (jnp.cumsum(flat, axis=0) - flat).reshape(row_count, 2, expert_count)
    slot_index = jnp.sum(jnp.where(picked, ranks, 0), axis=-1)
    slot_hit = slot_index[:, :, None] == jnp.arange(CAP, dtype=jnp.int32)[None, None, :]
    return picked, picked[:, :, :, None] & slot_hit[:, :, None, :]


def shards(
    tokens,
    queries,
    new_keys,
    new_values,
    key_cache,
    value_cache,
    lengths,
    routes,
    out_weight,
    norm_gain,
    router,
    gate_weight,
    up_weight,
    down_weight,
):
    row_count = tokens.shape[0]
    expert_count = router.shape[1]
    x, y, c = lax.axis_index("x"), lax.axis_index("y"), lax.axis_index("c")
    place = jnp.stack([x, y, c]).astype(jnp.int32)
    here = 2 * x + c

    def other_half(weight):
        return lax.dynamic_index_in_dim(weight.reshape(4, 2, BLK, HID), 1 - c, 1, keepdims=False)

    gate_far = swap_cores(other_half(gate_weight).reshape(4 * BLK, HID))
    up_far = swap_cores(other_half(up_weight).reshape(4 * BLK, HID))

    def down_half(half):
        return jnp.stack(
            [lax.dynamic_slice_in_dim(down_weight, (2 * k + half) * BLK, BLK, 1) for k in range(4)]
        )

    down_own = down_half(c)
    down_far = swap_cores(down_half(1 - c))
    gain = norm_gain.astype(jnp.float32).reshape(8, BLK)
    inverse = 1.0 / gain

    context = attend_local(queries, new_keys, new_values, key_cache, value_cache, lengths)
    core = c.astype(jnp.int32)[None]
    for_other = project(1 - core, context, out_weight, jnp.bfloat16)
    from_other = swap_cores(for_other)
    terms = project(core, context, out_weight, jnp.float32) + from_other.astype(jnp.float32)

    def column(shift):
        return lax.dynamic_index_in_dim(terms, (x + shift + 4) % 4, 0, keepdims=False)

    hidden = column(0) + tokens.astype(jnp.float32)
    for shift in (2, 1, -1):
        hidden = hidden + along_x(column(shift).astype(jnp.bfloat16), shift).astype(jnp.float32)

    picked, matched = slots(routes, expert_count)
    scaled = hidden * lax.dynamic_index_in_dim(gain, here, 0)
    selection = jnp.any(matched, axis=1).astype(jnp.bfloat16)
    outgoing = jnp.einsum(
        "rec,rd->ecd", selection, scaled.astype(jnp.bfloat16), preferred_element_type=jnp.float32
    ).astype(jnp.bfloat16)
    outgoing = jnp.broadcast_to(outgoing[None], (4, 4, CAP, BLK)).reshape(16, CAP, BLK)
    line = along_first(outgoing).reshape(4 * ROWS, BLK)
    pieces = [line] + [along_second(line, shift) for shift in OFFS[1:]]

    own_router = lax.dynamic_slice_in_dim(router, here * BLK, BLK, 0)
    partial = jnp.concatenate(
        [
            jnp.dot(scaled, own_router, precision=lax.Precision.HIGHEST),
            jnp.sum(hidden * hidden, axis=1, keepdims=True),
        ],
        axis=1,
    )
    partial = jnp.pad(partial, ((0, 0), (0, 128 - partial.shape[1])))
    partial = partial + swap_cores(partial)
    stats = partial + along_x(partial, 1) + along_x(partial, -1) + along_x(partial, 2)
    inverse_rms = lax.rsqrt(stats[:, expert_count : expert_count + 1] * (1.0 / D) + EPS)
    logits = stats[:, :expert_count] * inverse_rms
    chosen = jnp.sum(jnp.where(picked, logits[:, None, :], 0.0), axis=-1)
    first_weight = jax.nn.sigmoid(chosen[:, 0] - chosen[:, 1])
    route_weights = jnp.stack([first_weight, 1.0 - first_weight], axis=1)
    weighted = jnp.sum(jnp.where(matched, route_weights[:, :, None, None], 0.0), axis=1)

    far, square = enter_far(place, pieces, gate_far, up_far, inverse)
    own = enter_own(place, pieces, gate_weight, up_weight)
    act = activate(own, square, swap_cores(far))
    act_far = swap_cores(act)
    (out2,) = leave((2,), place, act, act_far, down_own, down_far)
    out1, out3 = leave((1, -1), place, act, act_far, down_own, down_far)
    (out0,) = leave((0,), place, act, act_far, down_own, down_far)
    total = out0.astype(jnp.float32) + along_second(out2, 2).astype(jnp.float32)
    total = total + along_second(out1, 1).astype(jnp.float32)
    total = total + along_second(out3, -1).astype(jnp.float32)
    returned = along_first(total.astype(jnp.bfloat16).reshape(16, CAP, BLK))
    arrived = jnp.sum(returned.reshape(4, 4, CAP, BLK).astype(jnp.float32), axis=0)
    mixture = jnp.einsum("rec,ecd->rd", weighted, arrived, precision=lax.Precision.HIGHEST)
    return (hidden + mixture).astype(jnp.bfloat16)


def solution(mesh):
    grid = Mesh(mesh.devices.reshape(4, 4, 4, 2), AXES)
    batch, tp = ("z", "y"), ("x", "c")
    return jax.shard_map(
        shards,
        mesh=grid,
        in_specs=(
            P(batch, tp),
            P(batch, tp, None),
            P(batch, tp, None),
            P(batch, tp, None),
            P(batch, tp, None, None),
            P(batch, tp, None, None),
            P(batch),
            P(batch, None),
            P(tp, None),
            P(),
            P(),
            P(None, (*batch, *tp)),
            P(None, (*batch, *tp)),
            P((*batch, *tp), None),
        ),
        out_specs=P(batch, tp),
        check_vma=False,
    )
```

time: 181 us -> 152 us (0.84)
  Pallas kernels: 35.5 us -> 19.2 us
  local copies, waits for them, and re-layouts: 30 us -> 19.2 us
  waiting for transfers between devices: 64.8 us -> 57.8 us
  starting transfers between devices: 35.2 us -> 40.5 us
    pallas_call x5 -> x8, Pallas kernels: 35.5 us -> 19.2 us  [the longest x3 6.55 us: leave(): pl.pallas_call(functools.partial(leave_kernel, offsets), out_shape=(pltpu...]
    dynamic_slice x1 -> x0, local copies, waits for them, and re-layouts: 13.2 us -> none  [shards(): lax.dynamic_index_in_dim(down_weight.reshape(HID, 4, 2, BLK), 1 - c, 2, k...]
    reshape x1 -> x0, local copies, waits for them, and re-layouts: 8.06 us -> none  [shards(): down_weight.reshape(HID, 4, 2, BLK)]
    unnamed x23 -> x28, local copies, waits for them, and re-layouts: 3.21 us -> 10.3 us
    ppermute x7, starting transfers between devices: 3.26 us -> 9.45 us  [swap_cores(): return lax.ppermute(a, 'c', [(0, 1), (1, 0)])]
    ppermute x6, waiting for transfers between devices: 19.4 us -> 15.9 us  [along_second(): return lax.ppermute(a, AXES, second_pairs(shift))]
    ppermute x6, waiting for transfers between devices: 22.2 us -> 19.4 us  [along_x(): return lax.ppermute(a, 'x', [(i, (i + shift) % 4) for i in range(4)])]
    another operation x0 -> x1, local copies, waits for them, and re-layouts: none -> 2.04 us  [down_half(): jnp.stack([lax.dynamic_slice_in_dim(down_weight, (2 * k + half) * BLK, BL...]
  transfers between devices with their start and end apart: 21 -> 21, of which waited for: 11 -> 11; matrix products, arithmetic and copies ran while one was open for 17% -> 9% of each run, Pallas kernels for 4% -> 11%
where the time goes in v2:
time: 152 us; the launch traced here: 151 us
  waiting for transfers between devices  57.8 us (38%)
  starting transfers between devices  40.5 us (27%)
  local copies, waits for them, and re-layouts  19.2 us (13%)
  Pallas kernels  19.2 us (13%)
  other arithmetic  7.83 us (5%)
  matrix products  6.33 us (4%)
    all_to_all x2, waiting for transfers between devices, along_first(): lax.all_to_all(a, AXES, 0, 0, tiled=True, axis_index_groups=first_groups())  20.2 us
    ppermute x6, waiting for transfers between devices, along_x(): return lax.ppermute(a, 'x', [(i, (i + shift) % 4) for i in range(4)])  19.4 us
    ppermute x6, waiting for transfers between devices, along_second(): return lax.ppermute(a, AXES, second_pairs(shift))  15.9 us
    all_to_all x2, starting transfers between devices, along_first(): lax.all_to_all(a, AXES, 0, 0, tiled=True, axis_index_groups=first_groups())  11.6 us
    unnamed x28, local copies, waits for them, and re-layouts  10.3 us
    ppermute x6, starting transfers between devices, along_x(): return lax.ppermute(a, 'x', [(i, (i + shift) % 4) for i in range(4)])  10 us
    ppermute x7, starting transfers between devices, swap_cores(): return lax.ppermute(a, 'c', [(0, 1), (1, 0)])  9.45 us
    ppermute x6, starting transfers between devices, along_second(): return lax.ppermute(a, AXES, second_pairs(shift))  9.37 us
  transfers between devices with their start and end apart: 21, of which 11 were waited for; matrix products, arithmetic and copies ran while one was open for 9% of the time, Pallas kernels for 11%

profile of v2, /device:TPU:1, one launch (start us, length us, event | category | flops | bytes accessed | tf_op | source)
XLA Modules:
  0.0 151.3 jit_solution(17126376082112206429)
XLA Ops:
  0.0 0.9 iota_compare_fusion.3
  0.9 1.1 fusion.22
  2.0 2.3 %select_reduce_fusion = (f32[64,6]{1,0:T(8,128)S(1)}, f32[64,6,128]{2,1,0:T(8,128)S(1)}) fusion(pred[64,128]{1,0:T(8,128)(4,1)S(1)} %iota_compare_fusion.3, bf16[64,1,128,128]{3,2,1,0:T(8,128)(2,1)S(1)} %copy-done, bf16[64,6,128]{2,0,1:T(8,128)(2,1)} %param.15), kind=kOutput, calls=%fused_computation.26 | convolution fusion | flops 12729984 | bytes 2401792 | tf_op jit(solution)/shard_map/tgqd,tgld->tgql/dot_general | solution.py:69
  4.3 0.2 fusion.15
  4.6 0.7 fusion.10
  5.4 3.7 %copy-done.1 = bf16[768,6144]{1,0:T(8,128)(2,1)S(1)} copy-done((bf16[768,6144]{1,0:T(8,128)(2,1)S(1)}, bf16[768,6144]{1,0:T(8,128)(2,1)}, u32[]{:S(2)}) %copy-start.1) | copy-done | bytes 9437208
  9.1 0.9 shard_map.137
  10.0 1.5 collective-permute-start
  11.5 2.6 %constant_dynamic-slice_fusion.1 = bf16[4,1,768,256]{3,2,1,0:T(8,128)(2,1)} fusion(bf16[4,2,768,256]{3,2,1,0:T(8,128)(2,1)} %bitcast.87, s32[]{:T(128)S(6)} %select_n.105), kind=kLoop, calls=%fused_computation.77 | loop fusion | bytes 3145732 | tf_op jit(solution)/shard_map/jit(dynamic_index_in_dim)/dynamic_slice | solution.py:305
  14.2 3.7 %copy-done.2 = bf16[768,6144]{1,0:T(8,128)(2,1)S(1)} copy-done((bf16[768,6144]{1,0:T(8,128)(2,1)S(1)}, bf16[768,6144]{1,0:T(8,128)(2,1)}, u32[]{:S(2)}) %copy-start.2) | copy-done | bytes 9437208
  17.9 0.9 shard_map.136
  19.0 0.1 eq.56
  19.2 0.2 reduce_window_sum.11
  19.4 0.2 select_reduce_fusion.1
  19.6 0.1 eq.60
  19.9 1.1 convert_add_fusion
  21.0 2.9 %collective-permute-start.1 = (bf16[64,768]{1,0:T(8,128)(2,1)S(1)}, bf16[64,768]{1,0:T(8,128)(2,1)S(1)}, u32[]{:S(2)}, u32[]{:S(2)}) collective-permute-start(bf16[64,768]{1,0:T(8,128)(2,1)S(1)} %get-tuple-element.25), channel_id=1, source_target_pairs={{0,4},{2,6},{4,0},{6,2},{1,5},{3,7},{5,1},{7,3},{8,12},{10,14},{12... | collective-permute-start | bytes 294920 | tf_op jit(solution)/shard_map/ppermute | solution.py:55
  23.9 0.3 collective-permute-start.2
  24.2 2.4 %collective-permute-start.3 = (bf16[64,768]{1,0:T(8,128)(2,1)S(1)}, bf16[64,768]{1,0:T(8,128)(2,1)S(1)}, u32[]{:S(2)}, u32[]{:S(2)}) collective-permute-start(bf16[64,768]{1,0:T(8,128)(2,1)S(1)} %get-tuple-element.26), channel_id=1, source_target_pairs={{0,6},{2,0},{4,2},{6,4},{1,7},{3,1},{5,3},{7,5},{8,14},{10,8},{12,... | collective-permute-start | bytes 294920 | tf_op jit(solution)/shard_map/ppermute | solution.py:55
  26.6 2.0 %collective-permute-done.2 = bf16[64,768]{1,0:T(8,128)(2,1)S(1)} collective-permute-done((bf16[64,768]{1,0:T(8,128)(2,1)S(1)}, bf16[64,768]{1,0:T(8,128)(2,1)S(1)}, u32[]{:S(2)}, u32[]{:S(2)}) %collective-permute-start.2) | collective-permute-done | bytes 98336 | tf_op jit(solution)/shard_map/ppermute | solution.py:55
  28.6 0.2 collective-permute-done.3
  28.8 1.1 multiply_reduce_fusion
  29.8 0.2 convolution_convert_fusion
  30.0 1.0 broadcast_in_dim.82
  31.1 7.8 %all-to-all-start = ((bf16[16,40,768]{2,1,0:T(8,128)(2,1)}), bf16[16,40,768]{2,1,0:T(8,128)(2,1)S(1)}, u32[]{:S(2)}, u32[]{:S(2)}) async-start(bf16[16,40,768]{2,1,0:T(8,128)(2,1)} %bitcast.97), calls=%async_computation | async-start | bytes 1966080 | tf_op jit(solution)/shard_map/all_to_all | solution.py:51
  38.8 2.7 %constant_dynamic-slice_fusion = bf16[4,1,768,256]{3,2,1,0:T(8,128)(2,1)} fusion(bf16[4,2,768,256]{3,2,1,0:T(8,128)(2,1)} %bitcast.88, s32[]{:T(128)S(6)} %select_n.105), kind=kLoop, calls=%fused_computation.76 | loop fusion | bytes 3145732 | tf_op jit(solution)/shard_map/jit(dynamic_index_in_dim)/dynamic_slice | solution.py:305
  41.5 2.1 %collective-permute-start.12 = (bf16[3072,256]{1,0:T(8,128)(2,1)}, bf16[3072,256]{1,0:T(8,128)(2,1)}, u32[]{:S(2)}, u32[]{:S(2)}) collective-permute-start(bf16[3072,256]{1,0:T(8,128)(2,1)} %bitcast.22), channel_id=1, source_target_pairs={{0,1},{1,0},{2,3},{3,2},{4,5},{5,4},{6,7},{7,6},{8,9},{9,8},{10,11... | collective-permute-start | bytes 4718600 | tf_op jit(solution)/shard_map/ppermute | solution.py:59
  43.6 8.9 %all-to-all-done = bf16[16,40,768]{2,1,0:T(8,128)(2,1)S(1)} async-done(((bf16[16,40,768]{2,1,0:T(8,128)(2,1)}), bf16[16,40,768]{2,1,0:T(8,128)(2,1)S(1)}, u32[]{:S(2)}, u32[]{:S(2)}) %all-to-all-start) | async-done | bytes 983072 | tf_op jit(solution)/shard_map/all_to_all | solution.py:51
  52.6 1.8 %collective-permute-start.10 = (bf16[640,768]{1,0:T(8,128)(2,1)S(1)}, bf16[640,768]{1,0:T(8,128)(2,1)}, u32[]{:S(2)}, u32[]{:S(2)}) collective-permute-start(bf16[640,768]{1,0:T(8,128)(2,1)S(1)} %bitcast.89), channel_id=1, source_target_pairs={{0,16},{1,5},{2,18},{3,7},{4,20},{5,1},{6,22},{7,3},{8,24},{9,13},... | collective-permute-start | bytes 2949128 | tf_op jit(solution)/shard_map/ppermute | solution.py:47
  54.4 1.6 %collective-permute-start.8 = (bf16[640,768]{1,0:T(8,128)(2,1)S(1)}, bf16[640,768]{1,0:T(8,128)(2,1)}, u32[]{:S(2)}, u32[]{:S(2)}) collective-permute-start(bf16[640,768]{1,0:T(8,128)(2,1)S(1)} %bitcast.90), channel_id=1, source_target_pairs={{0,8},{1,3},{2,10},{3,5},{4,12},{5,7},{6,14},{7,1},{8,16},{9,11},{... | collective-permute-start | bytes 2949128 | tf_op jit(solution)/shard_map/ppermute | solution.py:47
  55.9 1.6 %collective-permute-start.9 = (bf16[640,768]{1,0:T(8,128)(2,1)S(1)}, bf16[640,768]{1,0:T(8,128)(2,1)}, u32[]{:S(2)}, u32[]{:S(2)}) collective-permute-start(bf16[640,768]{1,0:T(8,128)(2,1)S(1)} %bitcast.91), channel_id=1, source_target_pairs={{0,24},{1,7},{2,26},{3,1},{4,28},{5,3},{6,30},{7,5},{8,0},{9,15},{... | collective-permute-start | bytes 2949128 | tf_op jit(solution)/shard_map/ppermute | solution.py:47
  57.6 2.0 %dynamic-slice_bitcast_fusion.3 = (bf16[1,256,768]{2,1,0:T(8,128)(2,1)S(1)}, bf16[1,256,768]{2,1,0:T(8,128)(2,1)S(1)}, bf16[1,256,768]{2,1,0:T(8,128)(2,1)S(1)},...) fusion(bf16[256,6144]{1,0:T(8,128)(2,1)} %param.27, ...), kind=kLoop, calls=%fused_computation.19 | loop fusion | bytes 6291488 | tf_op jit(solution)/shard_map/stack | solution.py:311
  59.6 0.2 pad_maximum_fusion.1
  59.8 2.5 %collective-permute-start.15 = (bf16[4,256,768]{2,1,0:T(8,128)(2,1)S(1)}, bf16[4,256,768]{2,1,0:T(8,128)(2,1)S(1)}, u32[]{:S(2)}, u32[]{:S(2)}) collective-permute-start(bf16[4,256,768]{2,1,0:T(8,128)(2,1)S(1)} %pad_maximum_fusion.1), channel_id=1, source_target_pairs={{0,1},{1,0},{2,3},{3,2},{4,5},{5,4},{6,7},{7,6},{8,9},{9,8},{10,11... | collective-permute-start | bytes 4718600 | tf_op jit(solution)/shard_map/ppermute | solution.py:59
  62.5 5.0 %collective-permute-done.10.g3 = bf16[640,768]{1,0:T(8,128)(2,1)} collective-permute-done((bf16[640,768]{1,0:T(8,128)(2,1)S(1)}, bf16[640,768]{1,0:T(8,128)(2,1)}, u32[]{:S(2)}, u32[]{:S(2)}) %collective-permute-start.10) | collective-permute-done | bytes 983072 | tf_op jit(solution)/shard_map/ppermute | solution.py:47
  67.5 10.5 %collective-permute-done.8.g1 = bf16[640,768]{1,0:T(8,128)(2,1)} collective-permute-done((bf16[640,768]{1,0:T(8,128)(2,1)S(1)}, bf16[640,768]{1,0:T(8,128)(2,1)}, u32[]{:S(2)}, u32[]{:S(2)}) %collective-permute-start.8) | collective-permute-done | bytes 983072 | tf_op jit(solution)/shard_map/ppermute | solution.py:47
  77.9 0.4 collective-permute-done.9.g2
  78.4 5.8 %shard_map.139 = (bf16[640,640]{1,0:T(8,128)(2,1)S(1)}, f32[640,128]{1,0:T(8,128)S(1)}) custom-call(s32[3]{0:T(128)S(1)} %pad_add_fusion.place, bf16[640,768]{1,0:T(8,128)(2,1)S(1)} %bitcast.92, bf16[640,768]{1,0:T(8,128)(2,1)} %collective-permute-done.8.g1, bf16[640,768]{1,0:T(8,128)(2,1)} %collective-permute-done.9.g2, ...), custom_call_target="tpu_custom_call" | custom-call | flops 2013265920 | bytes 4000000 | tf_op jit(solution)/shard_map/pallas_call | solution.py:180
  84.3 2.4 %collective-permute-start.13 = (bf16[640,640]{1,0:T(8,128)(2,1)S(1)}, bf16[640,640]{1,0:T(8,128)(2,1)S(1)}, u32[]{:S(2)}, u32[]{:S(2)}) collective-permute-start(bf16[640,640]{1,0:T(8,128)(2,1)S(1)} %get-tuple-element.10), channel_id=1, source_target_pairs={{0,1},{1,0},{2,3},{3,2},{4,5},{5,4},{6,7},{7,6},{8,9},{9,8},{10,11... | collective-permute-start | bytes 2457608 | tf_op jit(solution)/shard_map/ppermute | solution.py:59
  86.7 4.5 %shard_map.138.own = f32[640,512]{1,0:T(8,128)S(1)} custom-call(s32[3]{0:T(128)S(1)} %pad_add_fusion.place, bf16[640,768]{1,0:T(8,128)(2,1)S(1)} %bitcast.93, bf16[640,768]{1,0:T(8,128)(2,1)} %collective-permute-done.8.g1, bf16[640,768]{1,0:T(8,128)(2,1)} %collective-permute-done.9.g2, bf16[640,768]{1,0:T(8,128)(2,1)} %collective-permute-done.10.g3, ...), custom_call_target="tpu_custom_call" | custom-call | flops 2013265920 | bytes 4000000 | tf_op jit(solution)/shard_map/pallas_call | solution.py:204
  91.3 0.4 shard_map.140.act
  91.8 0.2 pad_maximum_fusion.down
  92.0 1.4 collective-permute-done.14.act_far
  93.4 2.2 %shard_map.142 = bf16[640,768]{1,0:T(8,128)(2,1)} custom-call(s32[3]{0:T(128)S(1)} %pad_add_fusion.place, bf16[640,256]{1,0:T(8,128)(2,1)S(1)} %shard_map.140.act, bf16[640,256]{1,0:T(8,128)(2,1)S(1)} %collective-permute-done.14.act_far, bf16[4,256,768]{2,1,0:T(8,128)(2,1)S(1)} %pad_maximum_fusion.down, bf16[4,256,768]{2,1,0:T(8,128)(2,1)S(1)} %collective-permute-done.15.down_far), custom_call_target="tpu_custom_call" | custom-call | flops 503316480 | bytes 2000000 | tf_op jit(solution)/shard_map/pallas_call | solution.py:259
  95.6 1.7 %collective-permute-start.16 = (bf16[640,768]{1,0:T(8,128)(2,1)}, bf16[640,768]{1,0:T(8,128)(2,1)}, u32[]{:S(2)}, u32[]{:S(2)}) collective-permute-start(bf16[640,768]{1,0:T(8,128)(2,1)} %shard_map.142), channel_id=1, source_target_pairs={{0,16},{1,5},{2,18},{3,7},{4,20},{5,1},{6,22},{7,3},{8,24},{9,13},... | collective-permute-start | bytes 2949128 | tf_op jit(solution)/shard_map/ppermute | solution.py:47
  97.3 3.1 %shard_map.143 = (bf16[640,768]{1,0:T(8,128)(2,1)}, bf16[640,768]{1,0:T(8,128)(2,1)}) custom-call(s32[3]{0:T(128)S(1)} %pad_add_fusion.place, bf16[640,256]{1,0:T(8,128)(2,1)S(1)} %shard_map.140.act, bf16[640,256]{1,0:T(8,128)(2,1)S(1)} %collective-permute-done.14.act_far, bf16[4,256,768]{2,1,0:T(8,128)(2,1)S(1)} %pad_maximum_fusion.down, ...), custom_call_target="tpu_custom_call" | custom-call | flops 1006632960 | bytes 2000000 | tf_op jit(solution)/shard_map/pallas_call | solution.py:259
  100.4 1.3 collective-permute-start.17
  101.7 1.4 collective-permute-start.18
  103.1 0.9 fusion.19
  104.1 0.8 collective-permute-start.4
  104.9 0.9 collective-permute-done.4
  105.8 1.6 %collective-permute-start.5 = (f32[64,128]{0,1:T(8,128)S(1)}, f32[64,128]{0,1:T(8,128)S(1)}, u32[]{:S(2)}, u32[]{:S(2)}) collective-permute-start(f32[64,128]{0,1:T(8,128)S(1)} %fusion.41), channel_id=1, source_target_pairs={{0,2},{2,4},{4,6},{6,0},{1,3},{3,5},{5,7},{7,1},{8,10},{10,12},{12... | collective-permute-start | bytes 98312 | tf_op jit(solution)/shard_map/ppermute | solution.py:55
  107.4 1.2 collective-permute-start.6
  108.5 14.3 %collective-permute-done.5 = f32[64,128]{0,1:T(8,128)S(1)} collective-permute-done((f32[64,128]{0,1:T(8,128)S(1)}, f32[64,128]{0,1:T(8,128)S(1)}, u32[]{:S(2)}, u32[]{:S(2)}) %collective-permute-start.5) | collective-permute-done | bytes 32800 | tf_op jit(solution)/shard_map/ppermute | solution.py:55
  122.9 1.7 %collective-permute-start.7 = (f32[64,128]{0,1:T(8,128)S(1)}, f32[64,128]{0,1:T(8,128)S(1)}, u32[]{:S(2)}, u32[]{:S(2)}) collective-permute-start(f32[64,128]{0,1:T(8,128)S(1)} %fusion.41), channel_id=1, source_target_pairs={{0,4},{2,6},{4,0},{6,2},{1,5},{3,7},{5,1},{7,3},{8,12},{10,14},{12... | collective-permute-start | bytes 98312 | tf_op jit(solution)/shard_map/ppermute | solution.py:55
  124.6 2.9 %collective-permute-done.7 = f32[64,128]{0,1:T(8,128)S(1)} collective-permute-done((f32[64,128]{0,1:T(8,128)S(1)}, f32[64,128]{0,1:T(8,128)S(1)}, u32[]{:S(2)}, u32[]{:S(2)}) %collective-permute-start.7) | collective-permute-done | bytes 32800 | tf_op jit(solution)/shard_map/ppermute | solution.py:55
  127.5 1.4 copy-done.4
  128.9 1.4 copy-done.6
  130.3 1.2 shard_map.141
  131.6 3.3 %add_convert_fusion = bf16[640,768]{1,0:T(8,128)(2,1)} fusion(bf16[640,768]{1,0:T(8,128)(2,1)} %collective-permute-done.18, bf16[640,768]{1,0:T(8,128)(2,1)} %collective-permute-done.17, bf16[640,768]{1,0:T(8,128)(2,1)} %collective-permute-done.16, bf16[640,768]{1,0:T(8,128)(2,1)S(1)} %shard_map.141), kind=kLoop, calls=%fused_computation.5 | loop fusion | flops 3932160 | bytes 4915200 | tf_op jit(solution)/shard_map/convert_element_type | solution.py:371
  134.9 3.8 %all-to-all-start.1 = ((bf16[16,40,768]{2,1,0:T(8,128)(2,1)}), bf16[16,40,768]{2,1,0:T(8,128)(2,1)S(1)}, u32[]{:S(2)}, u32[]{:S(2)}) async-start(bf16[16,40,768]{2,1,0:T(8,128)(2,1)} %bitcast.31), calls=%async_computation.1 | async-start | bytes 1966080 | tf_op jit(solution)/shard_map/all_to_all | solution.py:51
  138.9 11.3 %all-to-all-done.1 = bf16[16,40,768]{2,1,0:T(8,128)(2,1)S(1)} async-done(((bf16[16,40,768]{2,1,0:T(8,128)(2,1)}), bf16[16,40,768]{2,1,0:T(8,128)(2,1)S(1)}, u32[]{:S(2)}, u32[]{:S(2)}) %all-to-all-start.1) | async-done | bytes 983072 | tf_op jit(solution)/shard_map/all_to_all | solution.py:51
  150.2 0.1 convert_reduce_fusion
  150.3 1.1 fusion.14
  (58 shorter events, 0.9 us)
Async XLA Ops:
  0.0 2.0 %copy-start = (bf16[64,1,128,128]{3,2,1,0:T(8,128)(2,1)S(1)}, bf16[64,1,128,128]{3,2,1,0:T(8,128)(2,1)}, u32[]{:S(2)}) copy-start(bf16[64,1,128,128]{3,2,1,0:T(8,128)(2,1)} %param.18) | copy-start | bytes 6291460
  2.0 2.6 %copy-start.9 = (bf16[64,1,128]{2,0,1:T(8,128)(2,1)S(1)}, bf16[64,1,128]{2,0,1:T(8,128)(2,1)}, u32[]{:S(2)}) copy-start(bf16[64,1,128]{2,0,1:T(8,128)(2,1)} %param.17) | copy-start | bytes 49156
  2.0 2.6 %copy-start.12 = (bf16[64,1,128,128]{3,2,1,0:T(8,128)(2,1)S(1)}, bf16[64,1,128,128]{3,2,1,0:T(8,128)(2,1)}, u32[]{:S(2)}) copy-start(bf16[64,1,128,128]{3,2,1,0:T(8,128)(2,1)} %param.19) | copy-start | bytes 6291460
  5.4 3.7 %copy-start.1 = (bf16[768,6144]{1,0:T(8,128)(2,1)S(1)}, bf16[768,6144]{1,0:T(8,128)(2,1)}, u32[]{:S(2)}) copy-start(bf16[768,6144]{1,0:T(8,128)(2,1)} %weight.3) | copy-start | bytes 28311556
  10.0 9.8 %collective-permute-start = (bf16[4,64,768]{2,1,0:T(8,128)(2,1)S(1)}, bf16[4,64,768]{2,1,0:T(8,128)(2,1)}, u32[]{:S(2)}, u32[]{:S(2)}) collective-permute-start(bf16[4,64,768]{2,1,0:T(8,128)(2,1)S(1)} %shard_map.137), channel_id=1, source_target_pairs={{0,1},{1,0},{2,3},{3,2},{4,5},{5,4},{6,7},{7,6},{8,9},{9,8},{10,11... | collective-permute-start | bytes 1179656 | tf_op jit(solution)/shard_map/ppermute | solution.py:59
  14.2 45.6 %collective-permute-start.11 = (bf16[3072,256]{1,0:T(8,128)(2,1)}, bf16[3072,256]{1,0:T(8,128)(2,1)}, u32[]{:S(2)}, u32[]{:S(2)}) collective-permute-start(bf16[3072,256]{1,0:T(8,128)(2,1)} %bitcast.20), channel_id=1, source_target_pairs={{0,1},{1,0},{2,3},{3,2},{4,5},{5,4},{6,7},{7,6},{8,9},{9,8},{10,11... | collective-permute-start | bytes 4718600 | tf_op jit(solution)/shard_map/ppermute | solution.py:59
  14.2 3.7 %copy-start.2 = (bf16[768,6144]{1,0:T(8,128)(2,1)S(1)}, bf16[768,6144]{1,0:T(8,128)(2,1)}, u32[]{:S(2)}) copy-start(bf16[768,6144]{1,0:T(8,128)(2,1)} %weight.3) | copy-start | bytes 28311556
  17.9 1.0 copy-start.10
  17.9 1.0 copy-start.11
  21.0 5.6 %collective-permute-start.1 = (bf16[64,768]{1,0:T(8,128)(2,1)S(1)}, bf16[64,768]{1,0:T(8,128)(2,1)S(1)}, u32[]{:S(2)}, u32[]{:S(2)}) collective-permute-start(bf16[64,768]{1,0:T(8,128)(2,1)S(1)} %get-tuple-element.25), channel_id=1, source_target_pairs={{0,4},{2,6},{4,0},{6,2},{1,5},{3,7},{5,1},{7,3},{8,12},{10,14},{12... | collective-permute-start | bytes 294920 | tf_op jit(solution)/shard_map/ppermute | solution.py:55
  23.9 4.7 %collective-permute-start.2 = (bf16[64,768]{1,0:T(8,128)(2,1)S(1)}, bf16[64,768]{1,0:T(8,128)(2,1)S(1)}, u32[]{:S(2)}, u32[]{:S(2)}) collective-permute-start(bf16[64,768]{1,0:T(8,128)(2,1)S(1)} %get-tuple-element.27), channel_id=1, source_target_pairs={{0,2},{2,4},{4,6},{6,0},{1,3},{3,5},{5,7},{7,1},{8,10},{10,12},{12... | collective-permute-start | bytes 294920 | tf_op jit(solution)/shard_map/ppermute | solution.py:55
  24.2 4.5 %collective-permute-start.3 = (bf16[64,768]{1,0:T(8,128)(2,1)S(1)}, bf16[64,768]{1,0:T(8,128)(2,1)S(1)}, u32[]{:S(2)}, u32[]{:S(2)}) collective-permute-start(bf16[64,768]{1,0:T(8,128)(2,1)S(1)} %get-tuple-element.26), channel_id=1, source_target_pairs={{0,6},{2,0},{4,2},{6,4},{1,7},{3,1},{5,3},{7,5},{8,14},{10,8},{12,... | collective-permute-start | bytes 294920 | tf_op jit(solution)/shard_map/ppermute | solution.py:55
  31.1 21.5 %all-to-all-start = ((bf16[16,40,768]{2,1,0:T(8,128)(2,1)}), bf16[16,40,768]{2,1,0:T(8,128)(2,1)S(1)}, u32[]{:S(2)}, u32[]{:S(2)}) async-start(bf16[16,40,768]{2,1,0:T(8,128)(2,1)} %bitcast.97), calls=%async_computation | async-start | bytes 1966080 | tf_op jit(solution)/shard_map/all_to_all | solution.py:51
  41.5 20.9 %collective-permute-start.12 = (bf16[3072,256]{1,0:T(8,128)(2,1)}, bf16[3072,256]{1,0:T(8,128)(2,1)}, u32[]{:S(2)}, u32[]{:S(2)}) collective-permute-start(bf16[3072,256]{1,0:T(8,128)(2,1)} %bitcast.22), channel_id=1, source_target_pairs={{0,1},{1,0},{2,3},{3,2},{4,5},{5,4},{6,7},{7,6},{8,9},{9,8},{10,11... | collective-permute-start | bytes 4718600 | tf_op jit(solution)/shard_map/ppermute | solution.py:59
  52.6 14.9 %collective-permute-start.10 = (bf16[640,768]{1,0:T(8,128)(2,1)S(1)}, bf16[640,768]{1,0:T(8,128)(2,1)}, u32[]{:S(2)}, u32[]{:S(2)}) collective-permute-start(bf16[640,768]{1,0:T(8,128)(2,1)S(1)} %bitcast.89), channel_id=1, source_target_pairs={{0,16},{1,5},{2,18},{3,7},{4,20},{5,1},{6,22},{7,3},{8,24},{9,13},... | collective-permute-start | bytes 2949128 | tf_op jit(solution)/shard_map/ppermute | solution.py:47
  54.4 23.6 %collective-permute-start.8 = (bf16[640,768]{1,0:T(8,128)(2,1)S(1)}, bf16[640,768]{1,0:T(8,128)(2,1)}, u32[]{:S(2)}, u32[]{:S(2)}) collective-permute-start(bf16[640,768]{1,0:T(8,128)(2,1)S(1)} %bitcast.90), channel_id=1, source_target_pairs={{0,8},{1,3},{2,10},{3,5},{4,12},{5,7},{6,14},{7,1},{8,16},{9,11},{... | collective-permute-start | bytes 2949128 | tf_op jit(solution)/shard_map/ppermute | solution.py:47
  55.9 22.5 %collective-permute-start.9 = (bf16[640,768]{1,0:T(8,128)(2,1)S(1)}, bf16[640,768]{1,0:T(8,128)(2,1)}, u32[]{:S(2)}, u32[]{:S(2)}) collective-permute-start(bf16[640,768]{1,0:T(8,128)(2,1)S(1)} %bitcast.91), channel_id=1, source_target_pairs={{0,24},{1,7},{2,26},{3,1},{4,28},{5,3},{6,30},{7,5},{8,0},{9,15},{... | collective-permute-start | bytes 2949128 | tf_op jit(solution)/shard_map/ppermute | solution.py:47
  59.8 32.2 %collective-permute-start.15 = (bf16[4,256,768]{2,1,0:T(8,128)(2,1)S(1)}, bf16[4,256,768]{2,1,0:T(8,128)(2,1)S(1)}, u32[]{:S(2)}, u32[]{:S(2)}) collective-permute-start(bf16[4,256,768]{2,1,0:T(8,128)(2,1)S(1)} %pad_maximum_fusion.1), channel_id=1, source_target_pairs={{0,1},{1,0},{2,3},{3,2},{4,5},{5,4},{6,7},{7,6},{8,9},{9,8},{10,11... | collective-permute-start | bytes 4718600 | tf_op jit(solution)/shard_map/ppermute | solution.py:59
  78.4 8.3 %copy-start.7 = (bf16[6144,256]{1,0:T(8,128)(2,1)S(1)}, bf16[6144,256]{1,0:T(8,128)(2,1)}, u32[]{:S(2)}) copy-start(bf16[6144,256]{1,0:T(8,128)(2,1)} %gate.1) | copy-start | bytes 9437188
  78.4 8.3 %copy-start.8 = (bf16[6144,256]{1,0:T(8,128)(2,1)S(1)}, bf16[6144,256]{1,0:T(8,128)(2,1)}, u32[]{:S(2)}) copy-start(bf16[6144,256]{1,0:T(8,128)(2,1)} %up.1) | copy-start | bytes 9437188
  84.3 7.0 %collective-permute-start.13 = (bf16[640,640]{1,0:T(8,128)(2,1)S(1)}, bf16[640,640]{1,0:T(8,128)(2,1)S(1)}, u32[]{:S(2)}, u32[]{:S(2)}) collective-permute-start(bf16[640,640]{1,0:T(8,128)(2,1)S(1)} %get-tuple-element.10), channel_id=1, source_target_pairs={{0,1},{1,0},{2,3},{3,2},{4,5},{5,4},{6,7},{7,6},{8,9},{9,8},{10,11... | collective-permute-start | bytes 2457608 | tf_op jit(solution)/shard_map/ppermute | solution.py:59
  91.7 1.7 %collective-permute-start.14 = (bf16[640,256]{1,0:T(8,128)(2,1)S(1)}, bf16[640,256]{1,0:T(8,128)(2,1)S(1)}, u32[]{:S(2)}, u32[]{:S(2)}) collective-permute-start(bf16[640,256]{1,0:T(8,128)(2,1)S(1)} %shard_map.140.act), channel_id=1, source_target_pairs={{0,1},{1,0},{2,3},{3,2},{4,5},{5,4},{6,7},{7,6},{8,9},{9,8},{10,11... | collective-permute-start | bytes 983048 | tf_op jit(solution)/shard_map/ppermute | solution.py:59
  92.0 5.3 %copy-start.3 = (bf16[4,256,768]{2,1,0:T(8,128)(2,1)}, bf16[4,256,768]{2,1,0:T(8,128)(2,1)S(1)}, u32[]{:S(2)}) copy-start(bf16[4,256,768]{2,1,0:T(8,128)(2,1)S(1)} %pad_maximum_fusion.down) | copy-start | bytes 4718596
  92.0 5.3 %copy-start.5 = (bf16[4,256,768]{2,1,0:T(8,128)(2,1)}, bf16[4,256,768]{2,1,0:T(8,128)(2,1)S(1)}, u32[]{:S(2)}) copy-start(bf16[4,256,768]{2,1,0:T(8,128)(2,1)S(1)} %collective-permute-done.15.down_far) | copy-start | bytes 4718596
  95.6 36.0 %collective-permute-start.16 = (bf16[640,768]{1,0:T(8,128)(2,1)}, bf16[640,768]{1,0:T(8,128)(2,1)}, u32[]{:S(2)}, u32[]{:S(2)}) collective-permute-start(bf16[640,768]{1,0:T(8,128)(2,1)} %shard_map.142), channel_id=1, source_target_pairs={{0,16},{1,5},{2,18},{3,7},{4,20},{5,1},{6,22},{7,3},{8,24},{9,13},... | collective-permute-start | bytes 2949128 | tf_op jit(solution)/shard_map/ppermute | solution.py:47
  100.4 31.2 %collective-permute-start.17 = (bf16[640,768]{1,0:T(8,128)(2,1)}, bf16[640,768]{1,0:T(8,128)(2,1)}, u32[]{:S(2)}, u32[]{:S(2)}) collective-permute-start(bf16[640,768]{1,0:T(8,128)(2,1)} %get-tuple-element.11), channel_id=1, source_target_pairs={{0,8},{1,3},{2,10},{3,5},{4,12},{5,7},{6,14},{7,1},{8,16},{9,11},{... | collective-permute-start | bytes 2949128 | tf_op jit(solution)/shard_map/ppermute | solution.py:47
  101.7 29.9 %collective-permute-start.18 = (bf16[640,768]{1,0:T(8,128)(2,1)}, bf16[640,768]{1,0:T(8,128)(2,1)}, u32[]{:S(2)}, u32[]{:S(2)}) collective-permute-start(bf16[640,768]{1,0:T(8,128)(2,1)} %get-tuple-element.12), channel_id=1, source_target_pairs={{0,24},{1,7},{2,26},{3,1},{4,28},{5,3},{6,30},{7,5},{8,0},{9,15},{... | collective-permute-start | bytes 2949128 | tf_op jit(solution)/shard_map/ppermute | solution.py:47
  104.1 1.7 %collective-permute-start.4 = (f32[64,128]{0,1:T(8,128)S(1)}, f32[64,128]{0,1:T(8,128)S(1)}, u32[]{:S(2)}, u32[]{:S(2)}) collective-permute-start(f32[64,128]{0,1:T(8,128)S(1)} %select_maximum_fusion), channel_id=1, source_target_pairs={{0,1},{1,0},{2,3},{3,2},{4,5},{5,4},{6,7},{7,6},{8,9},{9,8},{10,11... | collective-permute-start | bytes 98312 | tf_op jit(solution)/shard_map/ppermute | solution.py:59
  105.8 17.1 %collective-permute-start.5 = (f32[64,128]{0,1:T(8,128)S(1)}, f32[64,128]{0,1:T(8,128)S(1)}, u32[]{:S(2)}, u32[]{:S(2)}) collective-permute-start(f32[64,128]{0,1:T(8,128)S(1)} %fusion.41), channel_id=1, source_target_pairs={{0,2},{2,4},{4,6},{6,0},{1,3},{3,5},{5,7},{7,1},{8,10},{10,12},{12... | collective-permute-start | bytes 98312 | tf_op jit(solution)/shard_map/ppermute | solution.py:55
  107.4 17.2 %collective-permute-start.6 = (f32[64,128]{0,1:T(8,128)S(1)}, f32[64,128]{0,1:T(8,128)S(1)}, u32[]{:S(2)}, u32[]{:S(2)}) collective-permute-start(f32[64,128]{0,1:T(8,128)S(1)} %fusion.41), channel_id=1, source_target_pairs={{0,6},{2,0},{4,2},{6,4},{1,7},{3,1},{5,3},{7,5},{8,14},{10,8},{12,... | collective-permute-start | bytes 98312 | tf_op jit(solution)/shard_map/ppermute | solution.py:55
  122.9 4.6 %collective-permute-start.7 = (f32[64,128]{0,1:T(8,128)S(1)}, f32[64,128]{0,1:T(8,128)S(1)}, u32[]{:S(2)}, u32[]{:S(2)}) collective-permute-start(f32[64,128]{0,1:T(8,128)S(1)} %fusion.41), channel_id=1, source_target_pairs={{0,4},{2,6},{4,0},{6,2},{1,5},{3,7},{5,1},{7,3},{8,12},{10,14},{12... | collective-permute-start | bytes 98312 | tf_op jit(solution)/shard_map/ppermute | solution.py:55
  127.5 1.4 copy-start.4
  128.9 1.4 copy-start.6
  134.9 15.3 %all-to-all-start.1 = ((bf16[16,40,768]{2,1,0:T(8,128)(2,1)}), bf16[16,40,768]{2,1,0:T(8,128)(2,1)S(1)}, u32[]{:S(2)}, u32[]{:S(2)}) async-start(bf16[16,40,768]{2,1,0:T(8,128)(2,1)} %bitcast.31), calls=%async_computation.1 | async-start | bytes 1966080 | tf_op jit(solution)/shard_map/all_to_all | solution.py:51

commit v3 on v2

v3 whole, which is shorter than its diff:
```python
import functools
import math

import jax
import jax.numpy as jnp
from jax import lax
from jax.experimental import pallas as pl
from jax.experimental.pallas import tpu as pltpu
from jax.sharding import Mesh
from jax.sharding import PartitionSpec as P

CAP = 40
EPS = 1e-05
D = 6144
BLK = 768
ROWS = 160
HID = 256
OFFS = (0, 1, -1, 2)
AXES = ("z", "y", "x", "c")
VMEM = pl.BlockSpec(memory_space=pltpu.VMEM)
SMEM = pl.BlockSpec(memory_space=pltpu.SMEM)
ANY = pl.BlockSpec(memory_space=pl.ANY)
LIMIT = 14 * 1024 * 1024


def device_index(z, y, x, c):
    return ((z * 4 + y) * 4 + x) * 2 + c


def plane_pairs(first, shift):
    pairs = []
    for z in range(4):
        for y in range(4):
            for x in range(4):
                for c in range(2):
                    if (c == 0) == first:
                        target = device_index(z, y, (x + shift) % 4, c)
                    else:
                        target = device_index(z, (y + shift) % 4, x, c)
                    pairs.append((device_index(z, y, x, c), target))
    return pairs


def along_first(a, shift):
    return lax.ppermute(a, AXES, plane_pairs(True, shift))


def along_second(a, shift):
    return lax.ppermute(a, AXES, plane_pairs(False, shift))


def along_z(a, shift):
    return lax.ppermute(a, "z", [(i, (i + shift) % 4) for i in range(4)])


def along_x(a, shift):
    return lax.ppermute(a, "x", [(i, (i + shift) % 4) for i in range(4)])


def swap_cores(a):
    return lax.ppermute(a, "c", [(0, 1), (1, 0)])


def attend_local(queries, new_keys, new_values, key_cache, value_cache, lengths):
    row_count, head_count, head_size = queries.shape
    kv_local = new_keys.shape[1]
    cache_len = key_cache.shape[2]
    grouped = queries.reshape(row_count, kv_local, head_count // kv_local, head_size)
    scale = 1.0 / math.sqrt(head_size)
    scores = (
        jnp.einsum("tgqd,tgld->tgql", grouped, key_cache, preferred_element_type=jnp.float32)
        * scale
    )
    own = jnp.einsum("tgqd,tgd->tgq", grouped, new_keys, preferred_element_type=jnp.float32) * scale
    position = jnp.arange(cache_len, dtype=jnp.int32)
    valid = position[None, None, None, :] < lengths[:, None, None, None]
    masked = jnp.where(valid, scores, -jnp.inf)
    top = jnp.maximum(jnp.max(masked, axis=-1), own)
    weights = jnp.where(valid, jnp.exp(scores - top[..., None]), 0.0)
    own_weight = jnp.exp(own - top)
    total = jnp.sum(weights, axis=-1) + own_weight
    probs = (weights / total[..., None]).astype(jnp.bfloat16)
    own_prob = (own_weight / total).astype(jnp.bfloat16)
    context = jnp.einsum("tgql,tgld->tgqd", probs, value_cache, preferred_element_type=jnp.float32)
    context = (
        context
        + own_prob.astype(jnp.float32)[..., None] * new_values.astype(jnp.float32)[:, :, None, :]
    )
    return context.astype(jnp.bfloat16).reshape(row_count, head_count * head_size)


def near(a):
    return pltpu.with_memory_space_constraint(a, pltpu.VMEM)


def distant(a):
    return pltpu.with_memory_space_constraint(a, pltpu.HBM)


def params():
    return pltpu.CompilerParams(vmem_limit_bytes=LIMIT)


def dot(a, b):
    return jnp.dot(a, b, preferred_element_type=jnp.float32)


def project_kernel(core, context, weight, far, own, buffer, sems):
    def copy(i):
        parity = 1 - core[0] if i < 4 else core[0]
        start = pl.multiple_of((2 * (i % 4) + parity) * BLK, BLK)
        return pltpu.make_async_copy(weight.at[:, pl.ds(start, BLK)], buffer.at[i], sems.at[i])

    for i in range(8):
        copy(i).start()
    for i in range(8):
        copy(i).wait()
        out = far if i < 4 else own
        out[i % 4] = dot(context[...], buffer[i]).astype(out.dtype)


def project(core, context, out_weight):
    rows = context.shape[0]
    return pl.pallas_call(
        project_kernel,
        out_shape=(
            pltpu.VMEM((4, rows, BLK), jnp.bfloat16),
            pltpu.VMEM((4, rows, BLK), jnp.float32),
        ),
        in_specs=[SMEM, VMEM, ANY],
        out_specs=(VMEM, VMEM),
        scratch_shapes=[pltpu.VMEM((8, BLK, BLK), jnp.bfloat16), pltpu.SemaphoreType.DMA((8,))],
        compiler_params=params(),
        cost_estimate=pl.CostEstimate(
            flops=2 * rows * BLK * BLK * 8, bytes_accessed=BLK * BLK * 16, transcendentals=0
        ),
    )(core, near(context), distant(out_weight))


def prepare_kernel(own, one, three, two, tokens, gain, selection, *rest):
    hidden, *outgoing = rest[-5:]
    total = own[...] + tokens[...].astype(jnp.float32)
    for part in (two, one, three):
        total = total + part[...].astype(jnp.float32)
    hidden[...] = total
    scaled = (total * gain[...]).astype(jnp.bfloat16)
    for i, out in enumerate(outgoing):
        out[...] = dot(selection[i], scaled).astype(jnp.bfloat16)


def prepare(own, one, three, two, tokens, gain, selection, swapped):
    rows = tokens.shape[0]
    return pl.pallas_call(
        prepare_kernel,
        out_shape=(pltpu.VMEM((rows, BLK), jnp.float32),)
        + (pltpu.VMEM((CAP, BLK), jnp.bfloat16),) * 4,
        in_specs=[VMEM] * 7 + [ANY] * len(swapped),
        out_specs=(VMEM,) * 5,
        compiler_params=params(),
        cost_estimate=pl.CostEstimate(
            flops=2 * rows * BLK * 4 * CAP, bytes_accessed=1000000, transcendentals=0
        ),
    )(own, one, three, two, tokens, gain, selection, *map(distant, swapped))


def line_rows(index):
    return pl.ds(pl.multiple_of(index * ROWS, ROWS), ROWS)


def squares(piece, inverse):
    value = piece.astype(jnp.float32) * inverse
    value = value * value
    total = value[:, :128]
    for i in range(1, BLK // 128):
        total += value[:, i * 128 : (i + 1) * 128]
    return total


def walk(place, pieces, emit, ready):
    x, y, c = place[0], place[1], place[2]

    def piece(j, i):
        return pieces[j, i * ROWS : (i + 1) * ROWS, :]

    def behind(position, shift):
        return (position - shift + 4) % 4

    @pl.when(c == 0)
    def _():
        blocks = [behind(x, shift) for shift in OFFS]
        for j, shift in enumerate(OFFS):
            ready(j)
            emit(line_rows(behind(y, shift)), [(piece(j, i), k, 2 * k) for i, k in enumerate(blocks)])

    @pl.when(c == 1)
    def _():
        blocks = [behind(x, shift) for shift in OFFS]
        for i, shift in enumerate(OFFS):
            if i == 0:
                for j in range(4):
                    ready(j)
            emit(line_rows(behind(y, shift)), [(piece(j, i), k, 2 * k + 1) for j, k in enumerate(blocks)])


def total_of(terms):
    return functools.reduce(lambda a, b: a + b, terms)


def load(place, given, gate, up, pieces, gate_here, up_here, sems):
    def weight(n):
        source, target = (gate, gate_here) if n < 4 else (up, up_here)
        start = pl.multiple_of((2 * (n % 4) + place[2]) * BLK, BLK)
        return pltpu.make_async_copy(source.at[pl.ds(start, BLK), :], target.at[n % 4], sems.at[n])

    def piece(j):
        return pltpu.make_async_copy(given[j], pieces.at[j], sems.at[8 + j])

    for n in range(8):
        weight(n).start()
    for j in range(4):
        piece(j).start()
    for n in range(8):
        weight(n).wait()
    return lambda j: piece(j).wait()


def enter_far_kernel(place, p0, p1, p2, p3, gate, up, inverse, stats, far, square, *scratch):
    ready = load(place, (p0, p1, p2, p3), gate, up, *scratch)
    pieces, gate_here, up_here, _ = scratch

    def emit(rows, parts):
        far[rows, :HID] = total_of([dot(p, gate_here[k]) for p, k, _ in parts]).astype(far.dtype)
        far[rows, HID : 2 * HID] = total_of([dot(p, up_here[k]) for p, k, _ in parts]).astype(far.dtype)
        sums = total_of([squares(p, inverse[pl.ds(b, 1), :]) for p, _, b in parts])
        far[rows, 2 * HID :] = sums.astype(far.dtype)
        square[rows, :] = sums

    walk(place, pieces, emit, ready)


def enter_own_kernel(place, p0, p1, p2, p3, gate, up, own, *scratch):
    ready = load(place, (p0, p1, p2, p3), gate, up, *scratch)
    pieces, gate_here, up_here, _ = scratch

    def emit(rows, parts):
        own[rows, :HID] = total_of([dot(p, gate_here[k]) for p, k, _ in parts])
        own[rows, HID:] = total_of([dot(p, up_here[k]) for p, k, _ in parts])

    walk(place, pieces, emit, ready)


def enter_scratch():
    return [
        pltpu.VMEM((4, 4 * ROWS, BLK), jnp.bfloat16),
        pltpu.VMEM((4, BLK, HID), jnp.bfloat16),
        pltpu.VMEM((4, BLK, HID), jnp.bfloat16),
        pltpu.SemaphoreType.DMA((12,)),
    ]


def enter_cost():
    return pl.CostEstimate(
        flops=2 * 4 * ROWS * 4 * BLK * 2 * HID, bytes_accessed=7000000, transcendentals=0
    )


def enter_far(place, pieces, gate, up, inverse, stats):
    return pl.pallas_call(
        enter_far_kernel,
        out_shape=(
            pltpu.VMEM((4 * ROWS, 2 * HID + 128), jnp.bfloat16),
            pltpu.VMEM((4 * ROWS, 128), jnp.float32),
        ),
        in_specs=[SMEM] + [ANY] * 6 + [VMEM, ANY],
        out_specs=(VMEM,) * 2,
        scratch_shapes=enter_scratch(),
        compiler_params=params(),
        cost_estimate=enter_cost(),
    )(place, *map(distant, (*pieces, gate, up)), near(inverse), stats)


def enter_own(place, pieces, gate, up):
    return pl.pallas_call(
        enter_own_kernel,
        out_shape=pltpu.VMEM((4 * ROWS, 2 * HID), jnp.float32),
        in_specs=[SMEM] + [ANY] * 6,
        out_specs=VMEM,
        scratch_shapes=enter_scratch(),
        compiler_params=params(),
        cost_estimate=enter_cost(),
    )(place, *map(distant, (*pieces, gate, up)))


def activate_kernel(own, square, far, out):
    for r in range(4):
        rows = slice(r * ROWS, (r + 1) * ROWS)
        other = far[rows, :].astype(jnp.float32)
        mean = jnp.sum(square[rows, :] + other[:, 2 * HID :], axis=1, keepdims=True) * (1.0 / D)
        scale = lax.rsqrt(mean + EPS)
        gate = (own[rows, :HID] + other[:, :HID]) * scale
        upper = (own[rows, HID:] + other[:, HID : 2 * HID]) * scale
        out[rows, :] = (gate * (1.0 / (1.0 + jnp.exp(-gate))) * upper).astype(jnp.bfloat16)


def activate(own, square, far):
    return pl.pallas_call(
        activate_kernel,
        out_shape=pltpu.VMEM((4 * ROWS, HID), jnp.bfloat16),
        in_specs=[VMEM] * 3,
        out_specs=VMEM,
        compiler_params=params(),
    )(near(own), near(square), near(far))


def leave_kernel(wanted, place, act, act_far, down, down_far, *rest):
    outs, (own_here, far_here, sems) = rest[:-3], rest[-3:]
    x, y, c = place[0], place[1], place[2]

    def ahead(position, shift):
        return (position + shift + 4) % 4

    def copies(k):
        start = pl.multiple_of((2 * k + c) * BLK, BLK)
        return (
            pltpu.make_async_copy(down.at[:, pl.ds(start, BLK)], own_here.at[k], sems.at[2 * k]),
            pltpu.make_async_copy(down_far.at[:, pl.ds(start, BLK)], far_here.at[k], sems.at[2 * k + 1]),
        )

    for k in range(4):
        for copy in copies(k):
            copy.start()
    for k in range(4):
        for copy in copies(k):
            copy.wait()

    def term(rows, k):
        return (dot(act[rows, :], own_here[k]) + dot(act_far[rows, :], far_here[k])).astype(jnp.bfloat16)

    for core in range(2):

        @pl.when(c == core)
        def _(core=core):
            for out, (second, firsts) in zip(outs, wanted):
                for i, first in enumerate(firsts):
                    on_x, on_y = (first, second) if core == 0 else (second, first)
                    out[i * ROWS : (i + 1) * ROWS, :] = term(line_rows(ahead(y, on_y)), ahead(x, on_x))


def leave(wanted, place, act, act_far, down, down_far):
    count = sum(len(firsts) for _, firsts in wanted)
    return pl.pallas_call(
        functools.partial(leave_kernel, wanted),
        out_shape=tuple(
            pltpu.VMEM((len(firsts) * ROWS, BLK), jnp.bfloat16) for _, firsts in wanted
        ),
        in_specs=[SMEM, VMEM, VMEM, ANY, ANY],
        out_specs=(VMEM,) * len(wanted),
        scratch_shapes=[
            pltpu.VMEM((4, HID, BLK), jnp.bfloat16),
            pltpu.VMEM((4, HID, BLK), jnp.bfloat16),
            pltpu.SemaphoreType.DMA((8,)),
        ],
        compiler_params=params(),
        cost_estimate=pl.CostEstimate(
            flops=2 * ROWS * count * BLK * 2 * HID, bytes_accessed=4000000, transcendentals=0
        ),
    )(place, near(act), near(act_far), distant(down), distant(down_far))


def slots(routes, expert_count):
    row_count = routes.shape[0]
    expert_ids = jnp.arange(expert_count, dtype=jnp.int32)
    picked = routes[:, :, None] == expert_ids[None, None, :]
    flat = picked.reshape(row_count * 2, expert_count).astype(jnp.int32)
    ranks = (jnp.cumsum(flat, axis=0) - flat).reshape(row_count, 2, expert_count)
    slot_index = jnp.sum(jnp.where(picked, ranks, 0), axis=-1)
    slot_hit = slot_index[:, :, None] == jnp.arange(CAP, dtype=jnp.int32)[None, None, :]
    return picked, picked[:, :, :, None] & slot_hit[:, :, None, :]


def shards(
    tokens,
    queries,
    new_keys,
    new_values,
    key_cache,
    value_cache,
    lengths,
    routes,
    out_weight,
    norm_gain,
    router,
    gate_weight,
    up_weight,
    down_weight,
):
    expert_count = router.shape[1]
    x, y, c = lax.axis_index("x"), lax.axis_index("y"), lax.axis_index("c")
    z = lax.axis_index("z")
    place = jnp.stack([x, y, c]).astype(jnp.int32)
    here = 2 * x + c

    gate_far, up_far, down_far = swap_cores(gate_weight), swap_cores(up_weight), swap_cores(down_weight)
    gain = norm_gain.astype(jnp.float32).reshape(8, BLK)
    inverse = 1.0 / gain

    context = attend_local(queries, new_keys, new_values, key_cache, value_cache, lengths)
    core = c.astype(jnp.int32)[None]
    for_other, for_own = project(core, context, out_weight)
    terms = for_own + swap_cores(for_other).astype(jnp.float32)

    def column(shift):
        return lax.dynamic_index_in_dim(terms, (x + shift + 4) % 4, 0, keepdims=False)

    moved = [along_x(column(shift).astype(jnp.bfloat16), shift) for shift in OFFS[1:]]

    picked, matched = slots(routes, expert_count)
    selection = jnp.any(matched, axis=1).astype(jnp.bfloat16)
    own_gain = lax.dynamic_index_in_dim(gain, here, 0)
    planes = [(z + shift + 4) % 4 for shift in OFFS]
    chosen_rows = jnp.stack(
        [lax.dynamic_index_in_dim(selection, plane, 1, keepdims=False).T for plane in planes]
    )
    hidden, *outgoing = prepare(
        column(0), *moved, tokens, own_gain, chosen_rows, (gate_far, up_far)
    )
    line = jnp.concatenate(
        [outgoing[0]] + [along_z(rows, shift) for rows, shift in zip(outgoing[1:], OFFS[1:])]
    )
    line = jnp.concatenate([line] + [along_first(line, shift) for shift in OFFS[1:]])
    pieces = [line] + [along_second(line, shift) for shift in OFFS[1:]]

    own_router = lax.dynamic_slice_in_dim(router, here * BLK, BLK, 0)
    partial = jnp.concatenate(
        [
            jnp.dot(hidden * own_gain, own_router, precision=lax.Precision.HIGHEST),
            jnp.sum(hidden * hidden, axis=1, keepdims=True),
        ],
        axis=1,
    )
    partial = jnp.pad(partial, ((0, 0), (0, 128 - partial.shape[1])))

    partial = partial + swap_cores(partial)
    stats = partial + along_x(partial, 1) + along_x(partial, -1) + along_x(partial, 2)

    far, square = enter_far(place, pieces, gate_far, up_far, inverse, stats)
    own = enter_own(place, pieces, gate_weight, up_weight)
    act = activate(own, square, swap_cores(far))
    operands = (place, act, swap_cores(act), down_weight, down_far)
    rest = OFFS[1:]
    far2, far1, far3 = leave(((2, rest), (1, rest), (-1, rest)), *operands)
    near2, near1, near3, far0, near0 = leave(
        ((2, (0,)), (1, (0,)), (-1, (0,)), (0, rest), (0, (0,))), *operands
    )

    inverse_rms = lax.rsqrt(stats[:, expert_count : expert_count + 1] * (1.0 / D) + EPS)
    logits = stats[:, :expert_count] * inverse_rms
    chosen = jnp.sum(jnp.where(picked, logits[:, None, :], 0.0), axis=-1)
    first_weight = jax.nn.sigmoid(chosen[:, 0] - chosen[:, 1])
    route_weights = jnp.stack([first_weight, 1.0 - first_weight], axis=1)
    weighted = jnp.sum(jnp.where(matched, route_weights[:, :, None, None], 0.0), axis=1)

    def gathered(own, one, three, two):
        total = own.astype(jnp.float32) + along_second(two, 2).astype(jnp.float32)
        total = total + along_second(one, 1).astype(jnp.float32)
        return total + along_second(three, -1).astype(jnp.float32)

    others = gathered(far0, far1, far3, far2).astype(jnp.bfloat16).reshape(3, ROWS, BLK)
    total = gathered(near0, near1, near3, near2)
    for i, shift in enumerate(rest):
        total = total + along_first(others[i], shift).astype(jnp.float32)
    total = total.reshape(4, CAP, BLK)
    back = total.astype(jnp.bfloat16)
    returned = [total[0]] + [
        along_z(back[i], -shift).astype(jnp.float32) for i, shift in enumerate(OFFS) if i > 0
    ]
    arrived = jnp.stack(returned)
    weighted = jnp.stack(
        [
            lax.dynamic_index_in_dim(weighted, plane, 1, keepdims=False) for plane in planes
        ],
        axis=1,
    )
    mixture = jnp.einsum("rec,ecd->rd", weighted, arrived, precision=lax.Precision.HIGHEST)
    return (hidden + mixture).astype(jnp.bfloat16)


def solution(mesh):
    grid = Mesh(mesh.devices.reshape(4, 4, 4, 2), AXES)
    batch, tp = ("z", "y"), ("x", "c")
    return jax.shard_map(
        shards,
        mesh=grid,
        in_specs=(
            P(batch, tp),
            P(batch, tp, None),
            P(batch, tp, None),
            P(batch, tp, None),
            P(batch, tp, None, None),
            P(batch, tp, None, None),
            P(batch),
            P(batch, None),
            P(tp, None),
            P(),
            P(),
            P(None, (*batch, *tp)),
            P(None, (*batch, *tp)),
            P((*batch, *tp), None),
        ),
        out_specs=P(batch, tp),
        check_vma=False,
    )
```

time: 152 us -> 139 us (0.914); the launches traced: 151 us -> 137 us
  local copies, waits for them, and re-layouts: 19.2 us -> 5.58 us
  waiting for transfers between devices: 57.8 us -> 48.2 us
  Pallas kernels: 19.2 us -> 25.5 us
  starting transfers between devices: 40.5 us -> 46.2 us
  other arithmetic: 7.83 us -> 5.48 us
    all_to_all x2 -> x0, waiting for transfers between devices: 20.2 us -> none  [along_first(): lax.all_to_all(a, AXES, 0, 0, tiled=True, axis_index_groups=first_groups())]
    ppermute x6 -> x21, starting transfers between devices: 9.37 us -> 26.8 us  [the longest x9 10.1 us: along_second(): return lax.ppermute(a, AXES, plane_pairs(False, shift))]
    all_to_all x2 -> x0, starting transfers between devices: 11.6 us -> none  [along_first(): lax.all_to_all(a, AXES, 0, 0, tiled=True, axis_index_groups=first_groups())]
    ppermute x6 -> x21, waiting for transfers between devices: 15.9 us -> 25.1 us  [the longest x9 10.4 us: along_second(): return lax.ppermute(a, AXES, plane_pairs(False, shift))]
    unnamed x28 -> x23, local copies, waits for them, and re-layouts: 10.3 us -> 3.48 us
    dynamic_slice x3 -> x2, local copies, waits for them, and re-layouts: 5.38 us -> 0.04 us  [the longest x1 0.02 us: shards(): own_gain = lax.dynamic_index_in_dim(gain, here, 0)]
    pallas_call x5 -> x4, Pallas kernels: 8.42 us -> 13.3 us  [the longest x2 8.71 us: leave(): pl.pallas_call(functools.partial(leave_kernel, wanted), out_shape=tuple((...]
    another operation x1, local copies, waits for them, and re-layouts: 2.04 us -> 0.02 us  [shards(): jnp.stack([lax.dynamic_index_in_dim(selection, plane, 1, keepdims=False)....]
  transfers between devices with their start and end apart: 21 -> 34, of which waited for: 11 -> 19; matrix products, arithmetic and copies ran while one was open for 9% -> 11% of each run, Pallas kernels for 11% -> 15%
where the time goes in v3:
time: 139 us; the launch traced here: 137 us
  waiting for transfers between devices  48.2 us (35%)
  starting transfers between devices  46.2 us (33%)
  Pallas kernels  25.5 us (18%)
  local copies, waits for them, and re-layouts  5.58 us (4%)
  other arithmetic  5.48 us (4%)
  matrix products  5.1 us (4%)
    ppermute x6, waiting for transfers between devices, along_x(): return lax.ppermute(a, 'x', [(i, (i + shift) % 4) for i in range(4)])  20.6 us
    ppermute x9, waiting for transfers between devices, along_second(): return lax.ppermute(a, AXES, plane_pairs(False, shift))  10.4 us
    ppermute x9, starting transfers between devices, along_second(): return lax.ppermute(a, AXES, plane_pairs(False, shift))  10.1 us
    ppermute x6, starting transfers between devices, along_x(): return lax.ppermute(a, 'x', [(i, (i + shift) % 4) for i in range(4)])  9.68 us
    ppermute x7, starting transfers between devices, swap_cores(): return lax.ppermute(a, 'c', [(0, 1), (1, 0)])  9.66 us
    ppermute x6, starting transfers between devices, along_first(): return lax.ppermute(a, AXES, plane_pairs(True, shift))  9.32 us
    ppermute x6, waiting for transfers between devices, along_first(): return lax.ppermute(a, AXES, plane_pairs(True, shift))  8.9 us
    pallas_call x2, Pallas kernels, leave(): pl.pallas_call(functools.partial(leave_kernel, wanted), out_shape=tuple((...  8.71 us
  transfers between devices with their start and end apart: 34, of which 19 were waited for; matrix products, arithmetic and copies ran while one was open for 11% of the time, Pallas kernels for 15%

profile of v3, /device:TPU:1, one launch (start us, length us, event | category | flops | bytes accessed | tf_op | source)
XLA Modules:
  0.0 136.7 jit_solution(2118892003212315842)
XLA Ops:
  0.0 1.5 %collective-permute-start.4 = (bf16[6144,256]{1,0:T(8,128)(2,1)}, bf16[6144,256]{1,0:T(8,128)(2,1)}, u32[]{:S(2)}, u32[]{:S(2)}) collective-permute-start(bf16[6144,256]{1,0:T(8,128)(2,1)} %gate.1), channel_id=1, source_target_pairs={{0,1},{1,0},{2,3},{3,2},{4,5},{5,4},{6,7},{7,6},{8,9},{9,8},{10,11... | collective-permute-start | bytes 9437192 | tf_op jit(solution)/shard_map/ppermute | solution.py:61
  1.6 0.9 iota_compare_fusion.2
  2.5 2.2 %select_reduce_fusion = (f32[64,6]{1,0:T(8,128)S(1)}, f32[64,6,128]{2,1,0:T(8,128)S(1)}) fusion(pred[64,128]{1,0:T(8,128)(4,1)S(1)} %iota_compare_fusion.2, bf16[64,1,128,128]{3,2,1,0:T(8,128)(2,1)S(1)} %copy-done, bf16[64,6,128]{2,0,1:T(8,128)(2,1)} %param.15), kind=kOutput, calls=%fused_computation.22 | convolution fusion | flops 12729984 | bytes 2401792 | tf_op jit(solution)/shard_map/tgqd,tgld->tgql/dot_general | solution.py:71
  5.2 0.7 fusion.10
  6.0 4.3 %shard_map.136 = (bf16[4,64,768]{2,1,0:T(8,128)(2,1)S(1)}, f32[4,64,768]{2,1,0:T(8,128)S(1)}) custom-call(s32[1]{0:T(128)} %bitcast.core, bf16[64,768]{1,0:T(8,128)(2,1)S(1)} %bitcast.78, bf16[768,6144]{1,0:T(8,128)(2,1)} %weight.1), custom_call_target="tpu_custom_call" | custom-call | flops 603979776 | bytes 9437184 | tf_op jit(solution)/shard_map/pallas_call | solution.py:124
  10.4 0.6 collective-permute-start
  12.4 1.1 convert_add_fusion
  13.6 2.9 %collective-permute-start.3 = (bf16[64,768]{1,0:T(8,128)(2,1)S(1)}, bf16[64,768]{1,0:T(8,128)(2,1)S(1)}, u32[]{:S(2)}, u32[]{:S(2)}) collective-permute-start(bf16[64,768]{1,0:T(8,128)(2,1)S(1)} %get-tuple-element.45), channel_id=1, source_target_pairs={{0,4},{2,6},{4,0},{6,2},{1,5},{3,7},{5,1},{7,3},{8,12},{10,14},{12... | collective-permute-start | bytes 294920 | tf_op jit(solution)/shard_map/ppermute | solution.py:57
  16.5 0.9 collective-permute-start.2
  17.3 0.6 collective-permute-start.1
  17.9 1.2 collective-permute-done.3.two
  19.1 1.3 collective-permute-start.21
  20.5 1.0 collective-permute-done.2.three
  21.4 0.6 collective-permute-done.1.one
  22.3 1.7 %collective-permute-start.10 = (bf16[40,768]{1,0:T(8,128)(2,1)S(1)}, bf16[40,768]{1,0:T(8,128)(2,1)S(1)}, u32[]{:S(2)}, u32[]{:S(2)}) collective-permute-start(bf16[40,768]{1,0:T(8,128)(2,1)S(1)} %get-tuple-element.26), channel_id=1, source_target_pairs={{0,32},{32,64},{64,96},{96,0},{1,33},{33,65},{65,97},{97,1},{2,34}... | collective-permute-start | bytes 184328 | tf_op jit(solution)/shard_map/ppermute | solution.py:53
  24.0 2.2 %collective-permute-start.11 = (bf16[40,768]{1,0:T(8,128)(2,1)S(1)}, bf16[40,768]{1,0:T(8,128)(2,1)S(1)}, u32[]{:S(2)}, u32[]{:S(2)}) collective-permute-start(bf16[40,768]{1,0:T(8,128)(2,1)S(1)} %get-tuple-element.27), channel_id=1, source_target_pairs={{0,96},{32,0},{64,32},{96,64},{1,97},{33,1},{65,33},{97,65},{2,98}... | collective-permute-start | bytes 184328 | tf_op jit(solution)/shard_map/ppermute | solution.py:53
  26.2 1.2 collective-permute-start.12
  27.4 0.6 constant_dynamic-update-slice_fusion.3
  28.0 0.6 constant_dynamic-update-slice_fusion.2
  28.7 0.6 constant_dynamic-update-slice_fusion.1
  29.3 1.5 %collective-permute-done.12 = bf16[40,768]{1,0:T(8,128)(2,1)S(1)} collective-permute-done((bf16[40,768]{1,0:T(8,128)(2,1)S(1)}, bf16[40,768]{1,0:T(8,128)(2,1)S(1)}, u32[]{:S(2)}, u32[]{:S(2)}) %collective-permute-start.12) | collective-permute-done | bytes 61472 | tf_op jit(solution)/shard_map/ppermute | solution.py:53
  30.8 0.6 constant_dynamic-update-slice_fusion
  31.4 1.3 collective-permute-start.13
  32.7 2.6 %collective-permute-start.15 = (bf16[160,768]{1,0:T(8,128)(2,1)S(1)}, bf16[160,768]{1,0:T(8,128)(2,1)S(1)}, u32[]{:S(2)}, u32[]{:S(2)}) collective-permute-start(bf16[160,768]{1,0:T(8,128)(2,1)S(1)} %get-tuple-element.60), channel_id=1, source_target_pairs={{0,4},{1,17},{2,6},{3,19},{4,0},{5,21},{6,2},{7,23},{8,12},{9,25},... | collective-permute-start | bytes 737288 | tf_op jit(solution)/shard_map/ppermute | solution.py:45
  35.3 1.1 collective-permute-start.14
  36.4 0.9 fusion.23
  37.7 0.7 constant_dynamic-update-slice_fusion.6
  38.5 2.8 %collective-permute-done.14 = bf16[160,768]{1,0:T(8,128)(2,1)S(1)} collective-permute-done((bf16[160,768]{1,0:T(8,128)(2,1)S(1)}, bf16[160,768]{1,0:T(8,128)(2,1)S(1)}, u32[]{:S(2)}, u32[]{:S(2)}) %collective-permute-start.14) | collective-permute-done | bytes 245792 | tf_op jit(solution)/shard_map/ppermute | solution.py:45
  41.2 0.7 constant_dynamic-update-slice_fusion.5
  42.0 0.7 constant_dynamic-update-slice_fusion.4.p0
  42.7 2.6 %collective-permute-start.18 = (bf16[640,768]{1,0:T(8,128)(2,1)}, bf16[640,768]{1,0:T(8,128)(2,1)}, u32[]{:S(2)}, u32[]{:S(2)}) collective-permute-start(bf16[640,768]{1,0:T(8,128)(2,1)} %constant_dynamic-update-slice_fusion.4.p0), channel_id=1, source_target_pairs={{0,16},{1,5},{2,18},{3,7},{4,20},{5,1},{6,22},{7,3},{8,24},{9,13},... | collective-permute-start | bytes 2949128 | tf_op jit(solution)/shard_map/ppermute | solution.py:49
  45.3 1.1 collective-permute-start.17
  47.0 5.9 %collective-permute-start.6 = (f32[64,128]{1,0:T(8,128)S(1)}, f32[64,128]{1,0:T(8,128)S(1)}, u32[]{:S(2)}, u32[]{:S(2)}) collective-permute-start(f32[64,128]{1,0:T(8,128)S(1)} %pad.4), channel_id=1, source_target_pairs={{0,1},{1,0},{2,3},{3,2},{4,5},{5,4},{6,7},{7,6},{8,9},{9,8},{10,11... | collective-permute-start | bytes 98312 | tf_op jit(solution)/shard_map/ppermute | solution.py:61
  52.8 0.9 collective-permute-done.6
  53.7 1.2 collective-permute-start.9
  54.9 13.7 %collective-permute-done.9 = f32[64,128]{1,0:T(8,128)S(1)} collective-permute-done((f32[64,128]{1,0:T(8,128)S(1)}, f32[64,128]{1,0:T(8,128)S(1)}, u32[]{:S(2)}, u32[]{:S(2)}) %collective-permute-start.9) | collective-permute-done | bytes 32800 | tf_op jit(solution)/shard_map/ppermute | solution.py:57
  68.6 2.7 %collective-permute-start.8 = (f32[64,128]{1,0:T(8,128)S(1)}, f32[64,128]{1,0:T(8,128)S(1)}, u32[]{:S(2)}, u32[]{:S(2)}) collective-permute-start(f32[64,128]{1,0:T(8,128)S(1)} %pad_add_fusion.1), channel_id=1, source_target_pairs={{0,6},{2,0},{4,2},{6,4},{1,7},{3,1},{5,3},{7,5},{8,14},{10,8},{12,... | collective-permute-start | bytes 98312 | tf_op jit(solution)/shard_map/ppermute | solution.py:57
  71.3 1.0 collective-permute-done.8
  72.3 1.5 %collective-permute-start.7 = (f32[64,128]{1,0:T(8,128)S(1)}, f32[64,128]{1,0:T(8,128)S(1)}, u32[]{:S(2)}, u32[]{:S(2)}) collective-permute-start(f32[64,128]{1,0:T(8,128)S(1)} %pad_add_fusion.1), channel_id=1, source_target_pairs={{0,2},{2,4},{4,6},{6,0},{1,3},{3,5},{5,7},{7,1},{8,10},{10,12},{12... | collective-permute-start | bytes 98312 | tf_op jit(solution)/shard_map/ppermute | solution.py:57
  73.9 3.1 %collective-permute-done.7 = f32[64,128]{1,0:T(8,128)S(1)} collective-permute-done((f32[64,128]{1,0:T(8,128)S(1)}, f32[64,128]{1,0:T(8,128)S(1)}, u32[]{:S(2)}, u32[]{:S(2)}) %collective-permute-start.7) | collective-permute-done | bytes 32800 | tf_op jit(solution)/shard_map/ppermute | solution.py:57
  77.0 5.9 %shard_map.139 = (bf16[640,640]{1,0:T(8,128)(2,1)S(1)}, f32[640,128]{1,0:T(8,128)S(1)}) custom-call(s32[3]{0:T(128)S(1)} %pad_add_fusion.place, bf16[640,768]{1,0:T(8,128)(2,1)} %constant_dynamic-update-slice_fusion.4.p0, bf16[640,768]{1,0:T(8,128)(2,1)} %collective-permute-done.16.p1, bf16[640,768]{1,0:T(8,128)(2,1)} %collective-permute-done.17.p2, ...), custom_call_target="tpu_custom_call" | custom-call | flops 2013265920 | bytes 7000000 | tf_op jit(solution)/shard_map/pallas_call | solution.py:268
  83.0 5.9 %shard_map.138.own = f32[640,512]{1,0:T(8,128)S(1)} custom-call(s32[3]{0:T(128)S(1)} %pad_add_fusion.place, bf16[640,768]{1,0:T(8,128)(2,1)} %constant_dynamic-update-slice_fusion.4.p0, bf16[640,768]{1,0:T(8,128)(2,1)} %collective-permute-done.16.p1, bf16[640,768]{1,0:T(8,128)(2,1)} %collective-permute-done.17.p2, ...), custom_call_target="tpu_custom_call" | custom-call | flops 2013265920 | bytes 7000000 | tf_op jit(solution)/shard_map/pallas_call | solution.py:283
  88.9 0.4 shard_map.140.act
  89.5 1.5 %collective-permute-done.20.act_far = bf16[640,256]{1,0:T(8,128)(2,1)S(1)} collective-permute-done((bf16[640,256]{1,0:T(8,128)(2,1)S(1)}, bf16[640,256]{1,0:T(8,128)(2,1)S(1)}, u32[]{:S(2)}, u32[]{:S(2)}) %collective-permute-start.20) | collective-permute-done | bytes 327712 | tf_op jit(solution)/shard_map/ppermute | solution.py:61
  91.0 5.2 %shard_map.142 = (bf16[480,768]{1,0:T(8,128)(2,1)}, bf16[480,768]{1,0:T(8,128)(2,1)}, bf16[480,768]{1,0:T(8,128)(2,1)}) custom-call(s32[3]{0:T(128)S(1)} %pad_add_fusion.place, bf16[640,256]{1,0:T(8,128)(2,1)S(1)} %shard_map.140.act, bf16[640,256]{1,0:T(8,128)(2,1)S(1)} %collective-permute-done.20.act_far, bf16[256,6144]{1,0:T(8,128)(2,1)} %down.3, ...), custom_call_target="tpu_custom_call" | custom-call | flops 1132462080 | bytes 4000000 | tf_op jit(solution)/shard_map/pallas_call | solution.py:351
  96.2 1.0 collective-permute-start.25
  97.2 1.1 collective-permute-start.26
  98.3 1.5 %collective-permute-start.27 = (bf16[480,768]{1,0:T(8,128)(2,1)}, bf16[480,768]{1,0:T(8,128)(2,1)}, u32[]{:S(2)}, u32[]{:S(2)}) collective-permute-start(bf16[480,768]{1,0:T(8,128)(2,1)} %get-tuple-element.38), channel_id=1, source_target_pairs={{0,24},{1,7},{2,26},{3,1},{4,28},{5,3},{6,30},{7,5},{8,0},{9,15},{... | collective-permute-start | bytes 2211848 | tf_op jit(solution)/shard_map/ppermute | solution.py:49
  100.3 3.5 %shard_map.141 = (bf16[160,768]{1,0:T(8,128)(2,1)S(1)}, bf16[160,768]{1,0:T(8,128)(2,1)S(1)}, bf16[160,768]{1,0:T(8,128)(2,1)S(1)}, bf16[480,768]{1,0:T(8,128)(2,1)S(1)}, bf16[160,768]{1,0:T(8,128)(2,1)S(1)}) custom-call(s32[3]{0:T(128)S(1)} %pad_add_fusion.place, bf16[640,256]{1,0:T(8,128)(2,1)S(1)} %shard_map.140.act, ...), custom_call_target="tpu_custom_call" | custom-call | flops 880803840 | bytes 4000000 | tf_op jit(solution)/shard_map/pallas_call | solution.py:351
  103.8 0.9 collective-permute-start.22
  104.8 4.0 %collective-permute-done.25 = bf16[480,768]{1,0:T(8,128)(2,1)} collective-permute-done((bf16[480,768]{1,0:T(8,128)(2,1)}, bf16[480,768]{1,0:T(8,128)(2,1)}, u32[]{:S(2)}, u32[]{:S(2)}) %collective-permute-start.25) | collective-permute-done | bytes 737312 | tf_op jit(solution)/shard_map/ppermute | solution.py:49
  108.8 1.5 %collective-permute-start.24 = (bf16[160,768]{1,0:T(8,128)(2,1)S(1)}, bf16[160,768]{1,0:T(8,128)(2,1)S(1)}, u32[]{:S(2)}, u32[]{:S(2)}) collective-permute-start(bf16[160,768]{1,0:T(8,128)(2,1)S(1)} %get-tuple-element.34), channel_id=1, source_target_pairs={{0,24},{1,7},{2,26},{3,1},{4,28},{5,3},{6,30},{7,5},{8,0},{9,15},{... | collective-permute-start | bytes 737288 | tf_op jit(solution)/shard_map/ppermute | solution.py:49
  110.2 6.4 %collective-permute-done.26 = bf16[480,768]{1,0:T(8,128)(2,1)} collective-permute-done((bf16[480,768]{1,0:T(8,128)(2,1)}, bf16[480,768]{1,0:T(8,128)(2,1)}, u32[]{:S(2)}, u32[]{:S(2)}) %collective-permute-start.26) | collective-permute-done | bytes 737312 | tf_op jit(solution)/shard_map/ppermute | solution.py:49
  116.6 2.0 %add_convert_fusion = bf16[480,768]{1,0:T(8,128)(2,1)S(1)} fusion(bf16[480,768]{1,0:T(8,128)(2,1)} %collective-permute-done.27, bf16[480,768]{1,0:T(8,128)(2,1)} %collective-permute-done.26, bf16[480,768]{1,0:T(8,128)(2,1)} %collective-permute-done.25, bf16[480,768]{1,0:T(8,128)(2,1)S(1)} %get-tuple-element.35), kind=kLoop, calls=%fused_computation.4 | loop fusion | flops 2949120 | bytes 3686400 | tf_op jit(solution)/shard_map/convert_element_type | solution.py:468
  118.7 0.8 collective-permute-start.28
  119.5 2.8 %collective-permute-start.30 = (bf16[160,768]{1,0:T(8,128)(2,1)S(1)}, bf16[160,768]{1,0:T(8,128)(2,1)S(1)}, u32[]{:S(2)}, u32[]{:S(2)}) collective-permute-start(bf16[160,768]{1,0:T(8,128)(2,1)S(1)} %get-tuple-element.49), channel_id=1, source_target_pairs={{0,4},{1,17},{2,6},{3,19},{4,0},{5,21},{6,2},{7,23},{8,12},{9,25},... | collective-permute-start | bytes 737288 | tf_op jit(solution)/shard_map/ppermute | solution.py:45
  122.3 0.7 collective-permute-start.29
  123.1 2.2 %collective-permute-done.28 = bf16[160,768]{1,0:T(8,128)(2,1)S(1)} collective-permute-done((bf16[160,768]{1,0:T(8,128)(2,1)S(1)}, bf16[160,768]{1,0:T(8,128)(2,1)S(1)}, u32[]{:S(2)}, u32[]{:S(2)}) %collective-permute-start.28) | collective-permute-done | bytes 245792 | tf_op jit(solution)/shard_map/ppermute | solution.py:45
  125.3 3.5 %collective-permute-done.30 = bf16[160,768]{1,0:T(8,128)(2,1)S(1)} collective-permute-done((bf16[160,768]{1,0:T(8,128)(2,1)S(1)}, bf16[160,768]{1,0:T(8,128)(2,1)S(1)}, u32[]{:S(2)}, u32[]{:S(2)}) %collective-permute-start.30) | collective-permute-done | bytes 245792 | tf_op jit(solution)/shard_map/ppermute | solution.py:45
  129.1 1.6 %collective-permute-start.31 = (bf16[40,768]{1,0:T(8,128)(2,1)S(1)}, bf16[40,768]{1,0:T(8,128)(2,1)S(1)}, u32[]{:S(2)}, u32[]{:S(2)}) collective-permute-start(bf16[40,768]{1,0:T(8,128)(2,1)S(1)} %get-tuple-element.51), channel_id=1, source_target_pairs={{0,96},{32,0},{64,32},{96,64},{1,97},{33,1},{65,33},{97,65},{2,98}... | collective-permute-start | bytes 184328 | tf_op jit(solution)/shard_map/ppermute | solution.py:53
  130.7 0.6 collective-permute-start.32
  131.3 0.9 collective-permute-done.31
  132.2 3.1 %collective-permute-done.33 = bf16[40,768]{1,0:T(8,128)(2,1)S(1)} collective-permute-done((bf16[40,768]{1,0:T(8,128)(2,1)S(1)}, bf16[40,768]{1,0:T(8,128)(2,1)S(1)}, u32[]{:S(2)}, u32[]{:S(2)}) %collective-permute-start.33) | collective-permute-done | bytes 61472 | tf_op jit(solution)/shard_map/ppermute | solution.py:53
  135.6 1.1 fusion.14
  (87 shorter events, 4.8 us)
Async XLA Ops:
  0.0 2.5 %copy-start = (bf16[64,1,128,128]{3,2,1,0:T(8,128)(2,1)S(1)}, bf16[64,1,128,128]{3,2,1,0:T(8,128)(2,1)}, u32[]{:S(2)}) copy-start(bf16[64,1,128,128]{3,2,1,0:T(8,128)(2,1)} %param.18) | copy-start | bytes 6291460
  0.0 4.7 %copy-start.2 = (bf16[64,6,128]{2,0,1:T(8,128)(2,1)S(1)}, bf16[64,6,128]{2,0,1:T(8,128)(2,1)}, u32[]{:S(2)}) copy-start(bf16[64,6,128]{2,0,1:T(8,128)(2,1)} %param.15) | copy-start | bytes 294916
  0.0 4.7 %copy-start.7 = (bf16[64,1,128]{2,0,1:T(8,128)(2,1)S(1)}, bf16[64,1,128]{2,0,1:T(8,128)(2,1)}, u32[]{:S(2)}) copy-start(bf16[64,1,128]{2,0,1:T(8,128)(2,1)} %param.16) | copy-start | bytes 49156
  0.0 5.1 %copy-start.3 = (bf16[64,1,128]{2,0,1:T(8,128)(2,1)S(1)}, bf16[64,1,128]{2,0,1:T(8,128)(2,1)}, u32[]{:S(2)}) copy-start(bf16[64,1,128]{2,0,1:T(8,128)(2,1)} %param.17) | copy-start | bytes 49156
  0.0 22.0 %collective-permute-start.4 = (bf16[6144,256]{1,0:T(8,128)(2,1)}, bf16[6144,256]{1,0:T(8,128)(2,1)}, u32[]{:S(2)}, u32[]{:S(2)}) collective-permute-start(bf16[6144,256]{1,0:T(8,128)(2,1)} %gate.1), channel_id=1, source_target_pairs={{0,1},{1,0},{2,3},{3,2},{4,5},{5,4},{6,7},{7,6},{8,9},{9,8},{10,11... | collective-permute-start | bytes 9437192 | tf_op jit(solution)/shard_map/ppermute | solution.py:61
  1.5 20.5 %collective-permute-start.5 = (bf16[6144,256]{1,0:T(8,128)(2,1)}, bf16[6144,256]{1,0:T(8,128)(2,1)}, u32[]{:S(2)}, u32[]{:S(2)}) collective-permute-start(bf16[6144,256]{1,0:T(8,128)(2,1)} %up.1), channel_id=1, source_target_pairs={{0,1},{1,0},{2,3},{3,2},{4,5},{5,4},{6,7},{7,6},{8,9},{9,8},{10,11... | collective-permute-start | bytes 9437192 | tf_op jit(solution)/shard_map/ppermute | solution.py:61
  1.6 3.6 %copy-start.6 = (bf16[64,1,128,128]{3,2,1,0:T(8,128)(2,1)S(1)}, bf16[64,1,128,128]{3,2,1,0:T(8,128)(2,1)}, u32[]{:S(2)}) copy-start(bf16[64,1,128,128]{3,2,1,0:T(8,128)(2,1)} %param.19) | copy-start | bytes 6291460
  6.0 5.0 %copy-start.5 = (s32[64,2]{0,1:T(2,128)S(1)}, s32[64,2]{0,1:T(2,128)}, u32[]{:S(2)}) copy-start(s32[64,2]{0,1:T(2,128)} %param.21) | copy-start | bytes 1540
  6.0 6.1 %copy-start.4 = (bf16[6144]{0:T(1024)(128)(2,1)S(1)}, bf16[6144]{0:T(1024)(128)(2,1)}, u32[]{:S(2)}) copy-start(bf16[6144]{0:T(1024)(128)(2,1)} %param.23) | copy-start | bytes 36868
  10.4 11.7 %copy-start.1 = (bf16[64,768]{1,0:T(8,128)(2,1)S(1)}, bf16[64,768]{1,0:T(8,128)(2,1)}, u32[]{:S(2)}) copy-start(bf16[64,768]{1,0:T(8,128)(2,1)} %tokens.1) | copy-start | bytes 294916
  10.4 2.1 %collective-permute-start = (bf16[4,64,768]{2,1,0:T(8,128)(2,1)S(1)}, bf16[4,64,768]{2,1,0:T(8,128)(2,1)}, u32[]{:S(2)}, u32[]{:S(2)}) collective-permute-start(bf16[4,64,768]{2,1,0:T(8,128)(2,1)S(1)} %get-tuple-element.23), channel_id=1, source_target_pairs={{0,1},{1,0},{2,3},{3,2},{4,5},{5,4},{6,7},{7,6},{8,9},{9,8},{10,11... | collective-permute-start | bytes 1179656 | tf_op jit(solution)/shard_map/ppermute | solution.py:61
  13.6 5.6 %collective-permute-start.3 = (bf16[64,768]{1,0:T(8,128)(2,1)S(1)}, bf16[64,768]{1,0:T(8,128)(2,1)S(1)}, u32[]{:S(2)}, u32[]{:S(2)}) collective-permute-start(bf16[64,768]{1,0:T(8,128)(2,1)S(1)} %get-tuple-element.45), channel_id=1, source_target_pairs={{0,4},{2,6},{4,0},{6,2},{1,5},{3,7},{5,1},{7,3},{8,12},{10,14},{12... | collective-permute-start | bytes 294920 | tf_op jit(solution)/shard_map/ppermute | solution.py:57
  16.5 5.0 %collective-permute-start.2 = (bf16[64,768]{1,0:T(8,128)(2,1)S(1)}, bf16[64,768]{1,0:T(8,128)(2,1)S(1)}, u32[]{:S(2)}, u32[]{:S(2)}) collective-permute-start(bf16[64,768]{1,0:T(8,128)(2,1)S(1)} %get-tuple-element.46), channel_id=1, source_target_pairs={{0,6},{2,0},{4,2},{6,4},{1,7},{3,1},{5,3},{7,5},{8,14},{10,8},{12,... | collective-permute-start | bytes 294920 | tf_op jit(solution)/shard_map/ppermute | solution.py:57
  17.3 4.7 %collective-permute-start.1 = (bf16[64,768]{1,0:T(8,128)(2,1)S(1)}, bf16[64,768]{1,0:T(8,128)(2,1)S(1)}, u32[]{:S(2)}, u32[]{:S(2)}) collective-permute-start(bf16[64,768]{1,0:T(8,128)(2,1)S(1)} %get-tuple-element.47), channel_id=1, source_target_pairs={{0,2},{2,4},{4,6},{6,0},{1,3},{3,5},{5,7},{7,1},{8,10},{10,12},{12... | collective-permute-start | bytes 294920 | tf_op jit(solution)/shard_map/ppermute | solution.py:57
  19.1 70.4 %collective-permute-start.21 = (bf16[256,6144]{1,0:T(8,128)(2,1)}, bf16[256,6144]{1,0:T(8,128)(2,1)}, u32[]{:S(2)}, u32[]{:S(2)}) collective-permute-start(bf16[256,6144]{1,0:T(8,128)(2,1)} %down.3), channel_id=1, source_target_pairs={{0,1},{1,0},{2,3},{3,2},{4,5},{5,4},{6,7},{7,6},{8,9},{9,8},{10,11... | collective-permute-start | bytes 9437192 | tf_op jit(solution)/shard_map/ppermute | solution.py:61
  22.3 5.8 %collective-permute-start.10 = (bf16[40,768]{1,0:T(8,128)(2,1)S(1)}, bf16[40,768]{1,0:T(8,128)(2,1)S(1)}, u32[]{:S(2)}, u32[]{:S(2)}) collective-permute-start(bf16[40,768]{1,0:T(8,128)(2,1)S(1)} %get-tuple-element.26), channel_id=1, source_target_pairs={{0,32},{32,64},{64,96},{96,0},{1,33},{33,65},{65,97},{97,1},{2,34}... | collective-permute-start | bytes 184328 | tf_op jit(solution)/shard_map/ppermute | solution.py:53
  24.0 4.7 %collective-permute-start.11 = (bf16[40,768]{1,0:T(8,128)(2,1)S(1)}, bf16[40,768]{1,0:T(8,128)(2,1)S(1)}, u32[]{:S(2)}, u32[]{:S(2)}) collective-permute-start(bf16[40,768]{1,0:T(8,128)(2,1)S(1)} %get-tuple-element.27), channel_id=1, source_target_pairs={{0,96},{32,0},{64,32},{96,64},{1,97},{33,1},{65,33},{97,65},{2,98}... | collective-permute-start | bytes 184328 | tf_op jit(solution)/shard_map/ppermute | solution.py:53
  26.2 4.6 %collective-permute-start.12 = (bf16[40,768]{1,0:T(8,128)(2,1)S(1)}, bf16[40,768]{1,0:T(8,128)(2,1)S(1)}, u32[]{:S(2)}, u32[]{:S(2)}) collective-permute-start(bf16[40,768]{1,0:T(8,128)(2,1)S(1)} %get-tuple-element.28), channel_id=1, source_target_pairs={{0,64},{32,96},{64,0},{96,32},{1,65},{33,97},{65,1},{97,33},{2,66}... | collective-permute-start | bytes 184328 | tf_op jit(solution)/shard_map/ppermute | solution.py:53
  31.4 6.3 %collective-permute-start.13 = (bf16[160,768]{1,0:T(8,128)(2,1)S(1)}, bf16[160,768]{1,0:T(8,128)(2,1)S(1)}, u32[]{:S(2)}, u32[]{:S(2)}) collective-permute-start(bf16[160,768]{1,0:T(8,128)(2,1)S(1)} %get-tuple-element.60), channel_id=1, source_target_pairs={{0,2},{1,9},{2,4},{3,11},{4,6},{5,13},{6,0},{7,15},{8,10},{9,17},{... | collective-permute-start | bytes 737288 | tf_op jit(solution)/shard_map/ppermute | solution.py:45
  32.7 9.2 %collective-permute-start.15 = (bf16[160,768]{1,0:T(8,128)(2,1)S(1)}, bf16[160,768]{1,0:T(8,128)(2,1)S(1)}, u32[]{:S(2)}, u32[]{:S(2)}) collective-permute-start(bf16[160,768]{1,0:T(8,128)(2,1)S(1)} %get-tuple-element.60), channel_id=1, source_target_pairs={{0,4},{1,17},{2,6},{3,19},{4,0},{5,21},{6,2},{7,23},{8,12},{9,25},... | collective-permute-start | bytes 737288 | tf_op jit(solution)/shard_map/ppermute | solution.py:45
  35.3 5.9 %collective-permute-start.14 = (bf16[160,768]{1,0:T(8,128)(2,1)S(1)}, bf16[160,768]{1,0:T(8,128)(2,1)S(1)}, u32[]{:S(2)}, u32[]{:S(2)}) collective-permute-start(bf16[160,768]{1,0:T(8,128)(2,1)S(1)} %get-tuple-element.60), channel_id=1, source_target_pairs={{0,6},{1,25},{2,0},{3,27},{4,2},{5,29},{6,4},{7,31},{8,14},{9,1},{... | collective-permute-start | bytes 737288 | tf_op jit(solution)/shard_map/ppermute | solution.py:45
  42.7 34.3 %collective-permute-start.18 = (bf16[640,768]{1,0:T(8,128)(2,1)}, bf16[640,768]{1,0:T(8,128)(2,1)}, u32[]{:S(2)}, u32[]{:S(2)}) collective-permute-start(bf16[640,768]{1,0:T(8,128)(2,1)} %constant_dynamic-update-slice_fusion.4.p0), channel_id=1, source_target_pairs={{0,16},{1,5},{2,18},{3,7},{4,20},{5,1},{6,22},{7,3},{8,24},{9,13},... | collective-permute-start | bytes 2949128 | tf_op jit(solution)/shard_map/ppermute | solution.py:49
  45.3 31.7 %collective-permute-start.17 = (bf16[640,768]{1,0:T(8,128)(2,1)}, bf16[640,768]{1,0:T(8,128)(2,1)}, u32[]{:S(2)}, u32[]{:S(2)}) collective-permute-start(bf16[640,768]{1,0:T(8,128)(2,1)} %constant_dynamic-update-slice_fusion.4.p0), channel_id=1, source_target_pairs={{0,24},{1,7},{2,26},{3,1},{4,28},{5,3},{6,30},{7,5},{8,0},{9,15},{... | collective-permute-start | bytes 2949128 | tf_op jit(solution)/shard_map/ppermute | solution.py:49
  46.3 30.7 %collective-permute-start.16 = (bf16[640,768]{1,0:T(8,128)(2,1)}, bf16[640,768]{1,0:T(8,128)(2,1)}, u32[]{:S(2)}, u32[]{:S(2)}) collective-permute-start(bf16[640,768]{1,0:T(8,128)(2,1)} %constant_dynamic-update-slice_fusion.4.p0), channel_id=1, source_target_pairs={{0,8},{1,3},{2,10},{3,5},{4,12},{5,7},{6,14},{7,1},{8,16},{9,11},{... | collective-permute-start | bytes 2949128 | tf_op jit(solution)/shard_map/ppermute | solution.py:49
  47.0 6.7 %collective-permute-start.6 = (f32[64,128]{1,0:T(8,128)S(1)}, f32[64,128]{1,0:T(8,128)S(1)}, u32[]{:S(2)}, u32[]{:S(2)}) collective-permute-start(f32[64,128]{1,0:T(8,128)S(1)} %pad.4), channel_id=1, source_target_pairs={{0,1},{1,0},{2,3},{3,2},{4,5},{5,4},{6,7},{7,6},{8,9},{9,8},{10,11... | collective-permute-start | bytes 98312 | tf_op jit(solution)/shard_map/ppermute | solution.py:61
  53.7 14.9 %collective-permute-start.9 = (f32[64,128]{1,0:T(8,128)S(1)}, f32[64,128]{1,0:T(8,128)S(1)}, u32[]{:S(2)}, u32[]{:S(2)}) collective-permute-start(f32[64,128]{1,0:T(8,128)S(1)} %pad_add_fusion.1), channel_id=1, source_target_pairs={{0,4},{2,6},{4,0},{6,2},{1,5},{3,7},{5,1},{7,3},{8,12},{10,14},{12... | collective-permute-start | bytes 98312 | tf_op jit(solution)/shard_map/ppermute | solution.py:57
  68.6 3.7 %collective-permute-start.8 = (f32[64,128]{1,0:T(8,128)S(1)}, f32[64,128]{1,0:T(8,128)S(1)}, u32[]{:S(2)}, u32[]{:S(2)}) collective-permute-start(f32[64,128]{1,0:T(8,128)S(1)} %pad_add_fusion.1), channel_id=1, source_target_pairs={{0,6},{2,0},{4,2},{6,4},{1,7},{3,1},{5,3},{7,5},{8,14},{10,8},{12,... | collective-permute-start | bytes 98312 | tf_op jit(solution)/shard_map/ppermute | solution.py:57
  72.3 4.6 %collective-permute-start.7 = (f32[64,128]{1,0:T(8,128)S(1)}, f32[64,128]{1,0:T(8,128)S(1)}, u32[]{:S(2)}, u32[]{:S(2)}) collective-permute-start(f32[64,128]{1,0:T(8,128)S(1)} %pad_add_fusion.1), channel_id=1, source_target_pairs={{0,2},{2,4},{4,6},{6,0},{1,3},{3,5},{5,7},{7,1},{8,10},{10,12},{12... | collective-permute-start | bytes 98312 | tf_op jit(solution)/shard_map/ppermute | solution.py:57
  82.9 6.0 %collective-permute-start.19 = (bf16[640,640]{1,0:T(8,128)(2,1)S(1)}, bf16[640,640]{1,0:T(8,128)(2,1)S(1)}, u32[]{:S(2)}, u32[]{:S(2)}) collective-permute-start(bf16[640,640]{1,0:T(8,128)(2,1)S(1)} %get-tuple-element.30), channel_id=1, source_target_pairs={{0,1},{1,0},{2,3},{3,2},{4,5},{5,4},{6,7},{7,6},{8,9},{9,8},{10,11... | collective-permute-start | bytes 2457608 | tf_op jit(solution)/shard_map/ppermute | solution.py:61
  89.3 1.7 %collective-permute-start.20 = (bf16[640,256]{1,0:T(8,128)(2,1)S(1)}, bf16[640,256]{1,0:T(8,128)(2,1)S(1)}, u32[]{:S(2)}, u32[]{:S(2)}) collective-permute-start(bf16[640,256]{1,0:T(8,128)(2,1)S(1)} %shard_map.140.act), channel_id=1, source_target_pairs={{0,1},{1,0},{2,3},{3,2},{4,5},{5,4},{6,7},{7,6},{8,9},{9,8},{10,11... | collective-permute-start | bytes 983048 | tf_op jit(solution)/shard_map/ppermute | solution.py:61
  96.2 12.6 %collective-permute-start.25 = (bf16[480,768]{1,0:T(8,128)(2,1)}, bf16[480,768]{1,0:T(8,128)(2,1)}, u32[]{:S(2)}, u32[]{:S(2)}) collective-permute-start(bf16[480,768]{1,0:T(8,128)(2,1)} %get-tuple-element.36), channel_id=1, source_target_pairs={{0,16},{1,5},{2,18},{3,7},{4,20},{5,1},{6,22},{7,3},{8,24},{9,13},... | collective-permute-start | bytes 2211848 | tf_op jit(solution)/shard_map/ppermute | solution.py:49
  97.2 19.4 %collective-permute-start.26 = (bf16[480,768]{1,0:T(8,128)(2,1)}, bf16[480,768]{1,0:T(8,128)(2,1)}, u32[]{:S(2)}, u32[]{:S(2)}) collective-permute-start(bf16[480,768]{1,0:T(8,128)(2,1)} %get-tuple-element.37), channel_id=1, source_target_pairs={{0,8},{1,3},{2,10},{3,5},{4,12},{5,7},{6,14},{7,1},{8,16},{9,11},{... | collective-permute-start | bytes 2211848 | tf_op jit(solution)/shard_map/ppermute | solution.py:49
  98.3 18.3 %collective-permute-start.27 = (bf16[480,768]{1,0:T(8,128)(2,1)}, bf16[480,768]{1,0:T(8,128)(2,1)}, u32[]{:S(2)}, u32[]{:S(2)}) collective-permute-start(bf16[480,768]{1,0:T(8,128)(2,1)} %get-tuple-element.38), channel_id=1, source_target_pairs={{0,24},{1,7},{2,26},{3,1},{4,28},{5,3},{6,30},{7,5},{8,0},{9,15},{... | collective-permute-start | bytes 2211848 | tf_op jit(solution)/shard_map/ppermute | solution.py:49
  103.8 18.5 %collective-permute-start.22 = (bf16[160,768]{1,0:T(8,128)(2,1)S(1)}, bf16[160,768]{1,0:T(8,128)(2,1)S(1)}, u32[]{:S(2)}, u32[]{:S(2)}) collective-permute-start(bf16[160,768]{1,0:T(8,128)(2,1)S(1)} %get-tuple-element.32), channel_id=1, source_target_pairs={{0,16},{1,5},{2,18},{3,7},{4,20},{5,1},{6,22},{7,3},{8,24},{9,13},... | collective-permute-start | bytes 737288 | tf_op jit(solution)/shard_map/ppermute | solution.py:49
  104.8 18.3 %collective-permute-start.23 = (bf16[160,768]{1,0:T(8,128)(2,1)S(1)}, bf16[160,768]{1,0:T(8,128)(2,1)S(1)}, u32[]{:S(2)}, u32[]{:S(2)}) collective-permute-start(bf16[160,768]{1,0:T(8,128)(2,1)S(1)} %get-tuple-element.33), channel_id=1, source_target_pairs={{0,8},{1,3},{2,10},{3,5},{4,12},{5,7},{6,14},{7,1},{8,16},{9,11},{... | collective-permute-start | bytes 737288 | tf_op jit(solution)/shard_map/ppermute | solution.py:49
  108.8 14.3 %collective-permute-start.24 = (bf16[160,768]{1,0:T(8,128)(2,1)S(1)}, bf16[160,768]{1,0:T(8,128)(2,1)S(1)}, u32[]{:S(2)}, u32[]{:S(2)}) collective-permute-start(bf16[160,768]{1,0:T(8,128)(2,1)S(1)} %get-tuple-element.34), channel_id=1, source_target_pairs={{0,24},{1,7},{2,26},{3,1},{4,28},{5,3},{6,30},{7,5},{8,0},{9,15},{... | collective-permute-start | bytes 737288 | tf_op jit(solution)/shard_map/ppermute | solution.py:49
  118.7 6.6 %collective-permute-start.28 = (bf16[160,768]{1,0:T(8,128)(2,1)S(1)}, bf16[160,768]{1,0:T(8,128)(2,1)S(1)}, u32[]{:S(2)}, u32[]{:S(2)}) collective-permute-start(bf16[160,768]{1,0:T(8,128)(2,1)S(1)} %get-tuple-element.48), channel_id=1, source_target_pairs={{0,2},{1,9},{2,4},{3,11},{4,6},{5,13},{6,0},{7,15},{8,10},{9,17},{... | collective-permute-start | bytes 737288 | tf_op jit(solution)/shard_map/ppermute | solution.py:45
  119.5 9.3 %collective-permute-start.30 = (bf16[160,768]{1,0:T(8,128)(2,1)S(1)}, bf16[160,768]{1,0:T(8,128)(2,1)S(1)}, u32[]{:S(2)}, u32[]{:S(2)}) collective-permute-start(bf16[160,768]{1,0:T(8,128)(2,1)S(1)} %get-tuple-element.49), channel_id=1, source_target_pairs={{0,4},{1,17},{2,6},{3,19},{4,0},{5,21},{6,2},{7,23},{8,12},{9,25},... | collective-permute-start | bytes 737288 | tf_op jit(solution)/shard_map/ppermute | solution.py:45
  122.3 6.5 %collective-permute-start.29 = (bf16[160,768]{1,0:T(8,128)(2,1)S(1)}, bf16[160,768]{1,0:T(8,128)(2,1)S(1)}, u32[]{:S(2)}, u32[]{:S(2)}) collective-permute-start(bf16[160,768]{1,0:T(8,128)(2,1)S(1)} %get-tuple-element.50), channel_id=1, source_target_pairs={{0,6},{1,25},{2,0},{3,27},{4,2},{5,29},{6,4},{7,31},{8,14},{9,1},{... | collective-permute-start | bytes 737288 | tf_op jit(solution)/shard_map/ppermute | solution.py:45
  129.1 3.1 %collective-permute-start.31 = (bf16[40,768]{1,0:T(8,128)(2,1)S(1)}, bf16[40,768]{1,0:T(8,128)(2,1)S(1)}, u32[]{:S(2)}, u32[]{:S(2)}) collective-permute-start(bf16[40,768]{1,0:T(8,128)(2,1)S(1)} %get-tuple-element.51), channel_id=1, source_target_pairs={{0,96},{32,0},{64,32},{96,64},{1,97},{33,1},{65,33},{97,65},{2,98}... | collective-permute-start | bytes 184328 | tf_op jit(solution)/shard_map/ppermute | solution.py:53
  130.6 4.7 %collective-permute-start.33 = (bf16[40,768]{1,0:T(8,128)(2,1)S(1)}, bf16[40,768]{1,0:T(8,128)(2,1)S(1)}, u32[]{:S(2)}, u32[]{:S(2)}) collective-permute-start(bf16[40,768]{1,0:T(8,128)(2,1)S(1)} %get-tuple-element.52), channel_id=1, source_target_pairs={{0,64},{32,96},{64,0},{96,32},{1,65},{33,97},{65,1},{97,33},{2,66}... | collective-permute-start | bytes 184328 | tf_op jit(solution)/shard_map/ppermute | solution.py:53
  130.7 4.9 %collective-permute-start.32 = (bf16[40,768]{1,0:T(8,128)(2,1)S(1)}, bf16[40,768]{1,0:T(8,128)(2,1)S(1)}, u32[]{:S(2)}, u32[]{:S(2)}) collective-permute-start(bf16[40,768]{1,0:T(8,128)(2,1)S(1)} %get-tuple-element.53), channel_id=1, source_target_pairs={{0,32},{32,64},{64,96},{96,0},{1,33},{33,65},{65,97},{97,1},{2,34}... | collective-permute-start | bytes 184328 | tf_op jit(solution)/shard_map/ppermute | solution.py:53

commit v4 on v0

v4 whole, which is shorter than its diff:
```python
import functools
import math

import jax
import jax.numpy as jnp
from jax import lax
from jax.experimental import pallas as pl
from jax.experimental.pallas import tpu as pltpu
from jax.sharding import Mesh
from jax.sharding import PartitionSpec as P

CAP = 40
EPS = 1e-05
D = 6144
BLK = 768
ROWS = 160
HID = 256
OFFS = (0, 1, -1, 2)
AXES = ("z", "y", "x", "c")
VMEM = pl.BlockSpec(memory_space=pltpu.VMEM)
ANY = pl.BlockSpec(memory_space=pl.ANY)


def device_index(z, y, x, c):
    return ((z * 4 + y) * 4 + x) * 2 + c


def plane_pairs(first, shift):
    pairs = []
    for z in range(4):
        for y in range(4):
            for x in range(4):
                for c in range(2):
                    if (c == 0) == first:
                        target = device_index(z, y, (x + shift) % 4, c)
                    else:
                        target = device_index(z, (y + shift) % 4, x, c)
                    pairs.append((device_index(z, y, x, c), target))
    return pairs


def along_first(a, shift):
    return lax.ppermute(a, AXES, plane_pairs(True, shift))


def along_second(a, shift):
    return lax.ppermute(a, AXES, plane_pairs(False, shift))


def along_z(a, shift):
    return lax.ppermute(a, "z", [(i, (i + shift) % 4) for i in range(4)])


def along_x(a, shift):
    return lax.ppermute(a, "x", [(i, (i + shift) % 4) for i in range(4)])


def swap_cores(a):
    return lax.ppermute(a, "c", [(0, 1), (1, 0)])


def position():
    return [lax.axis_index(name) for name in ("x", "y", "c", "z")]


def near(a):
    return pltpu.with_memory_space_constraint(a, pltpu.VMEM)


def distant(a):
    return pltpu.with_memory_space_constraint(a, pltpu.HBM)


def params(mebibytes):
    return pltpu.CompilerParams(vmem_limit_bytes=mebibytes * 1024 * 1024)


def dot(a, b):
    return jnp.dot(a, b, preferred_element_type=jnp.float32)


def attend_kernel(
    given_lengths, given_queries, given_keys, given_values, keys, values, weight, far, own,
    lengths, queries, new_keys, new_values, key_here, value_here, weight_here, query_here, score, context, joined,
    sems,
):
    small = [
        pltpu.make_async_copy(source, target, sems.at[16 + n])
        for n, (source, target) in enumerate(
            (
                (given_queries, queries),
                (given_keys, new_keys),
                (given_values, new_values),
                (given_lengths, lengths),
            )
        )
    ]
    for one in small:
        one.start()
    rows, heads, size = queries.shape[1], queries.shape[0], queries.shape[2]
    chunk, core = rows // 4, position()[2]

    def copy(n):
        if n < 8:
            source, target = (keys, key_here) if n < 4 else (values, value_here)
            part = pl.ds(n % 4 * chunk, chunk)
            return pltpu.make_async_copy(source.at[part], target.at[part], sems.at[n])
        parity = 1 - core if n < 12 else core
        start = pl.multiple_of((2 * (n % 4) + parity) * BLK, BLK)
        return pltpu.make_async_copy(weight.at[:, pl.ds(start, BLK)], weight_here.at[n - 8], sems.at[n])

    started = [0]

    def start(count):
        for n in range(started[0], min(count, 16)):
            copy(n).start()
        started[0] = max(started[0], min(count, 16))

    start(6)
    for one in small:
        one.wait()
    query_here[heads * rows :, :] = jnp.zeros(((8 - heads) * rows, size), jnp.float32)
    for head in range(heads):
        query_here[head * rows : (head + 1) * rows, :] = queries[head].astype(jnp.float32)

    def row(t):
        return slice(8 * t, 8 * t + 8)

    scale = 1.0 / math.sqrt(size)
    for n in range(4):
        copy(n).wait()
        start(n + 7)
        for t in range(n * chunk, (n + 1) * chunk):
            query = query_here[pl.ds(t, 8, stride=rows), :]
            score[row(t), :] = scale * lax.dot_general(
                query.astype(jnp.bfloat16), key_here[t],
                (((1,), (1,)), ((), ())), preferred_element_type=jnp.float32,
            )
    slot = lax.broadcasted_iota(jnp.int32, (8, score.shape[1]), 1)
    for n in range(4):
        copy(n + 4).wait()
        start(n + 11)
        for t in range(n * chunk, (n + 1) * chunk):
            query = query_here[pl.ds(t, 8, stride=rows), :]
            new_key = new_keys[t : t + 1, :].astype(jnp.float32)
            mine = scale * jnp.sum(query * new_key, axis=1, keepdims=True)
            scores = score[row(t), :]
            valid = slot < lengths[t]
            top = jnp.maximum(jnp.max(jnp.where(valid, scores, -jnp.inf), axis=1, keepdims=True), mine)
            weights = jnp.where(valid, jnp.exp(scores - top), 0.0)
            own_weight = jnp.exp(mine - top)
            total = jnp.sum(weights, axis=1, keepdims=True) + own_weight
            probs = (weights / total).astype(jnp.bfloat16)
            own_prob = (own_weight / total).astype(jnp.bfloat16).astype(jnp.float32)
            new_value = new_values[t : t + 1, :].astype(jnp.float32)
            context[row(t), :] = dot(probs, value_here[t]) + own_prob * new_value
    for head in range(heads):
        joined[:, head * size : (head + 1) * size] = context[pl.ds(head, rows, stride=8), :].astype(
            jnp.bfloat16
        )
    start(16)
    for n in range(8):
        copy(8 + n).wait()
        out = far if n < 4 else own
        out[n % 4] = dot(joined[...], weight_here[n]).astype(out.dtype)


def attend(lengths, queries, new_keys, new_values, keys, values, out_weight):
    rows, heads, size = queries.shape
    length = keys.shape[2]
    return pl.pallas_call(
        attend_kernel,
        out_shape=(
            pltpu.VMEM((4, rows, BLK), jnp.bfloat16),
            pltpu.VMEM((4, rows, BLK), jnp.float32),
        ),
        in_specs=[ANY] * 7,
        out_specs=(VMEM, VMEM),
        scratch_shapes=[
            pltpu.SMEM((rows,), jnp.int32),
            pltpu.VMEM((heads, rows, size), jnp.bfloat16),
            pltpu.VMEM((rows, size), jnp.bfloat16),
            pltpu.VMEM((rows, size), jnp.bfloat16),
            pltpu.VMEM((rows, length, size), jnp.bfloat16),
            pltpu.VMEM((rows, length, size), jnp.bfloat16),
            pltpu.VMEM((8, BLK, BLK), jnp.bfloat16),
            pltpu.VMEM((8 * rows, size), jnp.float32),
            pltpu.VMEM((8 * rows, length), jnp.float32),
            pltpu.VMEM((8 * rows, size), jnp.float32),
            pltpu.VMEM((rows, heads * size), jnp.bfloat16),
            pltpu.SemaphoreType.DMA((20,)),
        ],
        compiler_params=params(20),
        cost_estimate=pl.CostEstimate(
            flops=2 * rows * BLK * BLK * 8, bytes_accessed=14000000, transcendentals=0
        ),
    )(
        distant(lengths),
        distant(queries.transpose(1, 0, 2)),
        distant(new_keys.reshape(rows, size)),
        distant(new_values.reshape(rows, size)),
        distant(keys.reshape(rows, length, size)),
        distant(values.reshape(rows, length, size)),
        distant(out_weight),
    )


def combine_kernel(own, far, routes, mine, one, three, two, handed):
    handed[...] = routes[...]
    for out, shift in ((mine, 0), (one, 1), (three, -1), (two, 2)):
        block = behind(position()[0], -shift)
        out[...] = (own[block] + far[block].astype(jnp.float32)).astype(out.dtype)


def combine(own, far, routes):
    rows = own.shape[1]
    return pl.pallas_call(
        combine_kernel,
        out_shape=(pltpu.VMEM((rows, BLK), jnp.float32),)
        + (pltpu.VMEM((rows, BLK), jnp.bfloat16),) * 3
        + (jax.ShapeDtypeStruct(routes.shape, routes.dtype),),
        in_specs=[VMEM] * 3,
        out_specs=(VMEM,) * 5,
        compiler_params=params(4),
    )(near(own), near(far), routes)


def slots_kernel(routes, first, second):
    rows = routes.shape[0]
    lane = lax.broadcasted_iota(jnp.int32, (rows, 128), 1)
    plane = jnp.full((rows, 128), -1, jnp.int32)
    for i, shift in enumerate(OFFS):
        plane = jnp.where(lane == i, behind(position()[3], -shift), plane)
    one = jnp.where(routes[:, 0:1] == plane, 1.0, 0.0)
    two = jnp.where(routes[:, 1:2] == plane, 1.0, 0.0)
    before = lax.broadcasted_iota(jnp.int32, (rows, rows), 1) < lax.broadcasted_iota(
        jnp.int32, (rows, rows), 0
    )
    rank = dot(jnp.where(before, 1.0, 0.0).astype(jnp.bfloat16), (one + two).astype(jnp.bfloat16))
    slot = lax.broadcasted_iota(jnp.int32, (rows, CAP), 1).astype(jnp.float32)
    for i in range(4):
        hit = slot == rank[:, i : i + 1]
        first[i] = jnp.where(hit, one[:, i : i + 1], 0.0).astype(jnp.bfloat16)
        second[i] = jnp.where(hit, two[:, i : i + 1], 0.0).astype(jnp.bfloat16)


def slots(routes):
    shape = pltpu.VMEM((4, routes.shape[0], CAP), jnp.bfloat16)
    return pl.pallas_call(
        slots_kernel,
        out_shape=(shape, shape),
        in_specs=[VMEM],
        out_specs=(VMEM, VMEM),
        compiler_params=params(4),
    )(routes)


def prepare_kernel(own, one, three, two, tokens, gain, first, second, *rest):
    hidden, *outgoing = rest[-5:]
    total = own[...] + tokens[...].astype(jnp.float32)
    for part in (two, one, three):
        total = total + part[...].astype(jnp.float32)
    hidden[...] = total
    x, _, c, _ = position()
    scaled = (total * gain[pl.ds(2 * x + c, 1), :]).astype(jnp.bfloat16)
    for i, out in enumerate(outgoing):
        out[...] = lax.dot_general(
            first[i] + second[i], scaled, (((0,), (0,)), ((), ())), preferred_element_type=jnp.float32
        ).astype(jnp.bfloat16)


def prepare(own, one, three, two, tokens, gain, first, second, swapped):
    rows = tokens.shape[0]
    return pl.pallas_call(
        prepare_kernel,
        out_shape=(pltpu.VMEM((rows, BLK), jnp.float32),)
        + (pltpu.VMEM((CAP, BLK), jnp.bfloat16),) * 4,
        in_specs=[VMEM] * 8 + [ANY] * len(swapped),
        out_specs=(VMEM,) * 5,
        compiler_params=params(4),
        cost_estimate=pl.CostEstimate(
            flops=2 * rows * BLK * 4 * CAP, bytes_accessed=1000000, transcendentals=0
        ),
    )(own, one, three, two, tokens, gain, first, second, *map(distant, swapped))


def line_rows(index):
    return pl.ds(pl.multiple_of(index * ROWS, ROWS), ROWS)


def lanes(value):
    total = value[:, :128]
    for i in range(1, BLK // 128):
        total += value[:, i * 128 : (i + 1) * 128]
    return total


def behind(position, shift):
    return (position - shift + 4) % 4


def walk(pieces, emit):
    x, y, c, _ = position()
    blocks = [2 * behind(x, shift) + c for shift in OFFS]

    for core in range(2):

        @pl.when(c == core)
        def _(core=core):
            for m, shift in enumerate(OFFS):

                def found(n, m=m):
                    j, i = (m, n) if core == 0 else (n, m)
                    return pieces[j, i * ROWS : (i + 1) * ROWS, :]

                emit(line_rows(behind(y, shift)), found, blocks, m, core)


def stage_kernel(gate_far, up_far, gate, up, weights, sems):
    x, _, c, _ = position()
    copies = []
    for which, source in enumerate((gate_far, up_far, gate, up)):
        for n, shift in enumerate(OFFS):
            start = pl.multiple_of((2 * behind(x, shift) + c) * BLK, BLK)
            copies.append(
                pltpu.make_async_copy(
                    source.at[pl.ds(start, BLK), :], weights.at[which, n], sems.at[4 * which + n]
                )
            )
    for copy in copies:
        copy.start()
    for copy in copies:
        copy.wait()


def stage(gate_far, up_far, gate, up):
    return pl.pallas_call(
        stage_kernel,
        out_shape=pltpu.VMEM((4, 4, BLK, HID), jnp.bfloat16),
        in_specs=[ANY] * 4,
        out_specs=VMEM,
        scratch_shapes=[pltpu.SemaphoreType.DMA((16,))],
        compiler_params=params(8),
        cost_estimate=pl.CostEstimate(flops=0, bytes_accessed=12000000, transcendentals=0),
    )(*map(distant, (gate_far, up_far, gate, up)))


def enter_kernel(p0, p1, p2, p3, weights, inverse, route, own, sums, far, pieces, sems):
    given = (p0, p1, p2, p3)

    def line(core, m):
        copies = []
        for n in range(4):
            j, i = (m, n) if core == 0 else (n, m)
            rows = pl.ds(i * ROWS, ROWS)
            copies.append(
                pltpu.make_async_copy(given[j].at[rows, :], pieces.at[j, rows, :], sems.at[4 * j + i])
            )
        return copies

    def start(core, m):
        for copy in line(core, m):
            copy.start()

    def product(found, which):
        total = dot(found(0), weights[which, 0])
        for n in range(1, 4):
            total += dot(found(n), weights[which, n])
        return total

    def emit_far(rows, found, blocks, m, core):
        if m == 0:
            start(core, 0)
            start(core, 1)
        for copy in line(core, m):
            copy.wait()
        if m < 2:
            start(core, m + 2)
        far[rows, :HID] = product(found, 0).astype(far.dtype)
        far[rows, HID : 2 * HID] = product(found, 1).astype(far.dtype)
        for n, index in enumerate(blocks):
            value = found(n).astype(jnp.float32)
            plain = value * inverse[pl.ds(index, 1), :]
            terms = lanes(plain * plain), lanes(value * route[pl.ds(index, 1), :])
            totals = terms if n == 0 else [a + b for a, b in zip(totals, terms)]
        for n, total in enumerate(totals):
            sums[rows, n * 128 : (n + 1) * 128] = total
            far[rows, 2 * HID + n * 128 : 2 * HID + (n + 1) * 128] = total.astype(far.dtype)

    def emit_own(rows, found, blocks, m, core):
        own[rows, :HID] = product(found, 2)
        own[rows, HID:] = product(found, 3)

    walk(pieces, emit_far)
    walk(pieces, emit_own)


def enter(pieces, weights, inverse, route):
    return pl.pallas_call(
        enter_kernel,
        out_shape=(
            pltpu.VMEM((4 * ROWS, 2 * HID), jnp.float32),
            pltpu.VMEM((4 * ROWS, 256), jnp.float32),
            pltpu.VMEM((4 * ROWS, 2 * HID + 256), jnp.bfloat16),
        ),
        in_specs=[ANY] * 4 + [VMEM] * 3,
        out_specs=(VMEM,) * 3,
        scratch_shapes=[
            pltpu.VMEM((4, 4 * ROWS, BLK), jnp.bfloat16),
            pltpu.SemaphoreType.DMA((16,)),
        ],
        compiler_params=params(16),
        cost_estimate=pl.CostEstimate(
            flops=2 * 4 * ROWS * 4 * BLK * 4 * HID, bytes_accessed=10000000, transcendentals=0
        ),
    )(*map(distant, pieces), near(weights), near(inverse), near(route))


def activate_kernel(own, sums, far, out, logit):
    for r in range(4):
        rows = slice(r * ROWS, (r + 1) * ROWS)
        other = far[rows, :].astype(jnp.float32)
        both = sums[rows, :] + other[:, 2 * HID :]
        mean = jnp.sum(both[:, :128], axis=1, keepdims=True) * (1.0 / D)
        scale = lax.rsqrt(mean + EPS)
        gate = (own[rows, :HID] + other[:, :HID]) * scale
        upper = (own[rows, HID:] + other[:, HID : 2 * HID]) * scale
        out[rows, :] = (gate * (1.0 / (1.0 + jnp.exp(-gate))) * upper).astype(jnp.bfloat16)
        value = jnp.sum(both[:, 128:], axis=1, keepdims=True) * scale
        logit[rows, :] = jnp.broadcast_to(value, (ROWS, 128))


def activate(own, sums, far):
    return pl.pallas_call(
        activate_kernel,
        out_shape=(
            pltpu.VMEM((4 * ROWS, HID), jnp.bfloat16),
            pltpu.VMEM((4 * ROWS, 128), jnp.float32),
        ),
        in_specs=[VMEM] * 3,
        out_specs=(VMEM,) * 2,
        compiler_params=params(6),
    )(near(own), near(sums), near(far))


def leave_kernel(wanted, act, act_far, down, down_far, *rest):
    outs, (own_here, far_here, sems) = rest[:-3], rest[-3:]
    x, y, c, _ = position()

    def ahead(position, shift):
        return (position + shift + 4) % 4

    def copies(n):
        start = pl.multiple_of((2 * ahead(x, OFFS[n]) + c) * BLK, BLK)
        return (
            pltpu.make_async_copy(down.at[:, pl.ds(start, BLK)], own_here.at[n], sems.at[2 * n]),
            pltpu.make_async_copy(down_far.at[:, pl.ds(start, BLK)], far_here.at[n], sems.at[2 * n + 1]),
        )

    def term(rows, n):
        return (dot(act[rows, :], own_here[n]) + dot(act_far[rows, :], far_here[n])).astype(jnp.bfloat16)

    for core in range(2):
        steps = [
            (out, i, *((first, second) if core == 0 else (second, first)))
            for out, (second, firsts) in enumerate(wanted)
            for i, first in enumerate(firsts)
        ]
        order = list(dict.fromkeys(OFFS.index(on_x) for _, _, on_x, _ in steps))

        @pl.when(c == core)
        def _(steps=steps, order=order):
            waited = set()
            for n in order[:2]:
                for copy in copies(n):
                    copy.start()
            for out, i, on_x, on_y in steps:
                n = OFFS.index(on_x)
                if n not in waited:
                    for copy in copies(n):
                        copy.wait()
                    waited.add(n)
                    for later in order[len(waited) + 1 : len(waited) + 2]:
                        for copy in copies(later):
                            copy.start()
                outs[out][i * ROWS : (i + 1) * ROWS, :] = term(line_rows(ahead(y, on_y)), n)


def leave(wanted, act, act_far, down, down_far):
    count = sum(len(firsts) for _, firsts in wanted)
    return pl.pallas_call(
        functools.partial(leave_kernel, wanted),
        out_shape=tuple(
            pltpu.VMEM((len(firsts) * ROWS, BLK), jnp.bfloat16) for _, firsts in wanted
        ),
        in_specs=[VMEM, VMEM, ANY, ANY],
        out_specs=(VMEM,) * len(wanted),
        scratch_shapes=[
            pltpu.VMEM((4, HID, BLK), jnp.bfloat16),
            pltpu.VMEM((4, HID, BLK), jnp.bfloat16),
            pltpu.SemaphoreType.DMA((8,)),
        ],
        compiler_params=params(8),
        cost_estimate=pl.CostEstimate(
            flops=2 * ROWS * count * BLK * 2 * HID, bytes_accessed=4000000, transcendentals=0
        ),
    )(near(act), near(act_far), distant(down), distant(down_far))


def gather_kernel(own, logit, *rest):
    parts, outs = rest[:-4], rest[-4:]
    y = position()[1]
    total = own[...].astype(jnp.float32)
    for part in parts:
        total = total + part[...].astype(jnp.float32)
    for i, out in enumerate(outs):
        out[:, :BLK] = total[i * CAP : (i + 1) * CAP].astype(jnp.bfloat16)
        value = logit[pl.ds(pl.multiple_of(y * ROWS + i * CAP, CAP), CAP), :]
        high = value.astype(jnp.bfloat16)
        low = (value - high.astype(jnp.float32)).astype(jnp.bfloat16)
        lane = lax.broadcasted_iota(jnp.int32, (CAP, 128), 1)
        out[:, BLK:] = jnp.where(lane < 64, high.astype(jnp.float32), low.astype(jnp.float32)).astype(jnp.bfloat16)


def gather(own, parts, logit):
    return pl.pallas_call(
        gather_kernel,
        out_shape=(pltpu.VMEM((CAP, BLK + 128), jnp.bfloat16),) * 4,
        in_specs=[VMEM] * (2 + len(parts)),
        out_specs=(VMEM,) * 4,
        compiler_params=params(6),
        cost_estimate=pl.CostEstimate(flops=2000000, bytes_accessed=2000000, transcendentals=0),
    )(own, near(logit), *parts)


def finish_kernel(hidden, first, second, b0, b1, b2, b3, out):
    def pick(hits):
        return functools.reduce(
            lambda a, b: a + b, [dot(hits[i], block[...]) for i, block in enumerate((b0, b1, b2, b3))]
        )

    one, two = pick(first), pick(second)

    def logit(rows):
        return rows[:, BLK : BLK + 1] + rows[:, BLK + 64 : BLK + 65]

    weight = 1.0 / (1.0 + jnp.exp(logit(two) - logit(one)))
    mixture = weight * one[:, :BLK] + (1.0 - weight) * two[:, :BLK]
    out[...] = (hidden[...] + mixture).astype(jnp.bfloat16)


def finish(hidden, first, second, blocks):
    return pl.pallas_call(
        finish_kernel,
        out_shape=jax.ShapeDtypeStruct(hidden.shape, jnp.bfloat16),
        in_specs=[VMEM] * 7,
        out_specs=VMEM,
        compiler_params=params(6),
        cost_estimate=pl.CostEstimate(flops=40000000, bytes_accessed=2000000, transcendentals=0),
    )(near(hidden), near(first), near(second), *blocks)


def shards(
    tokens,
    queries,
    new_keys,
    new_values,
    key_cache,
    value_cache,
    lengths,
    routes,
    out_weight,
    norm_gain,
    router,
    gate_weight,
    up_weight,
    down_weight,
):
    z = lax.axis_index("z")

    gate_far, up_far, down_far = swap_cores(gate_weight), swap_cores(up_weight), swap_cores(down_weight)
    gain = norm_gain.astype(jnp.float32).reshape(8, BLK)
    inverse = 1.0 / gain

    for_other, for_own = attend(
        lengths, queries, new_keys, new_values, key_cache, value_cache, out_weight
    )
    mine, one, three, two, routes = combine(for_own, swap_cores(for_other), routes)
    moved = [along_x(one, 1), along_x(three, -1), along_x(two, 2)]
    first_hits, second_hits = slots(routes)
    hidden, *outgoing = prepare(
        mine, *moved, tokens, gain, first_hits, second_hits, (gate_far, up_far)
    )
    line = jnp.concatenate(
        [outgoing[0]] + [along_z(rows, shift) for rows, shift in zip(outgoing[1:], OFFS[1:])]
    )
    line = jnp.concatenate([line] + [along_first(line, shift) for shift in OFFS[1:]])
    pieces = [line] + [along_second(line, shift) for shift in OFFS[1:]]

    route = lax.dynamic_index_in_dim(router, z, 1, keepdims=False).reshape(8, BLK)
    own, sums, far = enter(
        pieces, stage(gate_far, up_far, gate_weight, up_weight), inverse, route
    )
    act, logit = activate(own, sums, swap_cores(far))
    operands = (act, swap_cores(act), down_weight, down_far)
    rest = OFFS[1:]
    (far2,) = leave(((2, rest),), *operands)
    far1, far3 = leave(((1, rest), (-1, rest)), *operands)
    near2, near1, near3, far0, near0 = leave(
        ((2, (0,)), (1, (0,)), (-1, (0,)), (0, rest), (0, (0,))), *operands
    )

    def gathered(own, one, three, two):
        total = own.astype(jnp.float32) + along_second(two, 2).astype(jnp.float32)
        total = total + along_second(one, 1).astype(jnp.float32)
        return total + along_second(three, -1).astype(jnp.float32)

    others = gathered(far0, far1, far3, far2).astype(jnp.bfloat16).reshape(3, ROWS, BLK)
    parts = [along_second(near2, 2), along_second(near1, 1), along_second(near3, -1)]
    parts += [along_first(others[i], shift) for i, shift in enumerate(rest)]
    back = gather(near0, parts, logit)
    blocks = [back[0]] + [along_z(block, -shift) for block, shift in zip(back[1:], rest)]
    return finish(hidden, first_hits, second_hits, blocks)


def solution(mesh):
    grid = Mesh(mesh.devices.reshape(4, 4, 4, 2), AXES)
    batch, tp = ("z", "y"), ("x", "c")
    return jax.shard_map(
        shards,
        mesh=grid,
        in_specs=(
            P(batch, tp),
            P(batch, tp, None),
            P(batch, tp, None),
            P(batch, tp, None),
            P(batch, tp, None, None),
            P(batch, tp, None, None),
            P(batch),
            P(batch, None),
            P(tp, None),
            P(),
            P(),
            P(None, (*batch, *tp)),
            P(None, (*batch, *tp)),
            P((*batch, *tp), None),
        ),
        out_specs=P(batch, tp),
        check_vma=False,
    )
```

time: 296 us -> 126 us (0.43); the launches traced: 292 us -> 125 us
  blocking collectives: 94.6 us -> 0 us
  waiting for transfers between devices: 123 us -> 56 us
  matrix products: 38 us -> 0 us
  starting transfers between devices: 6.78 us -> 39.1 us
  Pallas kernels: 0 us -> 29.4 us
  between operations: 13.6 us -> 0.22 us
  other arithmetic: 11 us -> 0.37 us
  local copies, waits for them, and re-layouts: 4.59 us -> 0.37 us
    all_to_all x1 -> x0, blocking collectives: 94.6 us -> none  [shards(): lax.all_to_all(outgoing, 'batch', split_axis=0, concat_axis=0, tiled=True)]
    psum x1 -> x0, waiting for transfers between devices: 61.8 us -> none  [shards(): lax.psum(placed.astype(jnp.bfloat16), 'tp').astype(jnp.float32)]
    ppermute x0 -> x30, waiting for transfers between devices: none -> 56 us  [the longest x9 29 us: along_second(): return lax.ppermute(a, AXES, plane_pairs(False, shift))]
    reduce_scatter x1 -> x0, waiting for transfers between devices: 50.9 us -> none  [finish(): lax.psum_scatter(term.astype(jnp.bfloat16), 'tp', scatter_dimension=2, ti...]
    ppermute x0 -> x30, starting transfers between devices: none -> 39.1 us  [the longest x6 9.61 us: along_first(): return lax.ppermute(a, AXES, plane_pairs(True, shift))]
    dot_general x9 -> x0, matrix products: 38 us -> none  [the longest x1 16.6 us: finish(): term = jnp.dot(activation, down_weight, preferred_element_type=jnp.float32)]
    pallas_call x0 -> x12, Pallas kernels: none -> 29.4 us  [the longest x1 8.52 us: enter(): pl.pallas_call(enter_kernel, out_shape=(pltpu.VMEM((4 * ROWS, 2 * HID), j...]
    all_to_all x1 -> x0, waiting for transfers between devices: 10.7 us -> none  [finish(): lax.all_to_all(summed.astype(jnp.bfloat16), 'batch', split_axis=0, concat...]
  transfers between devices with their start and end apart: 3 -> 30, of which waited for: 3 -> 19; matrix products, arithmetic and copies ran while one was open for 2% -> 1% of each run, Pallas kernels for 0% -> 21%
where the time goes in v4:
time: 126 us; the launch traced here: 125 us
  waiting for transfers between devices  56 us (44%)
  starting transfers between devices  39.1 us (31%)
  Pallas kernels  29.4 us (23%)
    ppermute x9, waiting for transfers between devices, along_second(): return lax.ppermute(a, AXES, plane_pairs(False, shift))  29 us
    ppermute x6, waiting for transfers between devices, along_first(): return lax.ppermute(a, AXES, plane_pairs(True, shift))  10.9 us
    ppermute x6, starting transfers between devices, along_first(): return lax.ppermute(a, AXES, plane_pairs(True, shift))  9.61 us
    ppermute x9, starting transfers between devices, along_second(): return lax.ppermute(a, AXES, plane_pairs(False, shift))  8.72 us
    pallas_call x1, Pallas kernels, enter(): pl.pallas_call(enter_kernel, out_shape=(pltpu.VMEM((4 * ROWS, 2 * HID), j...  8.52 us
    ppermute x6, starting transfers between devices, swap_cores(): return lax.ppermute(a, 'c', [(0, 1), (1, 0)])  8.28 us
    ppermute x6, starting transfers between devices, along_z(): return lax.ppermute(a, 'z', [(i, (i + shift) % 4) for i in range(4)])  8.17 us
    pallas_call x1, Pallas kernels, attend(): pl.pallas_call(attend_kernel, out_shape=(pltpu.VMEM((4, rows, BLK), jnp.b...  7.85 us
  transfers between devices with their start and end apart: 30, of which 19 were waited for; matrix products, arithmetic and copies ran while one was open for 1% of the time, Pallas kernels for 21%

profile of v4, /device:TPU:1, one launch (start us, length us, event | category | flops | bytes accessed | tf_op | source)
XLA Modules:
  0.0 125.4 jit_solution(10169884818615537778)
XLA Ops:
  0.0 1.4 %collective-permute-start.4 = (bf16[6144,256]{1,0:T(8,128)(2,1)}, bf16[6144,256]{1,0:T(8,128)(2,1)}, u32[]{:S(2)}, u32[]{:S(2)}) collective-permute-start(bf16[6144,256]{1,0:T(8,128)(2,1)} %gate.1), channel_id=1, source_target_pairs={{0,1},{1,0},{2,3},{3,2},{4,5},{5,4},{6,7},{7,6},{8,9},{9,8},{10,11... | collective-permute-start | bytes 9437192 | tf_op jit(solution)/shard_map/ppermute | solution.py:59
  1.4 7.9 %shard_map.136 = (bf16[4,64,768]{2,1,0:T(8,128)(2,1)S(1)}, f32[4,64,768]{2,1,0:T(8,128)S(1)}) custom-call(s32[64]{0:T(128)} %given_lengths.1, bf16[6,64,128]{2,1,0:T(8,128)(2,1)} %bitcast.7, bf16[64,128]{1,0:T(8,128)(2,1)} %bitcast.8, bf16[64,128]{1,0:T(8,128)(2,1)} %bitcast.9, bf16[64,128,128]{2,1,0:T(8,128)(2,1)} %bitcast.5, ...), custom_call_target="tpu_custom_call" | custom-call | flops 603979776 | bytes 14000000 | tf_op jit(solution)/shard_map/pallas_call | solution.py:171
  9.3 0.6 collective-permute-start
  9.9 0.1 copy.15.routes
  10.0 1.8 %collective-permute-done.far = bf16[4,64,768]{2,1,0:T(8,128)(2,1)S(1)} collective-permute-done((bf16[4,64,768]{2,1,0:T(8,128)(2,1)S(1)}, bf16[4,64,768]{2,1,0:T(8,128)(2,1)S(1)}, u32[]{:S(2)}, u32[]{:S(2)}) %collective-permute-start) | collective-permute-done | bytes 393248 | tf_op jit(solution)/shard_map/ppermute | solution.py:59
  11.8 0.1 shard_map.137
  11.8 1.4 %collective-permute-start.1 = (bf16[64,768]{1,0:T(8,128)(2,1)S(1)}, bf16[64,768]{1,0:T(8,128)(2,1)S(1)}, u32[]{:S(2)}, u32[]{:S(2)}) collective-permute-start(bf16[64,768]{1,0:T(8,128)(2,1)S(1)} %get-tuple-element.38), channel_id=1, source_target_pairs={{0,2},{2,4},{4,6},{6,0},{1,3},{3,5},{5,7},{7,1},{8,10},{10,12},{12... | collective-permute-start | bytes 294920 | tf_op jit(solution)/shard_map/ppermute | solution.py:55
  13.2 1.4 %collective-permute-start.2 = (bf16[64,768]{1,0:T(8,128)(2,1)S(1)}, bf16[64,768]{1,0:T(8,128)(2,1)S(1)}, u32[]{:S(2)}, u32[]{:S(2)}) collective-permute-start(bf16[64,768]{1,0:T(8,128)(2,1)S(1)} %get-tuple-element.39), channel_id=1, source_target_pairs={{0,6},{2,0},{4,2},{6,4},{1,7},{3,1},{5,3},{7,5},{8,14},{10,8},{12,... | collective-permute-start | bytes 294920 | tf_op jit(solution)/shard_map/ppermute | solution.py:55
  14.6 1.6 %collective-permute-start.3 = (bf16[64,768]{1,0:T(8,128)(2,1)S(1)}, bf16[64,768]{1,0:T(8,128)(2,1)S(1)}, u32[]{:S(2)}, u32[]{:S(2)}) collective-permute-start(bf16[64,768]{1,0:T(8,128)(2,1)S(1)} %get-tuple-element.40), channel_id=1, source_target_pairs={{0,4},{2,6},{4,0},{6,2},{1,5},{3,7},{5,1},{7,3},{8,12},{10,14},{12... | collective-permute-start | bytes 294920 | tf_op jit(solution)/shard_map/ppermute | solution.py:55
  16.2 0.3 shard_map.138
  16.6 0.6 collective-permute-done.1.one
  17.1 2.6 %collective-permute-done.3.two = bf16[64,768]{1,0:T(8,128)(2,1)S(1)} collective-permute-done((bf16[64,768]{1,0:T(8,128)(2,1)S(1)}, bf16[64,768]{1,0:T(8,128)(2,1)S(1)}, u32[]{:S(2)}, u32[]{:S(2)}) %collective-permute-start.3) | collective-permute-done | bytes 98336 | tf_op jit(solution)/shard_map/ppermute | solution.py:55
  19.8 0.0 collective-permute-done.4.rest_0_.gate_far
  19.8 0.0 collective-permute-done.5.rest_1_.up_far
  19.8 0.3 shard_map.139
  20.1 1.7 %collective-permute-start.6 = (bf16[40,768]{1,0:T(8,128)(2,1)S(1)}, bf16[40,768]{1,0:T(8,128)(2,1)S(1)}, u32[]{:S(2)}, u32[]{:S(2)}) collective-permute-start(bf16[40,768]{1,0:T(8,128)(2,1)S(1)} %get-tuple-element.46), channel_id=1, source_target_pairs={{0,32},{32,64},{64,96},{96,0},{1,33},{33,65},{65,97},{97,1},{2,34}... | collective-permute-start | bytes 184328 | tf_op jit(solution)/shard_map/ppermute | solution.py:51
  21.8 2.2 %collective-permute-start.7 = (bf16[40,768]{1,0:T(8,128)(2,1)S(1)}, bf16[40,768]{1,0:T(8,128)(2,1)S(1)}, u32[]{:S(2)}, u32[]{:S(2)}) collective-permute-start(bf16[40,768]{1,0:T(8,128)(2,1)S(1)} %get-tuple-element.47), channel_id=1, source_target_pairs={{0,96},{32,0},{64,32},{96,64},{1,97},{33,1},{65,33},{97,65},{2,98}... | collective-permute-start | bytes 184328 | tf_op jit(solution)/shard_map/ppermute | solution.py:51
  24.0 1.2 collective-permute-start.8
  25.2 0.3 collective-permute-done.6
  25.6 3.2 %collective-permute-done.8 = bf16[40,768]{1,0:T(8,128)(2,1)S(1)} collective-permute-done((bf16[40,768]{1,0:T(8,128)(2,1)S(1)}, bf16[40,768]{1,0:T(8,128)(2,1)S(1)}, u32[]{:S(2)}, u32[]{:S(2)}) %collective-permute-start.8) | collective-permute-done | bytes 61472 | tf_op jit(solution)/shard_map/ppermute | solution.py:51
  28.7 1.4 %collective-permute-start.9 = (bf16[160,768]{1,0:T(8,128)(2,1)S(1)}, bf16[160,768]{1,0:T(8,128)(2,1)S(1)}, u32[]{:S(2)}, u32[]{:S(2)}) collective-permute-start(bf16[160,768]{1,0:T(8,128)(2,1)S(1)} %get-tuple-element.68), channel_id=1, source_target_pairs={{0,2},{1,9},{2,4},{3,11},{4,6},{5,13},{6,0},{7,15},{8,10},{9,17},{... | collective-permute-start | bytes 737288 | tf_op jit(solution)/shard_map/ppermute | solution.py:43
  30.1 1.5 %collective-permute-start.10 = (bf16[160,768]{1,0:T(8,128)(2,1)S(1)}, bf16[160,768]{1,0:T(8,128)(2,1)S(1)}, u32[]{:S(2)}, u32[]{:S(2)}) collective-permute-start(bf16[160,768]{1,0:T(8,128)(2,1)S(1)} %get-tuple-element.68), channel_id=1, source_target_pairs={{0,6},{1,25},{2,0},{3,27},{4,2},{5,29},{6,4},{7,31},{8,14},{9,1},{... | collective-permute-start | bytes 737288 | tf_op jit(solution)/shard_map/ppermute | solution.py:43
  31.6 3.6 %collective-permute-start.17 = (bf16[256,6144]{1,0:T(8,128)(2,1)}, bf16[256,6144]{1,0:T(8,128)(2,1)}, u32[]{:S(2)}, u32[]{:S(2)}) collective-permute-start(bf16[256,6144]{1,0:T(8,128)(2,1)} %down.5), channel_id=1, source_target_pairs={{0,1},{1,0},{2,3},{3,2},{4,5},{5,4},{6,7},{7,6},{8,9},{9,8},{10,11... | collective-permute-start | bytes 9437192 | tf_op jit(solution)/shard_map/ppermute | solution.py:59
  35.3 2.9 %collective-permute-start.11 = (bf16[160,768]{1,0:T(8,128)(2,1)S(1)}, bf16[160,768]{1,0:T(8,128)(2,1)S(1)}, u32[]{:S(2)}, u32[]{:S(2)}) collective-permute-start(bf16[160,768]{1,0:T(8,128)(2,1)S(1)} %get-tuple-element.68), channel_id=1, source_target_pairs={{0,4},{1,17},{2,6},{3,19},{4,0},{5,21},{6,2},{7,23},{8,12},{9,25},... | collective-permute-start | bytes 737288 | tf_op jit(solution)/shard_map/ppermute | solution.py:43
  38.2 3.9 %collective-permute-done.11 = bf16[160,768]{1,0:T(8,128)(2,1)S(1)} collective-permute-done((bf16[160,768]{1,0:T(8,128)(2,1)S(1)}, bf16[160,768]{1,0:T(8,128)(2,1)S(1)}, u32[]{:S(2)}, u32[]{:S(2)}) %collective-permute-start.11) | collective-permute-done | bytes 245792 | tf_op jit(solution)/shard_map/ppermute | solution.py:43
  42.1 0.1 collective-permute-start.14
  42.3 1.6 %collective-permute-start.13 = (bf16[640,768]{1,0:T(8,128)(2,1)S(1)}, bf16[640,768]{1,0:T(8,128)(2,1)}, u32[]{:S(2)}, u32[]{:S(2)}) collective-permute-start(bf16[640,768]{1,0:T(8,128)(2,1)S(1)} %constant_dynamic-update-slice_fusion.4.p0), channel_id=1, source_target_pairs={{0,24},{1,7},{2,26},{3,1},{4,28},{5,3},{6,30},{7,5},{8,0},{9,15},{... | collective-permute-start | bytes 2949128 | tf_op jit(solution)/shard_map/ppermute | solution.py:47
  43.8 0.1 dynamic-slice_reduce_fusion
  43.9 2.9 %shard_map.140.weights = bf16[4,4,768,256]{3,2,1,0:T(8,128)(2,1)S(1)} custom-call(bf16[6144,256]{1,0:T(8,128)(2,1)} %collective-permute-done.4.rest_0_.gate_far, bf16[6144,256]{1,0:T(8,128)(2,1)} %collective-permute-done.5.rest_1_.up_far, bf16[6144,256]{1,0:T(8,128)(2,1)} %gate.1, bf16[6144,256]{1,0:T(8,128)(2,1)} %up.1), custom_call_target="tpu_custom_call" | custom-call | bytes 12000000 | tf_op jit(solution)/shard_map/pallas_call | solution.py:337
  46.9 10.1 %collective-permute-done.14.p3 = bf16[640,768]{1,0:T(8,128)(2,1)S(1)} collective-permute-done((bf16[640,768]{1,0:T(8,128)(2,1)S(1)}, bf16[640,768]{1,0:T(8,128)(2,1)S(1)}, u32[]{:S(2)}, u32[]{:S(2)}) %collective-permute-start.14) | collective-permute-done | bytes 983072 | tf_op jit(solution)/shard_map/ppermute | solution.py:47
  57.0 8.6 %collective-permute-done.13.p2 = bf16[640,768]{1,0:T(8,128)(2,1)} collective-permute-done((bf16[640,768]{1,0:T(8,128)(2,1)S(1)}, bf16[640,768]{1,0:T(8,128)(2,1)}, u32[]{:S(2)}, u32[]{:S(2)}) %collective-permute-start.13) | collective-permute-done | bytes 983072 | tf_op jit(solution)/shard_map/ppermute | solution.py:47
  65.6 2.0 %collective-permute-done.12.p1 = bf16[640,768]{1,0:T(8,128)(2,1)} collective-permute-done((bf16[640,768]{1,0:T(8,128)(2,1)S(1)}, bf16[640,768]{1,0:T(8,128)(2,1)}, u32[]{:S(2)}, u32[]{:S(2)}) %collective-permute-start.12) | collective-permute-done | bytes 983072 | tf_op jit(solution)/shard_map/ppermute | solution.py:47
  67.6 8.5 %shard_map.141 = (f32[640,512]{1,0:T(8,128)S(1)}, f32[640,256]{1,0:T(8,128)S(1)}, bf16[640,768]{1,0:T(8,128)(2,1)S(1)}) custom-call(bf16[640,768]{1,0:T(8,128)(2,1)} %copy-done.3, bf16[640,768]{1,0:T(8,128)(2,1)} %collective-permute-done.12.p1, bf16[640,768]{1,0:T(8,128)(2,1)} %collective-permute-done.13.p2, bf16[640,768]{1,0:T(8,128)(2,1)} %copy-done.5, ...), custom_call_target="tpu_custom_call" | custom-call | flops 4026531840 | bytes 10000000 | tf_op jit(solution)/shard_map/pallas_call | solution.py:399
  76.1 2.2 %collective-permute-start.15 = (bf16[640,768]{1,0:T(8,128)(2,1)S(1)}, bf16[640,768]{1,0:T(8,128)(2,1)S(1)}, u32[]{:S(2)}, u32[]{:S(2)}) collective-permute-start(bf16[640,768]{1,0:T(8,128)(2,1)S(1)} %get-tuple-element.51), channel_id=1, source_target_pairs={{0,1},{1,0},{2,3},{3,2},{4,5},{5,4},{6,7},{7,6},{8,9},{9,8},{10,11... | collective-permute-start | bytes 2949128 | tf_op jit(solution)/shard_map/ppermute | solution.py:59
  78.3 2.2 %collective-permute-done.15.far = bf16[640,768]{1,0:T(8,128)(2,1)S(1)} collective-permute-done((bf16[640,768]{1,0:T(8,128)(2,1)S(1)}, bf16[640,768]{1,0:T(8,128)(2,1)S(1)}, u32[]{:S(2)}, u32[]{:S(2)}) %collective-permute-start.15) | collective-permute-done | bytes 983072 | tf_op jit(solution)/shard_map/ppermute | solution.py:59
  80.5 0.4 shard_map.142
  80.9 0.5 collective-permute-start.16
  81.4 1.3 collective-permute-done.16.act_far
  82.6 1.7 %shard_map.144 = bf16[480,768]{1,0:T(8,128)(2,1)S(1)} custom-call(bf16[640,256]{1,0:T(8,128)(2,1)S(1)} %get-tuple-element.52.act, bf16[640,256]{1,0:T(8,128)(2,1)S(1)} %collective-permute-done.16.act_far, bf16[256,6144]{1,0:T(8,128)(2,1)} %down.5, bf16[256,6144]{1,0:T(8,128)(2,1)} %collective-permute-done.17.down_far), custom_call_target="tpu_custom_call" | custom-call | flops 377487360 | bytes 4000000 | tf_op jit(solution)/shard_map/pallas_call | solution.py:491
  84.4 0.4 collective-permute-start.21
  84.8 2.4 %shard_map.145 = (bf16[480,768]{1,0:T(8,128)(2,1)S(1)}, bf16[480,768]{1,0:T(8,128)(2,1)S(1)}) custom-call(bf16[640,256]{1,0:T(8,128)(2,1)S(1)} %get-tuple-element.52.act, bf16[640,256]{1,0:T(8,128)(2,1)S(1)} %collective-permute-done.16.act_far, bf16[256,6144]{1,0:T(8,128)(2,1)} %down.5, bf16[256,6144]{1,0:T(8,128)(2,1)} %collective-permute-done.17.down_far), custom_call_target="tpu_custom_call" | custom-call | flops 754974720 | bytes 4000000 | tf_op jit(solution)/shard_map/pallas_call | solution.py:491
  87.2 2.4 %collective-permute-start.22 = (bf16[480,768]{1,0:T(8,128)(2,1)S(1)}, bf16[480,768]{1,0:T(8,128)(2,1)S(1)}, u32[]{:S(2)}, u32[]{:S(2)}) collective-permute-start(bf16[480,768]{1,0:T(8,128)(2,1)S(1)} %get-tuple-element.59), channel_id=1, source_target_pairs={{0,8},{1,3},{2,10},{3,5},{4,12},{5,7},{6,14},{7,1},{8,16},{9,11},{... | collective-permute-start | bytes 2211848 | tf_op jit(solution)/shard_map/ppermute | solution.py:47
  89.6 0.3 collective-permute-start.23
  89.9 3.4 %shard_map.143 = (bf16[160,768]{1,0:T(8,128)(2,1)S(1)}, bf16[160,768]{1,0:T(8,128)(2,1)S(1)}, bf16[160,768]{1,0:T(8,128)(2,1)S(1)}, bf16[480,768]{1,0:T(8,128)(2,1)S(1)}, bf16[160,768]{1,0:T(8,128)(2,1)S(1)}) custom-call(bf16[640,256]{1,0:T(8,128)(2,1)S(1)} %get-tuple-element.52.act, bf16[640,256]{1,0:T(8,128)(2,1)S(1)} %collective-permute-done.16.act_far, ...), custom_call_target="tpu_custom_call" | custom-call | flops 880803840 | bytes 4000000 | tf_op jit(solution)/shard_map/pallas_call | solution.py:491
  93.3 1.6 %collective-permute-start.18 = (bf16[160,768]{1,0:T(8,128)(2,1)S(1)}, bf16[160,768]{1,0:T(8,128)(2,1)S(1)}, u32[]{:S(2)}, u32[]{:S(2)}) collective-permute-start(bf16[160,768]{1,0:T(8,128)(2,1)S(1)} %get-tuple-element.55), channel_id=1, source_target_pairs={{0,16},{1,5},{2,18},{3,7},{4,20},{5,1},{6,22},{7,3},{8,24},{9,13},... | collective-permute-start | bytes 737288 | tf_op jit(solution)/shard_map/ppermute | solution.py:47
  95.0 0.2 collective-permute-start.19
  95.1 1.5 %collective-permute-done.21 = bf16[480,768]{1,0:T(8,128)(2,1)S(1)} collective-permute-done((bf16[480,768]{1,0:T(8,128)(2,1)S(1)}, bf16[480,768]{1,0:T(8,128)(2,1)S(1)}, u32[]{:S(2)}, u32[]{:S(2)}) %collective-permute-start.21) | collective-permute-done | bytes 737312 | tf_op jit(solution)/shard_map/ppermute | solution.py:47
  96.6 2.1 %collective-permute-start.20 = (bf16[160,768]{1,0:T(8,128)(2,1)S(1)}, bf16[160,768]{1,0:T(8,128)(2,1)S(1)}, u32[]{:S(2)}, u32[]{:S(2)}) collective-permute-start(bf16[160,768]{1,0:T(8,128)(2,1)S(1)} %get-tuple-element.57), channel_id=1, source_target_pairs={{0,24},{1,7},{2,26},{3,1},{4,28},{5,3},{6,30},{7,5},{8,0},{9,15},{... | collective-permute-start | bytes 737288 | tf_op jit(solution)/shard_map/ppermute | solution.py:47
  98.7 5.8 %collective-permute-done.22 = bf16[480,768]{1,0:T(8,128)(2,1)S(1)} collective-permute-done((bf16[480,768]{1,0:T(8,128)(2,1)S(1)}, bf16[480,768]{1,0:T(8,128)(2,1)S(1)}, u32[]{:S(2)}, u32[]{:S(2)}) %collective-permute-start.22) | collective-permute-done | bytes 737312 | tf_op jit(solution)/shard_map/ppermute | solution.py:47
  104.5 0.4 add_convert_fusion
  104.9 0.1 fusion
  104.9 2.3 %collective-permute-start.26 = (bf16[160,768]{1,0:T(8,128)(2,1)S(1)}, bf16[160,768]{1,0:T(8,128)(2,1)S(1)}, u32[]{:S(2)}, u32[]{:S(2)}) collective-permute-start(bf16[160,768]{1,0:T(8,128)(2,1)S(1)} %get-tuple-element.65), channel_id=1, source_target_pairs={{0,4},{1,17},{2,6},{3,19},{4,0},{5,21},{6,2},{7,23},{8,12},{9,25},... | collective-permute-start | bytes 737288 | tf_op jit(solution)/shard_map/ppermute | solution.py:43
  107.3 0.9 collective-permute-start.25
  108.2 0.5 collective-permute-start.24
  108.7 1.0 collective-permute-done.19.rest_1_
  109.8 4.5 %collective-permute-done.26.rest_5_ = bf16[160,768]{1,0:T(8,128)(2,1)S(1)} collective-permute-done((bf16[160,768]{1,0:T(8,128)(2,1)S(1)}, bf16[160,768]{1,0:T(8,128)(2,1)S(1)}, u32[]{:S(2)}, u32[]{:S(2)}) %collective-permute-start.26) | collective-permute-done | bytes 245792 | tf_op jit(solution)/shard_map/ppermute | solution.py:43
  114.3 2.6 %collective-permute-done.25.rest_4_ = bf16[160,768]{1,0:T(8,128)(2,1)S(1)} collective-permute-done((bf16[160,768]{1,0:T(8,128)(2,1)S(1)}, bf16[160,768]{1,0:T(8,128)(2,1)S(1)}, u32[]{:S(2)}, u32[]{:S(2)}) %collective-permute-start.25) | collective-permute-done | bytes 245792 | tf_op jit(solution)/shard_map/ppermute | solution.py:43
  116.8 0.3 shard_map.146
  117.1 1.7 %collective-permute-start.27 = (bf16[40,896]{1,0:T(8,128)(2,1)S(1)}, bf16[40,896]{1,0:T(8,128)(2,1)S(1)}, u32[]{:S(2)}, u32[]{:S(2)}) collective-permute-start(bf16[40,896]{1,0:T(8,128)(2,1)S(1)} %get-tuple-element.62), channel_id=1, source_target_pairs={{0,96},{32,0},{64,32},{96,64},{1,97},{33,1},{65,33},{97,65},{2,98}... | collective-permute-start | bytes 215048 | tf_op jit(solution)/shard_map/ppermute | solution.py:51
  118.8 1.3 %collective-permute-start.29 = (bf16[40,896]{1,0:T(8,128)(2,1)S(1)}, bf16[40,896]{1,0:T(8,128)(2,1)S(1)}, u32[]{:S(2)}, u32[]{:S(2)}) collective-permute-start(bf16[40,896]{1,0:T(8,128)(2,1)S(1)} %get-tuple-element.64), channel_id=1, source_target_pairs={{0,64},{32,96},{64,0},{96,32},{1,65},{33,97},{65,1},{97,33},{2,66}... | collective-permute-start | bytes 215048 | tf_op jit(solution)/shard_map/ppermute | solution.py:51
  120.1 0.2 collective-permute-done.27.b1
  120.4 3.4 %collective-permute-done.28.b2 = bf16[40,896]{1,0:T(8,128)(2,1)S(1)} collective-permute-done((bf16[40,896]{1,0:T(8,128)(2,1)S(1)}, bf16[40,896]{1,0:T(8,128)(2,1)S(1)}, u32[]{:S(2)}, u32[]{:S(2)}) %collective-permute-start.28) | collective-permute-done | bytes 71712 | tf_op jit(solution)/shard_map/ppermute | solution.py:51
  123.8 0.4 collective-permute-done.29.b3
  124.2 1.2 shard_map.147
  (34 shorter events, 0.2 us)
Async XLA Ops:
  0.0 43.8 %copy-start = (f32[6144,4]{0,1:T(4,128)S(1)}, f32[6144,4]{0,1:T(4,128)}, u32[]{:S(2)}) copy-start(f32[6144,4]{0,1:T(4,128)} %param.24) | copy-start | bytes 294916
  0.0 19.8 %collective-permute-start.4 = (bf16[6144,256]{1,0:T(8,128)(2,1)}, bf16[6144,256]{1,0:T(8,128)(2,1)}, u32[]{:S(2)}, u32[]{:S(2)}) collective-permute-start(bf16[6144,256]{1,0:T(8,128)(2,1)} %gate.1), channel_id=1, source_target_pairs={{0,1},{1,0},{2,3},{3,2},{4,5},{5,4},{6,7},{7,6},{8,9},{9,8},{10,11... | collective-permute-start | bytes 9437192 | tf_op jit(solution)/shard_map/ppermute | solution.py:59
  1.4 18.3 %collective-permute-start.5 = (bf16[6144,256]{1,0:T(8,128)(2,1)}, bf16[6144,256]{1,0:T(8,128)(2,1)}, u32[]{:S(2)}, u32[]{:S(2)}) collective-permute-start(bf16[6144,256]{1,0:T(8,128)(2,1)} %up.1), channel_id=1, source_target_pairs={{0,1},{1,0},{2,3},{3,2},{4,5},{5,4},{6,7},{7,6},{8,9},{9,8},{10,11... | collective-permute-start | bytes 9437192 | tf_op jit(solution)/shard_map/ppermute | solution.py:59
  1.4 8.4 %copy-start.4 = (s32[64,2]{0,1:T(2,128)S(1)}, s32[64,2]{0,1:T(2,128)}, u32[]{:S(2)}) copy-start(s32[64,2]{0,1:T(2,128)} %param.21) | copy-start | bytes 1540
  1.4 14.8 %copy-start.2 = (bf16[6144]{0:T(1024)(128)(2,1)S(1)}, bf16[6144]{0:T(1024)(128)(2,1)}, u32[]{:S(2)}) copy-start(bf16[6144]{0:T(1024)(128)(2,1)} %param.23) | copy-start | bytes 36868
  1.4 18.3 %copy-start.1 = (bf16[64,768]{1,0:T(8,128)(2,1)S(1)}, bf16[64,768]{1,0:T(8,128)(2,1)}, u32[]{:S(2)}) copy-start(bf16[64,768]{1,0:T(8,128)(2,1)} %tokens.1) | copy-start | bytes 294916
  9.3 2.5 %collective-permute-start = (bf16[4,64,768]{2,1,0:T(8,128)(2,1)S(1)}, bf16[4,64,768]{2,1,0:T(8,128)(2,1)S(1)}, u32[]{:S(2)}, u32[]{:S(2)}) collective-permute-start(bf16[4,64,768]{2,1,0:T(8,128)(2,1)S(1)} %get-tuple-element.36), channel_id=1, source_target_pairs={{0,1},{1,0},{2,3},{3,2},{4,5},{5,4},{6,7},{7,6},{8,9},{9,8},{10,11... | collective-permute-start | bytes 1179656 | tf_op jit(solution)/shard_map/ppermute | solution.py:59
  11.8 5.3 %collective-permute-start.1 = (bf16[64,768]{1,0:T(8,128)(2,1)S(1)}, bf16[64,768]{1,0:T(8,128)(2,1)S(1)}, u32[]{:S(2)}, u32[]{:S(2)}) collective-permute-start(bf16[64,768]{1,0:T(8,128)(2,1)S(1)} %get-tuple-element.38), channel_id=1, source_target_pairs={{0,2},{2,4},{4,6},{6,0},{1,3},{3,5},{5,7},{7,1},{8,10},{10,12},{12... | collective-permute-start | bytes 294920 | tf_op jit(solution)/shard_map/ppermute | solution.py:55
  13.2 3.9 %collective-permute-start.2 = (bf16[64,768]{1,0:T(8,128)(2,1)S(1)}, bf16[64,768]{1,0:T(8,128)(2,1)S(1)}, u32[]{:S(2)}, u32[]{:S(2)}) collective-permute-start(bf16[64,768]{1,0:T(8,128)(2,1)S(1)} %get-tuple-element.39), channel_id=1, source_target_pairs={{0,6},{2,0},{4,2},{6,4},{1,7},{3,1},{5,3},{7,5},{8,14},{10,8},{12,... | collective-permute-start | bytes 294920 | tf_op jit(solution)/shard_map/ppermute | solution.py:55
  14.6 5.2 %collective-permute-start.3 = (bf16[64,768]{1,0:T(8,128)(2,1)S(1)}, bf16[64,768]{1,0:T(8,128)(2,1)S(1)}, u32[]{:S(2)}, u32[]{:S(2)}) collective-permute-start(bf16[64,768]{1,0:T(8,128)(2,1)S(1)} %get-tuple-element.40), channel_id=1, source_target_pairs={{0,4},{2,6},{4,0},{6,2},{1,5},{3,7},{5,1},{7,3},{8,12},{10,14},{12... | collective-permute-start | bytes 294920 | tf_op jit(solution)/shard_map/ppermute | solution.py:55
  20.1 5.4 %collective-permute-start.6 = (bf16[40,768]{1,0:T(8,128)(2,1)S(1)}, bf16[40,768]{1,0:T(8,128)(2,1)S(1)}, u32[]{:S(2)}, u32[]{:S(2)}) collective-permute-start(bf16[40,768]{1,0:T(8,128)(2,1)S(1)} %get-tuple-element.46), channel_id=1, source_target_pairs={{0,32},{32,64},{64,96},{96,0},{1,33},{33,65},{65,97},{97,1},{2,34}... | collective-permute-start | bytes 184328 | tf_op jit(solution)/shard_map/ppermute | solution.py:51
  21.8 3.7 %collective-permute-start.7 = (bf16[40,768]{1,0:T(8,128)(2,1)S(1)}, bf16[40,768]{1,0:T(8,128)(2,1)S(1)}, u32[]{:S(2)}, u32[]{:S(2)}) collective-permute-start(bf16[40,768]{1,0:T(8,128)(2,1)S(1)} %get-tuple-element.47), channel_id=1, source_target_pairs={{0,96},{32,0},{64,32},{96,64},{1,97},{33,1},{65,33},{97,65},{2,98}... | collective-permute-start | bytes 184328 | tf_op jit(solution)/shard_map/ppermute | solution.py:51
  24.0 4.7 %collective-permute-start.8 = (bf16[40,768]{1,0:T(8,128)(2,1)S(1)}, bf16[40,768]{1,0:T(8,128)(2,1)S(1)}, u32[]{:S(2)}, u32[]{:S(2)}) collective-permute-start(bf16[40,768]{1,0:T(8,128)(2,1)S(1)} %get-tuple-element.48), channel_id=1, source_target_pairs={{0,64},{32,96},{64,0},{96,32},{1,65},{33,97},{65,1},{97,33},{2,66}... | collective-permute-start | bytes 184328 | tf_op jit(solution)/shard_map/ppermute | solution.py:51
  28.7 9.4 %collective-permute-start.9 = (bf16[160,768]{1,0:T(8,128)(2,1)S(1)}, bf16[160,768]{1,0:T(8,128)(2,1)S(1)}, u32[]{:S(2)}, u32[]{:S(2)}) collective-permute-start(bf16[160,768]{1,0:T(8,128)(2,1)S(1)} %get-tuple-element.68), channel_id=1, source_target_pairs={{0,2},{1,9},{2,4},{3,11},{4,6},{5,13},{6,0},{7,15},{8,10},{9,17},{... | collective-permute-start | bytes 737288 | tf_op jit(solution)/shard_map/ppermute | solution.py:43
  30.1 8.1 %collective-permute-start.10 = (bf16[160,768]{1,0:T(8,128)(2,1)S(1)}, bf16[160,768]{1,0:T(8,128)(2,1)S(1)}, u32[]{:S(2)}, u32[]{:S(2)}) collective-permute-start(bf16[160,768]{1,0:T(8,128)(2,1)S(1)} %get-tuple-element.68), channel_id=1, source_target_pairs={{0,6},{1,25},{2,0},{3,27},{4,2},{5,29},{6,4},{7,31},{8,14},{9,1},{... | collective-permute-start | bytes 737288 | tf_op jit(solution)/shard_map/ppermute | solution.py:43
  31.6 49.8 %collective-permute-start.17 = (bf16[256,6144]{1,0:T(8,128)(2,1)}, bf16[256,6144]{1,0:T(8,128)(2,1)}, u32[]{:S(2)}, u32[]{:S(2)}) collective-permute-start(bf16[256,6144]{1,0:T(8,128)(2,1)} %down.5), channel_id=1, source_target_pairs={{0,1},{1,0},{2,3},{3,2},{4,5},{5,4},{6,7},{7,6},{8,9},{9,8},{10,11... | collective-permute-start | bytes 9437192 | tf_op jit(solution)/shard_map/ppermute | solution.py:59
  35.3 6.8 %collective-permute-start.11 = (bf16[160,768]{1,0:T(8,128)(2,1)S(1)}, bf16[160,768]{1,0:T(8,128)(2,1)S(1)}, u32[]{:S(2)}, u32[]{:S(2)}) collective-permute-start(bf16[160,768]{1,0:T(8,128)(2,1)S(1)} %get-tuple-element.68), channel_id=1, source_target_pairs={{0,4},{1,17},{2,6},{3,19},{4,0},{5,21},{6,2},{7,23},{8,12},{9,25},... | collective-permute-start | bytes 737288 | tf_op jit(solution)/shard_map/ppermute | solution.py:43
  42.1 4.7 %copy-start.3 = (bf16[640,768]{1,0:T(8,128)(2,1)}, bf16[640,768]{1,0:T(8,128)(2,1)S(1)}, u32[]{:S(2)}) copy-start(bf16[640,768]{1,0:T(8,128)(2,1)S(1)} %constant_dynamic-update-slice_fusion.4.p0) | copy-start | bytes 2949124
  42.1 14.9 %collective-permute-start.14 = (bf16[640,768]{1,0:T(8,128)(2,1)S(1)}, bf16[640,768]{1,0:T(8,128)(2,1)S(1)}, u32[]{:S(2)}, u32[]{:S(2)}) collective-permute-start(bf16[640,768]{1,0:T(8,128)(2,1)S(1)} %constant_dynamic-update-slice_fusion.4.p0), channel_id=1, source_target_pairs={{0,16},{1,5},{2,18},{3,7},{4,20},{5,1},{6,22},{7,3},{8,24},{9,13},... | collective-permute-start | bytes 2949128 | tf_op jit(solution)/shard_map/ppermute | solution.py:47
  42.3 23.3 %collective-permute-start.13 = (bf16[640,768]{1,0:T(8,128)(2,1)S(1)}, bf16[640,768]{1,0:T(8,128)(2,1)}, u32[]{:S(2)}, u32[]{:S(2)}) collective-permute-start(bf16[640,768]{1,0:T(8,128)(2,1)S(1)} %constant_dynamic-update-slice_fusion.4.p0), channel_id=1, source_target_pairs={{0,24},{1,7},{2,26},{3,1},{4,28},{5,3},{6,30},{7,5},{8,0},{9,15},{... | collective-permute-start | bytes 2949128 | tf_op jit(solution)/shard_map/ppermute | solution.py:47
  43.8 23.8 %collective-permute-start.12 = (bf16[640,768]{1,0:T(8,128)(2,1)S(1)}, bf16[640,768]{1,0:T(8,128)(2,1)}, u32[]{:S(2)}, u32[]{:S(2)}) collective-permute-start(bf16[640,768]{1,0:T(8,128)(2,1)S(1)} %constant_dynamic-update-slice_fusion.4.p0), channel_id=1, source_target_pairs={{0,8},{1,3},{2,10},{3,5},{4,12},{5,7},{6,14},{7,1},{8,16},{9,11},{... | collective-permute-start | bytes 2949128 | tf_op jit(solution)/shard_map/ppermute | solution.py:47
  57.0 10.6 %copy-start.5 = (bf16[640,768]{1,0:T(8,128)(2,1)}, bf16[640,768]{1,0:T(8,128)(2,1)S(1)}, u32[]{:S(2)}) copy-start(bf16[640,768]{1,0:T(8,128)(2,1)S(1)} %collective-permute-done.14.p3) | copy-start | bytes 2949124
  76.1 4.4 %collective-permute-start.15 = (bf16[640,768]{1,0:T(8,128)(2,1)S(1)}, bf16[640,768]{1,0:T(8,128)(2,1)S(1)}, u32[]{:S(2)}, u32[]{:S(2)}) collective-permute-start(bf16[640,768]{1,0:T(8,128)(2,1)S(1)} %get-tuple-element.51), channel_id=1, source_target_pairs={{0,1},{1,0},{2,3},{3,2},{4,5},{5,4},{6,7},{7,6},{8,9},{9,8},{10,11... | collective-permute-start | bytes 2949128 | tf_op jit(solution)/shard_map/ppermute | solution.py:59
  80.9 1.7 %collective-permute-start.16 = (bf16[640,256]{1,0:T(8,128)(2,1)S(1)}, bf16[640,256]{1,0:T(8,128)(2,1)S(1)}, u32[]{:S(2)}, u32[]{:S(2)}) collective-permute-start(bf16[640,256]{1,0:T(8,128)(2,1)S(1)} %get-tuple-element.52.act), channel_id=1, source_target_pairs={{0,1},{1,0},{2,3},{3,2},{4,5},{5,4},{6,7},{7,6},{8,9},{9,8},{10,11... | collective-permute-start | bytes 983048 | tf_op jit(solution)/shard_map/ppermute | solution.py:59
  84.4 12.2 %collective-permute-start.21 = (bf16[480,768]{1,0:T(8,128)(2,1)S(1)}, bf16[480,768]{1,0:T(8,128)(2,1)S(1)}, u32[]{:S(2)}, u32[]{:S(2)}) collective-permute-start(bf16[480,768]{1,0:T(8,128)(2,1)S(1)} %shard_map.144), channel_id=1, source_target_pairs={{0,16},{1,5},{2,18},{3,7},{4,20},{5,1},{6,22},{7,3},{8,24},{9,13},... | collective-permute-start | bytes 2211848 | tf_op jit(solution)/shard_map/ppermute | solution.py:47
  87.2 17.3 %collective-permute-start.22 = (bf16[480,768]{1,0:T(8,128)(2,1)S(1)}, bf16[480,768]{1,0:T(8,128)(2,1)S(1)}, u32[]{:S(2)}, u32[]{:S(2)}) collective-permute-start(bf16[480,768]{1,0:T(8,128)(2,1)S(1)} %get-tuple-element.59), channel_id=1, source_target_pairs={{0,8},{1,3},{2,10},{3,5},{4,12},{5,7},{6,14},{7,1},{8,16},{9,11},{... | collective-permute-start | bytes 2211848 | tf_op jit(solution)/shard_map/ppermute | solution.py:47
  89.6 14.9 %collective-permute-start.23 = (bf16[480,768]{1,0:T(8,128)(2,1)S(1)}, bf16[480,768]{1,0:T(8,128)(2,1)S(1)}, u32[]{:S(2)}, u32[]{:S(2)}) collective-permute-start(bf16[480,768]{1,0:T(8,128)(2,1)S(1)} %get-tuple-element.60), channel_id=1, source_target_pairs={{0,24},{1,7},{2,26},{3,1},{4,28},{5,3},{6,30},{7,5},{8,0},{9,15},{... | collective-permute-start | bytes 2211848 | tf_op jit(solution)/shard_map/ppermute | solution.py:47
  93.3 14.9 %collective-permute-start.18 = (bf16[160,768]{1,0:T(8,128)(2,1)S(1)}, bf16[160,768]{1,0:T(8,128)(2,1)S(1)}, u32[]{:S(2)}, u32[]{:S(2)}) collective-permute-start(bf16[160,768]{1,0:T(8,128)(2,1)S(1)} %get-tuple-element.55), channel_id=1, source_target_pairs={{0,16},{1,5},{2,18},{3,7},{4,20},{5,1},{6,22},{7,3},{8,24},{9,13},... | collective-permute-start | bytes 737288 | tf_op jit(solution)/shard_map/ppermute | solution.py:47
  95.0 14.8 %collective-permute-start.19 = (bf16[160,768]{1,0:T(8,128)(2,1)S(1)}, bf16[160,768]{1,0:T(8,128)(2,1)S(1)}, u32[]{:S(2)}, u32[]{:S(2)}) collective-permute-start(bf16[160,768]{1,0:T(8,128)(2,1)S(1)} %get-tuple-element.56), channel_id=1, source_target_pairs={{0,8},{1,3},{2,10},{3,5},{4,12},{5,7},{6,14},{7,1},{8,16},{9,11},{... | collective-permute-start | bytes 737288 | tf_op jit(solution)/shard_map/ppermute | solution.py:47
  96.6 13.1 %collective-permute-start.20 = (bf16[160,768]{1,0:T(8,128)(2,1)S(1)}, bf16[160,768]{1,0:T(8,128)(2,1)S(1)}, u32[]{:S(2)}, u32[]{:S(2)}) collective-permute-start(bf16[160,768]{1,0:T(8,128)(2,1)S(1)} %get-tuple-element.57), channel_id=1, source_target_pairs={{0,24},{1,7},{2,26},{3,1},{4,28},{5,3},{6,30},{7,5},{8,0},{9,15},{... | collective-permute-start | bytes 737288 | tf_op jit(solution)/shard_map/ppermute | solution.py:47
  104.9 9.3 %collective-permute-start.26 = (bf16[160,768]{1,0:T(8,128)(2,1)S(1)}, bf16[160,768]{1,0:T(8,128)(2,1)S(1)}, u32[]{:S(2)}, u32[]{:S(2)}) collective-permute-start(bf16[160,768]{1,0:T(8,128)(2,1)S(1)} %get-tuple-element.65), channel_id=1, source_target_pairs={{0,4},{1,17},{2,6},{3,19},{4,0},{5,21},{6,2},{7,23},{8,12},{9,25},... | collective-permute-start | bytes 737288 | tf_op jit(solution)/shard_map/ppermute | solution.py:43
  107.3 9.6 %collective-permute-start.25 = (bf16[160,768]{1,0:T(8,128)(2,1)S(1)}, bf16[160,768]{1,0:T(8,128)(2,1)S(1)}, u32[]{:S(2)}, u32[]{:S(2)}) collective-permute-start(bf16[160,768]{1,0:T(8,128)(2,1)S(1)} %get-tuple-element.66), channel_id=1, source_target_pairs={{0,6},{1,25},{2,0},{3,27},{4,2},{5,29},{6,4},{7,31},{8,14},{9,1},{... | collective-permute-start | bytes 737288 | tf_op jit(solution)/shard_map/ppermute | solution.py:43
  108.2 8.6 %collective-permute-start.24 = (bf16[160,768]{1,0:T(8,128)(2,1)S(1)}, bf16[160,768]{1,0:T(8,128)(2,1)S(1)}, u32[]{:S(2)}, u32[]{:S(2)}) collective-permute-start(bf16[160,768]{1,0:T(8,128)(2,1)S(1)} %get-tuple-element.67), channel_id=1, source_target_pairs={{0,2},{1,9},{2,4},{3,11},{4,6},{5,13},{6,0},{7,15},{8,10},{9,17},{... | collective-permute-start | bytes 737288 | tf_op jit(solution)/shard_map/ppermute | solution.py:43
  117.1 3.3 %collective-permute-start.27 = (bf16[40,896]{1,0:T(8,128)(2,1)S(1)}, bf16[40,896]{1,0:T(8,128)(2,1)S(1)}, u32[]{:S(2)}, u32[]{:S(2)}) collective-permute-start(bf16[40,896]{1,0:T(8,128)(2,1)S(1)} %get-tuple-element.62), channel_id=1, source_target_pairs={{0,96},{32,0},{64,32},{96,64},{1,97},{33,1},{65,33},{97,65},{2,98}... | collective-permute-start | bytes 215048 | tf_op jit(solution)/shard_map/ppermute | solution.py:51
  118.8 4.9 %collective-permute-start.28 = (bf16[40,896]{1,0:T(8,128)(2,1)S(1)}, bf16[40,896]{1,0:T(8,128)(2,1)S(1)}, u32[]{:S(2)}, u32[]{:S(2)}) collective-permute-start(bf16[40,896]{1,0:T(8,128)(2,1)S(1)} %get-tuple-element.63), channel_id=1, source_target_pairs={{0,32},{32,64},{64,96},{96,0},{1,33},{33,65},{65,97},{97,1},{2,34}... | collective-permute-start | bytes 215048 | tf_op jit(solution)/shard_map/ppermute | solution.py:51
  118.8 5.4 %collective-permute-start.29 = (bf16[40,896]{1,0:T(8,128)(2,1)S(1)}, bf16[40,896]{1,0:T(8,128)(2,1)S(1)}, u32[]{:S(2)}, u32[]{:S(2)}) collective-permute-start(bf16[40,896]{1,0:T(8,128)(2,1)S(1)} %get-tuple-element.64), channel_id=1, source_target_pairs={{0,64},{32,96},{64,0},{96,32},{1,65},{33,97},{65,1},{97,33},{2,66}... | collective-permute-start | bytes 215048 | tf_op jit(solution)/shard_map/ppermute | solution.py:51

commit v5 on v4

--- a/solution.py
+++ b/solution.py
@@ -129,7 +129,7 @@
     scale = 1.0 / math.sqrt(size)
     for n in range(4):
         copy(n).wait()
-        start(n + 7)
+        start((8, 10, 12, 12)[n])
         for t in range(n * chunk, (n + 1) * chunk):
             query = query_here[pl.ds(t, 8, stride=rows), :]
             score[row(t), :] = scale * lax.dot_general(
@@ -139,7 +139,7 @@
     slot = lax.broadcasted_iota(jnp.int32, (8, score.shape[1]), 1)
     for n in range(4):
         copy(n + 4).wait()
-        start(n + 11)
+        start(13 + n)
         for t in range(n * chunk, (n + 1) * chunk):
             query = query_here[pl.ds(t, 8, stride=rows), :]
             new_key = new_keys[t : t + 1, :].astype(jnp.float32)
@@ -225,7 +225,13 @@
     )(near(own), near(far), routes)
 
 
-def slots_kernel(routes, first, second):
+def slots_kernel(routes, down, first, second, down_half, sems):
+    c = position()[2]
+    copies = []
+    for k in range(4):
+        start = pl.multiple_of((2 * k + 1 - c) * BLK, BLK)
+        copies.append(pltpu.make_async_copy(down.at[:, pl.ds(start, BLK)], down_half.at[k], sems.at[k]))
+        copies[k].start()
     rows = routes.shape[0]
     lane = lax.broadcasted_iota(jnp.int32, (rows, 128), 1)
     plane = jnp.full((rows, 128), -1, jnp.int32)
@@ -242,17 +248,20 @@
         hit = slot == rank[:, i : i + 1]
         first[i] = jnp.where(hit, one[:, i : i + 1], 0.0).astype(jnp.bfloat16)
         second[i] = jnp.where(hit, two[:, i : i + 1], 0.0).astype(jnp.bfloat16)
-
-
-def slots(routes):
+    for copy in copies:
+        copy.wait()
+
+
+def slots(routes, down):
     shape = pltpu.VMEM((4, routes.shape[0], CAP), jnp.bfloat16)
     return pl.pallas_call(
         slots_kernel,
-        out_shape=(shape, shape),
-        in_specs=[VMEM],
-        out_specs=(VMEM, VMEM),
+        out_shape=(shape, shape, pltpu.VMEM((4, HID, BLK), jnp.bfloat16)),
+        in_specs=[VMEM, ANY],
+        out_specs=(VMEM,) * 3,
+        scratch_shapes=[pltpu.SemaphoreType.DMA((4,))],
         compiler_params=params(4),
-    )(routes)
+    )(routes, distant(down))
 
 
 def prepare_kernel(own, one, three, two, tokens, gain, first, second, *rest):
@@ -284,6 +293,23 @@
     )(own, one, three, two, tokens, gain, first, second, *map(distant, swapped))
 
 
+def join_kernel(a, b, c, d, token, out):
+    for i, part in enumerate((a, b, c, d)):
+        out[i * ROWS : (i + 1) * ROWS, :] = part[...]
+
+
+def join(parts):
+    token = swap_cores(sum(part[:16, :128].astype(jnp.float32) for part in parts[1:]))
+    return pl.pallas_call(
+        join_kernel,
+        out_shape=pltpu.VMEM((4 * ROWS, BLK), jnp.bfloat16),
+        in_specs=[VMEM] * 4 + [ANY],
+        out_specs=VMEM,
+        compiler_params=params(4),
+        cost_estimate=pl.CostEstimate(flops=0, bytes_accessed=2000000, transcendentals=0),
+    )(*parts, token)
+
+
 def line_rows(index):
     return pl.ds(pl.multiple_of(index * ROWS, ROWS), ROWS)
 
@@ -299,7 +325,7 @@
     return (position - shift + 4) % 4
 
 
-def walk(pieces, emit):
+def walk(held, emit):
     x, y, c, _ = position()
     blocks = [2 * behind(x, shift) + c for shift in OFFS]
 
@@ -308,112 +334,161 @@
         @pl.when(c == core)
         def _(core=core):
             for m, shift in enumerate(OFFS):
-
-                def found(n, m=m):
-                    j, i = (m, n) if core == 0 else (n, m)
-                    return pieces[j, i * ROWS : (i + 1) * ROWS, :]
-
-                emit(line_rows(behind(y, shift)), found, blocks, m, core)
-
-
-def stage_kernel(gate_far, up_far, gate, up, weights, sems):
+                if core == 0:
+                    spots = {n: (held.index(m), n) for n in range(4)} if m in held else {}
+                else:
+                    spots = {n: (j, m) for j, n in enumerate(held)}
+                emit(core, line_rows(behind(y, shift)), m, blocks, spots)
+
+
+def stage_kernel(gate_far, up_far, gate, up, down, down_far, weights, downs, sems):
     x, _, c, _ = position()
     copies = []
-    for which, source in enumerate((gate_far, up_far, gate, up)):
-        for n, shift in enumerate(OFFS):
-            start = pl.multiple_of((2 * behind(x, shift) + c) * BLK, BLK)
-            copies.append(
-                pltpu.make_async_copy(
-                    source.at[pl.ds(start, BLK), :], weights.at[which, n], sems.at[4 * which + n]
-                )
-            )
+    for n, shift in enumerate(OFFS):
+        rows = pl.ds(pl.multiple_of((2 * behind(x, shift) + c) * BLK, BLK), BLK)
+        columns = pl.ds(pl.multiple_of((2 * behind(x, -shift) + c) * BLK, BLK), BLK)
+        for which, source in enumerate((gate_far, up_far, gate, up)):
+            copies.append((source.at[rows, :], weights.at[which, n]))
+        copies.append((down.at[:, columns], downs.at[0, n]))
+        copies.append((down_far.at[behind(x, -shift)], downs.at[1, n]))
+    copies = [pltpu.make_async_copy(*ends, sems.at[i]) for i, ends in enumerate(copies)]
     for copy in copies:
         copy.start()
     for copy in copies:
         copy.wait()
 
 
-def stage(gate_far, up_far, gate, up):
+def stage(*sources):
     return pl.pallas_call(
         stage_kernel,
-        out_shape=pltpu.VMEM((4, 4, BLK, HID), jnp.bfloat16),
-        in_specs=[ANY] * 4,
-        out_specs=VMEM,
-        scratch_shapes=[pltpu.SemaphoreType.DMA((16,))],
-        compiler_params=params(8),
-        cost_estimate=pl.CostEstimate(flops=0, bytes_accessed=12000000, transcendentals=0),
-    )(*map(distant, (gate_far, up_far, gate, up)))
-
-
-def enter_kernel(p0, p1, p2, p3, weights, inverse, route, own, sums, far, pieces, sems):
-    given = (p0, p1, p2, p3)
-
-    def line(core, m):
-        copies = []
-        for n in range(4):
-            j, i = (m, n) if core == 0 else (n, m)
-            rows = pl.ds(i * ROWS, ROWS)
-            copies.append(
-                pltpu.make_async_copy(given[j].at[rows, :], pieces.at[j, rows, :], sems.at[4 * j + i])
-            )
-        return copies
-
-    def start(core, m):
-        for copy in line(core, m):
+        out_shape=(
+            pltpu.VMEM((4, 4, BLK, HID), jnp.bfloat16),
+            pltpu.VMEM((2, 4, HID, BLK), jnp.bfloat16),
+        ),
+        in_specs=[ANY] * 6,
+        out_specs=(VMEM, VMEM),
+        scratch_shapes=[pltpu.SemaphoreType.DMA((24,))],
+        compiler_params=params(12),
+        cost_estimate=pl.CostEstimate(flops=0, bytes_accessed=18000000, transcendentals=0),
+    )(*map(distant, sources))
+
+
+def enter_terms(pieces, weights, inverse, route, blocks, spots):
+    def found(n):
+        j, i = spots[n]
+        return pieces[j, i * ROWS : (i + 1) * ROWS, :]
+
+    def total(terms):
+        return functools.reduce(lambda a, b: a + b, terms)
+
+    sums = [total([dot(found(n), weights[which, n]) for n in spots]) for which in range(4)]
+    squares, products = [], []
+    for n in spots:
+        value = found(n).astype(jnp.float32)
+        plain = value * inverse[pl.ds(blocks[n], 1), :]
+        squares.append(lanes(plain * plain))
+        products.append(lanes(value * route[pl.ds(blocks[n], 1), :]))
+    return sums, (total(squares), total(products))
+
+
+def put(ref, rows, values):
+    start = 0
+    for value in values:
+        ref[rows, start : start + value.shape[1]] = value.astype(ref.dtype)
+        start += value.shape[1]
+
+
+def enter_first_kernel(p0, p1, weights, inverse, route, own, sums, far, pieces, sems):
+    copies = [pltpu.make_async_copy(p, pieces.at[j], sems.at[j]) for j, p in enumerate((p0, p1))]
+    for copy in copies:
+        copy.start()
+    for copy in copies:
+        copy.wait()
+
+    def emit(core, rows, m, blocks, spots):
+        if spots:
+            terms, both = enter_terms(pieces, weights, inverse, route, blocks, spots)
+            put(far, rows, terms[:2])
+            put(own, rows, terms[2:])
+            put(sums, rows, both)
+
+    walk((0, 3), emit)
+
+
+def enter_second_kernel(
+    p0, p1, weights, inverse, route, own_first, sums_first, far_first, own, sums, far, pieces, sems
+):
+    given = (p0, p1)
+
+    def copies(core, step):
+        parts = []
+        for j in range(2):
+            if core == 0 and j == step or core == 1:
+                rows = pl.ds(0, 4 * ROWS) if core == 0 else pl.ds(step * ROWS, ROWS)
+                parts.append(
+                    pltpu.make_async_copy(given[j].at[rows, :], pieces.at[j, rows, :], sems.at[4 * j + step])
+                )
+        return parts
+
+    def start(core, step):
+        for copy in copies(core, step):
             copy.start()
 
-    def product(found, which):
-        total = dot(found(0), weights[which, 0])
-        for n in range(1, 4):
-            total += dot(found(n), weights[which, n])
-        return total
-
-    def emit_far(rows, found, blocks, m, core):
+    def wait(core, step):
+        for copy in copies(core, step):
+            copy.wait()
+
+    def emit(core, rows, m, blocks, spots):
         if m == 0:
             start(core, 0)
             start(core, 1)
-        for copy in line(core, m):
-            copy.wait()
-        if m < 2:
-            start(core, m + 2)
-        far[rows, :HID] = product(found, 0).astype(far.dtype)
-        far[rows, HID : 2 * HID] = product(found, 1).astype(far.dtype)
-        for n, index in enumerate(blocks):
-            value = found(n).astype(jnp.float32)
-            plain = value * inverse[pl.ds(index, 1), :]
-            terms = lanes(plain * plain), lanes(value * route[pl.ds(index, 1), :])
-            totals = terms if n == 0 else [a + b for a, b in zip(totals, terms)]
-        for n, total in enumerate(totals):
-            sums[rows, n * 128 : (n + 1) * 128] = total
-            far[rows, 2 * HID + n * 128 : 2 * HID + (n + 1) * 128] = total.astype(far.dtype)
-
-    def emit_own(rows, found, blocks, m, core):
-        own[rows, :HID] = product(found, 2)
-        own[rows, HID:] = product(found, 3)
-
-    walk(pieces, emit_far)
-    walk(pieces, emit_own)
+        if core == 0 and m in (1, 2):
+            wait(core, m - 1)
+        if core == 1:
+            wait(core, m)
+            if m < 2:
+                start(core, m + 2)
+        before = (far_first[rows, :], own_first[rows, :], sums_first[rows, :])
+        if not spots:
+            far_all, own_all, both = before
+        else:
+            terms, both = enter_terms(pieces, weights, inverse, route, blocks, spots)
+            far_all, own_all, both = (jnp.concatenate(v, axis=1) for v in (terms[:2], terms[2:], both))
+            if core == 1:
+                far_all, own_all, both = far_all + before[0], own_all + before[1], both + before[2]
+        own[rows, :] = own_all
+        sums[rows, :] = both
+        put(far, rows, (far_all, both))
+
+    walk((1, 2), emit)
 
 
 def enter(pieces, weights, inverse, route):
-    return pl.pallas_call(
-        enter_kernel,
-        out_shape=(
-            pltpu.VMEM((4 * ROWS, 2 * HID), jnp.float32),
-            pltpu.VMEM((4 * ROWS, 256), jnp.float32),
-            pltpu.VMEM((4 * ROWS, 2 * HID + 256), jnp.bfloat16),
-        ),
-        in_specs=[ANY] * 4 + [VMEM] * 3,
+    own = pltpu.VMEM((4 * ROWS, 2 * HID), jnp.float32)
+    sums = pltpu.VMEM((4 * ROWS, 256), jnp.float32)
+    cost = pl.CostEstimate(
+        flops=2 * 4 * ROWS * 2 * BLK * 4 * HID, bytes_accessed=5000000, transcendentals=0
+    )
+    scratch = [pltpu.VMEM((2, 4 * ROWS, BLK), jnp.bfloat16), pltpu.SemaphoreType.DMA((8,))]
+    fixed = (near(weights), near(inverse), near(route))
+    first = pl.pallas_call(
+        enter_first_kernel,
+        out_shape=(own, sums, own),
+        in_specs=[ANY] * 2 + [VMEM] * 3,
         out_specs=(VMEM,) * 3,
-        scratch_shapes=[
-            pltpu.VMEM((4, 4 * ROWS, BLK), jnp.bfloat16),
-            pltpu.SemaphoreType.DMA((16,)),
-        ],
-        compiler_params=params(16),
-        cost_estimate=pl.CostEstimate(
-            flops=2 * 4 * ROWS * 4 * BLK * 4 * HID, bytes_accessed=10000000, transcendentals=0
-        ),
-    )(*map(distant, pieces), near(weights), near(inverse), near(route))
+        scratch_shapes=scratch,
+        compiler_params=params(10),
+        cost_estimate=cost,
+    )(distant(pieces[0]), distant(pieces[3]), *fixed)
+    return pl.pallas_call(
+        enter_second_kernel,
+        out_shape=(own, sums, pltpu.VMEM((4 * ROWS, 2 * HID + 256), jnp.bfloat16)),
+        in_specs=[ANY] * 2 + [VMEM] * 6,
+        out_specs=(VMEM,) * 3,
+        scratch_shapes=scratch,
+        compiler_params=params(10),
+        cost_estimate=cost,
+    )(distant(pieces[1]), distant(pieces[2]), *fixed, *map(near, first))
 
 
 def activate_kernel(own, sums, far, out, logit):
@@ -443,68 +518,35 @@
     )(near(own), near(sums), near(far))
 
 
-def leave_kernel(wanted, act, act_far, down, down_far, *rest):
-    outs, (own_here, far_here, sems) = rest[:-3], rest[-3:]
-    x, y, c, _ = position()
-
-    def ahead(position, shift):
-        return (position + shift + 4) % 4
-
-    def copies(n):
-        start = pl.multiple_of((2 * ahead(x, OFFS[n]) + c) * BLK, BLK)
-        return (
-            pltpu.make_async_copy(down.at[:, pl.ds(start, BLK)], own_here.at[n], sems.at[2 * n]),
-            pltpu.make_async_copy(down_far.at[:, pl.ds(start, BLK)], far_here.at[n], sems.at[2 * n + 1]),
-        )
-
-    def term(rows, n):
-        return (dot(act[rows, :], own_here[n]) + dot(act_far[rows, :], far_here[n])).astype(jnp.bfloat16)
+def leave_kernel(wanted, act, act_far, downs, *outs):
+    _, y, c, _ = position()
 
     for core in range(2):
-        steps = [
-            (out, i, *((first, second) if core == 0 else (second, first)))
-            for out, (second, firsts) in enumerate(wanted)
-            for i, first in enumerate(firsts)
-        ]
-        order = list(dict.fromkeys(OFFS.index(on_x) for _, _, on_x, _ in steps))
 
         @pl.when(c == core)
-        def _(steps=steps, order=order):
-            waited = set()
-            for n in order[:2]:
-                for copy in copies(n):
-                    copy.start()
-            for out, i, on_x, on_y in steps:
-                n = OFFS.index(on_x)
-                if n not in waited:
-                    for copy in copies(n):
-                        copy.wait()
-                    waited.add(n)
-                    for later in order[len(waited) + 1 : len(waited) + 2]:
-                        for copy in copies(later):
-                            copy.start()
-                outs[out][i * ROWS : (i + 1) * ROWS, :] = term(line_rows(ahead(y, on_y)), n)
-
-
-def leave(wanted, act, act_far, down, down_far):
+        def _(core=core):
+            for out, (second, firsts) in zip(outs, wanted):
+                for i, first in enumerate(firsts):
+                    on_x, on_y = (first, second) if core == 0 else (second, first)
+                    rows, n = line_rows(behind(y, -on_y)), OFFS.index(on_x)
+                    value = dot(act[rows, :], downs[0, n]) + dot(act_far[rows, :], downs[1, n])
+                    out[i * ROWS : (i + 1) * ROWS, :] = value.astype(jnp.bfloat16)
+
+
+def leave(wanted, act, act_far, downs):
     count = sum(len(firsts) for _, firsts in wanted)
     return pl.pallas_call(
         functools.partial(leave_kernel, wanted),
         out_shape=tuple(
             pltpu.VMEM((len(firsts) * ROWS, BLK), jnp.bfloat16) for _, firsts in wanted
         ),
-        in_specs=[VMEM, VMEM, ANY, ANY],
+        in_specs=[VMEM] * 3,
         out_specs=(VMEM,) * len(wanted),
-        scratch_shapes=[
-            pltpu.VMEM((4, HID, BLK), jnp.bfloat16),
-            pltpu.VMEM((4, HID, BLK), jnp.bfloat16),
-            pltpu.SemaphoreType.DMA((8,)),
-        ],
-        compiler_params=params(8),
+        compiler_params=params(6),
         cost_estimate=pl.CostEstimate(
             flops=2 * ROWS * count * BLK * 2 * HID, bytes_accessed=4000000, transcendentals=0
         ),
-    )(near(act), near(act_far), distant(down), distant(down_far))
+    )(near(act), near(act_far), near(downs))
 
 
 def gather_kernel(own, logit, *rest):
@@ -578,7 +620,7 @@
 ):
     z = lax.axis_index("z")
 
-    gate_far, up_far, down_far = swap_cores(gate_weight), swap_cores(up_weight), swap_cores(down_weight)
+    gate_far, up_far = swap_cores(gate_weight), swap_cores(up_weight)
     gain = norm_gain.astype(jnp.float32).reshape(8, BLK)
     inverse = 1.0 / gain
 
@@ -587,22 +629,22 @@
     )
     mine, one, three, two, routes = combine(for_own, swap_cores(for_other), routes)
     moved = [along_x(one, 1), along_x(three, -1), along_x(two, 2)]
-    first_hits, second_hits = slots(routes)
+    first_hits, second_hits, down_half = slots(routes, down_weight)
+    down_far = swap_cores(down_half)
     hidden, *outgoing = prepare(
         mine, *moved, tokens, gain, first_hits, second_hits, (gate_far, up_far)
     )
     line = jnp.concatenate(
         [outgoing[0]] + [along_z(rows, shift) for rows, shift in zip(outgoing[1:], OFFS[1:])]
     )
-    line = jnp.concatenate([line] + [along_first(line, shift) for shift in OFFS[1:]])
+    line = join([line] + [along_first(line, shift) for shift in OFFS[1:]])
     pieces = [line] + [along_second(line, shift) for shift in OFFS[1:]]
 
     route = lax.dynamic_index_in_dim(router, z, 1, keepdims=False).reshape(8, BLK)
-    own, sums, far = enter(
-        pieces, stage(gate_far, up_far, gate_weight, up_weight), inverse, route
-    )
+    weights, downs = stage(gate_far, up_far, gate_weight, up_weight, down_weight, down_far)
+    own, sums, far = enter(pieces, weights, inverse, route)
     act, logit = activate(own, sums, swap_cores(far))
-    operands = (act, swap_cores(act), down_weight, down_far)
+    operands = (act, swap_cores(act), downs)
     rest = OFFS[1:]
     (far2,) = leave(((2, rest),), *operands)
     far1, far3 = leave(((1, rest), (-1, rest)), *operands)

time: 126 us -> 122 us (0.968)
  Pallas kernels: 29.4 us -> 25.9 us
  starting transfers between devices: 39.1 us -> 37.2 us
    pallas_call x3, Pallas kernels: 7.51 us -> 2.55 us  [leave(): pl.pallas_call(functools.partial(leave_kernel, wanted), out_shape=tuple((...]
    ppermute x6, waiting for transfers between devices: 10.9 us -> 14.6 us  [along_first(): return lax.ppermute(a, AXES, plane_pairs(True, shift))]
    ppermute x3, waiting for transfers between devices: 3.2 us -> 0.75 us  [along_x(): return lax.ppermute(a, 'x', [(i, (i + shift) % 4) for i in range(4)])]
    ppermute x6, starting transfers between devices: 9.61 us -> 7.52 us  [along_first(): return lax.ppermute(a, AXES, plane_pairs(True, shift))]
    pallas_call x3 -> x5, Pallas kernels: 11.8 us -> 13.3 us  [the longest x1 4.02 us: stage(): pl.pallas_call(stage_kernel, out_shape=(pltpu.VMEM((4, 4, BLK, HID), jnp....]
    ppermute x6 -> x7, waiting for transfers between devices: 5.25 us -> 6.09 us  [swap_cores(): return lax.ppermute(a, 'c', [(0, 1), (1, 0)])]
    ppermute x6 -> x7, starting transfers between devices: 8.28 us -> 8.43 us  [swap_cores(): return lax.ppermute(a, 'c', [(0, 1), (1, 0)])]
  transfers between devices with their start and end apart: 30 -> 31, of which waited for: 19 -> 20; matrix products, arithmetic and copies ran while one was open for 1% -> 1% of each run, Pallas kernels for 21% -> 16%
where the time goes in v5:
time: 122 us; the launch traced here: 121 us
  waiting for transfers between devices  56.8 us (47%)
  starting transfers between devices  37.2 us (30%)
  Pallas kernels  25.9 us (21%)
    ppermute x9, waiting for transfers between devices, along_second(): return lax.ppermute(a, AXES, plane_pairs(False, shift))  27.9 us
    ppermute x6, waiting for transfers between devices, along_first(): return lax.ppermute(a, AXES, plane_pairs(True, shift))  14.6 us
    ppermute x9, starting transfers between devices, along_second(): return lax.ppermute(a, AXES, plane_pairs(False, shift))  8.67 us
    ppermute x7, starting transfers between devices, swap_cores(): return lax.ppermute(a, 'c', [(0, 1), (1, 0)])  8.43 us
    ppermute x6, starting transfers between devices, along_z(): return lax.ppermute(a, 'z', [(i, (i + shift) % 4) for i in range(4)])  8.17 us
    pallas_call x1, Pallas kernels, attend(): pl.pallas_call(attend_kernel, out_shape=(pltpu.VMEM((4, rows, BLK), jnp.b...  7.84 us
    ppermute x6, starting transfers between devices, along_first(): return lax.ppermute(a, AXES, plane_pairs(True, shift))  7.52 us
    ppermute x6, waiting for transfers between devices, along_z(): return lax.ppermute(a, 'z', [(i, (i + shift) % 4) for i in range(4)])  7.38 us
  transfers between devices with their start and end apart: 31, of which 20 were waited for; matrix products, arithmetic and copies ran while one was open for 1% of the time, Pallas kernels for 16%

profile of v5, /device:TPU:1, one launch (start us, length us, event | category | flops | bytes accessed | tf_op | source)
XLA Modules:
  0.0 120.8 jit_solution(760665811613274682)
XLA Ops:
  0.0 1.4 %collective-permute-start.4 = (bf16[6144,256]{1,0:T(8,128)(2,1)}, bf16[6144,256]{1,0:T(8,128)(2,1)}, u32[]{:S(2)}, u32[]{:S(2)}) collective-permute-start(bf16[6144,256]{1,0:T(8,128)(2,1)} %gate.1), channel_id=1, source_target_pairs={{0,1},{1,0},{2,3},{3,2},{4,5},{5,4},{6,7},{7,6},{8,9},{9,8},{10,11... | collective-permute-start | bytes 9437192 | tf_op jit(solution)/shard_map/ppermute | solution.py:59
  1.4 7.8 %shard_map.136 = (bf16[4,64,768]{2,1,0:T(8,128)(2,1)S(1)}, f32[4,64,768]{2,1,0:T(8,128)S(1)}) custom-call(s32[64]{0:T(128)} %given_lengths.1, bf16[6,64,128]{2,1,0:T(8,128)(2,1)} %bitcast.7, bf16[64,128]{1,0:T(8,128)(2,1)} %bitcast.8, bf16[64,128]{1,0:T(8,128)(2,1)} %bitcast.9, bf16[64,128,128]{2,1,0:T(8,128)(2,1)} %bitcast.5, ...), custom_call_target="tpu_custom_call" | custom-call | flops 603979776 | bytes 14000000 | tf_op jit(solution)/shard_map/pallas_call | solution.py:171
  9.3 0.6 collective-permute-start
  9.9 0.1 copy.15.routes
  10.0 1.8 %collective-permute-done.far = bf16[4,64,768]{2,1,0:T(8,128)(2,1)S(1)} collective-permute-done((bf16[4,64,768]{2,1,0:T(8,128)(2,1)S(1)}, bf16[4,64,768]{2,1,0:T(8,128)(2,1)S(1)}, u32[]{:S(2)}, u32[]{:S(2)}) %collective-permute-start) | collective-permute-done | bytes 393248 | tf_op jit(solution)/shard_map/ppermute | solution.py:59
  11.8 0.1 shard_map.137
  11.8 1.4 %collective-permute-start.1 = (bf16[64,768]{1,0:T(8,128)(2,1)S(1)}, bf16[64,768]{1,0:T(8,128)(2,1)S(1)}, u32[]{:S(2)}, u32[]{:S(2)}) collective-permute-start(bf16[64,768]{1,0:T(8,128)(2,1)S(1)} %get-tuple-element.44), channel_id=1, source_target_pairs={{0,2},{2,4},{4,6},{6,0},{1,3},{3,5},{5,7},{7,1},{8,10},{10,12},{12... | collective-permute-start | bytes 294920 | tf_op jit(solution)/shard_map/ppermute | solution.py:55
  13.2 1.4 %collective-permute-start.2 = (bf16[64,768]{1,0:T(8,128)(2,1)S(1)}, bf16[64,768]{1,0:T(8,128)(2,1)S(1)}, u32[]{:S(2)}, u32[]{:S(2)}) collective-permute-start(bf16[64,768]{1,0:T(8,128)(2,1)S(1)} %get-tuple-element.45), channel_id=1, source_target_pairs={{0,6},{2,0},{4,2},{6,4},{1,7},{3,1},{5,3},{7,5},{8,14},{10,8},{12,... | collective-permute-start | bytes 294920 | tf_op jit(solution)/shard_map/ppermute | solution.py:55
  14.6 1.6 %collective-permute-start.3 = (bf16[64,768]{1,0:T(8,128)(2,1)S(1)}, bf16[64,768]{1,0:T(8,128)(2,1)S(1)}, u32[]{:S(2)}, u32[]{:S(2)}) collective-permute-start(bf16[64,768]{1,0:T(8,128)(2,1)S(1)} %get-tuple-element.46), channel_id=1, source_target_pairs={{0,4},{2,6},{4,0},{6,2},{1,5},{3,7},{5,1},{7,3},{8,12},{10,14},{12... | collective-permute-start | bytes 294920 | tf_op jit(solution)/shard_map/ppermute | solution.py:55
  16.3 1.4 %shard_map.138 = (bf16[4,64,40]{2,1,0:T(8,128)(2,1)S(1)}, bf16[4,64,40]{2,1,0:T(8,128)(2,1)S(1)}, bf16[4,256,768]{2,1,0:T(8,128)(2,1)S(1)}) custom-call(s32[64,2]{1,0:T(8,128)S(1)} %get-tuple-element.47.routes, bf16[256,6144]{1,0:T(8,128)(2,1)} %down.3), custom_call_target="tpu_custom_call" | custom-call | tf_op jit(solution)/shard_map/pallas_call | solution.py:257
  17.7 1.3 %collective-permute-start.15 = (bf16[4,256,768]{2,1,0:T(8,128)(2,1)S(1)}, bf16[4,256,768]{2,1,0:T(8,128)(2,1)}, u32[]{:S(2)}, u32[]{:S(2)}) collective-permute-start(bf16[4,256,768]{2,1,0:T(8,128)(2,1)S(1)} %get-tuple-element.55), channel_id=1, source_target_pairs={{0,1},{1,0},{2,3},{3,2},{4,5},{5,4},{6,7},{7,6},{8,9},{9,8},{10,11... | collective-permute-start | bytes 4718600 | tf_op jit(solution)/shard_map/ppermute | solution.py:59
  19.0 0.7 collective-permute-done.3.two
  19.8 0.3 shard_map.139
  20.1 1.7 %collective-permute-start.6 = (bf16[40,768]{1,0:T(8,128)(2,1)S(1)}, bf16[40,768]{1,0:T(8,128)(2,1)S(1)}, u32[]{:S(2)}, u32[]{:S(2)}) collective-permute-start(bf16[40,768]{1,0:T(8,128)(2,1)S(1)} %get-tuple-element.52), channel_id=1, source_target_pairs={{0,32},{32,64},{64,96},{96,0},{1,33},{33,65},{65,97},{97,1},{2,34}... | collective-permute-start | bytes 184328 | tf_op jit(solution)/shard_map/ppermute | solution.py:51
  21.8 2.2 %collective-permute-start.7 = (bf16[40,768]{1,0:T(8,128)(2,1)S(1)}, bf16[40,768]{1,0:T(8,128)(2,1)S(1)}, u32[]{:S(2)}, u32[]{:S(2)}) collective-permute-start(bf16[40,768]{1,0:T(8,128)(2,1)S(1)} %get-tuple-element.53), channel_id=1, source_target_pairs={{0,96},{32,0},{64,32},{96,64},{1,97},{33,1},{65,33},{97,65},{2,98}... | collective-permute-start | bytes 184328 | tf_op jit(solution)/shard_map/ppermute | solution.py:51
  24.0 1.2 %collective-permute-start.8 = (bf16[40,768]{1,0:T(8,128)(2,1)S(1)}, bf16[40,768]{1,0:T(8,128)(2,1)S(1)}, u32[]{:S(2)}, u32[]{:S(2)}) collective-permute-start(bf16[40,768]{1,0:T(8,128)(2,1)S(1)} %get-tuple-element.54), channel_id=1, source_target_pairs={{0,64},{32,96},{64,0},{96,32},{1,65},{33,97},{65,1},{97,33},{2,66}... | collective-permute-start | bytes 184328 | tf_op jit(solution)/shard_map/ppermute | solution.py:51
  25.2 0.3 collective-permute-done.6
  25.5 3.2 %collective-permute-done.8 = bf16[40,768]{1,0:T(8,128)(2,1)S(1)} collective-permute-done((bf16[40,768]{1,0:T(8,128)(2,1)S(1)}, bf16[40,768]{1,0:T(8,128)(2,1)S(1)}, u32[]{:S(2)}, u32[]{:S(2)}) %collective-permute-start.8) | collective-permute-done | bytes 61472 | tf_op jit(solution)/shard_map/ppermute | solution.py:51
  28.7 2.7 %collective-permute-start.10 = (bf16[160,768]{1,0:T(8,128)(2,1)S(1)}, bf16[160,768]{1,0:T(8,128)(2,1)S(1)}, u32[]{:S(2)}, u32[]{:S(2)}) collective-permute-start(bf16[160,768]{1,0:T(8,128)(2,1)S(1)} %constant_dynamic-update-slice_fusion.a), channel_id=1, source_target_pairs={{0,6},{1,25},{2,0},{3,27},{4,2},{5,29},{6,4},{7,31},{8,14},{9,1},{... | collective-permute-start | bytes 737288 | tf_op jit(solution)/shard_map/ppermute | solution.py:43
  31.5 0.3 collective-permute-start.11
  31.8 0.7 collective-permute-start.9
  32.5 4.7 %collective-permute-done.10.c = bf16[160,768]{1,0:T(8,128)(2,1)S(1)} collective-permute-done((bf16[160,768]{1,0:T(8,128)(2,1)S(1)}, bf16[160,768]{1,0:T(8,128)(2,1)S(1)}, u32[]{:S(2)}, u32[]{:S(2)}) %collective-permute-start.10) | collective-permute-done | bytes 245792 | tf_op jit(solution)/shard_map/ppermute | solution.py:43
  37.2 0.9 collective-permute-done.11.d
  38.1 2.8 %collective-permute-done.9.b = bf16[160,768]{1,0:T(8,128)(2,1)S(1)} collective-permute-done((bf16[160,768]{1,0:T(8,128)(2,1)S(1)}, bf16[160,768]{1,0:T(8,128)(2,1)S(1)}, u32[]{:S(2)}, u32[]{:S(2)}) %collective-permute-start.9) | collective-permute-done | bytes 245792 | tf_op jit(solution)/shard_map/ppermute | solution.py:43
  40.9 3.2 %collective-permute-start.12 = (f32[16,128]{1,0:T(8,128)S(1)}, f32[16,128]{1,0:T(8,128)S(1)}, u32[]{:S(2)}, u32[]{:S(2)}) collective-permute-start(f32[16,128]{1,0:T(8,128)S(1)} %convert_add_fusion), channel_id=1, source_target_pairs={{0,1},{1,0},{2,3},{3,2},{4,5},{5,4},{6,7},{7,6},{8,9},{9,8},{10,11... | collective-permute-start | bytes 24584 | tf_op jit(solution)/shard_map/ppermute | solution.py:59
  44.1 0.8 collective-permute-done.12.token
  44.9 0.1 shard_map.140.p0
  45.0 1.0 collective-permute-start.16
  46.0 2.7 %collective-permute-start.14 = (bf16[640,768]{1,0:T(8,128)(2,1)S(1)}, bf16[640,768]{1,0:T(8,128)(2,1)}, u32[]{:S(2)}, u32[]{:S(2)}) collective-permute-start(bf16[640,768]{1,0:T(8,128)(2,1)S(1)} %shard_map.140.p0), channel_id=1, source_target_pairs={{0,24},{1,7},{2,26},{3,1},{4,28},{5,3},{6,30},{7,5},{8,0},{9,15},{... | collective-permute-start | bytes 2949128 | tf_op jit(solution)/shard_map/ppermute | solution.py:47
  48.7 0.1 dynamic-slice_reduce_fusion
  48.8 4.0 %shard_map.141 = (bf16[4,4,768,256]{3,2,1,0:T(8,128)(2,1)S(1)}, bf16[2,4,256,768]{3,2,1,0:T(8,128)(2,1)S(1)}) custom-call(bf16[6144,256]{1,0:T(8,128)(2,1)} %collective-permute-done.4.rest_0_.gate_far, bf16[6144,256]{1,0:T(8,128)(2,1)} %collective-permute-done.5.rest_1_.up_far, bf16[6144,256]{1,0:T(8,128)(2,1)} %gate.1, bf16[6144,256]{1,0:T(8,128)(2,1)} %up.1, ...), custom_call_target="tpu_custom_call" | custom-call | bytes 18000000 | tf_op jit(solution)/shard_map/pallas_call | solution.py:362
  52.9 7.1 %collective-permute-done.16.p1 = bf16[640,768]{1,0:T(8,128)(2,1)} collective-permute-done((bf16[640,768]{1,0:T(8,128)(2,1)S(1)}, bf16[640,768]{1,0:T(8,128)(2,1)}, u32[]{:S(2)}, u32[]{:S(2)}) %collective-permute-start.16) | collective-permute-done | bytes 983072 | tf_op jit(solution)/shard_map/ppermute | solution.py:47
  60.0 3.8 %shard_map.142 = (f32[640,512]{1,0:T(8,128)S(1)}, f32[640,256]{1,0:T(8,128)S(1)}, f32[640,512]{1,0:T(8,128)S(1)}) custom-call(bf16[640,768]{1,0:T(8,128)(2,1)} %copy-done.2, bf16[640,768]{1,0:T(8,128)(2,1)} %collective-permute-done.16.p1, bf16[4,4,768,256]{3,2,1,0:T(8,128)(2,1)S(1)} %get-tuple-element.56.weights, f32[8,768]{1,0:T(8,128)S(1)} %broadcast_divide_fusion.inverse, ...), custom_call_target="tpu_custom_call" | custom-call | flops 2013265920 | bytes 5000000 | tf_op jit(solution)/shard_map/pallas_call | solution.py:474
  63.8 6.7 %collective-permute-done.13.p0 = bf16[640,768]{1,0:T(8,128)(2,1)} collective-permute-done((bf16[640,768]{1,0:T(8,128)(2,1)S(1)}, bf16[640,768]{1,0:T(8,128)(2,1)}, u32[]{:S(2)}, u32[]{:S(2)}) %collective-permute-start.13) | collective-permute-done | bytes 983072 | tf_op jit(solution)/shard_map/ppermute | solution.py:47
  70.5 3.9 %shard_map.143 = (f32[640,512]{1,0:T(8,128)S(1)}, f32[640,256]{1,0:T(8,128)S(1)}, bf16[640,768]{1,0:T(8,128)(2,1)S(1)}) custom-call(bf16[640,768]{1,0:T(8,128)(2,1)} %collective-permute-done.13.p0, bf16[640,768]{1,0:T(8,128)(2,1)} %collective-permute-done.14.p1, bf16[4,4,768,256]{3,2,1,0:T(8,128)(2,1)S(1)} %get-tuple-element.56.weights, ...), custom_call_target="tpu_custom_call" | custom-call | flops 2013265920 | bytes 5000000 | tf_op jit(solution)/shard_map/pallas_call | solution.py:483
  74.4 1.5 %collective-permute-start.17 = (bf16[640,768]{1,0:T(8,128)(2,1)S(1)}, bf16[640,768]{1,0:T(8,128)(2,1)S(1)}, u32[]{:S(2)}, u32[]{:S(2)}) collective-permute-start(bf16[640,768]{1,0:T(8,128)(2,1)S(1)} %get-tuple-element.62), channel_id=1, source_target_pairs={{0,1},{1,0},{2,3},{3,2},{4,5},{5,4},{6,7},{7,6},{8,9},{9,8},{10,11... | collective-permute-start | bytes 2949128 | tf_op jit(solution)/shard_map/ppermute | solution.py:59
  76.0 2.2 %collective-permute-done.17.far = bf16[640,768]{1,0:T(8,128)(2,1)S(1)} collective-permute-done((bf16[640,768]{1,0:T(8,128)(2,1)S(1)}, bf16[640,768]{1,0:T(8,128)(2,1)S(1)}, u32[]{:S(2)}, u32[]{:S(2)}) %collective-permute-start.17) | collective-permute-done | bytes 983072 | tf_op jit(solution)/shard_map/ppermute | solution.py:59
  78.1 0.4 shard_map.144
  78.6 0.5 collective-permute-start.18
  79.0 1.3 %collective-permute-done.18.act_far = bf16[640,256]{1,0:T(8,128)(2,1)S(1)} collective-permute-done((bf16[640,256]{1,0:T(8,128)(2,1)S(1)}, bf16[640,256]{1,0:T(8,128)(2,1)S(1)}, u32[]{:S(2)}, u32[]{:S(2)}) %collective-permute-start.18) | collective-permute-done | bytes 327712 | tf_op jit(solution)/shard_map/ppermute | solution.py:59
  80.3 0.6 shard_map.146
  80.8 1.0 collective-permute-start.22
  81.9 0.9 shard_map.147
  82.8 0.1 collective-permute-start.23
  82.9 2.7 %collective-permute-start.24 = (bf16[480,768]{1,0:T(8,128)(2,1)S(1)}, bf16[480,768]{1,0:T(8,128)(2,1)S(1)}, u32[]{:S(2)}, u32[]{:S(2)}) collective-permute-start(bf16[480,768]{1,0:T(8,128)(2,1)S(1)} %get-tuple-element.72), channel_id=1, source_target_pairs={{0,24},{1,7},{2,26},{3,1},{4,28},{5,3},{6,30},{7,5},{8,0},{9,15},{... | collective-permute-start | bytes 2211848 | tf_op jit(solution)/shard_map/ppermute | solution.py:47
  85.5 1.1 shard_map.145
  86.6 0.9 collective-permute-start.19
  87.5 5.6 %collective-permute-done.22 = bf16[480,768]{1,0:T(8,128)(2,1)S(1)} collective-permute-done((bf16[480,768]{1,0:T(8,128)(2,1)S(1)}, bf16[480,768]{1,0:T(8,128)(2,1)S(1)}, u32[]{:S(2)}, u32[]{:S(2)}) %collective-permute-start.22) | collective-permute-done | bytes 737312 | tf_op jit(solution)/shard_map/ppermute | solution.py:47
  93.1 0.3 collective-permute-start.21
  93.4 7.6 %collective-permute-done.23 = bf16[480,768]{1,0:T(8,128)(2,1)S(1)} collective-permute-done((bf16[480,768]{1,0:T(8,128)(2,1)S(1)}, bf16[480,768]{1,0:T(8,128)(2,1)S(1)}, u32[]{:S(2)}, u32[]{:S(2)}) %collective-permute-start.23) | collective-permute-done | bytes 737312 | tf_op jit(solution)/shard_map/ppermute | solution.py:47
  100.9 0.4 add_convert_fusion
  101.4 0.8 collective-permute-start.25
  102.3 1.9 %collective-permute-start.26 = (bf16[160,768]{1,0:T(8,128)(2,1)S(1)}, bf16[160,768]{1,0:T(8,128)(2,1)S(1)}, u32[]{:S(2)}, u32[]{:S(2)}) collective-permute-start(bf16[160,768]{1,0:T(8,128)(2,1)S(1)} %get-tuple-element.78), channel_id=1, source_target_pairs={{0,6},{1,25},{2,0},{3,27},{4,2},{5,29},{6,4},{7,31},{8,14},{9,1},{... | collective-permute-start | bytes 737288 | tf_op jit(solution)/shard_map/ppermute | solution.py:43
  104.2 1.0 collective-permute-start.27
  105.2 1.0 collective-permute-done.20.rest_1_
  106.2 3.5 %collective-permute-done.25.rest_3_ = bf16[160,768]{1,0:T(8,128)(2,1)S(1)} collective-permute-done((bf16[160,768]{1,0:T(8,128)(2,1)S(1)}, bf16[160,768]{1,0:T(8,128)(2,1)S(1)}, u32[]{:S(2)}, u32[]{:S(2)}) %collective-permute-start.25) | collective-permute-done | bytes 245792 | tf_op jit(solution)/shard_map/ppermute | solution.py:43
  109.7 2.7 %collective-permute-done.27.rest_5_ = bf16[160,768]{1,0:T(8,128)(2,1)S(1)} collective-permute-done((bf16[160,768]{1,0:T(8,128)(2,1)S(1)}, bf16[160,768]{1,0:T(8,128)(2,1)S(1)}, u32[]{:S(2)}, u32[]{:S(2)}) %collective-permute-start.27) | collective-permute-done | bytes 245792 | tf_op jit(solution)/shard_map/ppermute | solution.py:43
  112.4 0.2 shard_map.148
  112.6 1.7 %collective-permute-start.28 = (bf16[40,896]{1,0:T(8,128)(2,1)S(1)}, bf16[40,896]{1,0:T(8,128)(2,1)S(1)}, u32[]{:S(2)}, u32[]{:S(2)}) collective-permute-start(bf16[40,896]{1,0:T(8,128)(2,1)S(1)} %get-tuple-element.74), channel_id=1, source_target_pairs={{0,96},{32,0},{64,32},{96,64},{1,97},{33,1},{65,33},{97,65},{2,98}... | collective-permute-start | bytes 215048 | tf_op jit(solution)/shard_map/ppermute | solution.py:51
  114.4 1.3 %collective-permute-start.30 = (bf16[40,896]{1,0:T(8,128)(2,1)S(1)}, bf16[40,896]{1,0:T(8,128)(2,1)S(1)}, u32[]{:S(2)}, u32[]{:S(2)}) collective-permute-start(bf16[40,896]{1,0:T(8,128)(2,1)S(1)} %get-tuple-element.76), channel_id=1, source_target_pairs={{0,64},{32,96},{64,0},{96,32},{1,65},{33,97},{65,1},{97,33},{2,66}... | collective-permute-start | bytes 215048 | tf_op jit(solution)/shard_map/ppermute | solution.py:51
  115.7 0.2 collective-permute-done.28.b1
  115.9 3.6 %collective-permute-done.29.b2 = bf16[40,896]{1,0:T(8,128)(2,1)S(1)} collective-permute-done((bf16[40,896]{1,0:T(8,128)(2,1)S(1)}, bf16[40,896]{1,0:T(8,128)(2,1)S(1)}, u32[]{:S(2)}, u32[]{:S(2)}) %collective-permute-start.29) | collective-permute-done | bytes 71712 | tf_op jit(solution)/shard_map/ppermute | solution.py:51
  119.5 0.1 collective-permute-done.30.b3
  119.6 1.2 shard_map.149
  (36 shorter events, 0.2 us)
Async XLA Ops:
  0.0 48.7 %copy-start = (f32[6144,4]{0,1:T(4,128)S(1)}, f32[6144,4]{0,1:T(4,128)}, u32[]{:S(2)}) copy-start(f32[6144,4]{0,1:T(4,128)} %param.24) | copy-start | bytes 294916
  0.0 19.8 %collective-permute-start.4 = (bf16[6144,256]{1,0:T(8,128)(2,1)}, bf16[6144,256]{1,0:T(8,128)(2,1)}, u32[]{:S(2)}, u32[]{:S(2)}) collective-permute-start(bf16[6144,256]{1,0:T(8,128)(2,1)} %gate.1), channel_id=1, source_target_pairs={{0,1},{1,0},{2,3},{3,2},{4,5},{5,4},{6,7},{7,6},{8,9},{9,8},{10,11... | collective-permute-start | bytes 9437192 | tf_op jit(solution)/shard_map/ppermute | solution.py:59
  1.4 18.3 %collective-permute-start.5 = (bf16[6144,256]{1,0:T(8,128)(2,1)}, bf16[6144,256]{1,0:T(8,128)(2,1)}, u32[]{:S(2)}, u32[]{:S(2)}) collective-permute-start(bf16[6144,256]{1,0:T(8,128)(2,1)} %up.1), channel_id=1, source_target_pairs={{0,1},{1,0},{2,3},{3,2},{4,5},{5,4},{6,7},{7,6},{8,9},{9,8},{10,11... | collective-permute-start | bytes 9437192 | tf_op jit(solution)/shard_map/ppermute | solution.py:59
  1.4 8.4 %copy-start.5 = (s32[64,2]{0,1:T(2,128)S(1)}, s32[64,2]{0,1:T(2,128)}, u32[]{:S(2)}) copy-start(s32[64,2]{0,1:T(2,128)} %param.21) | copy-start | bytes 1540
  1.4 14.8 %copy-start.4 = (bf16[6144]{0:T(1024)(128)(2,1)S(1)}, bf16[6144]{0:T(1024)(128)(2,1)}, u32[]{:S(2)}) copy-start(bf16[6144]{0:T(1024)(128)(2,1)} %param.23) | copy-start | bytes 36868
  9.3 2.5 %collective-permute-start = (bf16[4,64,768]{2,1,0:T(8,128)(2,1)S(1)}, bf16[4,64,768]{2,1,0:T(8,128)(2,1)S(1)}, u32[]{:S(2)}, u32[]{:S(2)}) collective-permute-start(bf16[4,64,768]{2,1,0:T(8,128)(2,1)S(1)} %get-tuple-element.42), channel_id=1, source_target_pairs={{0,1},{1,0},{2,3},{3,2},{4,5},{5,4},{6,7},{7,6},{8,9},{9,8},{10,11... | collective-permute-start | bytes 1179656 | tf_op jit(solution)/shard_map/ppermute | solution.py:59
  11.8 5.9 %collective-permute-start.1 = (bf16[64,768]{1,0:T(8,128)(2,1)S(1)}, bf16[64,768]{1,0:T(8,128)(2,1)S(1)}, u32[]{:S(2)}, u32[]{:S(2)}) collective-permute-start(bf16[64,768]{1,0:T(8,128)(2,1)S(1)} %get-tuple-element.44), channel_id=1, source_target_pairs={{0,2},{2,4},{4,6},{6,0},{1,3},{3,5},{5,7},{7,1},{8,10},{10,12},{12... | collective-permute-start | bytes 294920 | tf_op jit(solution)/shard_map/ppermute | solution.py:55
  13.2 5.8 %collective-permute-start.2 = (bf16[64,768]{1,0:T(8,128)(2,1)S(1)}, bf16[64,768]{1,0:T(8,128)(2,1)S(1)}, u32[]{:S(2)}, u32[]{:S(2)}) collective-permute-start(bf16[64,768]{1,0:T(8,128)(2,1)S(1)} %get-tuple-element.45), channel_id=1, source_target_pairs={{0,6},{2,0},{4,2},{6,4},{1,7},{3,1},{5,3},{7,5},{8,14},{10,8},{12,... | collective-permute-start | bytes 294920 | tf_op jit(solution)/shard_map/ppermute | solution.py:55
  14.6 5.2 %collective-permute-start.3 = (bf16[64,768]{1,0:T(8,128)(2,1)S(1)}, bf16[64,768]{1,0:T(8,128)(2,1)S(1)}, u32[]{:S(2)}, u32[]{:S(2)}) collective-permute-start(bf16[64,768]{1,0:T(8,128)(2,1)S(1)} %get-tuple-element.46), channel_id=1, source_target_pairs={{0,4},{2,6},{4,0},{6,2},{1,5},{3,7},{5,1},{7,3},{8,12},{10,14},{12... | collective-permute-start | bytes 294920 | tf_op jit(solution)/shard_map/ppermute | solution.py:55
  16.2 3.5 %copy-start.3 = (bf16[64,768]{1,0:T(8,128)(2,1)S(1)}, bf16[64,768]{1,0:T(8,128)(2,1)}, u32[]{:S(2)}) copy-start(bf16[64,768]{1,0:T(8,128)(2,1)} %tokens.1) | copy-start | bytes 294916
  17.7 31.1 %collective-permute-start.15 = (bf16[4,256,768]{2,1,0:T(8,128)(2,1)S(1)}, bf16[4,256,768]{2,1,0:T(8,128)(2,1)}, u32[]{:S(2)}, u32[]{:S(2)}) collective-permute-start(bf16[4,256,768]{2,1,0:T(8,128)(2,1)S(1)} %get-tuple-element.55), channel_id=1, source_target_pairs={{0,1},{1,0},{2,3},{3,2},{4,5},{5,4},{6,7},{7,6},{8,9},{9,8},{10,11... | collective-permute-start | bytes 4718600 | tf_op jit(solution)/shard_map/ppermute | solution.py:59
  20.1 5.4 %collective-permute-start.6 = (bf16[40,768]{1,0:T(8,128)(2,1)S(1)}, bf16[40,768]{1,0:T(8,128)(2,1)S(1)}, u32[]{:S(2)}, u32[]{:S(2)}) collective-permute-start(bf16[40,768]{1,0:T(8,128)(2,1)S(1)} %get-tuple-element.52), channel_id=1, source_target_pairs={{0,32},{32,64},{64,96},{96,0},{1,33},{33,65},{65,97},{97,1},{2,34}... | collective-permute-start | bytes 184328 | tf_op jit(solution)/shard_map/ppermute | solution.py:51
  21.8 3.7 %collective-permute-start.7 = (bf16[40,768]{1,0:T(8,128)(2,1)S(1)}, bf16[40,768]{1,0:T(8,128)(2,1)S(1)}, u32[]{:S(2)}, u32[]{:S(2)}) collective-permute-start(bf16[40,768]{1,0:T(8,128)(2,1)S(1)} %get-tuple-element.53), channel_id=1, source_target_pairs={{0,96},{32,0},{64,32},{96,64},{1,97},{33,1},{65,33},{97,65},{2,98}... | collective-permute-start | bytes 184328 | tf_op jit(solution)/shard_map/ppermute | solution.py:51
  24.0 4.7 %collective-permute-start.8 = (bf16[40,768]{1,0:T(8,128)(2,1)S(1)}, bf16[40,768]{1,0:T(8,128)(2,1)S(1)}, u32[]{:S(2)}, u32[]{:S(2)}) collective-permute-start(bf16[40,768]{1,0:T(8,128)(2,1)S(1)} %get-tuple-element.54), channel_id=1, source_target_pairs={{0,64},{32,96},{64,0},{96,32},{1,65},{33,97},{65,1},{97,33},{2,66}... | collective-permute-start | bytes 184328 | tf_op jit(solution)/shard_map/ppermute | solution.py:51
  28.7 8.5 %collective-permute-start.10 = (bf16[160,768]{1,0:T(8,128)(2,1)S(1)}, bf16[160,768]{1,0:T(8,128)(2,1)S(1)}, u32[]{:S(2)}, u32[]{:S(2)}) collective-permute-start(bf16[160,768]{1,0:T(8,128)(2,1)S(1)} %constant_dynamic-update-slice_fusion.a), channel_id=1, source_target_pairs={{0,6},{1,25},{2,0},{3,27},{4,2},{5,29},{6,4},{7,31},{8,14},{9,1},{... | collective-permute-start | bytes 737288 | tf_op jit(solution)/shard_map/ppermute | solution.py:43
  31.5 6.7 %collective-permute-start.11 = (bf16[160,768]{1,0:T(8,128)(2,1)S(1)}, bf16[160,768]{1,0:T(8,128)(2,1)S(1)}, u32[]{:S(2)}, u32[]{:S(2)}) collective-permute-start(bf16[160,768]{1,0:T(8,128)(2,1)S(1)} %constant_dynamic-update-slice_fusion.a), channel_id=1, source_target_pairs={{0,4},{1,17},{2,6},{3,19},{4,0},{5,21},{6,2},{7,23},{8,12},{9,25},... | collective-permute-start | bytes 737288 | tf_op jit(solution)/shard_map/ppermute | solution.py:43
  31.8 9.1 %collective-permute-start.9 = (bf16[160,768]{1,0:T(8,128)(2,1)S(1)}, bf16[160,768]{1,0:T(8,128)(2,1)S(1)}, u32[]{:S(2)}, u32[]{:S(2)}) collective-permute-start(bf16[160,768]{1,0:T(8,128)(2,1)S(1)} %constant_dynamic-update-slice_fusion.a), channel_id=1, source_target_pairs={{0,2},{1,9},{2,4},{3,11},{4,6},{5,13},{6,0},{7,15},{8,10},{9,17},{... | collective-permute-start | bytes 737288 | tf_op jit(solution)/shard_map/ppermute | solution.py:43
  40.9 4.0 %collective-permute-start.12 = (f32[16,128]{1,0:T(8,128)S(1)}, f32[16,128]{1,0:T(8,128)S(1)}, u32[]{:S(2)}, u32[]{:S(2)}) collective-permute-start(f32[16,128]{1,0:T(8,128)S(1)} %convert_add_fusion), channel_id=1, source_target_pairs={{0,1},{1,0},{2,3},{3,2},{4,5},{5,4},{6,7},{7,6},{8,9},{9,8},{10,11... | collective-permute-start | bytes 24584 | tf_op jit(solution)/shard_map/ppermute | solution.py:59
  45.0 7.9 %copy-start.2 = (bf16[640,768]{1,0:T(8,128)(2,1)}, bf16[640,768]{1,0:T(8,128)(2,1)S(1)}, u32[]{:S(2)}) copy-start(bf16[640,768]{1,0:T(8,128)(2,1)S(1)} %shard_map.140.p0) | copy-start | bytes 2949124
  45.0 15.0 %collective-permute-start.16 = (bf16[640,768]{1,0:T(8,128)(2,1)S(1)}, bf16[640,768]{1,0:T(8,128)(2,1)}, u32[]{:S(2)}, u32[]{:S(2)}) collective-permute-start(bf16[640,768]{1,0:T(8,128)(2,1)S(1)} %shard_map.140.p0), channel_id=1, source_target_pairs={{0,16},{1,5},{2,18},{3,7},{4,20},{5,1},{6,22},{7,3},{8,24},{9,13},... | collective-permute-start | bytes 2949128 | tf_op jit(solution)/shard_map/ppermute | solution.py:47
  46.0 24.4 %collective-permute-start.13 = (bf16[640,768]{1,0:T(8,128)(2,1)S(1)}, bf16[640,768]{1,0:T(8,128)(2,1)}, u32[]{:S(2)}, u32[]{:S(2)}) collective-permute-start(bf16[640,768]{1,0:T(8,128)(2,1)S(1)} %shard_map.140.p0), channel_id=1, source_target_pairs={{0,8},{1,3},{2,10},{3,5},{4,12},{5,7},{6,14},{7,1},{8,16},{9,11},{... | collective-permute-start | bytes 2949128 | tf_op jit(solution)/shard_map/ppermute | solution.py:47
  46.0 24.4 %collective-permute-start.14 = (bf16[640,768]{1,0:T(8,128)(2,1)S(1)}, bf16[640,768]{1,0:T(8,128)(2,1)}, u32[]{:S(2)}, u32[]{:S(2)}) collective-permute-start(bf16[640,768]{1,0:T(8,128)(2,1)S(1)} %shard_map.140.p0), channel_id=1, source_target_pairs={{0,24},{1,7},{2,26},{3,1},{4,28},{5,3},{6,30},{7,5},{8,0},{9,15},{... | collective-permute-start | bytes 2949128 | tf_op jit(solution)/shard_map/ppermute | solution.py:47
  74.4 3.7 %collective-permute-start.17 = (bf16[640,768]{1,0:T(8,128)(2,1)S(1)}, bf16[640,768]{1,0:T(8,128)(2,1)S(1)}, u32[]{:S(2)}, u32[]{:S(2)}) collective-permute-start(bf16[640,768]{1,0:T(8,128)(2,1)S(1)} %get-tuple-element.62), channel_id=1, source_target_pairs={{0,1},{1,0},{2,3},{3,2},{4,5},{5,4},{6,7},{7,6},{8,9},{9,8},{10,11... | collective-permute-start | bytes 2949128 | tf_op jit(solution)/shard_map/ppermute | solution.py:59
  78.6 1.7 %collective-permute-start.18 = (bf16[640,256]{1,0:T(8,128)(2,1)S(1)}, bf16[640,256]{1,0:T(8,128)(2,1)S(1)}, u32[]{:S(2)}, u32[]{:S(2)}) collective-permute-start(bf16[640,256]{1,0:T(8,128)(2,1)S(1)} %get-tuple-element.63.act), channel_id=1, source_target_pairs={{0,1},{1,0},{2,3},{3,2},{4,5},{5,4},{6,7},{7,6},{8,9},{9,8},{10,11... | collective-permute-start | bytes 983048 | tf_op jit(solution)/shard_map/ppermute | solution.py:59
  80.8 12.2 %collective-permute-start.22 = (bf16[480,768]{1,0:T(8,128)(2,1)S(1)}, bf16[480,768]{1,0:T(8,128)(2,1)S(1)}, u32[]{:S(2)}, u32[]{:S(2)}) collective-permute-start(bf16[480,768]{1,0:T(8,128)(2,1)S(1)} %shard_map.146), channel_id=1, source_target_pairs={{0,16},{1,5},{2,18},{3,7},{4,20},{5,1},{6,22},{7,3},{8,24},{9,13},... | collective-permute-start | bytes 2211848 | tf_op jit(solution)/shard_map/ppermute | solution.py:47
  82.8 18.1 %collective-permute-start.23 = (bf16[480,768]{1,0:T(8,128)(2,1)S(1)}, bf16[480,768]{1,0:T(8,128)(2,1)S(1)}, u32[]{:S(2)}, u32[]{:S(2)}) collective-permute-start(bf16[480,768]{1,0:T(8,128)(2,1)S(1)} %get-tuple-element.71), channel_id=1, source_target_pairs={{0,8},{1,3},{2,10},{3,5},{4,12},{5,7},{6,14},{7,1},{8,16},{9,11},{... | collective-permute-start | bytes 2211848 | tf_op jit(solution)/shard_map/ppermute | solution.py:47
  82.9 18.0 %collective-permute-start.24 = (bf16[480,768]{1,0:T(8,128)(2,1)S(1)}, bf16[480,768]{1,0:T(8,128)(2,1)S(1)}, u32[]{:S(2)}, u32[]{:S(2)}) collective-permute-start(bf16[480,768]{1,0:T(8,128)(2,1)S(1)} %get-tuple-element.72), channel_id=1, source_target_pairs={{0,24},{1,7},{2,26},{3,1},{4,28},{5,3},{6,30},{7,5},{8,0},{9,15},{... | collective-permute-start | bytes 2211848 | tf_op jit(solution)/shard_map/ppermute | solution.py:47
  86.6 17.6 %collective-permute-start.19 = (bf16[160,768]{1,0:T(8,128)(2,1)S(1)}, bf16[160,768]{1,0:T(8,128)(2,1)S(1)}, u32[]{:S(2)}, u32[]{:S(2)}) collective-permute-start(bf16[160,768]{1,0:T(8,128)(2,1)S(1)} %get-tuple-element.67), channel_id=1, source_target_pairs={{0,16},{1,5},{2,18},{3,7},{4,20},{5,1},{6,22},{7,3},{8,24},{9,13},... | collective-permute-start | bytes 737288 | tf_op jit(solution)/shard_map/ppermute | solution.py:47
  87.5 18.7 %collective-permute-start.20 = (bf16[160,768]{1,0:T(8,128)(2,1)S(1)}, bf16[160,768]{1,0:T(8,128)(2,1)S(1)}, u32[]{:S(2)}, u32[]{:S(2)}) collective-permute-start(bf16[160,768]{1,0:T(8,128)(2,1)S(1)} %get-tuple-element.68), channel_id=1, source_target_pairs={{0,8},{1,3},{2,10},{3,5},{4,12},{5,7},{6,14},{7,1},{8,16},{9,11},{... | collective-permute-start | bytes 737288 | tf_op jit(solution)/shard_map/ppermute | solution.py:47
  93.1 13.1 %collective-permute-start.21 = (bf16[160,768]{1,0:T(8,128)(2,1)S(1)}, bf16[160,768]{1,0:T(8,128)(2,1)S(1)}, u32[]{:S(2)}, u32[]{:S(2)}) collective-permute-start(bf16[160,768]{1,0:T(8,128)(2,1)S(1)} %get-tuple-element.69), channel_id=1, source_target_pairs={{0,24},{1,7},{2,26},{3,1},{4,28},{5,3},{6,30},{7,5},{8,0},{9,15},{... | collective-permute-start | bytes 737288 | tf_op jit(solution)/shard_map/ppermute | solution.py:47
  101.3 19.4 %copy-start.1 = (f32[6144,4]{0,1:T(4,128)S(1)}, f32[6144,4]{0,1:T(4,128)}, u32[]{:S(2)}) copy-start(f32[6144,4]{0,1:T(4,128)} %param.24) | copy-start | bytes 294916
  101.4 8.2 %collective-permute-start.25 = (bf16[160,768]{1,0:T(8,128)(2,1)S(1)}, bf16[160,768]{1,0:T(8,128)(2,1)S(1)}, u32[]{:S(2)}, u32[]{:S(2)}) collective-permute-start(bf16[160,768]{1,0:T(8,128)(2,1)S(1)} %get-tuple-element.79), channel_id=1, source_target_pairs={{0,2},{1,9},{2,4},{3,11},{4,6},{5,13},{6,0},{7,15},{8,10},{9,17},{... | collective-permute-start | bytes 737288 | tf_op jit(solution)/shard_map/ppermute | solution.py:43
  102.3 7.4 %collective-permute-start.26 = (bf16[160,768]{1,0:T(8,128)(2,1)S(1)}, bf16[160,768]{1,0:T(8,128)(2,1)S(1)}, u32[]{:S(2)}, u32[]{:S(2)}) collective-permute-start(bf16[160,768]{1,0:T(8,128)(2,1)S(1)} %get-tuple-element.78), channel_id=1, source_target_pairs={{0,6},{1,25},{2,0},{3,27},{4,2},{5,29},{6,4},{7,31},{8,14},{9,1},{... | collective-permute-start | bytes 737288 | tf_op jit(solution)/shard_map/ppermute | solution.py:43
  104.2 8.2 %collective-permute-start.27 = (bf16[160,768]{1,0:T(8,128)(2,1)S(1)}, bf16[160,768]{1,0:T(8,128)(2,1)S(1)}, u32[]{:S(2)}, u32[]{:S(2)}) collective-permute-start(bf16[160,768]{1,0:T(8,128)(2,1)S(1)} %get-tuple-element.77), channel_id=1, source_target_pairs={{0,4},{1,17},{2,6},{3,19},{4,0},{5,21},{6,2},{7,23},{8,12},{9,25},... | collective-permute-start | bytes 737288 | tf_op jit(solution)/shard_map/ppermute | solution.py:43
  112.6 3.3 %collective-permute-start.28 = (bf16[40,896]{1,0:T(8,128)(2,1)S(1)}, bf16[40,896]{1,0:T(8,128)(2,1)S(1)}, u32[]{:S(2)}, u32[]{:S(2)}) collective-permute-start(bf16[40,896]{1,0:T(8,128)(2,1)S(1)} %get-tuple-element.74), channel_id=1, source_target_pairs={{0,96},{32,0},{64,32},{96,64},{1,97},{33,1},{65,33},{97,65},{2,98}... | collective-permute-start | bytes 215048 | tf_op jit(solution)/shard_map/ppermute | solution.py:51
  114.4 5.1 %collective-permute-start.29 = (bf16[40,896]{1,0:T(8,128)(2,1)S(1)}, bf16[40,896]{1,0:T(8,128)(2,1)S(1)}, u32[]{:S(2)}, u32[]{:S(2)}) collective-permute-start(bf16[40,896]{1,0:T(8,128)(2,1)S(1)} %get-tuple-element.75), channel_id=1, source_target_pairs={{0,32},{32,64},{64,96},{96,0},{1,33},{33,65},{65,97},{97,1},{2,34}... | collective-permute-start | bytes 215048 | tf_op jit(solution)/shard_map/ppermute | solution.py:51
  114.4 5.2 %collective-permute-start.30 = (bf16[40,896]{1,0:T(8,128)(2,1)S(1)}, bf16[40,896]{1,0:T(8,128)(2,1)S(1)}, u32[]{:S(2)}, u32[]{:S(2)}) collective-permute-start(bf16[40,896]{1,0:T(8,128)(2,1)S(1)} %get-tuple-element.76), channel_id=1, source_target_pairs={{0,64},{32,96},{64,0},{96,32},{1,65},{33,97},{65,1},{97,33},{2,66}... | collective-permute-start | bytes 215048 | tf_op jit(solution)/shard_map/ppermute | solution.py:51

commit v6 on v5

--- a/solution.py
+++ b/solution.py
@@ -15,7 +15,7 @@
 BLK = 768
 ROWS = 160
 HID = 256
-OFFS = (0, 1, -1, 2)
+OFFS = (0, 1, 3, 2)
 AXES = ("z", "y", "x", "c")
 VMEM = pl.BlockSpec(memory_space=pltpu.VMEM)
 ANY = pl.BlockSpec(memory_space=pl.ANY)
@@ -32,9 +32,9 @@
             for x in range(4):
                 for c in range(2):
                     if (c == 0) == first:
-                        target = device_index(z, y, (x + shift) % 4, c)
+                        target = device_index(z, y, x ^ shift, c)
                     else:
-                        target = device_index(z, (y + shift) % 4, x, c)
+                        target = device_index(z, y ^ shift, x, c)
                     pairs.append((device_index(z, y, x, c), target))
     return pairs
 
@@ -48,11 +48,11 @@
 
 
 def along_z(a, shift):
-    return lax.ppermute(a, "z", [(i, (i + shift) % 4) for i in range(4)])
+    return lax.ppermute(a, "z", [(i, i ^ shift) for i in range(4)])
 
 
 def along_x(a, shift):
-    return lax.ppermute(a, "x", [(i, (i + shift) % 4) for i in range(4)])
+    return lax.ppermute(a, "x", [(i, i ^ shift) for i in range(4)])
 
 
 def swap_cores(a):
@@ -80,9 +80,8 @@
 
 
 def attend_kernel(
-    given_lengths, given_queries, given_keys, given_values, keys, values, weight, far, own,
-    lengths, queries, new_keys, new_values, key_here, value_here, weight_here, query_here, score, context, joined,
-    sems,
+    given_lengths, given_queries, given_keys, given_values, keys, values, weight, far, joined,
+    lengths, queries, new_keys, new_values, key_here, value_here, weight_here, query_here, score, context, sems,
 ):
     small = [
         pltpu.make_async_copy(source, target, sems.at[16 + n])
@@ -105,16 +104,15 @@
             source, target = (keys, key_here) if n < 4 else (values, value_here)
             part = pl.ds(n % 4 * chunk, chunk)
             return pltpu.make_async_copy(source.at[part], target.at[part], sems.at[n])
-        parity = 1 - core if n < 12 else core
-        start = pl.multiple_of((2 * (n % 4) + parity) * BLK, BLK)
+        start = pl.multiple_of((2 * (n % 4) + 1 - core) * BLK, BLK)
         return pltpu.make_async_copy(weight.at[:, pl.ds(start, BLK)], weight_here.at[n - 8], sems.at[n])
 
     started = [0]
 
-    def start(count):
-        for n in range(started[0], min(count, 16)):
+    def start(until):
+        for n in range(started[0], until):
             copy(n).start()
-        started[0] = max(started[0], min(count, 16))
+        started[0] = max(started[0], until)
 
     start(6)
     for one in small:
@@ -129,7 +127,7 @@
     scale = 1.0 / math.sqrt(size)
     for n in range(4):
         copy(n).wait()
-        start((8, 10, 12, 12)[n])
+        start((8, 9, 10, 11)[n])
         for t in range(n * chunk, (n + 1) * chunk):
             query = query_here[pl.ds(t, 8, stride=rows), :]
             score[row(t), :] = scale * lax.dot_general(
@@ -139,7 +137,7 @@
     slot = lax.broadcasted_iota(jnp.int32, (8, score.shape[1]), 1)
     for n in range(4):
         copy(n + 4).wait()
-        start(13 + n)
+        start(12)
         for t in range(n * chunk, (n + 1) * chunk):
             query = query_here[pl.ds(t, 8, stride=rows), :]
             new_key = new_keys[t : t + 1, :].astype(jnp.float32)
@@ -158,11 +156,9 @@
         joined[:, head * size : (head + 1) * size] = context[pl.ds(head, rows, stride=8), :].astype(
             jnp.bfloat16
         )
-    start(16)
-    for n in range(8):
+    for n in range(4):
         copy(8 + n).wait()
-        out = far if n < 4 else own
-        out[n % 4] = dot(joined[...], weight_here[n]).astype(out.dtype)
+        far[n] = dot(joined[...], weight_here[n]).astype(far.dtype)
 
 
 def attend(lengths, queries, new_keys, new_values, keys, values, out_weight):
@@ -172,7 +168,7 @@
         attend_kernel,
         out_shape=(
             pltpu.VMEM((4, rows, BLK), jnp.bfloat16),
-            pltpu.VMEM((4, rows, BLK), jnp.float32),
+            pltpu.VMEM((rows, heads * size), jnp.bfloat16),
         ),
         in_specs=[ANY] * 7,
         out_specs=(VMEM, VMEM),
@@ -183,11 +179,10 @@
             pltpu.VMEM((rows, size), jnp.bfloat16),
             pltpu.VMEM((rows, length, size), jnp.bfloat16),
             pltpu.VMEM((rows, length, size), jnp.bfloat16),
-            pltpu.VMEM((8, BLK, BLK), jnp.bfloat16),
+            pltpu.VMEM((4, BLK, BLK), jnp.bfloat16),
             pltpu.VMEM((8 * rows, size), jnp.float32),
             pltpu.VMEM((8 * rows, length), jnp.float32),
             pltpu.VMEM((8 * rows, size), jnp.float32),
-            pltpu.VMEM((rows, heads * size), jnp.bfloat16),
             pltpu.SemaphoreType.DMA((20,)),
         ],
         compiler_params=params(20),
@@ -205,10 +200,40 @@
     )
 
 
+def project_kernel(context, weight, own, weight_here, sems):
+    core = position()[2]
+    copies = []
+    for n in range(4):
+        start = pl.multiple_of((2 * n + core) * BLK, BLK)
+        copies.append(
+            pltpu.make_async_copy(weight.at[:, pl.ds(start, BLK)], weight_here.at[n], sems.at[n])
+        )
+    for copy in copies:
+        copy.start()
+    for n in range(4):
+        copies[n].wait()
+        own[n] = dot(context[...], weight_here[n])
+
+
+def project(context, out_weight):
+    rows = context.shape[0]
+    return pl.pallas_call(
+        project_kernel,
+        out_shape=pltpu.VMEM((4, rows, BLK), jnp.float32),
+        in_specs=[VMEM, ANY],
+        out_specs=VMEM,
+        scratch_shapes=[pltpu.VMEM((4, BLK, BLK), jnp.bfloat16), pltpu.SemaphoreType.DMA((4,))],
+        compiler_params=params(8),
+        cost_estimate=pl.CostEstimate(
+            flops=2 * rows * BLK * BLK * 4, bytes_accessed=5000000, transcendentals=0
+        ),
+    )(near(context), distant(out_weight))
+
+
 def combine_kernel(own, far, routes, mine, one, three, two, handed):
     handed[...] = routes[...]
-    for out, shift in ((mine, 0), (one, 1), (three, -1), (two, 2)):
-        block = behind(position()[0], -shift)
+    for out, shift in ((mine, 0), (one, 1), (three, 3), (two, 2)):
+        block = partner(position()[0], shift)
         out[...] = (own[block] + far[block].astype(jnp.float32)).astype(out.dtype)
 
 
@@ -236,7 +261,7 @@
     lane = lax.broadcasted_iota(jnp.int32, (rows, 128), 1)
     plane = jnp.full((rows, 128), -1, jnp.int32)
     for i, shift in enumerate(OFFS):
-        plane = jnp.where(lane == i, behind(position()[3], -shift), plane)
+        plane = jnp.where(lane == i, partner(position()[3], shift), plane)
     one = jnp.where(routes[:, 0:1] == plane, 1.0, 0.0)
     two = jnp.where(routes[:, 1:2] == plane, 1.0, 0.0)
     before = lax.broadcasted_iota(jnp.int32, (rows, rows), 1) < lax.broadcasted_iota(
@@ -321,13 +346,13 @@
     return total
 
 
-def behind(position, shift):
-    return (position - shift + 4) % 4
+def partner(position, shift):
+    return position ^ shift
 
 
 def walk(held, emit):
     x, y, c, _ = position()
-    blocks = [2 * behind(x, shift) + c for shift in OFFS]
+    blocks = [2 * partner(x, shift) + c for shift in OFFS]
 
     for core in range(2):
 
@@ -338,19 +363,19 @@
                     spots = {n: (held.index(m), n) for n in range(4)} if m in held else {}
                 else:
                     spots = {n: (j, m) for j, n in enumerate(held)}
-                emit(core, line_rows(behind(y, shift)), m, blocks, spots)
+                emit(core, line_rows(partner(y, shift)), m, blocks, spots)
 
 
 def stage_kernel(gate_far, up_far, gate, up, down, down_far, weights, downs, sems):
     x, _, c, _ = position()
     copies = []
     for n, shift in enumerate(OFFS):
-        rows = pl.ds(pl.multiple_of((2 * behind(x, shift) + c) * BLK, BLK), BLK)
-        columns = pl.ds(pl.multiple_of((2 * behind(x, -shift) + c) * BLK, BLK), BLK)
+        rows = pl.ds(pl.multiple_of((2 * partner(x, shift) + c) * BLK, BLK), BLK)
+        columns = pl.ds(pl.multiple_of((2 * partner(x, shift) + c) * BLK, BLK), BLK)
         for which, source in enumerate((gate_far, up_far, gate, up)):
             copies.append((source.at[rows, :], weights.at[which, n]))
         copies.append((down.at[:, columns], downs.at[0, n]))
-        copies.append((down_far.at[behind(x, -shift)], downs.at[1, n]))
+        copies.append((down_far.at[partner(x, shift)], downs.at[1, n]))
     copies = [pltpu.make_async_copy(*ends, sems.at[i]) for i, ends in enumerate(copies)]
     for copy in copies:
         copy.start()
@@ -373,7 +398,7 @@
     )(*map(distant, sources))
 
 
-def enter_terms(pieces, weights, inverse, route, blocks, spots):
+def enter_terms(pieces, weights, inverse, route, blocks, spots, which=range(4)):
     def found(n):
         j, i = spots[n]
         return pieces[j, i * ROWS : (i + 1) * ROWS, :]
@@ -381,7 +406,9 @@
     def total(terms):
         return functools.reduce(lambda a, b: a + b, terms)
 
-    sums = [total([dot(found(n), weights[which, n]) for n in spots]) for which in range(4)]
+    sums = [total([dot(found(n), weights[w, n]) for n in spots]) for w in which]
+    if inverse is None:
+        return sums, ()
     squares, products = [], []
     for n in spots:
         value = found(n).astype(jnp.float32)
@@ -415,11 +442,7 @@
     walk((0, 3), emit)
 
 
-def enter_second_kernel(
-    p0, p1, weights, inverse, route, own_first, sums_first, far_first, own, sums, far, pieces, sems
-):
-    given = (p0, p1)
-
+def enter_second(given, pieces, sems, emit_terms):
     def copies(core, step):
         parts = []
         for j in range(2):
@@ -448,19 +471,34 @@
             wait(core, m)
             if m < 2:
                 start(core, m + 2)
-        before = (far_first[rows, :], own_first[rows, :], sums_first[rows, :])
-        if not spots:
-            far_all, own_all, both = before
-        else:
-            terms, both = enter_terms(pieces, weights, inverse, route, blocks, spots)
-            far_all, own_all, both = (jnp.concatenate(v, axis=1) for v in (terms[:2], terms[2:], both))
-            if core == 1:
-                far_all, own_all, both = far_all + before[0], own_all + before[1], both + before[2]
-        own[rows, :] = own_all
+        emit_terms(core, rows, blocks, spots)
+
+    walk((1, 2), emit)
+
+
+def enter_far_kernel(p0, p1, weights, inverse, route, far_first, sums_first, far, sums, pieces, sems):
+    def emit(core, rows, blocks, spots):
+        far_all, both = far_first[rows, :], sums_first[rows, :]
+        if spots:
+            terms, more = enter_terms(pieces, weights, inverse, route, blocks, spots, (0, 1))
+            terms, more = jnp.concatenate(terms, axis=1), jnp.concatenate(more, axis=1)
+            far_all, both = (terms, more) if core == 0 else (terms + far_all, more + both)
         sums[rows, :] = both
         put(far, rows, (far_all, both))
 
-    walk((1, 2), emit)
+    enter_second((p0, p1), pieces, sems, emit)
+
+
+def enter_own_kernel(p0, p1, weights, own_first, own, pieces, sems):
+    def emit(core, rows, blocks, spots):
+        own_all = own_first[rows, :]
+        if spots:
+            terms, _ = enter_terms(pieces, weights, None, None, blocks, spots, (2, 3))
+            terms = jnp.concatenate(terms, axis=1)
+            own_all = terms if core == 0 else terms + own_all
+        own[rows, :] = own_all
+
+    enter_second((p0, p1), pieces, sems, emit)
 
 
 def enter(pieces, weights, inverse, route):
@@ -480,15 +518,27 @@
         compiler_params=params(10),
         cost_estimate=cost,
     )(distant(pieces[0]), distant(pieces[3]), *fixed)
-    return pl.pallas_call(
-        enter_second_kernel,
-        out_shape=(own, sums, pltpu.VMEM((4 * ROWS, 2 * HID + 256), jnp.bfloat16)),
-        in_specs=[ANY] * 2 + [VMEM] * 6,
-        out_specs=(VMEM,) * 3,
+    own_first, sums_first, far_first = map(near, first)
+    given = distant(pieces[1]), distant(pieces[2])
+    far, sums = pl.pallas_call(
+        enter_far_kernel,
+        out_shape=(pltpu.VMEM((4 * ROWS, 2 * HID + 256), jnp.bfloat16), sums),
+        in_specs=[ANY] * 2 + [VMEM] * 5,
+        out_specs=(VMEM,) * 2,
         scratch_shapes=scratch,
         compiler_params=params(10),
         cost_estimate=cost,
-    )(distant(pieces[1]), distant(pieces[2]), *fixed, *map(near, first))
+    )(*given, *fixed, far_first, sums_first)
+    own = pl.pallas_call(
+        enter_own_kernel,
+        out_shape=own,
+        in_specs=[ANY] * 2 + [VMEM] * 2,
+        out_specs=VMEM,
+        scratch_shapes=scratch,
+        compiler_params=params(10),
+        cost_estimate=cost,
+    )(*given, fixed[0], own_first)
+    return own, sums, far
 
 
 def activate_kernel(own, sums, far, out, logit):
@@ -528,7 +578,7 @@
             for out, (second, firsts) in zip(outs, wanted):
                 for i, first in enumerate(firsts):
                     on_x, on_y = (first, second) if core == 0 else (second, first)
-                    rows, n = line_rows(behind(y, -on_y)), OFFS.index(on_x)
+                    rows, n = line_rows(partner(y, on_y)), OFFS.index(on_x)
                     value = dot(act[rows, :], downs[0, n]) + dot(act_far[rows, :], downs[1, n])
                     out[i * ROWS : (i + 1) * ROWS, :] = value.astype(jnp.bfloat16)
 
@@ -624,11 +674,12 @@
     gain = norm_gain.astype(jnp.float32).reshape(8, BLK)
     inverse = 1.0 / gain
 
-    for_other, for_own = attend(
+    for_other, context = attend(
         lengths, queries, new_keys, new_values, key_cache, value_cache, out_weight
     )
+    for_own = project(context, out_weight)
     mine, one, three, two, routes = combine(for_own, swap_cores(for_other), routes)
-    moved = [along_x(one, 1), along_x(three, -1), along_x(two, 2)]
+    moved = [along_x(one, 1), along_x(three, 3), along_x(two, 2)]
     first_hits, second_hits, down_half = slots(routes, down_weight)
     down_far = swap_cores(down_half)
     hidden, *outgoing = prepare(
@@ -647,21 +698,21 @@
     operands = (act, swap_cores(act), downs)
     rest = OFFS[1:]
     (far2,) = leave(((2, rest),), *operands)
-    far1, far3 = leave(((1, rest), (-1, rest)), *operands)
+    far1, far3 = leave(((1, rest), (3, rest)), *operands)
     near2, near1, near3, far0, near0 = leave(
-        ((2, (0,)), (1, (0,)), (-1, (0,)), (0, rest), (0, (0,))), *operands
+        ((2, (0,)), (1, (0,)), (3, (0,)), (0, rest), (0, (0,))), *operands
     )
 
     def gathered(own, one, three, two):
         total = own.astype(jnp.float32) + along_second(two, 2).astype(jnp.float32)
         total = total + along_second(one, 1).astype(jnp.float32)
-        return total + along_second(three, -1).astype(jnp.float32)
+        return total + along_second(three, 3).astype(jnp.float32)
 
     others = gathered(far0, far1, far3, far2).astype(jnp.bfloat16).reshape(3, ROWS, BLK)
-    parts = [along_second(near2, 2), along_second(near1, 1), along_second(near3, -1)]
+    parts = [along_second(near2, 2), along_second(near1, 1), along_second(near3, 3)]
     parts += [along_first(others[i], shift) for i, shift in enumerate(rest)]
     back = gather(near0, parts, logit)
-    blocks = [back[0]] + [along_z(block, -shift) for block, shift in zip(back[1:], rest)]
+    blocks = [back[0]] + [along_z(block, shift) for block, shift in zip(back[1:], rest)]
     return finish(hidden, first_hits, second_hits, blocks)
 
 

time: 122 us -> 120 us (0.984)
  waiting for transfers between devices: 56.8 us -> 48.9 us
  Pallas kernels: 25.9 us -> 29.5 us
  starting transfers between devices: 37.2 us -> 39.5 us
    pallas_call x1 -> x3, Pallas kernels: 3.94 us -> 9.06 us  [the longest x1 3.17 us: enter(): pl.pallas_call(enter_far_kernel, out_shape=(pltpu.VMEM((4 * ROWS, 2 * HID...]
    ppermute x7, waiting for transfers between devices: 6.09 us -> 2.94 us  [swap_cores(): return lax.ppermute(a, 'c', [(0, 1), (1, 0)])]
    ppermute x9, waiting for transfers between devices: 27.9 us -> 25.3 us  [along_second(): return lax.ppermute(a, AXES, plane_pairs(False, shift))]
    ppermute x6, waiting for transfers between devices: 14.6 us -> 12.5 us  [along_first(): return lax.ppermute(a, AXES, plane_pairs(True, shift))]
    ppermute x9, starting transfers between devices: 8.67 us -> 10.5 us  [along_second(): return lax.ppermute(a, AXES, plane_pairs(False, shift))]
    pallas_call x1, Pallas kernels: 7.84 us -> 6.35 us  [attend(): pl.pallas_call(attend_kernel, out_shape=(pltpu.VMEM((4, rows, BLK), jnp.b...]
  transfers between devices with their start and end apart: 31 -> 31, of which waited for: 20 -> 19; matrix products, arithmetic and copies ran while one was open for 1% -> 1% of each run, Pallas kernels for 16% -> 20%
where the time goes in v6:
time: 120 us; the launch traced here: 119 us
  waiting for transfers between devices  48.9 us (41%)
  starting transfers between devices  39.5 us (33%)
  Pallas kernels  29.5 us (25%)
    ppermute x9, waiting for transfers between devices, along_second(): return lax.ppermute(a, AXES, plane_pairs(False, shift))  25.3 us
    ppermute x6, waiting for transfers between devices, along_first(): return lax.ppermute(a, AXES, plane_pairs(True, shift))  12.5 us
    ppermute x9, starting transfers between devices, along_second(): return lax.ppermute(a, AXES, plane_pairs(False, shift))  10.5 us
    ppermute x7, starting transfers between devices, swap_cores(): return lax.ppermute(a, 'c', [(0, 1), (1, 0)])  8.89 us
    ppermute x6, starting transfers between devices, along_z(): return lax.ppermute(a, 'z', [(i, i ^ shift) for i in range(4)])  8.36 us
    ppermute x6, starting transfers between devices, along_first(): return lax.ppermute(a, AXES, plane_pairs(True, shift))  7.94 us
    pallas_call x1, Pallas kernels, attend(): pl.pallas_call(attend_kernel, out_shape=(pltpu.VMEM((4, rows, BLK), jnp.b...  6.35 us
    ppermute x6, waiting for transfers between devices, along_z(): return lax.ppermute(a, 'z', [(i, i ^ shift) for i in range(4)])  6.28 us
  transfers between devices with their start and end apart: 31, of which 19 were waited for; matrix products, arithmetic and copies ran while one was open for 1% of the time, Pallas kernels for 20%

profile of v6, /device:TPU:1, one launch (start us, length us, event | category | flops | bytes accessed | tf_op | source)
XLA Modules:
  0.0 118.9 jit_solution(1964138805023017361)
XLA Ops:
  0.0 1.4 %collective-permute-start.4 = (bf16[6144,256]{1,0:T(8,128)(2,1)}, bf16[6144,256]{1,0:T(8,128)(2,1)}, u32[]{:S(2)}, u32[]{:S(2)}) collective-permute-start(bf16[6144,256]{1,0:T(8,128)(2,1)} %gate.1), channel_id=1, source_target_pairs={{0,1},{1,0},{2,3},{3,2},{4,5},{5,4},{6,7},{7,6},{8,9},{9,8},{10,11... | collective-permute-start | bytes 9437192 | tf_op jit(solution)/shard_map/ppermute | solution.py:59
  1.4 6.4 %shard_map.136 = (bf16[4,64,768]{2,1,0:T(8,128)(2,1)S(1)}, bf16[64,768]{1,0:T(8,128)(2,1)S(1)}) custom-call(s32[64]{0:T(128)} %given_lengths.1, bf16[6,64,128]{2,1,0:T(8,128)(2,1)} %bitcast.7, bf16[64,128]{1,0:T(8,128)(2,1)} %bitcast.8, bf16[64,128]{1,0:T(8,128)(2,1)} %bitcast.9, bf16[64,128,128]{2,1,0:T(8,128)(2,1)} %bitcast.5, ...), custom_call_target="tpu_custom_call" | custom-call | flops 603979776 | bytes 14000000 | tf_op jit(solution)/shard_map/pallas_call | solution.py:167
  7.8 0.6 collective-permute-start
  8.4 0.1 copy.15.routes
  8.5 2.8 %shard_map.137.own = f32[4,64,768]{2,1,0:T(8,128)S(1)} custom-call(bf16[64,768]{1,0:T(8,128)(2,1)S(1)} %get-tuple-element.40.context, bf16[768,6144]{1,0:T(8,128)(2,1)} %weight.3), custom_call_target="tpu_custom_call" | custom-call | flops 301989888 | bytes 5000000 | tf_op jit(solution)/shard_map/pallas_call | solution.py:220
  11.3 0.5 collective-permute-done.far
  11.8 1.4 %collective-permute-start.1 = (bf16[64,768]{1,0:T(8,128)(2,1)S(1)}, bf16[64,768]{1,0:T(8,128)(2,1)S(1)}, u32[]{:S(2)}, u32[]{:S(2)}) collective-permute-start(bf16[64,768]{1,0:T(8,128)(2,1)S(1)} %get-tuple-element.43), channel_id=1, source_target_pairs={{0,2},{2,0},{4,6},{6,4},{1,3},{3,1},{5,7},{7,5},{8,10},{10,8},{12,... | collective-permute-start | bytes 294920 | tf_op jit(solution)/shard_map/ppermute | solution.py:55
  13.2 1.8 %collective-permute-start.2 = (bf16[64,768]{1,0:T(8,128)(2,1)S(1)}, bf16[64,768]{1,0:T(8,128)(2,1)S(1)}, u32[]{:S(2)}, u32[]{:S(2)}) collective-permute-start(bf16[64,768]{1,0:T(8,128)(2,1)S(1)} %get-tuple-element.44), channel_id=1, source_target_pairs={{0,6},{2,4},{4,2},{6,0},{1,7},{3,5},{5,3},{7,1},{8,14},{10,12},{12... | collective-permute-start | bytes 294920 | tf_op jit(solution)/shard_map/ppermute | solution.py:55
  15.0 0.6 collective-permute-start.3
  15.7 1.4 %shard_map.139 = (bf16[4,64,40]{2,1,0:T(8,128)(2,1)S(1)}, bf16[4,64,40]{2,1,0:T(8,128)(2,1)S(1)}, bf16[4,256,768]{2,1,0:T(8,128)(2,1)S(1)}) custom-call(s32[64,2]{1,0:T(8,128)S(1)} %get-tuple-element.46.routes, bf16[256,6144]{1,0:T(8,128)(2,1)} %down.3), custom_call_target="tpu_custom_call" | custom-call | tf_op jit(solution)/shard_map/pallas_call | solution.py:282
  17.2 1.0 collective-permute-start.15
  18.2 1.9 %collective-permute-done.3.two = bf16[64,768]{1,0:T(8,128)(2,1)S(1)} collective-permute-done((bf16[64,768]{1,0:T(8,128)(2,1)S(1)}, bf16[64,768]{1,0:T(8,128)(2,1)S(1)}, u32[]{:S(2)}, u32[]{:S(2)}) %collective-permute-start.3) | collective-permute-done | bytes 98336 | tf_op jit(solution)/shard_map/ppermute | solution.py:55
  20.1 0.3 shard_map.140
  20.4 1.7 %collective-permute-start.6 = (bf16[40,768]{1,0:T(8,128)(2,1)S(1)}, bf16[40,768]{1,0:T(8,128)(2,1)S(1)}, u32[]{:S(2)}, u32[]{:S(2)}) collective-permute-start(bf16[40,768]{1,0:T(8,128)(2,1)S(1)} %get-tuple-element.51), channel_id=1, source_target_pairs={{0,32},{32,0},{64,96},{96,64},{1,33},{33,1},{65,97},{97,65},{2,34}... | collective-permute-start | bytes 184328 | tf_op jit(solution)/shard_map/ppermute | solution.py:51
  22.1 2.2 %collective-permute-start.7 = (bf16[40,768]{1,0:T(8,128)(2,1)S(1)}, bf16[40,768]{1,0:T(8,128)(2,1)S(1)}, u32[]{:S(2)}, u32[]{:S(2)}) collective-permute-start(bf16[40,768]{1,0:T(8,128)(2,1)S(1)} %get-tuple-element.52), channel_id=1, source_target_pairs={{0,96},{32,64},{64,32},{96,0},{1,97},{33,65},{65,33},{97,1},{2,98}... | collective-permute-start | bytes 184328 | tf_op jit(solution)/shard_map/ppermute | solution.py:51
  24.3 1.1 collective-permute-start.8
  25.4 0.9 collective-permute-done.7
  26.4 2.7 %collective-permute-done.8 = bf16[40,768]{1,0:T(8,128)(2,1)S(1)} collective-permute-done((bf16[40,768]{1,0:T(8,128)(2,1)S(1)}, bf16[40,768]{1,0:T(8,128)(2,1)S(1)}, u32[]{:S(2)}, u32[]{:S(2)}) %collective-permute-start.8) | collective-permute-done | bytes 61472 | tf_op jit(solution)/shard_map/ppermute | solution.py:51
  29.1 2.7 %collective-permute-start.10 = (bf16[160,768]{1,0:T(8,128)(2,1)S(1)}, bf16[160,768]{1,0:T(8,128)(2,1)S(1)}, u32[]{:S(2)}, u32[]{:S(2)}) collective-permute-start(bf16[160,768]{1,0:T(8,128)(2,1)S(1)} %constant_dynamic-update-slice_fusion.a), channel_id=1, source_target_pairs={{0,6},{1,25},{2,4},{3,27},{4,2},{5,29},{6,0},{7,31},{8,14},{9,17},... | collective-permute-start | bytes 737288 | tf_op jit(solution)/shard_map/ppermute | solution.py:43
  31.8 0.3 collective-permute-start.11
  32.1 0.3 collective-permute-start.9
  32.5 5.1 %collective-permute-done.10.c = bf16[160,768]{1,0:T(8,128)(2,1)S(1)} collective-permute-done((bf16[160,768]{1,0:T(8,128)(2,1)S(1)}, bf16[160,768]{1,0:T(8,128)(2,1)S(1)}, u32[]{:S(2)}, u32[]{:S(2)}) %collective-permute-start.10) | collective-permute-done | bytes 245792 | tf_op jit(solution)/shard_map/ppermute | solution.py:43
  37.6 0.8 collective-permute-done.11.d
  38.3 0.7 collective-permute-done.9.b
  39.0 4.6 %collective-permute-start.12 = (f32[16,128]{1,0:T(8,128)S(1)}, f32[16,128]{1,0:T(8,128)S(1)}, u32[]{:S(2)}, u32[]{:S(2)}) collective-permute-start(f32[16,128]{1,0:T(8,128)S(1)} %convert_add_fusion), channel_id=1, source_target_pairs={{0,1},{1,0},{2,3},{3,2},{4,5},{5,4},{6,7},{7,6},{8,9},{9,8},{10,11... | collective-permute-start | bytes 24584 | tf_op jit(solution)/shard_map/ppermute | solution.py:59
  43.6 0.8 collective-permute-done.12.token
  44.5 1.0 collective-permute-start.16
  45.5 1.2 collective-permute-start.13
  46.7 1.1 collective-permute-start.14
  48.0 4.0 %shard_map.142 = (bf16[4,4,768,256]{3,2,1,0:T(8,128)(2,1)S(1)}, bf16[2,4,256,768]{3,2,1,0:T(8,128)(2,1)S(1)}) custom-call(bf16[6144,256]{1,0:T(8,128)(2,1)} %collective-permute-done.4.rest_0_.gate_far, bf16[6144,256]{1,0:T(8,128)(2,1)} %collective-permute-done.5.rest_1_.up_far, bf16[6144,256]{1,0:T(8,128)(2,1)} %gate.1, bf16[6144,256]{1,0:T(8,128)(2,1)} %up.1, ...), custom_call_target="tpu_custom_call" | custom-call | bytes 18000000 | tf_op jit(solution)/shard_map/pallas_call | solution.py:387
  52.0 7.5 %collective-permute-done.16.p1 = bf16[640,768]{1,0:T(8,128)(2,1)} collective-permute-done((bf16[640,768]{1,0:T(8,128)(2,1)S(1)}, bf16[640,768]{1,0:T(8,128)(2,1)}, u32[]{:S(2)}, u32[]{:S(2)}) %collective-permute-start.16) | collective-permute-done | bytes 983072 | tf_op jit(solution)/shard_map/ppermute | solution.py:47
  59.5 3.8 %shard_map.143 = (f32[640,512]{1,0:T(8,128)S(1)}, f32[640,256]{1,0:T(8,128)S(1)}, f32[640,512]{1,0:T(8,128)S(1)}) custom-call(bf16[640,768]{1,0:T(8,128)(2,1)} %copy-done.2, bf16[640,768]{1,0:T(8,128)(2,1)} %collective-permute-done.16.p1, bf16[4,4,768,256]{3,2,1,0:T(8,128)(2,1)S(1)} %get-tuple-element.55.weights, f32[8,768]{1,0:T(8,128)S(1)} %broadcast_divide_fusion.inverse, ...), custom_call_target="tpu_custom_call" | custom-call | flops 2013265920 | bytes 5000000 | tf_op jit(solution)/shard_map/pallas_call | solution.py:512
  63.3 5.9 %collective-permute-done.13.p0 = bf16[640,768]{1,0:T(8,128)(2,1)} collective-permute-done((bf16[640,768]{1,0:T(8,128)(2,1)S(1)}, bf16[640,768]{1,0:T(8,128)(2,1)}, u32[]{:S(2)}, u32[]{:S(2)}) %collective-permute-start.13) | collective-permute-done | bytes 983072 | tf_op jit(solution)/shard_map/ppermute | solution.py:47
  69.2 0.8 collective-permute-done.14.p1
  70.0 3.2 %shard_map.145 = (bf16[640,768]{1,0:T(8,128)(2,1)S(1)}, f32[640,256]{1,0:T(8,128)S(1)}) custom-call(bf16[640,768]{1,0:T(8,128)(2,1)} %collective-permute-done.13.p0, bf16[640,768]{1,0:T(8,128)(2,1)} %collective-permute-done.14.p1, bf16[4,4,768,256]{3,2,1,0:T(8,128)(2,1)S(1)} %get-tuple-element.55.weights, f32[8,768]{1,0:T(8,128)S(1)} %broadcast_divide_fusion.inverse, ...), custom_call_target="tpu_custom_call" | custom-call | flops 2013265920 | bytes 5000000 | tf_op jit(solution)/shard_map/pallas_call | solution.py:523
  73.1 1.2 %collective-permute-start.17 = (bf16[640,768]{1,0:T(8,128)(2,1)S(1)}, bf16[640,768]{1,0:T(8,128)(2,1)S(1)}, u32[]{:S(2)}, u32[]{:S(2)}) collective-permute-start(bf16[640,768]{1,0:T(8,128)(2,1)S(1)} %get-tuple-element.60), channel_id=1, source_target_pairs={{0,1},{1,0},{2,3},{3,2},{4,5},{5,4},{6,7},{7,6},{8,9},{9,8},{10,11... | collective-permute-start | bytes 2949128 | tf_op jit(solution)/shard_map/ppermute | solution.py:59
  74.3 3.1 %shard_map.144.own = f32[640,512]{1,0:T(8,128)S(1)} custom-call(bf16[640,768]{1,0:T(8,128)(2,1)} %collective-permute-done.13.p0, bf16[640,768]{1,0:T(8,128)(2,1)} %collective-permute-done.14.p1, bf16[4,4,768,256]{3,2,1,0:T(8,128)(2,1)S(1)} %get-tuple-element.55.weights, f32[640,512]{1,0:T(8,128)S(1)} %get-tuple-element.56.own_first), custom_call_target="tpu_custom_call" | custom-call | flops 2013265920 | bytes 5000000 | tf_op jit(solution)/shard_map/pallas_call | solution.py:532
  77.5 0.4 shard_map.146
  78.0 1.6 %collective-permute-done.18.act_far = bf16[640,256]{1,0:T(8,128)(2,1)S(1)} collective-permute-done((bf16[640,256]{1,0:T(8,128)(2,1)S(1)}, bf16[640,256]{1,0:T(8,128)(2,1)S(1)}, u32[]{:S(2)}, u32[]{:S(2)}) %collective-permute-start.18) | collective-permute-done | bytes 327712 | tf_op jit(solution)/shard_map/ppermute | solution.py:59
  79.6 0.5 shard_map.148
  80.1 1.0 collective-permute-start.22
  81.2 0.9 shard_map.149
  82.1 1.2 %collective-permute-start.23 = (bf16[480,768]{1,0:T(8,128)(2,1)S(1)}, bf16[480,768]{1,0:T(8,128)(2,1)S(1)}, u32[]{:S(2)}, u32[]{:S(2)}) collective-permute-start(bf16[480,768]{1,0:T(8,128)(2,1)S(1)} %get-tuple-element.69), channel_id=1, source_target_pairs={{0,8},{1,3},{2,10},{3,1},{4,12},{5,7},{6,14},{7,5},{8,0},{9,11},{1... | collective-permute-start | bytes 2211848 | tf_op jit(solution)/shard_map/ppermute | solution.py:47
  83.4 1.1 collective-permute-start.24
  84.5 1.1 shard_map.147
  85.6 1.0 collective-permute-start.19
  86.6 1.2 collective-permute-start.20
  87.8 4.6 %collective-permute-done.22 = bf16[480,768]{1,0:T(8,128)(2,1)S(1)} collective-permute-done((bf16[480,768]{1,0:T(8,128)(2,1)S(1)}, bf16[480,768]{1,0:T(8,128)(2,1)S(1)}, u32[]{:S(2)}, u32[]{:S(2)}) %collective-permute-start.22) | collective-permute-done | bytes 737312 | tf_op jit(solution)/shard_map/ppermute | solution.py:47
  92.4 1.5 %collective-permute-start.21 = (bf16[160,768]{1,0:T(8,128)(2,1)S(1)}, bf16[160,768]{1,0:T(8,128)(2,1)S(1)}, u32[]{:S(2)}, u32[]{:S(2)}) collective-permute-start(bf16[160,768]{1,0:T(8,128)(2,1)S(1)} %get-tuple-element.67), channel_id=1, source_target_pairs={{0,24},{1,7},{2,26},{3,5},{4,28},{5,3},{6,30},{7,1},{8,16},{9,15},... | collective-permute-start | bytes 737288 | tf_op jit(solution)/shard_map/ppermute | solution.py:47
  93.9 5.5 %collective-permute-done.23 = bf16[480,768]{1,0:T(8,128)(2,1)S(1)} collective-permute-done((bf16[480,768]{1,0:T(8,128)(2,1)S(1)}, bf16[480,768]{1,0:T(8,128)(2,1)S(1)}, u32[]{:S(2)}, u32[]{:S(2)}) %collective-permute-start.23) | collective-permute-done | bytes 737312 | tf_op jit(solution)/shard_map/ppermute | solution.py:47
  99.4 0.8 collective-permute-done.24
  100.2 0.4 add_convert_fusion
  100.7 0.9 collective-permute-start.25
  101.6 1.7 %collective-permute-start.26 = (bf16[160,768]{1,0:T(8,128)(2,1)S(1)}, bf16[160,768]{1,0:T(8,128)(2,1)S(1)}, u32[]{:S(2)}, u32[]{:S(2)}) collective-permute-start(bf16[160,768]{1,0:T(8,128)(2,1)S(1)} %get-tuple-element.76), channel_id=1, source_target_pairs={{0,6},{1,25},{2,4},{3,27},{4,2},{5,29},{6,0},{7,31},{8,14},{9,17},... | collective-permute-start | bytes 737288 | tf_op jit(solution)/shard_map/ppermute | solution.py:43
  103.3 1.9 %collective-permute-start.27 = (bf16[160,768]{1,0:T(8,128)(2,1)S(1)}, bf16[160,768]{1,0:T(8,128)(2,1)S(1)}, u32[]{:S(2)}, u32[]{:S(2)}) collective-permute-start(bf16[160,768]{1,0:T(8,128)(2,1)S(1)} %get-tuple-element.75), channel_id=1, source_target_pairs={{0,4},{1,17},{2,6},{3,19},{4,0},{5,21},{6,2},{7,23},{8,12},{9,25},... | collective-permute-start | bytes 737288 | tf_op jit(solution)/shard_map/ppermute | solution.py:43
  105.3 0.2 collective-permute-done.21.rest_2_
  105.5 3.3 %collective-permute-done.25.rest_3_ = bf16[160,768]{1,0:T(8,128)(2,1)S(1)} collective-permute-done((bf16[160,768]{1,0:T(8,128)(2,1)S(1)}, bf16[160,768]{1,0:T(8,128)(2,1)S(1)}, u32[]{:S(2)}, u32[]{:S(2)}) %collective-permute-start.25) | collective-permute-done | bytes 245792 | tf_op jit(solution)/shard_map/ppermute | solution.py:43
  108.8 2.7 %collective-permute-done.27.rest_5_ = bf16[160,768]{1,0:T(8,128)(2,1)S(1)} collective-permute-done((bf16[160,768]{1,0:T(8,128)(2,1)S(1)}, bf16[160,768]{1,0:T(8,128)(2,1)S(1)}, u32[]{:S(2)}, u32[]{:S(2)}) %collective-permute-start.27) | collective-permute-done | bytes 245792 | tf_op jit(solution)/shard_map/ppermute | solution.py:43
  111.5 0.2 shard_map.150
  111.7 0.8 collective-permute-start.28
  112.5 0.3 collective-permute-start.29
  112.9 2.2 %collective-permute-start.30 = (bf16[40,896]{1,0:T(8,128)(2,1)S(1)}, bf16[40,896]{1,0:T(8,128)(2,1)S(1)}, u32[]{:S(2)}, u32[]{:S(2)}) collective-permute-start(bf16[40,896]{1,0:T(8,128)(2,1)S(1)} %get-tuple-element.74), channel_id=1, source_target_pairs={{0,64},{32,96},{64,0},{96,32},{1,65},{33,97},{65,1},{97,33},{2,66}... | collective-permute-start | bytes 215048 | tf_op jit(solution)/shard_map/ppermute | solution.py:51
  115.0 2.6 %collective-permute-done.29.b2 = bf16[40,896]{1,0:T(8,128)(2,1)S(1)} collective-permute-done((bf16[40,896]{1,0:T(8,128)(2,1)S(1)}, bf16[40,896]{1,0:T(8,128)(2,1)S(1)}, u32[]{:S(2)}, u32[]{:S(2)}) %collective-permute-start.29) | collective-permute-done | bytes 71712 | tf_op jit(solution)/shard_map/ppermute | solution.py:51
  117.7 1.2 %shard_map.151 = bf16[64,768]{1,0:T(8,128)(2,1)} custom-call(f32[64,768]{1,0:T(8,128)S(1)} %get-tuple-element.49.hidden, bf16[4,64,40]{2,1,0:T(8,128)(2,1)S(1)} %get-tuple-element.47.first, bf16[4,64,40]{2,1,0:T(8,128)(2,1)S(1)} %get-tuple-element.48.second, bf16[40,896]{1,0:T(8,128)(2,1)S(1)} %get-tuple-element.71.b0, ...), custom_call_target="tpu_custom_call" | custom-call | flops 40000000 | bytes 2000000 | tf_op jit(solution)/shard_map/pallas_call | solution.py:645
  (38 shorter events, 0.5 us)
Async XLA Ops:
  0.0 47.8 %copy-start = (f32[6144,4]{0,1:T(4,128)S(1)}, f32[6144,4]{0,1:T(4,128)}, u32[]{:S(2)}) copy-start(f32[6144,4]{0,1:T(4,128)} %param.24) | copy-start | bytes 294916
  0.0 20.1 %collective-permute-start.4 = (bf16[6144,256]{1,0:T(8,128)(2,1)}, bf16[6144,256]{1,0:T(8,128)(2,1)}, u32[]{:S(2)}, u32[]{:S(2)}) collective-permute-start(bf16[6144,256]{1,0:T(8,128)(2,1)} %gate.1), channel_id=1, source_target_pairs={{0,1},{1,0},{2,3},{3,2},{4,5},{5,4},{6,7},{7,6},{8,9},{9,8},{10,11... | collective-permute-start | bytes 9437192 | tf_op jit(solution)/shard_map/ppermute | solution.py:59
  1.4 18.6 %collective-permute-start.5 = (bf16[6144,256]{1,0:T(8,128)(2,1)}, bf16[6144,256]{1,0:T(8,128)(2,1)}, u32[]{:S(2)}, u32[]{:S(2)}) collective-permute-start(bf16[6144,256]{1,0:T(8,128)(2,1)} %up.1), channel_id=1, source_target_pairs={{0,1},{1,0},{2,3},{3,2},{4,5},{5,4},{6,7},{7,6},{8,9},{9,8},{10,11... | collective-permute-start | bytes 9437192 | tf_op jit(solution)/shard_map/ppermute | solution.py:59
  1.4 7.0 %copy-start.5 = (s32[64,2]{0,1:T(2,128)S(1)}, s32[64,2]{0,1:T(2,128)}, u32[]{:S(2)}) copy-start(s32[64,2]{0,1:T(2,128)} %param.21) | copy-start | bytes 1540
  7.8 4.0 %collective-permute-start = (bf16[4,64,768]{2,1,0:T(8,128)(2,1)S(1)}, bf16[4,64,768]{2,1,0:T(8,128)(2,1)S(1)}, u32[]{:S(2)}, u32[]{:S(2)}) collective-permute-start(bf16[4,64,768]{2,1,0:T(8,128)(2,1)S(1)} %get-tuple-element.41), channel_id=1, source_target_pairs={{0,1},{1,0},{2,3},{3,2},{4,5},{5,4},{6,7},{7,6},{8,9},{9,8},{10,11... | collective-permute-start | bytes 1179656 | tf_op jit(solution)/shard_map/ppermute | solution.py:59
  8.5 7.2 %copy-start.4 = (bf16[6144]{0:T(1024)(128)(2,1)S(1)}, bf16[6144]{0:T(1024)(128)(2,1)}, u32[]{:S(2)}) copy-start(bf16[6144]{0:T(1024)(128)(2,1)} %param.23) | copy-start | bytes 36868
  11.8 5.3 %collective-permute-start.1 = (bf16[64,768]{1,0:T(8,128)(2,1)S(1)}, bf16[64,768]{1,0:T(8,128)(2,1)S(1)}, u32[]{:S(2)}, u32[]{:S(2)}) collective-permute-start(bf16[64,768]{1,0:T(8,128)(2,1)S(1)} %get-tuple-element.43), channel_id=1, source_target_pairs={{0,2},{2,0},{4,6},{6,4},{1,3},{3,1},{5,7},{7,5},{8,10},{10,8},{12,... | collective-permute-start | bytes 294920 | tf_op jit(solution)/shard_map/ppermute | solution.py:55
  13.2 5.0 %collective-permute-start.2 = (bf16[64,768]{1,0:T(8,128)(2,1)S(1)}, bf16[64,768]{1,0:T(8,128)(2,1)S(1)}, u32[]{:S(2)}, u32[]{:S(2)}) collective-permute-start(bf16[64,768]{1,0:T(8,128)(2,1)S(1)} %get-tuple-element.44), channel_id=1, source_target_pairs={{0,6},{2,4},{4,2},{6,0},{1,7},{3,5},{5,3},{7,1},{8,14},{10,12},{12... | collective-permute-start | bytes 294920 | tf_op jit(solution)/shard_map/ppermute | solution.py:55
  15.0 5.0 %collective-permute-start.3 = (bf16[64,768]{1,0:T(8,128)(2,1)S(1)}, bf16[64,768]{1,0:T(8,128)(2,1)S(1)}, u32[]{:S(2)}, u32[]{:S(2)}) collective-permute-start(bf16[64,768]{1,0:T(8,128)(2,1)S(1)} %get-tuple-element.45), channel_id=1, source_target_pairs={{0,4},{2,6},{4,0},{6,2},{1,5},{3,7},{5,1},{7,3},{8,12},{10,14},{12... | collective-permute-start | bytes 294920 | tf_op jit(solution)/shard_map/ppermute | solution.py:55
  15.7 4.4 %copy-start.3 = (bf16[64,768]{1,0:T(8,128)(2,1)S(1)}, bf16[64,768]{1,0:T(8,128)(2,1)}, u32[]{:S(2)}) copy-start(bf16[64,768]{1,0:T(8,128)(2,1)} %tokens.1) | copy-start | bytes 294916
  17.2 30.8 %collective-permute-start.15 = (bf16[4,256,768]{2,1,0:T(8,128)(2,1)S(1)}, bf16[4,256,768]{2,1,0:T(8,128)(2,1)}, u32[]{:S(2)}, u32[]{:S(2)}) collective-permute-start(bf16[4,256,768]{2,1,0:T(8,128)(2,1)S(1)} %get-tuple-element.54), channel_id=1, source_target_pairs={{0,1},{1,0},{2,3},{3,2},{4,5},{5,4},{6,7},{7,6},{8,9},{9,8},{10,11... | collective-permute-start | bytes 4718600 | tf_op jit(solution)/shard_map/ppermute | solution.py:59
  20.4 5.0 %collective-permute-start.6 = (bf16[40,768]{1,0:T(8,128)(2,1)S(1)}, bf16[40,768]{1,0:T(8,128)(2,1)S(1)}, u32[]{:S(2)}, u32[]{:S(2)}) collective-permute-start(bf16[40,768]{1,0:T(8,128)(2,1)S(1)} %get-tuple-element.51), channel_id=1, source_target_pairs={{0,32},{32,0},{64,96},{96,64},{1,33},{33,1},{65,97},{97,65},{2,34}... | collective-permute-start | bytes 184328 | tf_op jit(solution)/shard_map/ppermute | solution.py:51
  22.1 4.3 %collective-permute-start.7 = (bf16[40,768]{1,0:T(8,128)(2,1)S(1)}, bf16[40,768]{1,0:T(8,128)(2,1)S(1)}, u32[]{:S(2)}, u32[]{:S(2)}) collective-permute-start(bf16[40,768]{1,0:T(8,128)(2,1)S(1)} %get-tuple-element.52), channel_id=1, source_target_pairs={{0,96},{32,64},{64,32},{96,0},{1,97},{33,65},{65,33},{97,1},{2,98}... | collective-permute-start | bytes 184328 | tf_op jit(solution)/shard_map/ppermute | solution.py:51
  24.3 4.7 %collective-permute-start.8 = (bf16[40,768]{1,0:T(8,128)(2,1)S(1)}, bf16[40,768]{1,0:T(8,128)(2,1)S(1)}, u32[]{:S(2)}, u32[]{:S(2)}) collective-permute-start(bf16[40,768]{1,0:T(8,128)(2,1)S(1)} %get-tuple-element.53), channel_id=1, source_target_pairs={{0,64},{32,96},{64,0},{96,32},{1,65},{33,97},{65,1},{97,33},{2,66}... | collective-permute-start | bytes 184328 | tf_op jit(solution)/shard_map/ppermute | solution.py:51
  29.1 8.5 %collective-permute-start.10 = (bf16[160,768]{1,0:T(8,128)(2,1)S(1)}, bf16[160,768]{1,0:T(8,128)(2,1)S(1)}, u32[]{:S(2)}, u32[]{:S(2)}) collective-permute-start(bf16[160,768]{1,0:T(8,128)(2,1)S(1)} %constant_dynamic-update-slice_fusion.a), channel_id=1, source_target_pairs={{0,6},{1,25},{2,4},{3,27},{4,2},{5,29},{6,0},{7,31},{8,14},{9,17},... | collective-permute-start | bytes 737288 | tf_op jit(solution)/shard_map/ppermute | solution.py:43
  31.8 6.6 %collective-permute-start.11 = (bf16[160,768]{1,0:T(8,128)(2,1)S(1)}, bf16[160,768]{1,0:T(8,128)(2,1)S(1)}, u32[]{:S(2)}, u32[]{:S(2)}) collective-permute-start(bf16[160,768]{1,0:T(8,128)(2,1)S(1)} %constant_dynamic-update-slice_fusion.a), channel_id=1, source_target_pairs={{0,4},{1,17},{2,6},{3,19},{4,0},{5,21},{6,2},{7,23},{8,12},{9,25},... | collective-permute-start | bytes 737288 | tf_op jit(solution)/shard_map/ppermute | solution.py:43
  32.1 6.9 %collective-permute-start.9 = (bf16[160,768]{1,0:T(8,128)(2,1)S(1)}, bf16[160,768]{1,0:T(8,128)(2,1)S(1)}, u32[]{:S(2)}, u32[]{:S(2)}) collective-permute-start(bf16[160,768]{1,0:T(8,128)(2,1)S(1)} %constant_dynamic-update-slice_fusion.a), channel_id=1, source_target_pairs={{0,2},{1,9},{2,0},{3,11},{4,6},{5,13},{6,4},{7,15},{8,10},{9,1},{1... | collective-permute-start | bytes 737288 | tf_op jit(solution)/shard_map/ppermute | solution.py:43
  39.0 5.4 %collective-permute-start.12 = (f32[16,128]{1,0:T(8,128)S(1)}, f32[16,128]{1,0:T(8,128)S(1)}, u32[]{:S(2)}, u32[]{:S(2)}) collective-permute-start(f32[16,128]{1,0:T(8,128)S(1)} %convert_add_fusion), channel_id=1, source_target_pairs={{0,1},{1,0},{2,3},{3,2},{4,5},{5,4},{6,7},{7,6},{8,9},{9,8},{10,11... | collective-permute-start | bytes 24584 | tf_op jit(solution)/shard_map/ppermute | solution.py:59
  44.5 7.5 %copy-start.2 = (bf16[640,768]{1,0:T(8,128)(2,1)}, bf16[640,768]{1,0:T(8,128)(2,1)S(1)}, u32[]{:S(2)}) copy-start(bf16[640,768]{1,0:T(8,128)(2,1)S(1)} %shard_map.141.p0) | copy-start | bytes 2949124
  44.5 15.0 %collective-permute-start.16 = (bf16[640,768]{1,0:T(8,128)(2,1)S(1)}, bf16[640,768]{1,0:T(8,128)(2,1)}, u32[]{:S(2)}, u32[]{:S(2)}) collective-permute-start(bf16[640,768]{1,0:T(8,128)(2,1)S(1)} %shard_map.141.p0), channel_id=1, source_target_pairs={{0,16},{1,5},{2,18},{3,7},{4,20},{5,1},{6,22},{7,3},{8,24},{9,13},... | collective-permute-start | bytes 2949128 | tf_op jit(solution)/shard_map/ppermute | solution.py:47
  45.5 23.6 %collective-permute-start.13 = (bf16[640,768]{1,0:T(8,128)(2,1)S(1)}, bf16[640,768]{1,0:T(8,128)(2,1)}, u32[]{:S(2)}, u32[]{:S(2)}) collective-permute-start(bf16[640,768]{1,0:T(8,128)(2,1)S(1)} %shard_map.141.p0), channel_id=1, source_target_pairs={{0,8},{1,3},{2,10},{3,1},{4,12},{5,7},{6,14},{7,5},{8,0},{9,11},{1... | collective-permute-start | bytes 2949128 | tf_op jit(solution)/shard_map/ppermute | solution.py:47
  46.7 23.3 %collective-permute-start.14 = (bf16[640,768]{1,0:T(8,128)(2,1)S(1)}, bf16[640,768]{1,0:T(8,128)(2,1)}, u32[]{:S(2)}, u32[]{:S(2)}) collective-permute-start(bf16[640,768]{1,0:T(8,128)(2,1)S(1)} %shard_map.141.p0), channel_id=1, source_target_pairs={{0,24},{1,7},{2,26},{3,5},{4,28},{5,3},{6,30},{7,1},{8,16},{9,15},... | collective-permute-start | bytes 2949128 | tf_op jit(solution)/shard_map/ppermute | solution.py:47
  73.1 4.3 %collective-permute-start.17 = (bf16[640,768]{1,0:T(8,128)(2,1)S(1)}, bf16[640,768]{1,0:T(8,128)(2,1)S(1)}, u32[]{:S(2)}, u32[]{:S(2)}) collective-permute-start(bf16[640,768]{1,0:T(8,128)(2,1)S(1)} %get-tuple-element.60), channel_id=1, source_target_pairs={{0,1},{1,0},{2,3},{3,2},{4,5},{5,4},{6,7},{7,6},{8,9},{9,8},{10,11... | collective-permute-start | bytes 2949128 | tf_op jit(solution)/shard_map/ppermute | solution.py:59
  77.9 1.7 %collective-permute-start.18 = (bf16[640,256]{1,0:T(8,128)(2,1)S(1)}, bf16[640,256]{1,0:T(8,128)(2,1)S(1)}, u32[]{:S(2)}, u32[]{:S(2)}) collective-permute-start(bf16[640,256]{1,0:T(8,128)(2,1)S(1)} %get-tuple-element.61.act), channel_id=1, source_target_pairs={{0,1},{1,0},{2,3},{3,2},{4,5},{5,4},{6,7},{7,6},{8,9},{9,8},{10,11... | collective-permute-start | bytes 983048 | tf_op jit(solution)/shard_map/ppermute | solution.py:59
  80.1 12.2 %collective-permute-start.22 = (bf16[480,768]{1,0:T(8,128)(2,1)S(1)}, bf16[480,768]{1,0:T(8,128)(2,1)S(1)}, u32[]{:S(2)}, u32[]{:S(2)}) collective-permute-start(bf16[480,768]{1,0:T(8,128)(2,1)S(1)} %shard_map.148), channel_id=1, source_target_pairs={{0,16},{1,5},{2,18},{3,7},{4,20},{5,1},{6,22},{7,3},{8,24},{9,13},... | collective-permute-start | bytes 2211848 | tf_op jit(solution)/shard_map/ppermute | solution.py:47
  82.1 17.3 %collective-permute-start.23 = (bf16[480,768]{1,0:T(8,128)(2,1)S(1)}, bf16[480,768]{1,0:T(8,128)(2,1)S(1)}, u32[]{:S(2)}, u32[]{:S(2)}) collective-permute-start(bf16[480,768]{1,0:T(8,128)(2,1)S(1)} %get-tuple-element.69), channel_id=1, source_target_pairs={{0,8},{1,3},{2,10},{3,1},{4,12},{5,7},{6,14},{7,5},{8,0},{9,11},{1... | collective-permute-start | bytes 2211848 | tf_op jit(solution)/shard_map/ppermute | solution.py:47
  83.4 16.9 %collective-permute-start.24 = (bf16[480,768]{1,0:T(8,128)(2,1)S(1)}, bf16[480,768]{1,0:T(8,128)(2,1)S(1)}, u32[]{:S(2)}, u32[]{:S(2)}) collective-permute-start(bf16[480,768]{1,0:T(8,128)(2,1)S(1)} %get-tuple-element.70), channel_id=1, source_target_pairs={{0,24},{1,7},{2,26},{3,5},{4,28},{5,3},{6,30},{7,1},{8,16},{9,15},... | collective-permute-start | bytes 2211848 | tf_op jit(solution)/shard_map/ppermute | solution.py:47
  85.6 17.7 %collective-permute-start.19 = (bf16[160,768]{1,0:T(8,128)(2,1)S(1)}, bf16[160,768]{1,0:T(8,128)(2,1)S(1)}, u32[]{:S(2)}, u32[]{:S(2)}) collective-permute-start(bf16[160,768]{1,0:T(8,128)(2,1)S(1)} %get-tuple-element.65), channel_id=1, source_target_pairs={{0,16},{1,5},{2,18},{3,7},{4,20},{5,1},{6,22},{7,3},{8,24},{9,13},... | collective-permute-start | bytes 737288 | tf_op jit(solution)/shard_map/ppermute | solution.py:47
  86.6 18.6 %collective-permute-start.20 = (bf16[160,768]{1,0:T(8,128)(2,1)S(1)}, bf16[160,768]{1,0:T(8,128)(2,1)S(1)}, u32[]{:S(2)}, u32[]{:S(2)}) collective-permute-start(bf16[160,768]{1,0:T(8,128)(2,1)S(1)} %get-tuple-element.66), channel_id=1, source_target_pairs={{0,8},{1,3},{2,10},{3,1},{4,12},{5,7},{6,14},{7,5},{8,0},{9,11},{1... | collective-permute-start | bytes 737288 | tf_op jit(solution)/shard_map/ppermute | solution.py:47
  92.4 13.1 %collective-permute-start.21 = (bf16[160,768]{1,0:T(8,128)(2,1)S(1)}, bf16[160,768]{1,0:T(8,128)(2,1)S(1)}, u32[]{:S(2)}, u32[]{:S(2)}) collective-permute-start(bf16[160,768]{1,0:T(8,128)(2,1)S(1)} %get-tuple-element.67), channel_id=1, source_target_pairs={{0,24},{1,7},{2,26},{3,5},{4,28},{5,3},{6,30},{7,1},{8,16},{9,15},... | collective-permute-start | bytes 737288 | tf_op jit(solution)/shard_map/ppermute | solution.py:47
  100.6 18.3 %copy-start.1 = (f32[6144,4]{0,1:T(4,128)S(1)}, f32[6144,4]{0,1:T(4,128)}, u32[]{:S(2)}) copy-start(f32[6144,4]{0,1:T(4,128)} %param.24) | copy-start | bytes 294916
  100.7 8.1 %collective-permute-start.25 = (bf16[160,768]{1,0:T(8,128)(2,1)S(1)}, bf16[160,768]{1,0:T(8,128)(2,1)S(1)}, u32[]{:S(2)}, u32[]{:S(2)}) collective-permute-start(bf16[160,768]{1,0:T(8,128)(2,1)S(1)} %get-tuple-element.77), channel_id=1, source_target_pairs={{0,2},{1,9},{2,0},{3,11},{4,6},{5,13},{6,4},{7,15},{8,10},{9,1},{1... | collective-permute-start | bytes 737288 | tf_op jit(solution)/shard_map/ppermute | solution.py:43
  101.6 7.2 %collective-permute-start.26 = (bf16[160,768]{1,0:T(8,128)(2,1)S(1)}, bf16[160,768]{1,0:T(8,128)(2,1)S(1)}, u32[]{:S(2)}, u32[]{:S(2)}) collective-permute-start(bf16[160,768]{1,0:T(8,128)(2,1)S(1)} %get-tuple-element.76), channel_id=1, source_target_pairs={{0,6},{1,25},{2,4},{3,27},{4,2},{5,29},{6,0},{7,31},{8,14},{9,17},... | collective-permute-start | bytes 737288 | tf_op jit(solution)/shard_map/ppermute | solution.py:43
  103.3 8.2 %collective-permute-start.27 = (bf16[160,768]{1,0:T(8,128)(2,1)S(1)}, bf16[160,768]{1,0:T(8,128)(2,1)S(1)}, u32[]{:S(2)}, u32[]{:S(2)}) collective-permute-start(bf16[160,768]{1,0:T(8,128)(2,1)S(1)} %get-tuple-element.75), channel_id=1, source_target_pairs={{0,4},{1,17},{2,6},{3,19},{4,0},{5,21},{6,2},{7,23},{8,12},{9,25},... | collective-permute-start | bytes 737288 | tf_op jit(solution)/shard_map/ppermute | solution.py:43
  111.7 3.3 %collective-permute-start.28 = (bf16[40,896]{1,0:T(8,128)(2,1)S(1)}, bf16[40,896]{1,0:T(8,128)(2,1)S(1)}, u32[]{:S(2)}, u32[]{:S(2)}) collective-permute-start(bf16[40,896]{1,0:T(8,128)(2,1)S(1)} %get-tuple-element.72), channel_id=1, source_target_pairs={{0,32},{32,0},{64,96},{96,64},{1,33},{33,1},{65,97},{97,65},{2,34}... | collective-permute-start | bytes 215048 | tf_op jit(solution)/shard_map/ppermute | solution.py:51
  112.5 5.2 %collective-permute-start.29 = (bf16[40,896]{1,0:T(8,128)(2,1)S(1)}, bf16[40,896]{1,0:T(8,128)(2,1)S(1)}, u32[]{:S(2)}, u32[]{:S(2)}) collective-permute-start(bf16[40,896]{1,0:T(8,128)(2,1)S(1)} %get-tuple-element.73), channel_id=1, source_target_pairs={{0,96},{32,64},{64,32},{96,0},{1,97},{33,65},{65,33},{97,1},{2,98}... | collective-permute-start | bytes 215048 | tf_op jit(solution)/shard_map/ppermute | solution.py:51
  112.9 4.8 %collective-permute-start.30 = (bf16[40,896]{1,0:T(8,128)(2,1)S(1)}, bf16[40,896]{1,0:T(8,128)(2,1)S(1)}, u32[]{:S(2)}, u32[]{:S(2)}) collective-permute-start(bf16[40,896]{1,0:T(8,128)(2,1)S(1)} %get-tuple-element.74), channel_id=1, source_target_pairs={{0,64},{32,96},{64,0},{96,32},{1,65},{33,97},{65,1},{97,33},{2,66}... | collective-permute-start | bytes 215048 | tf_op jit(solution)/shard_map/ppermute | solution.py:51

commit v7 on v6

--- a/solution.py
+++ b/solution.py
@@ -81,7 +81,7 @@
 
 def attend_kernel(
     given_lengths, given_queries, given_keys, given_values, keys, values, weight, far, joined,
-    lengths, queries, new_keys, new_values, key_here, value_here, weight_here, query_here, score, context, sems,
+    lengths, queries, new_keys, new_values, new_key_rows, new_value_rows, key_here, value_here, weight_here, query_here, score, context, sems,
 ):
     small = [
         pltpu.make_async_copy(source, target, sems.at[16 + n])
@@ -118,6 +118,8 @@
     for one in small:
         one.wait()
     query_here[heads * rows :, :] = jnp.zeros(((8 - heads) * rows, size), jnp.float32)
+    new_key_rows[...] = new_keys[...].astype(jnp.float32)
+    new_value_rows[...] = new_values[...].astype(jnp.float32)
     for head in range(heads):
         query_here[head * rows : (head + 1) * rows, :] = queries[head].astype(jnp.float32)
 
@@ -140,8 +142,7 @@
         start(12)
         for t in range(n * chunk, (n + 1) * chunk):
             query = query_here[pl.ds(t, 8, stride=rows), :]
-            new_key = new_keys[t : t + 1, :].astype(jnp.float32)
-            mine = scale * jnp.sum(query * new_key, axis=1, keepdims=True)
+            mine = scale * jnp.sum(query * new_key_rows[t : t + 1, :], axis=1, keepdims=True)
             scores = score[row(t), :]
             valid = slot < lengths[t]
             top = jnp.maximum(jnp.max(jnp.where(valid, scores, -jnp.inf), axis=1, keepdims=True), mine)
@@ -150,8 +151,7 @@
             total = jnp.sum(weights, axis=1, keepdims=True) + own_weight
             probs = (weights / total).astype(jnp.bfloat16)
             own_prob = (own_weight / total).astype(jnp.bfloat16).astype(jnp.float32)
-            new_value = new_values[t : t + 1, :].astype(jnp.float32)
-            context[row(t), :] = dot(probs, value_here[t]) + own_prob * new_value
+            context[row(t), :] = dot(probs, value_here[t]) + own_prob * new_value_rows[t : t + 1, :]
     for head in range(heads):
         joined[:, head * size : (head + 1) * size] = context[pl.ds(head, rows, stride=8), :].astype(
             jnp.bfloat16
@@ -177,6 +177,8 @@
             pltpu.VMEM((heads, rows, size), jnp.bfloat16),
             pltpu.VMEM((rows, size), jnp.bfloat16),
             pltpu.VMEM((rows, size), jnp.bfloat16),
+            pltpu.VMEM((rows, size), jnp.float32),
+            pltpu.VMEM((rows, size), jnp.float32),
             pltpu.VMEM((rows, length, size), jnp.bfloat16),
             pltpu.VMEM((rows, length, size), jnp.bfloat16),
             pltpu.VMEM((4, BLK, BLK), jnp.bfloat16),

time: 120 us -> 120 us (level)
  no operation moved by 1% of the time
where the time goes in v7:
time: 120 us; the launch traced here: 119 us
  waiting for transfers between devices  48.9 us (41%)
  starting transfers between devices  39.5 us (33%)
  Pallas kernels  29.5 us (25%)
    ppermute x9, waiting for transfers between devices, along_second(): return lax.ppermute(a, AXES, plane_pairs(False, shift))  25.3 us
    ppermute x6, waiting for transfers between devices, along_first(): return lax.ppermute(a, AXES, plane_pairs(True, shift))  12.5 us
    ppermute x9, starting transfers between devices, along_second(): return lax.ppermute(a, AXES, plane_pairs(False, shift))  10.5 us
    ppermute x7, starting transfers between devices, swap_cores(): return lax.ppermute(a, 'c', [(0, 1), (1, 0)])  8.89 us
    ppermute x6, starting transfers between devices, along_z(): return lax.ppermute(a, 'z', [(i, i ^ shift) for i in range(4)])  8.36 us
    ppermute x6, starting transfers between devices, along_first(): return lax.ppermute(a, AXES, plane_pairs(True, shift))  7.94 us
    pallas_call x1, Pallas kernels, attend(): pl.pallas_call(attend_kernel, out_shape=(pltpu.VMEM((4, rows, BLK), jnp.b...  6.35 us
    ppermute x6, waiting for transfers between devices, along_z(): return lax.ppermute(a, 'z', [(i, i ^ shift) for i in range(4)])  6.28 us
  transfers between devices with their start and end apart: 31, of which 19 were waited for; matrix products, arithmetic and copies ran while one was open for 1% of the time, Pallas kernels for 20%

profile of v7, /device:TPU:1, one launch (start us, length us, event | category | flops | bytes accessed | tf_op | source)
XLA Modules:
  0.0 118.9 jit_solution(11144436439187614034)
XLA Ops:
  0.0 1.4 %collective-permute-start.4 = (bf16[6144,256]{1,0:T(8,128)(2,1)}, bf16[6144,256]{1,0:T(8,128)(2,1)}, u32[]{:S(2)}, u32[]{:S(2)}) collective-permute-start(bf16[6144,256]{1,0:T(8,128)(2,1)} %gate.1), channel_id=1, source_target_pairs={{0,1},{1,0},{2,3},{3,2},{4,5},{5,4},{6,7},{7,6},{8,9},{9,8},{10,11... | collective-permute-start | bytes 9437192 | tf_op jit(solution)/shard_map/ppermute | solution.py:59
  1.4 6.4 %shard_map.136 = (bf16[4,64,768]{2,1,0:T(8,128)(2,1)S(1)}, bf16[64,768]{1,0:T(8,128)(2,1)S(1)}) custom-call(s32[64]{0:T(128)} %given_lengths.1, bf16[6,64,128]{2,1,0:T(8,128)(2,1)} %bitcast.7, bf16[64,128]{1,0:T(8,128)(2,1)} %bitcast.8, bf16[64,128]{1,0:T(8,128)(2,1)} %bitcast.9, bf16[64,128,128]{2,1,0:T(8,128)(2,1)} %bitcast.5, ...), custom_call_target="tpu_custom_call" | custom-call | flops 603979776 | bytes 14000000 | tf_op jit(solution)/shard_map/pallas_call | solution.py:167
  7.8 0.6 collective-permute-start
  8.4 0.1 copy.15.routes
  8.5 2.8 %shard_map.137.own = f32[4,64,768]{2,1,0:T(8,128)S(1)} custom-call(bf16[64,768]{1,0:T(8,128)(2,1)S(1)} %get-tuple-element.40.context, bf16[768,6144]{1,0:T(8,128)(2,1)} %weight.3), custom_call_target="tpu_custom_call" | custom-call | flops 301989888 | bytes 5000000 | tf_op jit(solution)/shard_map/pallas_call | solution.py:222
  11.3 0.5 collective-permute-done.far
  11.8 1.4 %collective-permute-start.1 = (bf16[64,768]{1,0:T(8,128)(2,1)S(1)}, bf16[64,768]{1,0:T(8,128)(2,1)S(1)}, u32[]{:S(2)}, u32[]{:S(2)}) collective-permute-start(bf16[64,768]{1,0:T(8,128)(2,1)S(1)} %get-tuple-element.43), channel_id=1, source_target_pairs={{0,2},{2,0},{4,6},{6,4},{1,3},{3,1},{5,7},{7,5},{8,10},{10,8},{12,... | collective-permute-start | bytes 294920 | tf_op jit(solution)/shard_map/ppermute | solution.py:55
  13.2 1.8 %collective-permute-start.2 = (bf16[64,768]{1,0:T(8,128)(2,1)S(1)}, bf16[64,768]{1,0:T(8,128)(2,1)S(1)}, u32[]{:S(2)}, u32[]{:S(2)}) collective-permute-start(bf16[64,768]{1,0:T(8,128)(2,1)S(1)} %get-tuple-element.44), channel_id=1, source_target_pairs={{0,6},{2,4},{4,2},{6,0},{1,7},{3,5},{5,3},{7,1},{8,14},{10,12},{12... | collective-permute-start | bytes 294920 | tf_op jit(solution)/shard_map/ppermute | solution.py:55
  15.0 0.6 collective-permute-start.3
  15.7 1.4 %shard_map.139 = (bf16[4,64,40]{2,1,0:T(8,128)(2,1)S(1)}, bf16[4,64,40]{2,1,0:T(8,128)(2,1)S(1)}, bf16[4,256,768]{2,1,0:T(8,128)(2,1)S(1)}) custom-call(s32[64,2]{1,0:T(8,128)S(1)} %get-tuple-element.46.routes, bf16[256,6144]{1,0:T(8,128)(2,1)} %down.3), custom_call_target="tpu_custom_call" | custom-call | tf_op jit(solution)/shard_map/pallas_call | solution.py:284
  17.2 1.0 collective-permute-start.15
  18.2 1.9 %collective-permute-done.3.two = bf16[64,768]{1,0:T(8,128)(2,1)S(1)} collective-permute-done((bf16[64,768]{1,0:T(8,128)(2,1)S(1)}, bf16[64,768]{1,0:T(8,128)(2,1)S(1)}, u32[]{:S(2)}, u32[]{:S(2)}) %collective-permute-start.3) | collective-permute-done | bytes 98336 | tf_op jit(solution)/shard_map/ppermute | solution.py:55
  20.1 0.3 shard_map.140
  20.4 1.7 %collective-permute-start.6 = (bf16[40,768]{1,0:T(8,128)(2,1)S(1)}, bf16[40,768]{1,0:T(8,128)(2,1)S(1)}, u32[]{:S(2)}, u32[]{:S(2)}) collective-permute-start(bf16[40,768]{1,0:T(8,128)(2,1)S(1)} %get-tuple-element.51), channel_id=1, source_target_pairs={{0,32},{32,0},{64,96},{96,64},{1,33},{33,1},{65,97},{97,65},{2,34}... | collective-permute-start | bytes 184328 | tf_op jit(solution)/shard_map/ppermute | solution.py:51
  22.1 2.2 %collective-permute-start.7 = (bf16[40,768]{1,0:T(8,128)(2,1)S(1)}, bf16[40,768]{1,0:T(8,128)(2,1)S(1)}, u32[]{:S(2)}, u32[]{:S(2)}) collective-permute-start(bf16[40,768]{1,0:T(8,128)(2,1)S(1)} %get-tuple-element.52), channel_id=1, source_target_pairs={{0,96},{32,64},{64,32},{96,0},{1,97},{33,65},{65,33},{97,1},{2,98}... | collective-permute-start | bytes 184328 | tf_op jit(solution)/shard_map/ppermute | solution.py:51
  24.3 1.1 collective-permute-start.8
  25.4 0.9 collective-permute-done.7
  26.4 2.7 %collective-permute-done.8 = bf16[40,768]{1,0:T(8,128)(2,1)S(1)} collective-permute-done((bf16[40,768]{1,0:T(8,128)(2,1)S(1)}, bf16[40,768]{1,0:T(8,128)(2,1)S(1)}, u32[]{:S(2)}, u32[]{:S(2)}) %collective-permute-start.8) | collective-permute-done | bytes 61472 | tf_op jit(solution)/shard_map/ppermute | solution.py:51
  29.1 2.7 %collective-permute-start.10 = (bf16[160,768]{1,0:T(8,128)(2,1)S(1)}, bf16[160,768]{1,0:T(8,128)(2,1)S(1)}, u32[]{:S(2)}, u32[]{:S(2)}) collective-permute-start(bf16[160,768]{1,0:T(8,128)(2,1)S(1)} %constant_dynamic-update-slice_fusion.a), channel_id=1, source_target_pairs={{0,6},{1,25},{2,4},{3,27},{4,2},{5,29},{6,0},{7,31},{8,14},{9,17},... | collective-permute-start | bytes 737288 | tf_op jit(solution)/shard_map/ppermute | solution.py:43
  31.8 0.3 collective-permute-start.11
  32.1 0.3 collective-permute-start.9
  32.5 5.1 %collective-permute-done.10.c = bf16[160,768]{1,0:T(8,128)(2,1)S(1)} collective-permute-done((bf16[160,768]{1,0:T(8,128)(2,1)S(1)}, bf16[160,768]{1,0:T(8,128)(2,1)S(1)}, u32[]{:S(2)}, u32[]{:S(2)}) %collective-permute-start.10) | collective-permute-done | bytes 245792 | tf_op jit(solution)/shard_map/ppermute | solution.py:43
  37.6 0.8 collective-permute-done.11.d
  38.3 0.7 collective-permute-done.9.b
  39.0 4.6 %collective-permute-start.12 = (f32[16,128]{1,0:T(8,128)S(1)}, f32[16,128]{1,0:T(8,128)S(1)}, u32[]{:S(2)}, u32[]{:S(2)}) collective-permute-start(f32[16,128]{1,0:T(8,128)S(1)} %convert_add_fusion), channel_id=1, source_target_pairs={{0,1},{1,0},{2,3},{3,2},{4,5},{5,4},{6,7},{7,6},{8,9},{9,8},{10,11... | collective-permute-start | bytes 24584 | tf_op jit(solution)/shard_map/ppermute | solution.py:59
  43.6 0.8 collective-permute-done.12.token
  44.5 1.0 collective-permute-start.16
  45.5 1.2 collective-permute-start.13
  46.7 1.1 collective-permute-start.14
  48.0 4.0 %shard_map.142 = (bf16[4,4,768,256]{3,2,1,0:T(8,128)(2,1)S(1)}, bf16[2,4,256,768]{3,2,1,0:T(8,128)(2,1)S(1)}) custom-call(bf16[6144,256]{1,0:T(8,128)(2,1)} %collective-permute-done.4.rest_0_.gate_far, bf16[6144,256]{1,0:T(8,128)(2,1)} %collective-permute-done.5.rest_1_.up_far, bf16[6144,256]{1,0:T(8,128)(2,1)} %gate.1, bf16[6144,256]{1,0:T(8,128)(2,1)} %up.1, ...), custom_call_target="tpu_custom_call" | custom-call | bytes 18000000 | tf_op jit(solution)/shard_map/pallas_call | solution.py:389
  52.0 7.5 %collective-permute-done.16.p1 = bf16[640,768]{1,0:T(8,128)(2,1)} collective-permute-done((bf16[640,768]{1,0:T(8,128)(2,1)S(1)}, bf16[640,768]{1,0:T(8,128)(2,1)}, u32[]{:S(2)}, u32[]{:S(2)}) %collective-permute-start.16) | collective-permute-done | bytes 983072 | tf_op jit(solution)/shard_map/ppermute | solution.py:47
  59.5 3.8 %shard_map.143 = (f32[640,512]{1,0:T(8,128)S(1)}, f32[640,256]{1,0:T(8,128)S(1)}, f32[640,512]{1,0:T(8,128)S(1)}) custom-call(bf16[640,768]{1,0:T(8,128)(2,1)} %copy-done.2, bf16[640,768]{1,0:T(8,128)(2,1)} %collective-permute-done.16.p1, bf16[4,4,768,256]{3,2,1,0:T(8,128)(2,1)S(1)} %get-tuple-element.55.weights, f32[8,768]{1,0:T(8,128)S(1)} %broadcast_divide_fusion.inverse, ...), custom_call_target="tpu_custom_call" | custom-call | flops 2013265920 | bytes 5000000 | tf_op jit(solution)/shard_map/pallas_call | solution.py:514
  63.3 5.9 %collective-permute-done.13.p0 = bf16[640,768]{1,0:T(8,128)(2,1)} collective-permute-done((bf16[640,768]{1,0:T(8,128)(2,1)S(1)}, bf16[640,768]{1,0:T(8,128)(2,1)}, u32[]{:S(2)}, u32[]{:S(2)}) %collective-permute-start.13) | collective-permute-done | bytes 983072 | tf_op jit(solution)/shard_map/ppermute | solution.py:47
  69.2 0.8 collective-permute-done.14.p1
  70.0 3.2 %shard_map.145 = (bf16[640,768]{1,0:T(8,128)(2,1)S(1)}, f32[640,256]{1,0:T(8,128)S(1)}) custom-call(bf16[640,768]{1,0:T(8,128)(2,1)} %collective-permute-done.13.p0, bf16[640,768]{1,0:T(8,128)(2,1)} %collective-permute-done.14.p1, bf16[4,4,768,256]{3,2,1,0:T(8,128)(2,1)S(1)} %get-tuple-element.55.weights, f32[8,768]{1,0:T(8,128)S(1)} %broadcast_divide_fusion.inverse, ...), custom_call_target="tpu_custom_call" | custom-call | flops 2013265920 | bytes 5000000 | tf_op jit(solution)/shard_map/pallas_call | solution.py:525
  73.1 1.2 %collective-permute-start.17 = (bf16[640,768]{1,0:T(8,128)(2,1)S(1)}, bf16[640,768]{1,0:T(8,128)(2,1)S(1)}, u32[]{:S(2)}, u32[]{:S(2)}) collective-permute-start(bf16[640,768]{1,0:T(8,128)(2,1)S(1)} %get-tuple-element.60), channel_id=1, source_target_pairs={{0,1},{1,0},{2,3},{3,2},{4,5},{5,4},{6,7},{7,6},{8,9},{9,8},{10,11... | collective-permute-start | bytes 2949128 | tf_op jit(solution)/shard_map/ppermute | solution.py:59
  74.3 3.1 %shard_map.144.own = f32[640,512]{1,0:T(8,128)S(1)} custom-call(bf16[640,768]{1,0:T(8,128)(2,1)} %collective-permute-done.13.p0, bf16[640,768]{1,0:T(8,128)(2,1)} %collective-permute-done.14.p1, bf16[4,4,768,256]{3,2,1,0:T(8,128)(2,1)S(1)} %get-tuple-element.55.weights, f32[640,512]{1,0:T(8,128)S(1)} %get-tuple-element.56.own_first), custom_call_target="tpu_custom_call" | custom-call | flops 2013265920 | bytes 5000000 | tf_op jit(solution)/shard_map/pallas_call | solution.py:534
  77.5 0.4 shard_map.146
  78.0 1.6 %collective-permute-done.18.act_far = bf16[640,256]{1,0:T(8,128)(2,1)S(1)} collective-permute-done((bf16[640,256]{1,0:T(8,128)(2,1)S(1)}, bf16[640,256]{1,0:T(8,128)(2,1)S(1)}, u32[]{:S(2)}, u32[]{:S(2)}) %collective-permute-start.18) | collective-permute-done | bytes 327712 | tf_op jit(solution)/shard_map/ppermute | solution.py:59
  79.6 0.5 shard_map.148
  80.1 1.0 collective-permute-start.22
  81.2 0.9 shard_map.149
  82.1 1.2 %collective-permute-start.23 = (bf16[480,768]{1,0:T(8,128)(2,1)S(1)}, bf16[480,768]{1,0:T(8,128)(2,1)S(1)}, u32[]{:S(2)}, u32[]{:S(2)}) collective-permute-start(bf16[480,768]{1,0:T(8,128)(2,1)S(1)} %get-tuple-element.69), channel_id=1, source_target_pairs={{0,8},{1,3},{2,10},{3,1},{4,12},{5,7},{6,14},{7,5},{8,0},{9,11},{1... | collective-permute-start | bytes 2211848 | tf_op jit(solution)/shard_map/ppermute | solution.py:47
  83.4 1.1 collective-permute-start.24
  84.5 1.1 shard_map.147
  85.6 1.0 collective-permute-start.19
  86.6 1.2 collective-permute-start.20
  87.8 4.6 %collective-permute-done.22 = bf16[480,768]{1,0:T(8,128)(2,1)S(1)} collective-permute-done((bf16[480,768]{1,0:T(8,128)(2,1)S(1)}, bf16[480,768]{1,0:T(8,128)(2,1)S(1)}, u32[]{:S(2)}, u32[]{:S(2)}) %collective-permute-start.22) | collective-permute-done | bytes 737312 | tf_op jit(solution)/shard_map/ppermute | solution.py:47
  92.4 1.5 %collective-permute-start.21 = (bf16[160,768]{1,0:T(8,128)(2,1)S(1)}, bf16[160,768]{1,0:T(8,128)(2,1)S(1)}, u32[]{:S(2)}, u32[]{:S(2)}) collective-permute-start(bf16[160,768]{1,0:T(8,128)(2,1)S(1)} %get-tuple-element.67), channel_id=1, source_target_pairs={{0,24},{1,7},{2,26},{3,5},{4,28},{5,3},{6,30},{7,1},{8,16},{9,15},... | collective-permute-start | bytes 737288 | tf_op jit(solution)/shard_map/ppermute | solution.py:47
  93.9 5.5 %collective-permute-done.23 = bf16[480,768]{1,0:T(8,128)(2,1)S(1)} collective-permute-done((bf16[480,768]{1,0:T(8,128)(2,1)S(1)}, bf16[480,768]{1,0:T(8,128)(2,1)S(1)}, u32[]{:S(2)}, u32[]{:S(2)}) %collective-permute-start.23) | collective-permute-done | bytes 737312 | tf_op jit(solution)/shard_map/ppermute | solution.py:47
  99.4 0.8 collective-permute-done.24
  100.2 0.4 add_convert_fusion
  100.7 0.9 collective-permute-start.25
  101.6 1.7 %collective-permute-start.26 = (bf16[160,768]{1,0:T(8,128)(2,1)S(1)}, bf16[160,768]{1,0:T(8,128)(2,1)S(1)}, u32[]{:S(2)}, u32[]{:S(2)}) collective-permute-start(bf16[160,768]{1,0:T(8,128)(2,1)S(1)} %get-tuple-element.76), channel_id=1, source_target_pairs={{0,6},{1,25},{2,4},{3,27},{4,2},{5,29},{6,0},{7,31},{8,14},{9,17},... | collective-permute-start | bytes 737288 | tf_op jit(solution)/shard_map/ppermute | solution.py:43
  103.3 1.9 %collective-permute-start.27 = (bf16[160,768]{1,0:T(8,128)(2,1)S(1)}, bf16[160,768]{1,0:T(8,128)(2,1)S(1)}, u32[]{:S(2)}, u32[]{:S(2)}) collective-permute-start(bf16[160,768]{1,0:T(8,128)(2,1)S(1)} %get-tuple-element.75), channel_id=1, source_target_pairs={{0,4},{1,17},{2,6},{3,19},{4,0},{5,21},{6,2},{7,23},{8,12},{9,25},... | collective-permute-start | bytes 737288 | tf_op jit(solution)/shard_map/ppermute | solution.py:43
  105.3 0.2 collective-permute-done.21.rest_2_
  105.5 3.3 %collective-permute-done.25.rest_3_ = bf16[160,768]{1,0:T(8,128)(2,1)S(1)} collective-permute-done((bf16[160,768]{1,0:T(8,128)(2,1)S(1)}, bf16[160,768]{1,0:T(8,128)(2,1)S(1)}, u32[]{:S(2)}, u32[]{:S(2)}) %collective-permute-start.25) | collective-permute-done | bytes 245792 | tf_op jit(solution)/shard_map/ppermute | solution.py:43
  108.8 2.7 %collective-permute-done.27.rest_5_ = bf16[160,768]{1,0:T(8,128)(2,1)S(1)} collective-permute-done((bf16[160,768]{1,0:T(8,128)(2,1)S(1)}, bf16[160,768]{1,0:T(8,128)(2,1)S(1)}, u32[]{:S(2)}, u32[]{:S(2)}) %collective-permute-start.27) | collective-permute-done | bytes 245792 | tf_op jit(solution)/shard_map/ppermute | solution.py:43
  111.5 0.2 shard_map.150
  111.7 0.8 collective-permute-start.28
  112.5 0.3 collective-permute-start.29
  112.9 2.2 %collective-permute-start.30 = (bf16[40,896]{1,0:T(8,128)(2,1)S(1)}, bf16[40,896]{1,0:T(8,128)(2,1)S(1)}, u32[]{:S(2)}, u32[]{:S(2)}) collective-permute-start(bf16[40,896]{1,0:T(8,128)(2,1)S(1)} %get-tuple-element.74), channel_id=1, source_target_pairs={{0,64},{32,96},{64,0},{96,32},{1,65},{33,97},{65,1},{97,33},{2,66}... | collective-permute-start | bytes 215048 | tf_op jit(solution)/shard_map/ppermute | solution.py:51
  115.0 2.6 %collective-permute-done.29.b2 = bf16[40,896]{1,0:T(8,128)(2,1)S(1)} collective-permute-done((bf16[40,896]{1,0:T(8,128)(2,1)S(1)}, bf16[40,896]{1,0:T(8,128)(2,1)S(1)}, u32[]{:S(2)}, u32[]{:S(2)}) %collective-permute-start.29) | collective-permute-done | bytes 71712 | tf_op jit(solution)/shard_map/ppermute | solution.py:51
  117.7 1.2 %shard_map.151 = bf16[64,768]{1,0:T(8,128)(2,1)} custom-call(f32[64,768]{1,0:T(8,128)S(1)} %get-tuple-element.49.hidden, bf16[4,64,40]{2,1,0:T(8,128)(2,1)S(1)} %get-tuple-element.47.first, bf16[4,64,40]{2,1,0:T(8,128)(2,1)S(1)} %get-tuple-element.48.second, bf16[40,896]{1,0:T(8,128)(2,1)S(1)} %get-tuple-element.71.b0, ...), custom_call_target="tpu_custom_call" | custom-call | flops 40000000 | bytes 2000000 | tf_op jit(solution)/shard_map/pallas_call | solution.py:647
  (38 shorter events, 0.5 us)
Async XLA Ops:
  0.0 47.8 %copy-start = (f32[6144,4]{0,1:T(4,128)S(1)}, f32[6144,4]{0,1:T(4,128)}, u32[]{:S(2)}) copy-start(f32[6144,4]{0,1:T(4,128)} %param.24) | copy-start | bytes 294916
  0.0 20.1 %collective-permute-start.4 = (bf16[6144,256]{1,0:T(8,128)(2,1)}, bf16[6144,256]{1,0:T(8,128)(2,1)}, u32[]{:S(2)}, u32[]{:S(2)}) collective-permute-start(bf16[6144,256]{1,0:T(8,128)(2,1)} %gate.1), channel_id=1, source_target_pairs={{0,1},{1,0},{2,3},{3,2},{4,5},{5,4},{6,7},{7,6},{8,9},{9,8},{10,11... | collective-permute-start | bytes 9437192 | tf_op jit(solution)/shard_map/ppermute | solution.py:59
  1.4 18.6 %collective-permute-start.5 = (bf16[6144,256]{1,0:T(8,128)(2,1)}, bf16[6144,256]{1,0:T(8,128)(2,1)}, u32[]{:S(2)}, u32[]{:S(2)}) collective-permute-start(bf16[6144,256]{1,0:T(8,128)(2,1)} %up.1), channel_id=1, source_target_pairs={{0,1},{1,0},{2,3},{3,2},{4,5},{5,4},{6,7},{7,6},{8,9},{9,8},{10,11... | collective-permute-start | bytes 9437192 | tf_op jit(solution)/shard_map/ppermute | solution.py:59
  1.4 7.0 %copy-start.5 = (s32[64,2]{0,1:T(2,128)S(1)}, s32[64,2]{0,1:T(2,128)}, u32[]{:S(2)}) copy-start(s32[64,2]{0,1:T(2,128)} %param.21) | copy-start | bytes 1540
  7.8 4.0 %collective-permute-start = (bf16[4,64,768]{2,1,0:T(8,128)(2,1)S(1)}, bf16[4,64,768]{2,1,0:T(8,128)(2,1)S(1)}, u32[]{:S(2)}, u32[]{:S(2)}) collective-permute-start(bf16[4,64,768]{2,1,0:T(8,128)(2,1)S(1)} %get-tuple-element.41), channel_id=1, source_target_pairs={{0,1},{1,0},{2,3},{3,2},{4,5},{5,4},{6,7},{7,6},{8,9},{9,8},{10,11... | collective-permute-start | bytes 1179656 | tf_op jit(solution)/shard_map/ppermute | solution.py:59
  8.5 7.2 %copy-start.4 = (bf16[6144]{0:T(1024)(128)(2,1)S(1)}, bf16[6144]{0:T(1024)(128)(2,1)}, u32[]{:S(2)}) copy-start(bf16[6144]{0:T(1024)(128)(2,1)} %param.23) | copy-start | bytes 36868
  11.8 5.3 %collective-permute-start.1 = (bf16[64,768]{1,0:T(8,128)(2,1)S(1)}, bf16[64,768]{1,0:T(8,128)(2,1)S(1)}, u32[]{:S(2)}, u32[]{:S(2)}) collective-permute-start(bf16[64,768]{1,0:T(8,128)(2,1)S(1)} %get-tuple-element.43), channel_id=1, source_target_pairs={{0,2},{2,0},{4,6},{6,4},{1,3},{3,1},{5,7},{7,5},{8,10},{10,8},{12,... | collective-permute-start | bytes 294920 | tf_op jit(solution)/shard_map/ppermute | solution.py:55
  13.2 5.0 %collective-permute-start.2 = (bf16[64,768]{1,0:T(8,128)(2,1)S(1)}, bf16[64,768]{1,0:T(8,128)(2,1)S(1)}, u32[]{:S(2)}, u32[]{:S(2)}) collective-permute-start(bf16[64,768]{1,0:T(8,128)(2,1)S(1)} %get-tuple-element.44), channel_id=1, source_target_pairs={{0,6},{2,4},{4,2},{6,0},{1,7},{3,5},{5,3},{7,1},{8,14},{10,12},{12... | collective-permute-start | bytes 294920 | tf_op jit(solution)/shard_map/ppermute | solution.py:55
  15.0 5.0 %collective-permute-start.3 = (bf16[64,768]{1,0:T(8,128)(2,1)S(1)}, bf16[64,768]{1,0:T(8,128)(2,1)S(1)}, u32[]{:S(2)}, u32[]{:S(2)}) collective-permute-start(bf16[64,768]{1,0:T(8,128)(2,1)S(1)} %get-tuple-element.45), channel_id=1, source_target_pairs={{0,4},{2,6},{4,0},{6,2},{1,5},{3,7},{5,1},{7,3},{8,12},{10,14},{12... | collective-permute-start | bytes 294920 | tf_op jit(solution)/shard_map/ppermute | solution.py:55
  15.7 4.4 %copy-start.3 = (bf16[64,768]{1,0:T(8,128)(2,1)S(1)}, bf16[64,768]{1,0:T(8,128)(2,1)}, u32[]{:S(2)}) copy-start(bf16[64,768]{1,0:T(8,128)(2,1)} %tokens.1) | copy-start | bytes 294916
  17.2 30.8 %collective-permute-start.15 = (bf16[4,256,768]{2,1,0:T(8,128)(2,1)S(1)}, bf16[4,256,768]{2,1,0:T(8,128)(2,1)}, u32[]{:S(2)}, u32[]{:S(2)}) collective-permute-start(bf16[4,256,768]{2,1,0:T(8,128)(2,1)S(1)} %get-tuple-element.54), channel_id=1, source_target_pairs={{0,1},{1,0},{2,3},{3,2},{4,5},{5,4},{6,7},{7,6},{8,9},{9,8},{10,11... | collective-permute-start | bytes 4718600 | tf_op jit(solution)/shard_map/ppermute | solution.py:59
  20.4 5.0 %collective-permute-start.6 = (bf16[40,768]{1,0:T(8,128)(2,1)S(1)}, bf16[40,768]{1,0:T(8,128)(2,1)S(1)}, u32[]{:S(2)}, u32[]{:S(2)}) collective-permute-start(bf16[40,768]{1,0:T(8,128)(2,1)S(1)} %get-tuple-element.51), channel_id=1, source_target_pairs={{0,32},{32,0},{64,96},{96,64},{1,33},{33,1},{65,97},{97,65},{2,34}... | collective-permute-start | bytes 184328 | tf_op jit(solution)/shard_map/ppermute | solution.py:51
  22.1 4.3 %collective-permute-start.7 = (bf16[40,768]{1,0:T(8,128)(2,1)S(1)}, bf16[40,768]{1,0:T(8,128)(2,1)S(1)}, u32[]{:S(2)}, u32[]{:S(2)}) collective-permute-start(bf16[40,768]{1,0:T(8,128)(2,1)S(1)} %get-tuple-element.52), channel_id=1, source_target_pairs={{0,96},{32,64},{64,32},{96,0},{1,97},{33,65},{65,33},{97,1},{2,98}... | collective-permute-start | bytes 184328 | tf_op jit(solution)/shard_map/ppermute | solution.py:51
  24.3 4.7 %collective-permute-start.8 = (bf16[40,768]{1,0:T(8,128)(2,1)S(1)}, bf16[40,768]{1,0:T(8,128)(2,1)S(1)}, u32[]{:S(2)}, u32[]{:S(2)}) collective-permute-start(bf16[40,768]{1,0:T(8,128)(2,1)S(1)} %get-tuple-element.53), channel_id=1, source_target_pairs={{0,64},{32,96},{64,0},{96,32},{1,65},{33,97},{65,1},{97,33},{2,66}... | collective-permute-start | bytes 184328 | tf_op jit(solution)/shard_map/ppermute | solution.py:51
  29.1 8.5 %collective-permute-start.10 = (bf16[160,768]{1,0:T(8,128)(2,1)S(1)}, bf16[160,768]{1,0:T(8,128)(2,1)S(1)}, u32[]{:S(2)}, u32[]{:S(2)}) collective-permute-start(bf16[160,768]{1,0:T(8,128)(2,1)S(1)} %constant_dynamic-update-slice_fusion.a), channel_id=1, source_target_pairs={{0,6},{1,25},{2,4},{3,27},{4,2},{5,29},{6,0},{7,31},{8,14},{9,17},... | collective-permute-start | bytes 737288 | tf_op jit(solution)/shard_map/ppermute | solution.py:43
  31.8 6.6 %collective-permute-start.11 = (bf16[160,768]{1,0:T(8,128)(2,1)S(1)}, bf16[160,768]{1,0:T(8,128)(2,1)S(1)}, u32[]{:S(2)}, u32[]{:S(2)}) collective-permute-start(bf16[160,768]{1,0:T(8,128)(2,1)S(1)} %constant_dynamic-update-slice_fusion.a), channel_id=1, source_target_pairs={{0,4},{1,17},{2,6},{3,19},{4,0},{5,21},{6,2},{7,23},{8,12},{9,25},... | collective-permute-start | bytes 737288 | tf_op jit(solution)/shard_map/ppermute | solution.py:43
  32.1 6.9 %collective-permute-start.9 = (bf16[160,768]{1,0:T(8,128)(2,1)S(1)}, bf16[160,768]{1,0:T(8,128)(2,1)S(1)}, u32[]{:S(2)}, u32[]{:S(2)}) collective-permute-start(bf16[160,768]{1,0:T(8,128)(2,1)S(1)} %constant_dynamic-update-slice_fusion.a), channel_id=1, source_target_pairs={{0,2},{1,9},{2,0},{3,11},{4,6},{5,13},{6,4},{7,15},{8,10},{9,1},{1... | collective-permute-start | bytes 737288 | tf_op jit(solution)/shard_map/ppermute | solution.py:43
  39.0 5.4 %collective-permute-start.12 = (f32[16,128]{1,0:T(8,128)S(1)}, f32[16,128]{1,0:T(8,128)S(1)}, u32[]{:S(2)}, u32[]{:S(2)}) collective-permute-start(f32[16,128]{1,0:T(8,128)S(1)} %convert_add_fusion), channel_id=1, source_target_pairs={{0,1},{1,0},{2,3},{3,2},{4,5},{5,4},{6,7},{7,6},{8,9},{9,8},{10,11... | collective-permute-start | bytes 24584 | tf_op jit(solution)/shard_map/ppermute | solution.py:59
  44.5 7.5 %copy-start.2 = (bf16[640,768]{1,0:T(8,128)(2,1)}, bf16[640,768]{1,0:T(8,128)(2,1)S(1)}, u32[]{:S(2)}) copy-start(bf16[640,768]{1,0:T(8,128)(2,1)S(1)} %shard_map.141.p0) | copy-start | bytes 2949124
  44.5 15.0 %collective-permute-start.16 = (bf16[640,768]{1,0:T(8,128)(2,1)S(1)}, bf16[640,768]{1,0:T(8,128)(2,1)}, u32[]{:S(2)}, u32[]{:S(2)}) collective-permute-start(bf16[640,768]{1,0:T(8,128)(2,1)S(1)} %shard_map.141.p0), channel_id=1, source_target_pairs={{0,16},{1,5},{2,18},{3,7},{4,20},{5,1},{6,22},{7,3},{8,24},{9,13},... | collective-permute-start | bytes 2949128 | tf_op jit(solution)/shard_map/ppermute | solution.py:47
  45.5 23.6 %collective-permute-start.13 = (bf16[640,768]{1,0:T(8,128)(2,1)S(1)}, bf16[640,768]{1,0:T(8,128)(2,1)}, u32[]{:S(2)}, u32[]{:S(2)}) collective-permute-start(bf16[640,768]{1,0:T(8,128)(2,1)S(1)} %shard_map.141.p0), channel_id=1, source_target_pairs={{0,8},{1,3},{2,10},{3,1},{4,12},{5,7},{6,14},{7,5},{8,0},{9,11},{1... | collective-permute-start | bytes 2949128 | tf_op jit(solution)/shard_map/ppermute | solution.py:47
  46.7 23.3 %collective-permute-start.14 = (bf16[640,768]{1,0:T(8,128)(2,1)S(1)}, bf16[640,768]{1,0:T(8,128)(2,1)}, u32[]{:S(2)}, u32[]{:S(2)}) collective-permute-start(bf16[640,768]{1,0:T(8,128)(2,1)S(1)} %shard_map.141.p0), channel_id=1, source_target_pairs={{0,24},{1,7},{2,26},{3,5},{4,28},{5,3},{6,30},{7,1},{8,16},{9,15},... | collective-permute-start | bytes 2949128 | tf_op jit(solution)/shard_map/ppermute | solution.py:47
  73.1 4.3 %collective-permute-start.17 = (bf16[640,768]{1,0:T(8,128)(2,1)S(1)}, bf16[640,768]{1,0:T(8,128)(2,1)S(1)}, u32[]{:S(2)}, u32[]{:S(2)}) collective-permute-start(bf16[640,768]{1,0:T(8,128)(2,1)S(1)} %get-tuple-element.60), channel_id=1, source_target_pairs={{0,1},{1,0},{2,3},{3,2},{4,5},{5,4},{6,7},{7,6},{8,9},{9,8},{10,11... | collective-permute-start | bytes 2949128 | tf_op jit(solution)/shard_map/ppermute | solution.py:59
  77.9 1.7 %collective-permute-start.18 = (bf16[640,256]{1,0:T(8,128)(2,1)S(1)}, bf16[640,256]{1,0:T(8,128)(2,1)S(1)}, u32[]{:S(2)}, u32[]{:S(2)}) collective-permute-start(bf16[640,256]{1,0:T(8,128)(2,1)S(1)} %get-tuple-element.61.act), channel_id=1, source_target_pairs={{0,1},{1,0},{2,3},{3,2},{4,5},{5,4},{6,7},{7,6},{8,9},{9,8},{10,11... | collective-permute-start | bytes 983048 | tf_op jit(solution)/shard_map/ppermute | solution.py:59
  80.1 12.2 %collective-permute-start.22 = (bf16[480,768]{1,0:T(8,128)(2,1)S(1)}, bf16[480,768]{1,0:T(8,128)(2,1)S(1)}, u32[]{:S(2)}, u32[]{:S(2)}) collective-permute-start(bf16[480,768]{1,0:T(8,128)(2,1)S(1)} %shard_map.148), channel_id=1, source_target_pairs={{0,16},{1,5},{2,18},{3,7},{4,20},{5,1},{6,22},{7,3},{8,24},{9,13},... | collective-permute-start | bytes 2211848 | tf_op jit(solution)/shard_map/ppermute | solution.py:47
  82.1 17.3 %collective-permute-start.23 = (bf16[480,768]{1,0:T(8,128)(2,1)S(1)}, bf16[480,768]{1,0:T(8,128)(2,1)S(1)}, u32[]{:S(2)}, u32[]{:S(2)}) collective-permute-start(bf16[480,768]{1,0:T(8,128)(2,1)S(1)} %get-tuple-element.69), channel_id=1, source_target_pairs={{0,8},{1,3},{2,10},{3,1},{4,12},{5,7},{6,14},{7,5},{8,0},{9,11},{1... | collective-permute-start | bytes 2211848 | tf_op jit(solution)/shard_map/ppermute | solution.py:47
  83.4 16.9 %collective-permute-start.24 = (bf16[480,768]{1,0:T(8,128)(2,1)S(1)}, bf16[480,768]{1,0:T(8,128)(2,1)S(1)}, u32[]{:S(2)}, u32[]{:S(2)}) collective-permute-start(bf16[480,768]{1,0:T(8,128)(2,1)S(1)} %get-tuple-element.70), channel_id=1, source_target_pairs={{0,24},{1,7},{2,26},{3,5},{4,28},{5,3},{6,30},{7,1},{8,16},{9,15},... | collective-permute-start | bytes 2211848 | tf_op jit(solution)/shard_map/ppermute | solution.py:47
  85.6 17.7 %collective-permute-start.19 = (bf16[160,768]{1,0:T(8,128)(2,1)S(1)}, bf16[160,768]{1,0:T(8,128)(2,1)S(1)}, u32[]{:S(2)}, u32[]{:S(2)}) collective-permute-start(bf16[160,768]{1,0:T(8,128)(2,1)S(1)} %get-tuple-element.65), channel_id=1, source_target_pairs={{0,16},{1,5},{2,18},{3,7},{4,20},{5,1},{6,22},{7,3},{8,24},{9,13},... | collective-permute-start | bytes 737288 | tf_op jit(solution)/shard_map/ppermute | solution.py:47
  86.6 18.6 %collective-permute-start.20 = (bf16[160,768]{1,0:T(8,128)(2,1)S(1)}, bf16[160,768]{1,0:T(8,128)(2,1)S(1)}, u32[]{:S(2)}, u32[]{:S(2)}) collective-permute-start(bf16[160,768]{1,0:T(8,128)(2,1)S(1)} %get-tuple-element.66), channel_id=1, source_target_pairs={{0,8},{1,3},{2,10},{3,1},{4,12},{5,7},{6,14},{7,5},{8,0},{9,11},{1... | collective-permute-start | bytes 737288 | tf_op jit(solution)/shard_map/ppermute | solution.py:47
  92.4 13.1 %collective-permute-start.21 = (bf16[160,768]{1,0:T(8,128)(2,1)S(1)}, bf16[160,768]{1,0:T(8,128)(2,1)S(1)}, u32[]{:S(2)}, u32[]{:S(2)}) collective-permute-start(bf16[160,768]{1,0:T(8,128)(2,1)S(1)} %get-tuple-element.67), channel_id=1, source_target_pairs={{0,24},{1,7},{2,26},{3,5},{4,28},{5,3},{6,30},{7,1},{8,16},{9,15},... | collective-permute-start | bytes 737288 | tf_op jit(solution)/shard_map/ppermute | solution.py:47
  100.6 18.3 %copy-start.1 = (f32[6144,4]{0,1:T(4,128)S(1)}, f32[6144,4]{0,1:T(4,128)}, u32[]{:S(2)}) copy-start(f32[6144,4]{0,1:T(4,128)} %param.24) | copy-start | bytes 294916
  100.7 8.1 %collective-permute-start.25 = (bf16[160,768]{1,0:T(8,128)(2,1)S(1)}, bf16[160,768]{1,0:T(8,128)(2,1)S(1)}, u32[]{:S(2)}, u32[]{:S(2)}) collective-permute-start(bf16[160,768]{1,0:T(8,128)(2,1)S(1)} %get-tuple-element.77), channel_id=1, source_target_pairs={{0,2},{1,9},{2,0},{3,11},{4,6},{5,13},{6,4},{7,15},{8,10},{9,1},{1... | collective-permute-start | bytes 737288 | tf_op jit(solution)/shard_map/ppermute | solution.py:43
  101.6 7.2 %collective-permute-start.26 = (bf16[160,768]{1,0:T(8,128)(2,1)S(1)}, bf16[160,768]{1,0:T(8,128)(2,1)S(1)}, u32[]{:S(2)}, u32[]{:S(2)}) collective-permute-start(bf16[160,768]{1,0:T(8,128)(2,1)S(1)} %get-tuple-element.76), channel_id=1, source_target_pairs={{0,6},{1,25},{2,4},{3,27},{4,2},{5,29},{6,0},{7,31},{8,14},{9,17},... | collective-permute-start | bytes 737288 | tf_op jit(solution)/shard_map/ppermute | solution.py:43
  103.3 8.2 %collective-permute-start.27 = (bf16[160,768]{1,0:T(8,128)(2,1)S(1)}, bf16[160,768]{1,0:T(8,128)(2,1)S(1)}, u32[]{:S(2)}, u32[]{:S(2)}) collective-permute-start(bf16[160,768]{1,0:T(8,128)(2,1)S(1)} %get-tuple-element.75), channel_id=1, source_target_pairs={{0,4},{1,17},{2,6},{3,19},{4,0},{5,21},{6,2},{7,23},{8,12},{9,25},... | collective-permute-start | bytes 737288 | tf_op jit(solution)/shard_map/ppermute | solution.py:43
  111.7 3.3 %collective-permute-start.28 = (bf16[40,896]{1,0:T(8,128)(2,1)S(1)}, bf16[40,896]{1,0:T(8,128)(2,1)S(1)}, u32[]{:S(2)}, u32[]{:S(2)}) collective-permute-start(bf16[40,896]{1,0:T(8,128)(2,1)S(1)} %get-tuple-element.72), channel_id=1, source_target_pairs={{0,32},{32,0},{64,96},{96,64},{1,33},{33,1},{65,97},{97,65},{2,34}... | collective-permute-start | bytes 215048 | tf_op jit(solution)/shard_map/ppermute | solution.py:51
  112.5 5.2 %collective-permute-start.29 = (bf16[40,896]{1,0:T(8,128)(2,1)S(1)}, bf16[40,896]{1,0:T(8,128)(2,1)S(1)}, u32[]{:S(2)}, u32[]{:S(2)}) collective-permute-start(bf16[40,896]{1,0:T(8,128)(2,1)S(1)} %get-tuple-element.73), channel_id=1, source_target_pairs={{0,96},{32,64},{64,32},{96,0},{1,97},{33,65},{65,33},{97,1},{2,98}... | collective-permute-start | bytes 215048 | tf_op jit(solution)/shard_map/ppermute | solution.py:51
  112.9 4.8 %collective-permute-start.30 = (bf16[40,896]{1,0:T(8,128)(2,1)S(1)}, bf16[40,896]{1,0:T(8,128)(2,1)S(1)}, u32[]{:S(2)}, u32[]{:S(2)}) collective-permute-start(bf16[40,896]{1,0:T(8,128)(2,1)S(1)} %get-tuple-element.74), channel_id=1, source_target_pairs={{0,64},{32,96},{64,0},{96,32},{1,65},{33,97},{65,1},{97,33},{2,66}... | collective-permute-start | bytes 215048 | tf_op jit(solution)/shard_map/ppermute | solution.py:51
